TPU v7x, 32 devices: a whole 2x2x4 slice. The times are simulated.
32 devices in a mesh: band: 2 (over y), row: 4 (over z), col: 4 (over x, core).
Axes of the slice: x: 2, y: 2, z: 4, core: 2. Of those that a mesh axis runs over, the one named last changes fastest.
Arguments:
- source: float32 [3, 512, 4096], P(None, ('band', 'row'), 'col'), parts along dimension 1, may hold values from -50 to 50
- weight: float32 [512, 4096], P(('band', 'row'), 'col'), parts along dimension 0, may hold values from 0.05 to 0.15
- seam_right: int32 [512, 4096], P(('band', 'row'), 'col'), parts along dimension 0, may hold values 0 or 1
- seam_down: int32 [512, 4096], P(('band', 'row'), 'col'), parts along dimension 0, may hold values 0 or 1
- offsets: int32 [2, 16, 3], P('band'), parts along dimension 0, may hold values from -64 to 64
Outputs:
- solution: float32 [3, 512, 4096], P(None, ('band', 'row'), 'col'), parts along dimension 1
- residual: float32 [3, 512, 4096], P(None, ('band', 'row'), 'col'), parts along dimension 1
- smoothed: float32 [3, 512, 4096], P(None, ('band', 'row'), 'col'), parts along dimension 1
There are 2 independent parts, one for each index of `band`. A program takes and returns all parts, laid end to end along the dimension named above; each array names one. Nothing has to cross between parts.
All inputs are finite; a program needn't handle non-finite values. No bound on the sum of `seam_right` or of `seam_down` on one device may be relied on, other than what follows from the above.
Results may differ from a plain program's by a relative error of at most 0.0003.
Values sent between devices are 32-bit elements; how exact they have to be, the bound alone decides.
No kernel may reach another device: no remote copies, remote signals or barrier semaphores. Data moves between devices by JAX's collectives and lax.ppermute only.
A program may use at most 64 MiB of HBM per device.

v0:
```python
import jax
import jax.numpy as jnp
from jax import lax
from jax.sharding import PartitionSpec as P

TILE = 256
ITERS = 2
SWEEPS = 8


seam_damping = 0.8
offset_unit = 32.0
spectrum_low = 0.08
spectrum_high = 2.0


def with_halo(value, sides, width):
    for axis, dim in sides:
        size, length = (lax.axis_size(axis), value.shape[dim])
        up = [(i, (i + 1) % size) for i in range(size - 1)]
        down = [(j, i) for i, j in up]
        last = lax.slice_in_dim(value, length - width, length, axis=dim)
        first = lax.slice_in_dim(value, 0, width, axis=dim)
        before = lax.ppermute(last, axis, up)
        after = lax.ppermute(first, axis, down)
        value = jnp.concatenate([before, value, after], axis=dim)
    return value


def from_behind(value, axis, by):
    length = lax.axis_size(axis)
    pairs = [(i, i + by) for i in range(length) if 0 <= i + by < length]
    return lax.ppermute(value, axis, pairs)


def apply_operator(values, coefficients):
    diagonal, cond_right, cond_left, cond_down, cond_up = coefficients
    padded = with_halo(values, (("row", 1), ("col", 2)), 1)
    neighbours = (
        cond_right * padded[:, 1:-1, 2:]
        + cond_left * padded[:, 1:-1, :-2]
        + cond_down * padded[:, 2:, 1:-1]
        + cond_up * padded[:, :-2, 1:-1]
    )
    return diagonal * values - neighbours


def chebyshev(residual, inverse, coefficients):
    centre = (spectrum_high + spectrum_low) / 2.0
    radius = (spectrum_high - spectrum_low) / 2.0
    sigma_ratio = centre / radius
    update = residual * inverse / centre
    smoothed = update
    recurrence = 1.0 / sigma_ratio
    for sweep_index in range(SWEEPS - 1):
        remainder = residual - apply_operator(smoothed, coefficients)
        following = 1.0 / (2.0 * sigma_ratio - recurrence)
        update = following * recurrence * update + 2.0 * following / radius * inverse * remainder
        smoothed = smoothed + update
        recurrence = following
    return smoothed


def per_device(source, weight, seam_right, seam_down, offsets):
    rows_dev, cols_dev = weight.shape
    total_rows = rows_dev * lax.axis_size("row")
    total_cols = cols_dev * lax.axis_size("col")
    row_index = lax.axis_index("row") * rows_dev + jnp.arange(rows_dev, dtype=jnp.int32)
    col_index = lax.axis_index("col") * cols_dev + jnp.arange(cols_dev, dtype=jnp.int32)
    cond_right = jnp.where(
        col_index[None, :] < total_cols - 1,
        1.0 - seam_damping * seam_right.astype(jnp.float32),
        jnp.float32(0.0),
    )
    cond_down = jnp.where(
        row_index[:, None] < total_rows - 1,
        1.0 - seam_damping * seam_down.astype(jnp.float32),
        jnp.float32(0.0),
    )
    left_column = from_behind(cond_right[:, -1], "col", 1)
    cond_left = jnp.concatenate([left_column[:, None], cond_right[:, :-1]], axis=1)
    upper_row = from_behind(cond_down[-1, :], "row", 1)
    cond_up = jnp.concatenate([upper_row[None, :], cond_down[:-1, :]], axis=0)
    diagonal = weight + cond_right + cond_left + cond_down + cond_up
    inverse = 1.0 / diagonal
    coefficients = (diagonal, cond_right, cond_left, cond_down, cond_up)
    tile_rows = offsets.shape[0]
    tile_cols = offsets.shape[1]
    row_pick = (
        row_index[:, None] // TILE == jnp.arange(tile_rows, dtype=jnp.int32)[None, :]
    ).astype(jnp.float32)
    col_pick = (
        col_index[:, None] // TILE == jnp.arange(tile_cols, dtype=jnp.int32)[None, :]
    ).astype(jnp.float32)
    offset_field = jnp.einsum(
        "it,tuc,ju->cij",
        row_pick,
        offsets.astype(jnp.float32),
        col_pick,
        precision=lax.Precision.HIGHEST,
    )
    right_side = source + offset_field / offset_unit

    def precondition(residual):
        return chebyshev(residual, inverse, coefficients)

    solution = jnp.zeros_like(right_side)
    residual = right_side

    def inner_sum(residual, smoothed):
        return lax.psum(jnp.sum(residual * smoothed), ("row", "col"))

    smoothed = precondition(residual)
    direction = smoothed
    inner_now = inner_sum(residual, smoothed)
    for iteration in range(ITERS):
        applied = apply_operator(direction, coefficients)
        step_size = inner_now / lax.psum(jnp.sum(direction * applied), ("row", "col"))
        solution = solution + step_size * direction
        residual = residual - step_size * applied
        smoothed = precondition(residual)
        if iteration + 1 < ITERS:
            inner_next = inner_sum(residual, smoothed)
            direction = smoothed + inner_next / inner_now * direction
            inner_now = inner_next
    return (solution, residual, smoothed)


def solution(mesh):
    placed = (
        P(None, ("band", "row"), "col"),
        P(("band", "row"), "col"),
        P(("band", "row"), "col"),
        P(("band", "row"), "col"),
        P("band", None, None),
    )
    return jax.shard_map(
        per_device,
        mesh=mesh,
        in_specs=placed,
        out_specs=(
            P(None, ("band", "row"), "col"),
            P(None, ("band", "row"), "col"),
            P(None, ("band", "row"), "col"),
        ),
        check_vma=False,
    )
```

profile of v0, /device:TPU:0, one launch (start us, length us, event | category | flops | bytes accessed | tf_op | source)
XLA Modules:
  0.0 510.3 jit_solution(17491365418668147562)
XLA Ops:
  12.9 4.8 collective-permute-start.2
  26.6 4.8 collective-permute-start.6
  50.5 6.0 %collective-permute-start.13 = (f32[3,66,1]{2,1,0:T(8,128)S(1)}, f32[3,66,1]{2,1,0:T(8,128)S(1)}, u32[]{:S(2)}, u32[]{:S(2)}) collective-permute-start(f32[3,66,1]{2,1,0:T(8,128)S(1)} %get-tuple-element.80), channel_id=1, source_target_pairs={{0,1},{1,2},{2,3},{4,5},{5,6},{6,7},{8,9},{9,10},{10,11},{12,13},{... | collective-permute-start | bytes 2384 | tf_op jit(solution)/shard_map/ppermute | solution.py:24
  67.0 6.1 %collective-permute-start.17 = (f32[3,66,1]{2,1,0:T(8,128)S(1)}, f32[3,66,1]{2,1,0:T(8,128)S(1)}, u32[]{:S(2)}, u32[]{:S(2)}) collective-permute-start(f32[3,66,1]{2,1,0:T(8,128)S(1)} %get-tuple-element.78), channel_id=1, source_target_pairs={{0,1},{1,2},{2,3},{4,5},{5,6},{6,7},{8,9},{9,10},{10,11},{12,13},{... | collective-permute-start | bytes 2384 | tf_op jit(solution)/shard_map/ppermute | solution.py:24
  85.6 6.0 %collective-permute-start.21 = (f32[3,66,1]{2,1,0:T(8,128)S(1)}, f32[3,66,1]{2,1,0:T(8,128)S(1)}, u32[]{:S(2)}, u32[]{:S(2)}) collective-permute-start(f32[3,66,1]{2,1,0:T(8,128)S(1)} %get-tuple-element.76), channel_id=1, source_target_pairs={{0,1},{1,2},{2,3},{4,5},{5,6},{6,7},{8,9},{9,10},{10,11},{12,13},{... | collective-permute-start | bytes 2384 | tf_op jit(solution)/shard_map/ppermute | solution.py:24
  102.0 6.0 %collective-permute-start.25 = (f32[3,66,1]{2,1,0:T(8,128)S(1)}, f32[3,66,1]{2,1,0:T(8,128)S(1)}, u32[]{:S(2)}, u32[]{:S(2)}) collective-permute-start(f32[3,66,1]{2,1,0:T(8,128)S(1)} %get-tuple-element.74), channel_id=1, source_target_pairs={{0,1},{1,2},{2,3},{4,5},{5,6},{6,7},{8,9},{9,10},{10,11},{12,13},{... | collective-permute-start | bytes 2384 | tf_op jit(solution)/shard_map/ppermute | solution.py:24
  120.6 6.0 %collective-permute-start.29 = (f32[3,66,1]{2,1,0:T(8,128)S(1)}, f32[3,66,1]{2,1,0:T(8,128)S(1)}, u32[]{:S(2)}, u32[]{:S(2)}) collective-permute-start(f32[3,66,1]{2,1,0:T(8,128)S(1)} %get-tuple-element.72), channel_id=1, source_target_pairs={{0,1},{1,2},{2,3},{4,5},{5,6},{6,7},{8,9},{9,10},{10,11},{12,13},{... | collective-permute-start | bytes 2384 | tf_op jit(solution)/shard_map/ppermute | solution.py:24
  137.2 6.0 %collective-permute-start.33 = (f32[3,66,1]{2,1,0:T(8,128)S(1)}, f32[3,66,1]{2,1,0:T(8,128)S(1)}, u32[]{:S(2)}, u32[]{:S(2)}) collective-permute-start(f32[3,66,1]{2,1,0:T(8,128)S(1)} %get-tuple-element.70), channel_id=1, source_target_pairs={{0,1},{1,2},{2,3},{4,5},{5,6},{6,7},{8,9},{9,10},{10,11},{12,13},{... | collective-permute-start | bytes 2384 | tf_op jit(solution)/shard_map/ppermute | solution.py:24
  146.5 38.4 %all-reduce = (f32[]{:T(128)}, f32[]{:T(128)}) all-reduce(f32[]{:T(128)} %get-tuple-element.4, f32[]{:T(128)} %get-tuple-element.3), channel_id=1, replica_groups=mesh['band'=2,'row'=4,'col'=4] {'row','col'}, use_global_device_ids=true, to_apply=%region_1.2 | all-reduce | flops 2 | bytes 16 | tf_op jit(solution)/shard_map/psum | solution.py:111
  188.9 4.7 collective-permute-start.34
  202.5 5.0 collective-permute-start.38
  218.1 5.0 collective-permute-start.42
  225.8 5.2 %collective-permute-start.45 = (f32[3,66,1]{2,1,0:T(8,128)S(1)}, f32[3,66,1]{2,1,0:T(8,128)S(1)}, u32[]{:S(2)}, u32[]{:S(2)}) collective-permute-start(f32[3,66,1]{2,1,0:T(8,128)S(1)} %get-tuple-element.64), channel_id=1, source_target_pairs={{0,1},{1,2},{2,3},{4,5},{5,6},{6,7},{8,9},{9,10},{10,11},{12,13},{... | collective-permute-start | bytes 2384 | tf_op jit(solution)/shard_map/ppermute | solution.py:24
  234.1 4.7 collective-permute-start.46
  241.6 6.0 %collective-permute-start.49 = (f32[3,66,1]{2,1,0:T(8,128)S(1)}, f32[3,66,1]{2,1,0:T(8,128)S(1)}, u32[]{:S(2)}, u32[]{:S(2)}) collective-permute-start(f32[3,66,1]{2,1,0:T(8,128)S(1)} %get-tuple-element.62), channel_id=1, source_target_pairs={{0,1},{1,2},{2,3},{4,5},{5,6},{6,7},{8,9},{9,10},{10,11},{12,13},{... | collective-permute-start | bytes 2384 | tf_op jit(solution)/shard_map/ppermute | solution.py:24
  260.0 6.0 %collective-permute-start.53 = (f32[3,66,1]{2,1,0:T(8,128)S(1)}, f32[3,66,1]{2,1,0:T(8,128)S(1)}, u32[]{:S(2)}, u32[]{:S(2)}) collective-permute-start(f32[3,66,1]{2,1,0:T(8,128)S(1)} %get-tuple-element.60), channel_id=1, source_target_pairs={{0,1},{1,2},{2,3},{4,5},{5,6},{6,7},{8,9},{9,10},{10,11},{12,13},{... | collective-permute-start | bytes 2384 | tf_op jit(solution)/shard_map/ppermute | solution.py:24
  269.1 4.7 collective-permute-start.54
  276.5 6.0 %collective-permute-start.57 = (f32[3,66,1]{2,1,0:T(8,128)S(1)}, f32[3,66,1]{2,1,0:T(8,128)S(1)}, u32[]{:S(2)}, u32[]{:S(2)}) collective-permute-start(f32[3,66,1]{2,1,0:T(8,128)S(1)} %get-tuple-element.58), channel_id=1, source_target_pairs={{0,1},{1,2},{2,3},{4,5},{5,6},{6,7},{8,9},{9,10},{10,11},{12,13},{... | collective-permute-start | bytes 2384 | tf_op jit(solution)/shard_map/ppermute | solution.py:24
  287.6 4.7 collective-permute-start.58
  295.1 6.0 %collective-permute-start.61 = (f32[3,66,1]{2,1,0:T(8,128)S(1)}, f32[3,66,1]{2,1,0:T(8,128)S(1)}, u32[]{:S(2)}, u32[]{:S(2)}) collective-permute-start(f32[3,66,1]{2,1,0:T(8,128)S(1)} %get-tuple-element.56), channel_id=1, source_target_pairs={{0,1},{1,2},{2,3},{4,5},{5,6},{6,7},{8,9},{9,10},{10,11},{12,13},{... | collective-permute-start | bytes 2384 | tf_op jit(solution)/shard_map/ppermute | solution.py:24
  304.3 38.4 %psum.30 = f32[]{:T(128)} all-reduce(f32[]{:T(128)} %get-tuple-element.17), channel_id=1, replica_groups=mesh['band'=2,'row'=4,'col'=4] {'row','col'}, use_global_device_ids=true, to_apply=%region_5.6 | all-reduce | flops 1 | bytes 8 | tf_op jit(solution)/shard_map/psum | solution.py:111
  360.3 30.9 %psum.31 = f32[]{:T(128)} all-reduce(f32[]{:T(128)} %get-tuple-element.15), channel_id=1, replica_groups=mesh['band'=2,'row'=4,'col'=4] {'row','col'}, use_global_device_ids=true, to_apply=%region_7.8 | all-reduce | flops 1 | bytes 8 | tf_op jit(solution)/shard_map/psum | solution.py:118
  395.2 4.7 collective-permute-start.66
  408.8 5.0 collective-permute-start.70
  424.4 5.0 collective-permute-start.74
  432.1 5.2 %collective-permute-start.77 = (f32[3,66,1]{2,1,0:T(8,128)S(1)}, f32[3,66,1]{2,1,0:T(8,128)S(1)}, u32[]{:S(2)}, u32[]{:S(2)}) collective-permute-start(f32[3,66,1]{2,1,0:T(8,128)S(1)} %get-tuple-element.48), channel_id=1, source_target_pairs={{0,1},{1,2},{2,3},{4,5},{5,6},{6,7},{8,9},{9,10},{10,11},{12,13},{... | collective-permute-start | bytes 2384 | tf_op jit(solution)/shard_map/ppermute | solution.py:24
  440.4 4.7 collective-permute-start.78
  447.9 6.0 %collective-permute-start.81 = (f32[3,66,1]{2,1,0:T(8,128)S(1)}, f32[3,66,1]{2,1,0:T(8,128)S(1)}, u32[]{:S(2)}, u32[]{:S(2)}) collective-permute-start(f32[3,66,1]{2,1,0:T(8,128)S(1)} %get-tuple-element.46), channel_id=1, source_target_pairs={{0,1},{1,2},{2,3},{4,5},{5,6},{6,7},{8,9},{9,10},{10,11},{12,13},{... | collective-permute-start | bytes 2384 | tf_op jit(solution)/shard_map/ppermute | solution.py:24
  466.3 6.0 %collective-permute-start.85 = (f32[3,66,1]{2,1,0:T(8,128)S(1)}, f32[3,66,1]{2,1,0:T(8,128)S(1)}, u32[]{:S(2)}, u32[]{:S(2)}) collective-permute-start(f32[3,66,1]{2,1,0:T(8,128)S(1)} %get-tuple-element.44), channel_id=1, source_target_pairs={{0,1},{1,2},{2,3},{4,5},{5,6},{6,7},{8,9},{9,10},{10,11},{12,13},{... | collective-permute-start | bytes 2384 | tf_op jit(solution)/shard_map/ppermute | solution.py:24
  475.4 4.7 collective-permute-start.86
  482.9 6.0 %collective-permute-start.89 = (f32[3,66,1]{2,1,0:T(8,128)S(1)}, f32[3,66,1]{2,1,0:T(8,128)S(1)}, u32[]{:S(2)}, u32[]{:S(2)}) collective-permute-start(f32[3,66,1]{2,1,0:T(8,128)S(1)} %get-tuple-element.42), channel_id=1, source_target_pairs={{0,1},{1,2},{2,3},{4,5},{5,6},{6,7},{8,9},{9,10},{10,11},{12,13},{... | collective-permute-start | bytes 2384 | tf_op jit(solution)/shard_map/ppermute | solution.py:24
  501.5 6.2 %collective-permute-start.93 = (f32[3,66,1]{2,1,0:T(8,128)S(1)}, f32[3,66,1]{2,1,0:T(8,128)S(1)}, u32[]{:S(2)}, u32[]{:S(2)}) collective-permute-start(f32[3,66,1]{2,1,0:T(8,128)S(1)} %get-tuple-element.40), channel_id=1, source_target_pairs={{0,1},{1,2},{2,3},{4,5},{5,6},{6,7},{8,9},{9,10},{10,11},{12,13},{... | collective-permute-start | bytes 2384 | tf_op jit(solution)/shard_map/ppermute | solution.py:24
  (312 shorter events, 238.9 us)
Async XLA Ops:
  1.9 7.5 %collective-permute-start = (f32[64]{0:T(128)S(1)}, f32[64]{0:T(128)S(1)}, u32[]{:S(2)}, u32[]{:S(2)}) collective-permute-start(f32[64]{0:T(128)S(1)} %slice_reduce_fusion), channel_id=1, source_target_pairs={{0,1},{1,2},{2,3},{4,5},{5,6},{6,7},{8,9},{9,10},{10,11},{12,13},{... | collective-permute-start | bytes 776 | tf_op jit(solution)/shard_map/ppermute | solution.py:33
  11.6 6.4 %collective-permute-start.3 = (f32[3,1,1024]{2,1,0:T(1,128)S(1)}, f32[3,1,1024]{2,1,0:T(1,128)S(1)}, u32[]{:S(2)}, u32[]{:S(2)}) collective-permute-start(f32[3,1,1024]{2,1,0:T(1,128)S(1)} %get-tuple-element.131), channel_id=1, source_target_pairs={{4,0},{8,4},{12,8},{5,1},{9,5},{13,9},{6,2},{10,6},{14,10},{7,3},{... | collective-permute-start | bytes 36872 | tf_op jit(solution)/shard_map/ppermute | solution.py:25
  49.2 7.3 %collective-permute-start.12 = (f32[3,66,1]{2,1,0:T(8,128)S(1)}, f32[3,66,1]{2,1,0:T(8,128)S(1)}, u32[]{:S(2)}, u32[]{:S(2)}) collective-permute-start(f32[3,66,1]{2,1,0:T(8,128)S(1)} %get-tuple-element.79), channel_id=1, source_target_pairs={{1,0},{2,1},{3,2},{5,4},{6,5},{7,6},{9,8},{10,9},{11,10},{13,12},{... | collective-permute-start | bytes 2384 | tf_op jit(solution)/shard_map/ppermute | solution.py:25
  50.5 7.0 %collective-permute-start.13 = (f32[3,66,1]{2,1,0:T(8,128)S(1)}, f32[3,66,1]{2,1,0:T(8,128)S(1)}, u32[]{:S(2)}, u32[]{:S(2)}) collective-permute-start(f32[3,66,1]{2,1,0:T(8,128)S(1)} %get-tuple-element.80), channel_id=1, source_target_pairs={{0,1},{1,2},{2,3},{4,5},{5,6},{6,7},{8,9},{9,10},{10,11},{12,13},{... | collective-permute-start | bytes 2384 | tf_op jit(solution)/shard_map/ppermute | solution.py:24
  65.7 7.4 %collective-permute-start.16 = (f32[3,66,1]{2,1,0:T(8,128)S(1)}, f32[3,66,1]{2,1,0:T(8,128)S(1)}, u32[]{:S(2)}, u32[]{:S(2)}) collective-permute-start(f32[3,66,1]{2,1,0:T(8,128)S(1)} %get-tuple-element.77), channel_id=1, source_target_pairs={{1,0},{2,1},{3,2},{5,4},{6,5},{7,6},{9,8},{10,9},{11,10},{13,12},{... | collective-permute-start | bytes 2384 | tf_op jit(solution)/shard_map/ppermute | solution.py:25
  67.0 7.0 %collective-permute-start.17 = (f32[3,66,1]{2,1,0:T(8,128)S(1)}, f32[3,66,1]{2,1,0:T(8,128)S(1)}, u32[]{:S(2)}, u32[]{:S(2)}) collective-permute-start(f32[3,66,1]{2,1,0:T(8,128)S(1)} %get-tuple-element.78), channel_id=1, source_target_pairs={{0,1},{1,2},{2,3},{4,5},{5,6},{6,7},{8,9},{9,10},{10,11},{12,13},{... | collective-permute-start | bytes 2384 | tf_op jit(solution)/shard_map/ppermute | solution.py:24
  84.3 7.3 %collective-permute-start.20 = (f32[3,66,1]{2,1,0:T(8,128)S(1)}, f32[3,66,1]{2,1,0:T(8,128)S(1)}, u32[]{:S(2)}, u32[]{:S(2)}) collective-permute-start(f32[3,66,1]{2,1,0:T(8,128)S(1)} %get-tuple-element.75), channel_id=1, source_target_pairs={{1,0},{2,1},{3,2},{5,4},{6,5},{7,6},{9,8},{10,9},{11,10},{13,12},{... | collective-permute-start | bytes 2384 | tf_op jit(solution)/shard_map/ppermute | solution.py:25
  85.6 7.0 %collective-permute-start.21 = (f32[3,66,1]{2,1,0:T(8,128)S(1)}, f32[3,66,1]{2,1,0:T(8,128)S(1)}, u32[]{:S(2)}, u32[]{:S(2)}) collective-permute-start(f32[3,66,1]{2,1,0:T(8,128)S(1)} %get-tuple-element.76), channel_id=1, source_target_pairs={{0,1},{1,2},{2,3},{4,5},{5,6},{6,7},{8,9},{9,10},{10,11},{12,13},{... | collective-permute-start | bytes 2384 | tf_op jit(solution)/shard_map/ppermute | solution.py:24
  100.7 7.3 %collective-permute-start.24 = (f32[3,66,1]{2,1,0:T(8,128)S(1)}, f32[3,66,1]{2,1,0:T(8,128)S(1)}, u32[]{:S(2)}, u32[]{:S(2)}) collective-permute-start(f32[3,66,1]{2,1,0:T(8,128)S(1)} %get-tuple-element.73), channel_id=1, source_target_pairs={{1,0},{2,1},{3,2},{5,4},{6,5},{7,6},{9,8},{10,9},{11,10},{13,12},{... | collective-permute-start | bytes 2384 | tf_op jit(solution)/shard_map/ppermute | solution.py:25
  102.0 7.0 %collective-permute-start.25 = (f32[3,66,1]{2,1,0:T(8,128)S(1)}, f32[3,66,1]{2,1,0:T(8,128)S(1)}, u32[]{:S(2)}, u32[]{:S(2)}) collective-permute-start(f32[3,66,1]{2,1,0:T(8,128)S(1)} %get-tuple-element.74), channel_id=1, source_target_pairs={{0,1},{1,2},{2,3},{4,5},{5,6},{6,7},{8,9},{9,10},{10,11},{12,13},{... | collective-permute-start | bytes 2384 | tf_op jit(solution)/shard_map/ppermute | solution.py:24
  119.3 7.3 %collective-permute-start.28 = (f32[3,66,1]{2,1,0:T(8,128)S(1)}, f32[3,66,1]{2,1,0:T(8,128)S(1)}, u32[]{:S(2)}, u32[]{:S(2)}) collective-permute-start(f32[3,66,1]{2,1,0:T(8,128)S(1)} %get-tuple-element.71), channel_id=1, source_target_pairs={{1,0},{2,1},{3,2},{5,4},{6,5},{7,6},{9,8},{10,9},{11,10},{13,12},{... | collective-permute-start | bytes 2384 | tf_op jit(solution)/shard_map/ppermute | solution.py:25
  120.6 7.0 %collective-permute-start.29 = (f32[3,66,1]{2,1,0:T(8,128)S(1)}, f32[3,66,1]{2,1,0:T(8,128)S(1)}, u32[]{:S(2)}, u32[]{:S(2)}) collective-permute-start(f32[3,66,1]{2,1,0:T(8,128)S(1)} %get-tuple-element.72), channel_id=1, source_target_pairs={{0,1},{1,2},{2,3},{4,5},{5,6},{6,7},{8,9},{9,10},{10,11},{12,13},{... | collective-permute-start | bytes 2384 | tf_op jit(solution)/shard_map/ppermute | solution.py:24
  135.7 7.5 %collective-permute-start.32 = (f32[3,66,1]{2,1,0:T(8,128)S(1)}, f32[3,66,1]{2,1,0:T(8,128)S(1)}, u32[]{:S(2)}, u32[]{:S(2)}) collective-permute-start(f32[3,66,1]{2,1,0:T(8,128)S(1)} %get-tuple-element.69), channel_id=1, source_target_pairs={{1,0},{2,1},{3,2},{5,4},{6,5},{7,6},{9,8},{10,9},{11,10},{13,12},{... | collective-permute-start | bytes 2384 | tf_op jit(solution)/shard_map/ppermute | solution.py:25
  137.2 7.0 %collective-permute-start.33 = (f32[3,66,1]{2,1,0:T(8,128)S(1)}, f32[3,66,1]{2,1,0:T(8,128)S(1)}, u32[]{:S(2)}, u32[]{:S(2)}) collective-permute-start(f32[3,66,1]{2,1,0:T(8,128)S(1)} %get-tuple-element.70), channel_id=1, source_target_pairs={{0,1},{1,2},{2,3},{4,5},{5,6},{6,7},{8,9},{9,10},{10,11},{12,13},{... | collective-permute-start | bytes 2384 | tf_op jit(solution)/shard_map/ppermute | solution.py:24
  224.5 6.5 %collective-permute-start.44 = (f32[3,66,1]{2,1,0:T(8,128)S(1)}, f32[3,66,1]{2,1,0:T(8,128)S(1)}, u32[]{:S(2)}, u32[]{:S(2)}) collective-permute-start(f32[3,66,1]{2,1,0:T(8,128)S(1)} %get-tuple-element.63), channel_id=1, source_target_pairs={{1,0},{2,1},{3,2},{5,4},{6,5},{7,6},{9,8},{10,9},{11,10},{13,12},{... | collective-permute-start | bytes 2384 | tf_op jit(solution)/shard_map/ppermute | solution.py:25
  240.3 7.3 %collective-permute-start.48 = (f32[3,66,1]{2,1,0:T(8,128)S(1)}, f32[3,66,1]{2,1,0:T(8,128)S(1)}, u32[]{:S(2)}, u32[]{:S(2)}) collective-permute-start(f32[3,66,1]{2,1,0:T(8,128)S(1)} %get-tuple-element.61), channel_id=1, source_target_pairs={{1,0},{2,1},{3,2},{5,4},{6,5},{7,6},{9,8},{10,9},{11,10},{13,12},{... | collective-permute-start | bytes 2384 | tf_op jit(solution)/shard_map/ppermute | solution.py:25
  241.6 7.0 %collective-permute-start.49 = (f32[3,66,1]{2,1,0:T(8,128)S(1)}, f32[3,66,1]{2,1,0:T(8,128)S(1)}, u32[]{:S(2)}, u32[]{:S(2)}) collective-permute-start(f32[3,66,1]{2,1,0:T(8,128)S(1)} %get-tuple-element.62), channel_id=1, source_target_pairs={{0,1},{1,2},{2,3},{4,5},{5,6},{6,7},{8,9},{9,10},{10,11},{12,13},{... | collective-permute-start | bytes 2384 | tf_op jit(solution)/shard_map/ppermute | solution.py:24
  258.7 7.3 %collective-permute-start.52 = (f32[3,66,1]{2,1,0:T(8,128)S(1)}, f32[3,66,1]{2,1,0:T(8,128)S(1)}, u32[]{:S(2)}, u32[]{:S(2)}) collective-permute-start(f32[3,66,1]{2,1,0:T(8,128)S(1)} %get-tuple-element.59), channel_id=1, source_target_pairs={{1,0},{2,1},{3,2},{5,4},{6,5},{7,6},{9,8},{10,9},{11,10},{13,12},{... | collective-permute-start | bytes 2384 | tf_op jit(solution)/shard_map/ppermute | solution.py:25
  260.0 7.0 %collective-permute-start.53 = (f32[3,66,1]{2,1,0:T(8,128)S(1)}, f32[3,66,1]{2,1,0:T(8,128)S(1)}, u32[]{:S(2)}, u32[]{:S(2)}) collective-permute-start(f32[3,66,1]{2,1,0:T(8,128)S(1)} %get-tuple-element.60), channel_id=1, source_target_pairs={{0,1},{1,2},{2,3},{4,5},{5,6},{6,7},{8,9},{9,10},{10,11},{12,13},{... | collective-permute-start | bytes 2384 | tf_op jit(solution)/shard_map/ppermute | solution.py:24
  275.2 7.3 %collective-permute-start.56 = (f32[3,66,1]{2,1,0:T(8,128)S(1)}, f32[3,66,1]{2,1,0:T(8,128)S(1)}, u32[]{:S(2)}, u32[]{:S(2)}) collective-permute-start(f32[3,66,1]{2,1,0:T(8,128)S(1)} %get-tuple-element.57), channel_id=1, source_target_pairs={{1,0},{2,1},{3,2},{5,4},{6,5},{7,6},{9,8},{10,9},{11,10},{13,12},{... | collective-permute-start | bytes 2384 | tf_op jit(solution)/shard_map/ppermute | solution.py:25
  276.5 7.0 %collective-permute-start.57 = (f32[3,66,1]{2,1,0:T(8,128)S(1)}, f32[3,66,1]{2,1,0:T(8,128)S(1)}, u32[]{:S(2)}, u32[]{:S(2)}) collective-permute-start(f32[3,66,1]{2,1,0:T(8,128)S(1)} %get-tuple-element.58), channel_id=1, source_target_pairs={{0,1},{1,2},{2,3},{4,5},{5,6},{6,7},{8,9},{9,10},{10,11},{12,13},{... | collective-permute-start | bytes 2384 | tf_op jit(solution)/shard_map/ppermute | solution.py:24
  293.8 7.3 %collective-permute-start.60 = (f32[3,66,1]{2,1,0:T(8,128)S(1)}, f32[3,66,1]{2,1,0:T(8,128)S(1)}, u32[]{:S(2)}, u32[]{:S(2)}) collective-permute-start(f32[3,66,1]{2,1,0:T(8,128)S(1)} %get-tuple-element.55), channel_id=1, source_target_pairs={{1,0},{2,1},{3,2},{5,4},{6,5},{7,6},{9,8},{10,9},{11,10},{13,12},{... | collective-permute-start | bytes 2384 | tf_op jit(solution)/shard_map/ppermute | solution.py:25
  295.1 7.0 %collective-permute-start.61 = (f32[3,66,1]{2,1,0:T(8,128)S(1)}, f32[3,66,1]{2,1,0:T(8,128)S(1)}, u32[]{:S(2)}, u32[]{:S(2)}) collective-permute-start(f32[3,66,1]{2,1,0:T(8,128)S(1)} %get-tuple-element.56), channel_id=1, source_target_pairs={{0,1},{1,2},{2,3},{4,5},{5,6},{6,7},{8,9},{9,10},{10,11},{12,13},{... | collective-permute-start | bytes 2384 | tf_op jit(solution)/shard_map/ppermute | solution.py:24
  430.8 6.5 %collective-permute-start.76 = (f32[3,66,1]{2,1,0:T(8,128)S(1)}, f32[3,66,1]{2,1,0:T(8,128)S(1)}, u32[]{:S(2)}, u32[]{:S(2)}) collective-permute-start(f32[3,66,1]{2,1,0:T(8,128)S(1)} %get-tuple-element.47), channel_id=1, source_target_pairs={{1,0},{2,1},{3,2},{5,4},{6,5},{7,6},{9,8},{10,9},{11,10},{13,12},{... | collective-permute-start | bytes 2384 | tf_op jit(solution)/shard_map/ppermute | solution.py:25
  446.6 7.3 %collective-permute-start.80 = (f32[3,66,1]{2,1,0:T(8,128)S(1)}, f32[3,66,1]{2,1,0:T(8,128)S(1)}, u32[]{:S(2)}, u32[]{:S(2)}) collective-permute-start(f32[3,66,1]{2,1,0:T(8,128)S(1)} %get-tuple-element.45), channel_id=1, source_target_pairs={{1,0},{2,1},{3,2},{5,4},{6,5},{7,6},{9,8},{10,9},{11,10},{13,12},{... | collective-permute-start | bytes 2384 | tf_op jit(solution)/shard_map/ppermute | solution.py:25
  447.9 7.0 %collective-permute-start.81 = (f32[3,66,1]{2,1,0:T(8,128)S(1)}, f32[3,66,1]{2,1,0:T(8,128)S(1)}, u32[]{:S(2)}, u32[]{:S(2)}) collective-permute-start(f32[3,66,1]{2,1,0:T(8,128)S(1)} %get-tuple-element.46), channel_id=1, source_target_pairs={{0,1},{1,2},{2,3},{4,5},{5,6},{6,7},{8,9},{9,10},{10,11},{12,13},{... | collective-permute-start | bytes 2384 | tf_op jit(solution)/shard_map/ppermute | solution.py:24
  465.0 7.3 %collective-permute-start.84 = (f32[3,66,1]{2,1,0:T(8,128)S(1)}, f32[3,66,1]{2,1,0:T(8,128)S(1)}, u32[]{:S(2)}, u32[]{:S(2)}) collective-permute-start(f32[3,66,1]{2,1,0:T(8,128)S(1)} %get-tuple-element.43), channel_id=1, source_target_pairs={{1,0},{2,1},{3,2},{5,4},{6,5},{7,6},{9,8},{10,9},{11,10},{13,12},{... | collective-permute-start | bytes 2384 | tf_op jit(solution)/shard_map/ppermute | solution.py:25
  466.3 7.0 %collective-permute-start.85 = (f32[3,66,1]{2,1,0:T(8,128)S(1)}, f32[3,66,1]{2,1,0:T(8,128)S(1)}, u32[]{:S(2)}, u32[]{:S(2)}) collective-permute-start(f32[3,66,1]{2,1,0:T(8,128)S(1)} %get-tuple-element.44), channel_id=1, source_target_pairs={{0,1},{1,2},{2,3},{4,5},{5,6},{6,7},{8,9},{9,10},{10,11},{12,13},{... | collective-permute-start | bytes 2384 | tf_op jit(solution)/shard_map/ppermute | solution.py:24
  481.6 7.3 %collective-permute-start.88 = (f32[3,66,1]{2,1,0:T(8,128)S(1)}, f32[3,66,1]{2,1,0:T(8,128)S(1)}, u32[]{:S(2)}, u32[]{:S(2)}) collective-permute-start(f32[3,66,1]{2,1,0:T(8,128)S(1)} %get-tuple-element.41), channel_id=1, source_target_pairs={{1,0},{2,1},{3,2},{5,4},{6,5},{7,6},{9,8},{10,9},{11,10},{13,12},{... | collective-permute-start | bytes 2384 | tf_op jit(solution)/shard_map/ppermute | solution.py:25
  482.9 7.0 %collective-permute-start.89 = (f32[3,66,1]{2,1,0:T(8,128)S(1)}, f32[3,66,1]{2,1,0:T(8,128)S(1)}, u32[]{:S(2)}, u32[]{:S(2)}) collective-permute-start(f32[3,66,1]{2,1,0:T(8,128)S(1)} %get-tuple-element.42), channel_id=1, source_target_pairs={{0,1},{1,2},{2,3},{4,5},{5,6},{6,7},{8,9},{9,10},{10,11},{12,13},{... | collective-permute-start | bytes 2384 | tf_op jit(solution)/shard_map/ppermute | solution.py:24
  500.1 8.5 %collective-permute-start.92 = (f32[3,66,1]{2,1,0:T(8,128)S(1)}, f32[3,66,1]{2,1,0:T(8,128)S(1)}, u32[]{:S(2)}, u32[]{:S(2)}) collective-permute-start(f32[3,66,1]{2,1,0:T(8,128)S(1)} %get-tuple-element.39), channel_id=1, source_target_pairs={{1,0},{2,1},{3,2},{5,4},{6,5},{7,6},{9,8},{10,9},{11,10},{13,12},{... | collective-permute-start | bytes 2384 | tf_op jit(solution)/shard_map/ppermute | solution.py:25
  501.5 7.2 %collective-permute-start.93 = (f32[3,66,1]{2,1,0:T(8,128)S(1)}, f32[3,66,1]{2,1,0:T(8,128)S(1)}, u32[]{:S(2)}, u32[]{:S(2)}) collective-permute-start(f32[3,66,1]{2,1,0:T(8,128)S(1)} %get-tuple-element.40), channel_id=1, source_target_pairs={{0,1},{1,2},{2,3},{4,5},{5,6},{6,7},{8,9},{9,10},{10,11},{12,13},{... | collective-permute-start | bytes 2384 | tf_op jit(solution)/shard_map/ppermute | solution.py:24
  (95 other events, 1153.9 us)
where the time goes:
time: 518 us; the launch traced here: 510 us
  starting transfers between devices  291 us (56%)
  blocking collectives  108 us (21%)
  waiting for transfers between devices  52.2 us (10%)
  other arithmetic  50.1 us (10%)
  between operations  6.61 us (1%)
    ppermute x46, starting transfers between devices, with_halo(): before = lax.ppermute(last, axis, up)  225 us
    psum x2, blocking collectives, inner_sum(): return lax.psum(jnp.sum(residual * smoothed), ('row', 'col'))  76.7 us
    ppermute x46, starting transfers between devices, with_halo(): after = lax.ppermute(first, axis, down)  59.7 us
    ppermute x46, waiting for transfers between devices, with_halo(): before = lax.ppermute(last, axis, up)  51.4 us
    add x20, other arithmetic, chebyshev(): smoothed = smoothed + update  34 us
    psum x1, blocking collectives, per_device(): lax.psum(jnp.sum(direction * applied), ('row', 'col'))  30.9 us
  transfers between devices with their start and end apart: 94, of which 46 were waited for; matrix products, arithmetic and copies ran while one was open for 0% of the time, Pallas kernels for 0%

commit v1 on v0

v1 whole, which is shorter than its diff:
```python
import functools

import jax
import jax.numpy as jnp
from jax import lax
from jax.experimental import pallas as pl
from jax.experimental.pallas import tpu as pltpu
from jax.sharding import PartitionSpec as P

TILE = 256
SWEEPS = 8
LANES = 128
HALO = 24
PAD = 8

seam_damping = 0.8
offset_unit = 32.0
spectrum_low = 0.08
spectrum_high = 2.0
MIX = 2.4

VMEM_LIMIT = 48 * 1024 * 1024


def chebyshev_polynomial():
    centre = (spectrum_high + spectrum_low) / 2.0
    radius = (spectrum_high - spectrum_low) / 2.0
    sigma = centre / radius
    size = SWEEPS
    update = [1.0 / centre] + [0.0] * (size - 1)
    smoothed = list(update)
    rho = 1.0 / sigma
    for _ in range(SWEEPS - 1):
        remainder = [-s for s in smoothed]
        remainder[0] += 1.0
        for k in range(size - 1):
            remainder[k + 1] += smoothed[k]
        following = 1.0 / (2.0 * sigma - rho)
        update = [following * rho * u + 2.0 * following / radius * r for u, r in zip(update, remainder)]
        smoothed = [s + u for s, u in zip(smoothed, update)]
        rho = following
    return smoothed


def tile_range(application, rows):
    low = 1 + application
    high = rows + 2 * HALO - 1 - application
    return low // 8, -(-high // 8)


def stencil(z_ref, coefs, tile, chans, tiles):
    base = pl.multiple_of(PAD + 8 * tile, 8)
    lane = lax.broadcasted_iota(jnp.int32, (8, LANES), 1)
    first, last = (lane == 0, lane == LANES - 1)
    right_ref, left_ref, down_ref, up_ref = coefs
    centre = [[z_ref[c, j, pl.ds(base, 8), :] for j in range(tiles)] for c in range(chans)]
    ahead = [[pltpu.roll(v, LANES - 1, 1) for v in row] for row in centre]
    behind = [[pltpu.roll(v, 1, 1) for v in row] for row in centre]
    out = [[None] * tiles for _ in range(chans)]
    for j in range(tiles):
        a_right = right_ref[j, pl.ds(base, 8), :]
        a_left = left_ref[j, pl.ds(base, 8), :]
        a_down = down_ref[j, pl.ds(base, 8), :]
        a_up = up_ref[j, pl.ds(base, 8), :]
        for c in range(chans):
            to_right = jnp.where(last, ahead[c][(j + 1) % tiles], ahead[c][j])
            to_left = jnp.where(first, behind[c][(j - 1) % tiles], behind[c][j])
            below = z_ref[c, j, pl.ds(base + 1, 8), :]
            above = z_ref[c, j, pl.ds(base - 1, 8), :]
            out[c][j] = (a_right * to_right + a_left * to_left) + (a_down * below + a_up * above)
    return base, centre, out


def horner(g_ref, buffers, final_ref, coefs, first_application, rows, chans, tiles, count):
    poly = chebyshev_polynomial()
    degree = SWEEPS - 1
    source = g_ref
    for k in range(count):
        target = final_ref if k == degree - 1 else buffers[k % 2]
        low, high = tile_range(first_application + k, rows)
        scale = poly[degree] if k == 0 else None
        add = poly[degree - 1 - k]

        def body(tile, carry, source=source, target=target, scale=scale, add=add):
            base, _, moved = stencil(source, coefs, tile, chans, tiles)
            for c in range(chans):
                for j in range(tiles):
                    value = moved[c][j] if scale is None else scale * moved[c][j]
                    target[c, j, pl.ds(base, 8), :] = value + add * g_ref[c, j, pl.ds(base, 8), :]
            return carry

        lax.fori_loop(low, high, body, 0)
        source = target
    return source


def residual_step(g_ref, z_ref, next_ref, coefs, diag_ref, application, rows, chans, tiles, own_tiles):
    low, high = tile_range(application, rows)
    own_low = HALO // 8
    own_high = own_low + rows // 8

    def body(tile, carry, own):
        base, centre, moved = stencil(z_ref, coefs, tile, chans, tiles)
        for j in range(tiles):
            weigh = own and j < own_tiles
            diag = diag_ref[j, pl.ds(base, 8), :] if weigh else None
            for c in range(chans):
                g = g_ref[c, j, pl.ds(base, 8), :]
                z = centre[c][j]
                following = g - MIX * (z - moved[c][j])
                next_ref[c, j, pl.ds(base, 8), :] = following
                if weigh:
                    dz = diag * z
                    carry = (carry[0] + g * dz, carry[1] + following * dz)
        return carry

    zero = jnp.zeros((8, LANES), jnp.float32)
    lax.fori_loop(low, own_low, functools.partial(body, own=False), 0)
    lax.fori_loop(own_high, high, functools.partial(body, own=False), 0)
    return lax.fori_loop(own_low, own_high, functools.partial(body, own=True), (zero, zero))


def first_kernel(
    flags_ref, shift_ref, src_ref, weight_ref, seam_right_ref, seam_down_ref, top_ref, bottom_ref, before_ref, after_ref,
    right_ref, left_ref, down_ref, up_ref, diag_ref, g0_ref, z0_ref, g1_ref, f1_ref, g2_ref, sums_ref,
    cond_right, cond_down, work_a, work_b,
):
    chans, rows, cols = src_ref.shape
    own_tiles = cols // LANES
    tiles = own_tiles + 1
    total = rows + 2 * HALO
    lane = lax.broadcasted_iota(jnp.int32, (8, LANES), 1)
    sub = lax.broadcasted_iota(jnp.int32, (8, LANES), 0)
    zero = jnp.zeros((8, LANES), jnp.float32)

    for j in range(tiles):
        for at in (0, PAD + total):
            cond_down[j, pl.ds(at, 8), :] = zero
            for c in range(chans):
                for ref in (g0_ref, g1_ref, work_a, work_b, z0_ref, f1_ref):
                    ref[c, j, pl.ds(at, 8), :] = zero

    def put(base, j, planes):
        for c in range(chans):
            g0_ref[c, j, pl.ds(base, 8), :] = planes[c]
        diag_ref[j, pl.ds(base, 8), :] = planes[chans]
        cond_right[j, pl.ds(base, 8), :] = planes[chans + 1]
        cond_down[j, pl.ds(base, 8), :] = planes[chans + 2]

    def edge_rows(slab_ref, start):
        def body(t, carry):
            at = pl.multiple_of(8 * t, 8)
            base = pl.multiple_of(PAD + start + 8 * t, 8)
            for j in range(own_tiles):
                put(base, j, [slab_ref[p, pl.ds(at, 8), j * LANES:(j + 1) * LANES] for p in range(chans + 3)])
            return carry

        lax.fori_loop(0, HALO // 8, body, 0)

    edge_rows(top_ref, 0)
    edge_rows(bottom_ref, HALO + rows)

    def own_rows(t, carry):
        at = pl.multiple_of(8 * t, 8)
        base = pl.multiple_of(PAD + HALO + 8 * t, 8)
        bottom_row = (at + sub) == jnp.where(flags_ref[0] == 1, rows - 1, -1)
        for j in range(own_tiles):
            here = pl.ds(at, 8), pl.ds(j * LANES, LANES)
            planes = [src_ref[c, here[0], here[1]] + shift_ref[c, j * LANES // TILE] for c in range(chans)]
            planes.append(weight_ref[here[0], here[1]])
            to_right = 1.0 - seam_damping * seam_right_ref[here[0], here[1]].astype(jnp.float32)
            if j == own_tiles - 1:
                to_right = jnp.where(lane == jnp.where(flags_ref[1] == 1, LANES - 1, -1), 0.0, to_right)
            to_down = 1.0 - seam_damping * seam_down_ref[here[0], here[1]].astype(jnp.float32)
            planes.append(to_right)
            planes.append(jnp.where(bottom_row, 0.0, to_down))
            put(base, j, planes)
        return carry

    lax.fori_loop(0, rows // 8, own_rows, 0)

    def side_columns(t, carry):
        at = pl.multiple_of(8 * t, 8)
        base = pl.multiple_of(PAD + 8 * t, 8)
        put(
            base,
            own_tiles,
            [
                jnp.where(lane < LANES // 2, after_ref[p, pl.ds(at, 8), :], before_ref[p, pl.ds(at, 8), :])
                for p in range(chans + 3)
            ],
        )
        return carry

    lax.fori_loop(0, total // 8, side_columns, 0)

    def coefficients(t, carry):
        base = pl.multiple_of(PAD + 8 * t, 8)
        to_right = [cond_right[j, pl.ds(base, 8), :] for j in range(tiles)]
        behind = [pltpu.roll(v, 1, 1) for v in to_right]
        for j in range(tiles):
            to_left = jnp.where(lane == 0, behind[(j - 1) % tiles], behind[j])
            to_down = cond_down[j, pl.ds(base, 8), :]
            to_up = cond_down[j, pl.ds(base - 1, 8), :]
            diag = diag_ref[j, pl.ds(base, 8), :] + to_right[j] + to_left + to_down + to_up
            inverse = 1.0 / jnp.where(diag > 0.0, diag, 1.0)
            diag_ref[j, pl.ds(base, 8), :] = diag
            right_ref[j, pl.ds(base, 8), :] = to_right[j] * inverse
            left_ref[j, pl.ds(base, 8), :] = to_left * inverse
            down_ref[j, pl.ds(base, 8), :] = to_down * inverse
            up_ref[j, pl.ds(base, 8), :] = to_up * inverse
            for c in range(chans):
                g0_ref[c, j, pl.ds(base, 8), :] = g0_ref[c, j, pl.ds(base, 8), :] * inverse
        return carry

    lax.fori_loop(0, total // 8, coefficients, 0)

    coefs = (right_ref, left_ref, down_ref, up_ref)
    horner(g0_ref, (work_a, work_b), z0_ref, coefs, 1, rows, chans, tiles, SWEEPS - 1)
    sum0, sum1 = residual_step(g0_ref, z0_ref, g1_ref, coefs, diag_ref, SWEEPS, rows, chans, tiles, own_tiles)
    horner(g1_ref, (work_a, work_b), f1_ref, coefs, SWEEPS + 1, rows, chans, tiles, SWEEPS - 1)
    sum2, sum3 = residual_step(g1_ref, f1_ref, g2_ref, coefs, diag_ref, 2 * SWEEPS, rows, chans, tiles, own_tiles)
    row = lax.broadcasted_iota(jnp.int32, (8, LANES), 0)
    sums = zero
    for k, part in enumerate((sum0, sum1, sum2, sum3)):
        sums = jnp.where(row == k, jnp.sum(part), sums)
    sums_ref[...] = sums


def second_kernel(
    scalars_ref, right_ref, left_ref, down_ref, up_ref, diag_ref, g0_ref, z0_ref, g1_ref, f1_ref, g2_ref,
    solution_ref, residual_ref, smoothed_ref, work_a, work_b,
):
    chans, rows, cols = solution_ref.shape
    own_tiles = cols // LANES
    tiles = own_tiles + 1
    coefs = (right_ref, left_ref, down_ref, up_ref)
    degree = SWEEPS - 1
    source = horner(g2_ref, (work_a, work_b), None, coefs, 2 * SWEEPS + 1, rows, chans, tiles, degree - 1)
    add = chebyshev_polynomial()[0]
    x0, x1, r0, r1, r2, s0, s1, s2 = [scalars_ref[k] for k in range(8)]

    def body(t, carry):
        base, _, moved = stencil(source, coefs, t + HALO // 8, chans, tiles)
        at = pl.multiple_of(8 * t, 8)
        for j in range(own_tiles):
            diag = diag_ref[j, pl.ds(base, 8), :]
            for c in range(chans):
                g0 = g0_ref[c, j, pl.ds(base, 8), :]
                g1 = g1_ref[c, j, pl.ds(base, 8), :]
                g2 = g2_ref[c, j, pl.ds(base, 8), :]
                z0 = z0_ref[c, j, pl.ds(base, 8), :]
                f1 = f1_ref[c, j, pl.ds(base, 8), :]
                f2 = moved[c][j] + add * g2
                here = (c, pl.ds(at, 8), pl.ds(j * LANES, LANES))
                solution_ref[here] = x0 * z0 + x1 * f1
                residual_ref[here] = diag * (r0 * g0 + r1 * g1 + r2 * g2)
                smoothed_ref[here] = s0 * z0 + s1 * f1 + s2 * f2
        return carry

    lax.fori_loop(0, rows // 8, body, 0)


def combine(sums):
    n0, n1, n2, n3 = [sums[k] for k in range(4)]
    spread = n0 - n1
    keep = -n1 / spread
    step = n0 / spread
    beta = (n0 * n2 - n1 * n1) / (spread * spread)
    along = keep + beta
    curvature = along * along * spread + 2.0 * along * step * (n1 - n2) + step * step * (n2 - n3)
    scaled = n0 * beta / curvature
    first_size = step * MIX
    second_size = scaled * MIX
    x0 = first_size + second_size * along
    x1 = second_size * step
    r0 = keep - scaled * along
    r1 = step + scaled * (along - step)
    r2 = scaled * step
    return jnp.stack([x0, x1, r0, r1, r2, r0, r1, r2])


def per_device(source, weight, seam_right, seam_down, offsets):
    chans, rows, cols = source.shape
    row_axis, col_axis = lax.axis_size("row"), lax.axis_size("col")
    row_at, col_at = lax.axis_index("row"), lax.axis_index("col")
    last_row = row_at == row_axis - 1
    last_col = col_at == col_axis - 1
    per_tile = cols // TILE
    shift = lax.dynamic_slice(
        offsets, (row_at * rows // TILE, col_at * per_tile, 0), (1, per_tile, chans)
    )[0].T.astype(jnp.float32) / offset_unit
    shift_cols = jnp.repeat(shift, TILE, axis=1)[:, None, :]

    right_side = source + shift_cols
    row_number = lax.broadcasted_iota(jnp.int32, (rows, cols), 0)
    col_number = lax.broadcasted_iota(jnp.int32, (rows, cols), 1)
    cond_right = jnp.where(
        jnp.logical_and(last_col, col_number == cols - 1), 0.0, 1.0 - seam_damping * seam_right.astype(jnp.float32)
    )
    cond_down = jnp.where(
        jnp.logical_and(last_row, row_number == rows - 1), 0.0, 1.0 - seam_damping * seam_down.astype(jnp.float32)
    )

    def planes(at_rows, at_cols):
        return jnp.concatenate(
            [right_side[:, at_rows, at_cols]]
            + [v[None, at_rows, at_cols] for v in (weight, cond_right, cond_down)],
            axis=0,
        )

    every = slice(None)
    up = [(i, i + 1) for i in range(row_axis - 1)]
    down = [(j, i) for i, j in up]
    top = lax.ppermute(planes(slice(rows - HALO, rows), every), "row", up)
    bottom = lax.ppermute(planes(slice(0, HALO), every), "row", down)

    def side(at_cols):
        return jnp.concatenate([top[:, :, at_cols], planes(every, at_cols), bottom[:, :, at_cols]], axis=1)

    ahead = [(i, i + 1) for i in range(col_axis - 1)]
    back = [(j, i) for i, j in ahead]
    before = lax.ppermute(side(slice(cols - LANES, cols)), "col", ahead)
    after = lax.ppermute(side(slice(0, LANES)), "col", back)

    flags = jnp.stack([last_row, last_col]).astype(jnp.int32)
    tiles = cols // LANES + 1
    height = rows + 2 * HALO + 2 * PAD
    plane = jax.ShapeDtypeStruct((tiles, height, LANES), jnp.float32)
    field = jax.ShapeDtypeStruct((chans, tiles, height, LANES), jnp.float32)
    in_vmem = pl.BlockSpec(memory_space=pltpu.VMEM)
    in_smem = pl.BlockSpec(memory_space=pltpu.SMEM)
    work = [pltpu.VMEM(field.shape, jnp.float32)] * 2
    params = pltpu.CompilerParams(vmem_limit_bytes=VMEM_LIMIT)
    *basis, sums = pl.pallas_call(
        first_kernel,
        out_shape=[plane] * 5 + [field] * 5 + [jax.ShapeDtypeStruct((8, LANES), jnp.float32)],
        in_specs=[in_smem] * 2 + [in_vmem] * 8,
        out_specs=[in_vmem] * 11,
        scratch_shapes=[pltpu.VMEM(plane.shape, jnp.float32)] * 2 + work,
        compiler_params=params,
    )(flags, shift, source, weight, seam_right, seam_down, top, bottom, before, after)

    total = lax.psum(sums[:4, 0], ("row", "col"))
    outcome = jax.ShapeDtypeStruct(source.shape, jnp.float32)
    return pl.pallas_call(
        second_kernel,
        out_shape=[outcome] * 3,
        in_specs=[in_smem] + [in_vmem] * 10,
        out_specs=[in_vmem] * 3,
        scratch_shapes=work,
        compiler_params=params,
    )(combine(total), *basis)


def solution(mesh):
    placed = (
        P(None, ("band", "row"), "col"),
        P(("band", "row"), "col"),
        P(("band", "row"), "col"),
        P(("band", "row"), "col"),
        P("band", None, None),
    )
    return jax.shard_map(
        per_device,
        mesh=mesh,
        in_specs=placed,
        out_specs=(
            P(None, ("band", "row"), "col"),
            P(None, ("band", "row"), "col"),
            P(None, ("band", "row"), "col"),
        ),
        check_vma=False,
    )
```

time: 518 us -> 129 us (0.25); the launches traced: 510 us -> 128 us
  starting transfers between devices: 291 us -> 8.86 us
  blocking collectives: 108 us -> 35 us
  Pallas kernels: 0 us -> 50.3 us
  other arithmetic: 50.1 us -> 2.38 us
  waiting for transfers between devices: 52.2 us -> 19.2 us
    ppermute x94 -> x4, starting transfers between devices: 291 us -> 8.86 us  [the longest x1 4.96 us: per_device(): top = lax.ppermute(planes(slice(rows - HALO, rows), every), 'row', up)]
    psum x3 -> x1, blocking collectives: 108 us -> 35 us  [per_device(): total = lax.psum(sums[:4, 0], ('row', 'col'))]
    pallas_call x0 -> x2, Pallas kernels: none -> 50.3 us  [the longest x1 35.8 us: per_device(): pl.pallas_call(first_kernel, out_shape=[plane] * 5 + [field] * 5 + [jax.S...]
    add x23 -> x1, other arithmetic: 36.4 us -> 1.21 us  [per_device(): right_side = source + shift_cols]
    ppermute x94 -> x4, waiting for transfers between devices: 52.2 us -> 19.2 us  [the longest x1 11.1 us: per_device(): top = lax.ppermute(planes(slice(rows - HALO, rows), every), 'row', up)]
    reduce_sum x3 -> x0, other arithmetic: 6.81 us -> none  [the longest x2 4.56 us: per_device(): jnp.sum(direction * applied)]
  transfers between devices with their start and end apart: 94 -> 4, of which waited for: 46 -> 3; matrix products, arithmetic and copies ran while one was open for 0% -> 0% of each run, Pallas kernels for 0% -> 0%
where the time goes in v1:
time: 129 us; the launch traced here: 128 us
  Pallas kernels  50.3 us (39%)
  blocking collectives  35 us (27%)
  waiting for transfers between devices  19.2 us (15%)
  between operations  9.02 us (7%)
  starting transfers between devices  8.86 us (7%)
  local copies, waits for them, and re-layouts  3.5 us (3%)
  other arithmetic  2.38 us (2%)
    pallas_call x1, Pallas kernels, per_device(): pl.pallas_call(first_kernel, out_shape=[plane] * 5 + [field] * 5 + [jax.S...  35.8 us
    psum x1, blocking collectives, per_device(): total = lax.psum(sums[:4, 0], ('row', 'col'))  35 us
    pallas_call x1, Pallas kernels, per_device(): pl.pallas_call(second_kernel, out_shape=[outcome] * 3, in_specs=[in_smem]...  14.5 us
    ppermute x1, waiting for transfers between devices, per_device(): top = lax.ppermute(planes(slice(rows - HALO, rows), every), 'row', up)  11.1 us
    ppermute x1, starting transfers between devices, per_device(): top = lax.ppermute(planes(slice(rows - HALO, rows), every), 'row', up)  4.96 us
    ppermute x1, waiting for transfers between devices, per_device(): bottom = lax.ppermute(planes(slice(0, HALO), every), 'row', down)  4.19 us
    ppermute x1, waiting for transfers between devices, per_device(): after = lax.ppermute(side(slice(0, LANES)), 'col', back)  3.87 us
  transfers between devices with their start and end apart: 4, of which 3 were waited for; matrix products, arithmetic and copies ran while one was open for 0% of the time, Pallas kernels for 0%

profile of v1, /device:TPU:0, one launch (start us, length us, event | category | flops | bytes accessed | tf_op | source)
XLA Modules:
  0.0 128.3 jit_solution(4730705835788430895)
XLA Ops:
  0.6 0.0 copy-start.3
  0.7 0.8 convert_multiply_fusion
  1.5 0.1 broadcast_bitcast_fusion
  1.6 0.0 copy-start.2
  1.6 1.0 slice_bitcast_fusion.4
  2.6 1.2 broadcast_add_fusion
  3.8 0.0 copy-done.3
  3.9 0.0 copy-done.2
  3.9 0.1 subtract_select_fusion
  4.0 0.0 copy-start.1
  4.1 5.0 %collective-permute-start = (f32[6,24,1024]{2,1,0:T(8,128)S(1)}, f32[6,24,1024]{2,1,0:T(8,128)S(1)}, u32[]{:S(2)}, u32[]{:S(2)}) collective-permute-start(f32[6,24,1024]{2,1,0:T(8,128)S(1)} %pad_maximum_fusion), channel_id=1, source_target_pairs={{0,4},{4,8},{8,12},{1,5},{5,9},{9,13},{2,6},{6,10},{10,14},{3,7},{... | collective-permute-start | bytes 1769480 | tf_op jit(solution)/shard_map/ppermute | solution.py:315
  9.1 1.3 %collective-permute-start.1 = (f32[6,24,1024]{2,1,0:T(8,128)S(1)}, f32[6,24,1024]{2,1,0:T(8,128)S(1)}, u32[]{:S(2)}, u32[]{:S(2)}) collective-permute-start(f32[6,24,1024]{2,1,0:T(8,128)S(1)} %pad_maximum_fusion.1), channel_id=1, source_target_pairs={{4,0},{8,4},{12,8},{5,1},{9,5},{13,9},{6,2},{10,6},{14,10},{7,3},{... | collective-permute-start | bytes 1769480 | tf_op jit(solution)/shard_map/ppermute | solution.py:316
  10.4 0.0 copy-done.1
  10.5 11.1 %collective-permute-done.top_ref = f32[6,24,1024]{2,1,0:T(8,128)S(1)} collective-permute-done((f32[6,24,1024]{2,1,0:T(8,128)S(1)}, f32[6,24,1024]{2,1,0:T(8,128)S(1)}, u32[]{:S(2)}, u32[]{:S(2)}) %collective-permute-start) | collective-permute-done | bytes 589856 | tf_op jit(solution)/shard_map/ppermute | solution.py:315
  21.6 4.2 %collective-permute-done.1.bottom_ref = f32[6,24,1024]{2,1,0:T(8,128)S(1)} collective-permute-done((f32[6,24,1024]{2,1,0:T(8,128)S(1)}, f32[6,24,1024]{2,1,0:T(8,128)S(1)}, u32[]{:S(2)}, u32[]{:S(2)}) %collective-permute-start.1) | collective-permute-done | bytes 589856 | tf_op jit(solution)/shard_map/ppermute | solution.py:316
  25.9 1.3 %collective-permute-start.2 = (f32[6,112,128]{2,1,0:T(8,128)S(1)}, f32[6,112,128]{2,1,0:T(8,128)S(1)}, u32[]{:S(2)}, u32[]{:S(2)}) collective-permute-start(f32[6,112,128]{2,1,0:T(8,128)S(1)} %pad_maximum_fusion.2), channel_id=1, source_target_pairs={{0,1},{1,2},{2,3},{4,5},{5,6},{6,7},{8,9},{9,10},{10,11},{12,13},{... | collective-permute-start | bytes 1032200 | tf_op jit(solution)/shard_map/ppermute | solution.py:323
  27.2 1.3 %collective-permute-start.3 = (f32[6,112,128]{2,1,0:T(8,128)S(1)}, f32[6,112,128]{2,1,0:T(8,128)S(1)}, u32[]{:S(2)}, u32[]{:S(2)}) collective-permute-start(f32[6,112,128]{2,1,0:T(8,128)S(1)} %pad_maximum_fusion.3), channel_id=1, source_target_pairs={{1,0},{2,1},{3,2},{5,4},{6,5},{7,6},{9,8},{10,9},{11,10},{13,12},{... | collective-permute-start | bytes 1032200 | tf_op jit(solution)/shard_map/ppermute | solution.py:324
  28.5 0.1 add_convert_fusion.flags_ref
  28.6 0.0 collective-permute-done.2.before_ref
  28.6 3.9 %collective-permute-done.3.after_ref = f32[6,112,128]{2,1,0:T(8,128)S(1)} collective-permute-done((f32[6,112,128]{2,1,0:T(8,128)S(1)}, f32[6,112,128]{2,1,0:T(8,128)S(1)}, u32[]{:S(2)}, u32[]{:S(2)}) %collective-permute-start.3) | collective-permute-done | bytes 344096 | tf_op jit(solution)/shard_map/ppermute | solution.py:324
  32.5 35.8 %shard_map.76 = (f32[9,128,128]{2,1,0:T(8,128)S(1)}, f32[9,128,128]{2,1,0:T(8,128)S(1)}, f32[9,128,128]{2,1,0:T(8,128)S(1)}, f32[9,128,128]{2,1,0:T(8,128)S(1)},...) custom-call(s32[2]{0:T(128)S(1)} %add_convert_fusion.flags_ref, ...), custom_call_target="tpu_custom_call" | custom-call | tf_op jit(solution)/shard_map/pallas_call | solution.py:335
  68.3 0.1 slice_reduce_fusion
  68.4 35.0 %psum.7 = f32[4]{0:T(128)S(1)} all-reduce(f32[4]{0:T(128)S(1)} %slice_reduce_fusion), channel_id=1, replica_groups=mesh['band'=2,'row'=4,'col'=4] {'row','col'}, use_global_device_ids=true, to_apply=%region_0.1 | all-reduce | flops 4 | bytes 32 | tf_op jit(solution)/shard_map/psum | solution.py:344
  103.4 0.6 fusion.5
  112.2 0.1 stack.38.scalars_ref
  112.3 0.0 copy-start
  112.3 1.5 %copy-done = f32[3,9,128,128]{3,2,1,0:T(8,128)S(1)} copy-done((f32[3,9,128,128]{3,2,1,0:T(8,128)S(1)}, f32[3,9,128,128]{3,2,1,0:T(8,128)}, u32[]{:S(2)}) %copy-start) | copy-done | bytes 1769496
  113.8 14.5 %shard_map.77 = (f32[3,64,1024]{2,1,0:T(8,128)}, f32[3,64,1024]{2,1,0:T(8,128)}, f32[3,64,1024]{2,1,0:T(8,128)}) custom-call(f32[8]{0:T(128)S(1)} %stack.38.scalars_ref, f32[9,128,128]{2,1,0:T(8,128)S(1)} %get-tuple-element.15.right_ref, f32[9,128,128]{2,1,0:T(8,128)S(1)} %get-tuple-element.16.left_ref, f32[9,128,128]{2,1,0:T(8,128)S(1)} %get-tuple-element.17.down_ref, ...), custom_call_target="tpu_custom_call" | custom-call | tf_op jit(solution)/shard_map/pallas_call | solution.py:346
  (16 shorter events, 0.4 us)
Async XLA Ops:
  0.6 3.2 %copy-start.3 = (s32[64,1024]{1,0:T(8,128)S(1)}, s32[64,1024]{1,0:T(8,128)}, u32[]{:S(2)}) copy-start(s32[64,1024]{1,0:T(8,128)} %seam_right_ref.1) | copy-start | bytes 786436
  1.6 2.3 %copy-start.2 = (s32[64,1024]{1,0:T(8,128)S(1)}, s32[64,1024]{1,0:T(8,128)}, u32[]{:S(2)}) copy-start(s32[64,1024]{1,0:T(8,128)} %seam_down_ref.1) | copy-start | bytes 786436
  4.0 6.5 %copy-start.1 = (f32[64,1024]{1,0:T(8,128)S(1)}, f32[64,1024]{1,0:T(8,128)}, u32[]{:S(2)}) copy-start(f32[64,1024]{1,0:T(8,128)} %weight_ref.1) | copy-start | bytes 786436
  4.1 17.5 %collective-permute-start = (f32[6,24,1024]{2,1,0:T(8,128)S(1)}, f32[6,24,1024]{2,1,0:T(8,128)S(1)}, u32[]{:S(2)}, u32[]{:S(2)}) collective-permute-start(f32[6,24,1024]{2,1,0:T(8,128)S(1)} %pad_maximum_fusion), channel_id=1, source_target_pairs={{0,4},{4,8},{8,12},{1,5},{5,9},{9,13},{2,6},{6,10},{10,14},{3,7},{... | collective-permute-start | bytes 1769480 | tf_op jit(solution)/shard_map/ppermute | solution.py:315
  9.1 16.7 %collective-permute-start.1 = (f32[6,24,1024]{2,1,0:T(8,128)S(1)}, f32[6,24,1024]{2,1,0:T(8,128)S(1)}, u32[]{:S(2)}, u32[]{:S(2)}) collective-permute-start(f32[6,24,1024]{2,1,0:T(8,128)S(1)} %pad_maximum_fusion.1), channel_id=1, source_target_pairs={{4,0},{8,4},{12,8},{5,1},{9,5},{13,9},{6,2},{10,6},{14,10},{7,3},{... | collective-permute-start | bytes 1769480 | tf_op jit(solution)/shard_map/ppermute | solution.py:316
  25.9 2.7 %collective-permute-start.2 = (f32[6,112,128]{2,1,0:T(8,128)S(1)}, f32[6,112,128]{2,1,0:T(8,128)S(1)}, u32[]{:S(2)}, u32[]{:S(2)}) collective-permute-start(f32[6,112,128]{2,1,0:T(8,128)S(1)} %pad_maximum_fusion.2), channel_id=1, source_target_pairs={{0,1},{1,2},{2,3},{4,5},{5,6},{6,7},{8,9},{9,10},{10,11},{12,13},{... | collective-permute-start | bytes 1032200 | tf_op jit(solution)/shard_map/ppermute | solution.py:323
  27.2 5.3 %collective-permute-start.3 = (f32[6,112,128]{2,1,0:T(8,128)S(1)}, f32[6,112,128]{2,1,0:T(8,128)S(1)}, u32[]{:S(2)}, u32[]{:S(2)}) collective-permute-start(f32[6,112,128]{2,1,0:T(8,128)S(1)} %pad_maximum_fusion.3), channel_id=1, source_target_pairs={{1,0},{2,1},{3,2},{5,4},{6,5},{7,6},{9,8},{10,9},{11,10},{13,12},{... | collective-permute-start | bytes 1032200 | tf_op jit(solution)/shard_map/ppermute | solution.py:324
  112.3 1.5 %copy-start = (f32[3,9,128,128]{3,2,1,0:T(8,128)S(1)}, f32[3,9,128,128]{3,2,1,0:T(8,128)}, u32[]{:S(2)}) copy-start(f32[3,9,128,128]{3,2,1,0:T(8,128)} %get-tuple-element.20.g0_ref) | copy-start | bytes 5308420

commit v2 on v1

v2 whole, which is shorter than its diff:
```python
import functools

import jax
import jax.numpy as jnp
from jax import lax
from jax.experimental import pallas as pl
from jax.experimental.pallas import tpu as pltpu
from jax.sharding import PartitionSpec as P

TILE = 256
SWEEPS = 8
LANES = 128
HALO = 24
PAD = 8

seam_damping = 0.8
offset_unit = 32.0
spectrum_low = 0.08
spectrum_high = 2.0
MIX = 2.4

VMEM_LIMIT = 28 * 1024 * 1024


def chebyshev_polynomial():
    centre = (spectrum_high + spectrum_low) / 2.0
    radius = (spectrum_high - spectrum_low) / 2.0
    sigma = centre / radius
    size = SWEEPS
    update = [1.0 / centre] + [0.0] * (size - 1)
    smoothed = list(update)
    rho = 1.0 / sigma
    for _ in range(SWEEPS - 1):
        remainder = [-s for s in smoothed]
        remainder[0] += 1.0
        for k in range(size - 1):
            remainder[k + 1] += smoothed[k]
        following = 1.0 / (2.0 * sigma - rho)
        update = [following * rho * u + 2.0 * following / radius * r for u, r in zip(update, remainder)]
        smoothed = [s + u for s, u in zip(smoothed, update)]
        rho = following
    return smoothed


def tile_range(application, rows):
    low = 1 + application
    high = rows + 2 * HALO - 1 - application
    return low // 8, -(-high // 8)


def stencil(z_ref, coefs, tile, chans, tiles, emit):
    base = pl.multiple_of(PAD + 8 * tile, 8)
    lane = lax.broadcasted_iota(jnp.int32, (8, LANES), 1)
    first, last = (lane == 0, lane == LANES - 1)
    right_ref, left_ref, down_ref, up_ref = coefs
    every = range(chans)

    def here(j):
        return [z_ref[c, j, pl.ds(base, 8), :] for c in every]

    def ahead_of(values):
        return [pltpu.roll(v, LANES - 1, 1) for v in values]

    def behind_of(values):
        return [pltpu.roll(v, 1, 1) for v in values]

    behind_before = behind_of(here(tiles - 1))
    centre = here(0)
    ahead_first = ahead_now = ahead_of(centre)
    for j in range(tiles):
        behind_now = behind_of(centre)
        if j + 1 < tiles:
            centre_next = here(j + 1)
            ahead_next = ahead_of(centre_next)
        else:
            centre_next, ahead_next = None, ahead_first
        a_right = right_ref[j, pl.ds(base, 8), :]
        a_left = left_ref[j, pl.ds(base, 8), :]
        a_down = down_ref[j, pl.ds(base, 8), :]
        a_up = up_ref[j, pl.ds(base, 8), :]
        for c in every:
            to_right = jnp.where(last, ahead_next[c], ahead_now[c])
            to_left = jnp.where(first, behind_before[c], behind_now[c])
            below = z_ref[c, j, pl.ds(base + 1, 8), :]
            above = z_ref[c, j, pl.ds(base - 1, 8), :]
            moved = (a_right * to_right + a_left * to_left) + (a_down * below + a_up * above)
            emit(base, c, j, centre[c], moved)
        behind_before, centre, ahead_now = behind_now, centre_next, ahead_next


def over_tiles(low, high, body, carry):
    pairs = (high - low) // 2

    def pair(k, carry):
        return body(low + 2 * k + 1, body(low + 2 * k, carry))

    carry = lax.fori_loop(0, pairs, pair, carry)
    return body(high - 1, carry) if (high - low) % 2 else carry


def horner(g_ref, buffers, final_ref, coefs, first_application, rows, chans, tiles, count):
    poly = chebyshev_polynomial()
    degree = SWEEPS - 1
    source = g_ref
    for k in range(count):
        target = final_ref if k == degree - 1 else buffers[k % 2]
        low, high = tile_range(first_application + k, rows)
        scale = poly[degree] if k == 0 else None
        add = poly[degree - 1 - k]

        def body(tile, carry, source=source, target=target, scale=scale, add=add):
            def emit(base, c, j, centre, moved):
                g = centre if scale is not None else g_ref[c, j, pl.ds(base, 8), :]
                value = moved if scale is None else scale * moved
                target[c, j, pl.ds(base, 8), :] = value + add * g

            stencil(source, coefs, tile, chans, tiles, emit)
            return carry

        over_tiles(low, high, body, 0)
        source = target
    return source


def residual_step(g_ref, z_ref, next_ref, coefs, diag_ref, application, rows, chans, tiles, own_tiles):
    low, high = tile_range(application, rows)
    own_low = HALO // 8
    own_high = own_low + rows // 8

    def body(tile, carry, own):
        sums = list(carry)

        def emit(base, c, j, centre, moved):
            g = g_ref[c, j, pl.ds(base, 8), :]
            following = g - MIX * (centre - moved)
            next_ref[c, j, pl.ds(base, 8), :] = following
            if own and j < own_tiles:
                dz = diag_ref[j, pl.ds(base, 8), :] * centre
                sums[0] += g * dz
                sums[1] += following * dz

        stencil(z_ref, coefs, tile, chans, tiles, emit)
        return tuple(sums)

    zero = jnp.zeros((8, LANES), jnp.float32)
    over_tiles(low, own_low, functools.partial(body, own=False), (zero, zero))
    over_tiles(own_high, high, functools.partial(body, own=False), (zero, zero))
    return over_tiles(own_low, own_high, functools.partial(body, own=True), (zero, zero))


SLOT = 32
SLOTS = LANES // SLOT


def edges_kernel(flags_ref, shift_ref, src_ref, weight_ref, seam_right_ref, seam_down_ref, *outs):
    first_rows, last_rows, first_cols, last_cols, first_first, first_last, last_first, last_last = outs
    chans, rows, cols = src_ref.shape
    own_tiles = cols // LANES
    lane = lax.broadcasted_iota(jnp.int32, (8, LANES), 1)
    for t in range(rows // 8):
        packs = {}
        for j in range(own_tiles):
            edge_row = t < HALO // 8 or t >= (rows - HALO) // 8
            if not edge_row and j not in (0, own_tiles - 1):
                continue
            planes = own_planes(
                flags_ref, shift_ref, src_ref, weight_ref, seam_right_ref, seam_down_ref, 8 * t, j
            )
            if edge_row:
                for p, plane in enumerate(planes):
                    if t < HALO // 8:
                        first_rows[p, 8 * t:8 * t + 8, j * LANES:(j + 1) * LANES] = plane
                    if t >= (rows - HALO) // 8:
                        at = 8 * t - (rows - HALO)
                        last_rows[p, at:at + 8, j * LANES:(j + 1) * LANES] = plane
            for side, cols_ref in ((0, first_cols), (own_tiles - 1, last_cols)):
                if j != side:
                    continue
                start = 0 if side == 0 else LANES - SLOT
                packed = [None] * (-(-len(planes) // SLOTS))
                for p, plane in enumerate(planes):
                    slot = p % SLOTS
                    by = (slot * SLOT - start) % LANES
                    moved = pltpu.roll(plane, by, 1) if by else plane
                    at = p // SLOTS
                    packed[at] = moved if slot == 0 else jnp.where(lane < slot * SLOT, packed[at], moved)
                for q, value in enumerate(packed):
                    cols_ref[q, 8 * t:8 * t + 8, :] = value
                    if t < HALO // 8:
                        (first_first if side == 0 else first_last)[q, 8 * t:8 * t + 8, :] = value
                    if t >= (rows - HALO) // 8:
                        at = 8 * t - (rows - HALO)
                        (last_first if side == 0 else last_last)[q, at:at + 8, :] = value


def own_planes(flags_ref, shift_ref, src_ref, weight_ref, seam_right_ref, seam_down_ref, at, j):
    chans, rows, cols = src_ref.shape
    lane = lax.broadcasted_iota(jnp.int32, (8, LANES), 1)
    sub = lax.broadcasted_iota(jnp.int32, (8, LANES), 0)
    here = pl.ds(at, 8), pl.ds(j * LANES, LANES)
    planes = [src_ref[c, here[0], here[1]] + shift_ref[c, j * LANES // TILE] for c in range(chans)]
    planes.append(weight_ref[here[0], here[1]])
    to_right = 1.0 - seam_damping * seam_right_ref[here[0], here[1]].astype(jnp.float32)
    if j == cols // LANES - 1:
        to_right = jnp.where(lane == jnp.where(flags_ref[1] == 1, LANES - 1, -1), 0.0, to_right)
    to_down = 1.0 - seam_damping * seam_down_ref[here[0], here[1]].astype(jnp.float32)
    bottom = (at + sub) == jnp.where(flags_ref[0] == 1, rows - 1, -1)
    return planes + [to_right, jnp.where(bottom, 0.0, to_down)]


def first_kernel(
    flags_ref, shift_ref, src_ref, weight_ref, seam_right_ref, seam_down_ref,
    top_ref, bottom_ref, before_ref, after_ref, top_before_ref, top_after_ref, bottom_before_ref, bottom_after_ref,
    right_ref, left_ref, down_ref, up_ref, diag_ref, g0_ref, z0_ref, g1_ref, f1_ref, g2_ref, sums_ref,
    cond_right, cond_down, work_a, work_b,
):
    chans, rows, cols = src_ref.shape
    own_tiles = cols // LANES
    tiles = own_tiles + 1
    total = rows + 2 * HALO
    lane = lax.broadcasted_iota(jnp.int32, (8, LANES), 1)
    zero = jnp.zeros((8, LANES), jnp.float32)

    for j in range(tiles):
        for at in (0, PAD + total):
            cond_down[j, pl.ds(at, 8), :] = zero
            for c in range(chans):
                for ref in (g0_ref, g1_ref, work_a, work_b, z0_ref, f1_ref):
                    ref[c, j, pl.ds(at, 8), :] = zero

    def put(base, j, planes):
        for c in range(chans):
            g0_ref[c, j, pl.ds(base, 8), :] = planes[c]
        diag_ref[j, pl.ds(base, 8), :] = planes[chans]
        cond_right[j, pl.ds(base, 8), :] = planes[chans + 1]
        cond_down[j, pl.ds(base, 8), :] = planes[chans + 2]

    def edge_rows(slab_ref, start):
        def body(t, carry):
            at = pl.multiple_of(8 * t, 8)
            base = pl.multiple_of(PAD + start + 8 * t, 8)
            for j in range(own_tiles):
                put(base, j, [slab_ref[p, pl.ds(at, 8), j * LANES:(j + 1) * LANES] for p in range(chans + 3)])
            return carry

        lax.fori_loop(0, HALO // 8, body, 0)

    edge_rows(top_ref, 0)
    edge_rows(bottom_ref, HALO + rows)

    def own_rows(t, carry):
        at = pl.multiple_of(8 * t, 8)
        base = pl.multiple_of(PAD + HALO + 8 * t, 8)
        for j in range(own_tiles):
            put(
                base, j,
                own_planes(flags_ref, shift_ref, src_ref, weight_ref, seam_right_ref, seam_down_ref, at, j),
            )
        return carry

    lax.fori_loop(0, rows // 8, own_rows, 0)

    def side_columns(left_from, right_from, start, count):
        def body(t, carry):
            at = pl.multiple_of(8 * t, 8)
            base = pl.multiple_of(PAD + start + 8 * t, 8)
            planes = []
            for p in range(chans + 3):
                lefts = left_from[p // SLOTS, pl.ds(at, 8), :]
                rights = right_from[p // SLOTS, pl.ds(at, 8), :]
                slot = p % SLOTS
                lefts = pltpu.roll(lefts, (LANES - SLOT - slot * SLOT) % LANES, 1) if slot != SLOTS - 1 else lefts
                rights = pltpu.roll(rights, (-slot * SLOT) % LANES, 1) if slot else rights
                planes.append(jnp.where(lane < SLOT, rights, jnp.where(lane >= LANES - SLOT, lefts, 0.0)))
            put(base, own_tiles, planes)
            return carry

        lax.fori_loop(0, count // 8, body, 0)

    side_columns(top_before_ref, top_after_ref, 0, HALO)
    side_columns(before_ref, after_ref, HALO, rows)
    side_columns(bottom_before_ref, bottom_after_ref, HALO + rows, HALO)

    def coefficients(t, carry):
        base = pl.multiple_of(PAD + 8 * t, 8)
        to_right = [cond_right[j, pl.ds(base, 8), :] for j in range(tiles)]
        behind = [pltpu.roll(v, 1, 1) for v in to_right]
        for j in range(tiles):
            to_left = jnp.where(lane == 0, behind[(j - 1) % tiles], behind[j])
            to_down = cond_down[j, pl.ds(base, 8), :]
            to_up = cond_down[j, pl.ds(base - 1, 8), :]
            diag = diag_ref[j, pl.ds(base, 8), :] + to_right[j] + to_left + to_down + to_up
            inverse = 1.0 / jnp.where(diag > 0.0, diag, 1.0)
            diag_ref[j, pl.ds(base, 8), :] = diag
            right_ref[j, pl.ds(base, 8), :] = to_right[j] * inverse
            left_ref[j, pl.ds(base, 8), :] = to_left * inverse
            down_ref[j, pl.ds(base, 8), :] = to_down * inverse
            up_ref[j, pl.ds(base, 8), :] = to_up * inverse
            for c in range(chans):
                g0_ref[c, j, pl.ds(base, 8), :] = g0_ref[c, j, pl.ds(base, 8), :] * inverse
        return carry

    lax.fori_loop(0, total // 8, coefficients, 0)

    coefs = (right_ref, left_ref, down_ref, up_ref)
    horner(g0_ref, (work_a, work_b), z0_ref, coefs, 1, rows, chans, tiles, SWEEPS - 1)
    sum0, sum1 = residual_step(g0_ref, z0_ref, g1_ref, coefs, diag_ref, SWEEPS, rows, chans, tiles, own_tiles)
    horner(g1_ref, (work_a, work_b), f1_ref, coefs, SWEEPS + 1, rows, chans, tiles, SWEEPS - 1)
    sum2, sum3 = residual_step(g1_ref, f1_ref, g2_ref, coefs, diag_ref, 2 * SWEEPS, rows, chans, tiles, own_tiles)
    row = lax.broadcasted_iota(jnp.int32, (8, LANES), 0)
    sums = zero
    for k, part in enumerate((sum0, sum1, sum2, sum3)):
        sums = jnp.where(row == k, jnp.sum(part), sums)
    sums_ref[...] = sums


def second_kernel(right_ref, left_ref, down_ref, up_ref, g2_ref, f2_ref, work_a, work_b):
    chans, tiles = g2_ref.shape[:2]
    rows = g2_ref.shape[2] - 2 * PAD - 2 * HALO
    coefs = (right_ref, left_ref, down_ref, up_ref)
    horner(g2_ref, (work_a, work_b), f2_ref, coefs, 2 * SWEEPS + 1, rows, chans, tiles, SWEEPS - 1)


def combine(n0, n1, n2, n3):
    spread = n0 - n1
    keep = -n1 / spread
    step = n0 / spread
    beta = (n0 * n2 - n1 * n1) / (spread * spread)
    along = keep + beta
    curvature = along * along * spread + 2.0 * along * step * (n1 - n2) + step * step * (n2 - n3)
    scaled = n0 * beta / curvature
    first_size = step * MIX
    second_size = scaled * MIX
    x0 = first_size + second_size * along
    x1 = second_size * step
    r0 = keep - scaled * along
    r1 = step + scaled * (along - step)
    r2 = scaled * step
    return x0, x1, r0, r1, r2


def third_kernel(
    sums_ref, diag_ref, g0_ref, z0_ref, g1_ref, f1_ref, g2_ref, f2_ref, solution_ref, residual_ref, smoothed_ref
):
    chans, rows, cols = solution_ref.shape
    own_tiles = cols // LANES
    total = jnp.sum(sums_ref[...], axis=0)
    x0, x1, r0, r1, r2 = combine(*[jnp.broadcast_to(total[k:k + 1, :], (8, LANES)) for k in range(4)])

    def body(t, carry):
        base = pl.multiple_of(PAD + HALO + 8 * t, 8)
        at = pl.multiple_of(8 * t, 8)
        for j in range(own_tiles):
            diag = diag_ref[j, pl.ds(base, 8), :]
            for c in range(chans):
                g0, g1, g2, z0, f1, f2 = [
                    ref[c, j, pl.ds(base, 8), :] for ref in (g0_ref, g1_ref, g2_ref, z0_ref, f1_ref, f2_ref)
                ]
                here = (c, pl.ds(at, 8), pl.ds(j * LANES, LANES))
                solution_ref[here] = x0 * z0 + x1 * f1
                residual_ref[here] = diag * (r0 * g0 + r1 * g1 + r2 * g2)
                smoothed_ref[here] = r0 * z0 + r1 * f1 + r2 * f2
        return carry

    lax.fori_loop(0, rows // 8, body, 0)


def per_device(source, weight, seam_right, seam_down, offsets):
    chans, rows, cols = source.shape
    row_axis, col_axis = lax.axis_size("row"), lax.axis_size("col")
    row_at, col_at = lax.axis_index("row"), lax.axis_index("col")
    flags = jnp.stack([row_at == row_axis - 1, col_at == col_axis - 1]).astype(jnp.int32)
    per_tile = cols // TILE
    shift = lax.dynamic_slice(
        offsets, (row_at * rows // TILE, col_at * per_tile, 0), (1, per_tile, chans)
    )[0].T.astype(jnp.float32) / offset_unit

    in_vmem = pl.BlockSpec(memory_space=pltpu.VMEM)
    in_smem = pl.BlockSpec(memory_space=pltpu.SMEM)
    params = pltpu.CompilerParams(vmem_limit_bytes=VMEM_LIMIT)
    own = (flags, shift, source, weight, seam_right, seam_down)
    own_specs = [in_smem] * 2 + [in_vmem] * 4

    def shaped(*shape):
        return jax.ShapeDtypeStruct(shape, jnp.float32)

    packs = -(-(chans + 3) // SLOTS)
    first_rows, last_rows, first_cols, last_cols, first_first, first_last, last_first, last_last = pl.pallas_call(
        edges_kernel,
        out_shape=[shaped(chans + 3, HALO, cols)] * 2
        + [shaped(packs, rows, LANES)] * 2
        + [shaped(packs, HALO, LANES)] * 4,
        in_specs=own_specs,
        out_specs=[in_vmem] * 8,
        compiler_params=params,
    )(*own)

    def moved(value, down, right):
        pairs = [
            (r * col_axis + c, (r + down) * col_axis + c + right)
            for r in range(row_axis)
            for c in range(col_axis)
            if 0 <= r + down < row_axis and 0 <= c + right < col_axis
        ]
        return lax.ppermute(value, ("row", "col"), pairs)

    halo = (
        moved(last_rows, 1, 0),
        moved(first_rows, -1, 0),
        moved(last_cols, 0, 1),
        moved(first_cols, 0, -1),
        moved(last_last, 1, 1),
        moved(last_first, 1, -1),
        moved(first_last, -1, 1),
        moved(first_first, -1, -1),
    )

    tiles = cols // LANES + 1
    height = rows + 2 * HALO + 2 * PAD
    plane = shaped(tiles, height, LANES)
    field = shaped(chans, tiles, height, LANES)
    work = [pltpu.VMEM(field.shape, jnp.float32)] * 2
    right, left, down, up, diag, g0, z0, g1, f1, g2, sums = pl.pallas_call(
        first_kernel,
        out_shape=[plane] * 5 + [field] * 5 + [shaped(8, LANES)],
        in_specs=own_specs + [in_vmem] * 8,
        out_specs=[in_vmem] * 11,
        scratch_shapes=[pltpu.VMEM(plane.shape, jnp.float32)] * 2 + work,
        compiler_params=params,
    )(*own, *halo)

    every_sum = lax.all_gather(sums, ("row", "col"))
    f2 = pl.pallas_call(
        second_kernel,
        out_shape=field,
        in_specs=[in_vmem] * 5,
        out_specs=in_vmem,
        scratch_shapes=work,
        compiler_params=params,
        cost_estimate=pl.CostEstimate(flops=10**9, bytes_accessed=10**7, transcendentals=0),
    )(right, left, down, up, g2)
    return pl.pallas_call(
        third_kernel,
        out_shape=[shaped(chans, rows, cols)] * 3,
        in_specs=[in_vmem] * 8,
        out_specs=[in_vmem] * 3,
        compiler_params=params,
    )(every_sum, diag, g0, z0, g1, f1, g2, f2)


def solution(mesh):
    placed = (
        P(None, ("band", "row"), "col"),
        P(("band", "row"), "col"),
        P(("band", "row"), "col"),
        P(("band", "row"), "col"),
        P("band", None, None),
    )
    return jax.shard_map(
        per_device,
        mesh=mesh,
        in_specs=placed,
        out_specs=(
            P(None, ("band", "row"), "col"),
            P(None, ("band", "row"), "col"),
            P(None, ("band", "row"), "col"),
        ),
        check_vma=False,
    )
```

time: 129 us -> 90.6 us (0.70)
  Pallas kernels: 50.3 us -> 33 us
  blocking collectives: 35 us -> 20.7 us
  starting transfers between devices: 8.86 us -> 18.4 us
  between operations: 9.02 us -> 0.76 us
  waiting for transfers between devices: 19.2 us -> 12.5 us
  other arithmetic: 2.38 us -> 0.83 us
    psum x1 -> x0, blocking collectives: 35 us -> none  [per_device(): total = lax.psum(sums[:4, 0], ('row', 'col'))]
    all_gather x0 -> x1, blocking collectives: none -> 20.7 us  [per_device(): every_sum = lax.all_gather(sums, ('row', 'col'))]
    pallas_call x2 -> x4, Pallas kernels: 50.3 us -> 33 us  [the longest x1 23.5 us: per_device(): pl.pallas_call(first_kernel, out_shape=[plane] * 5 + [field] * 5 + [shape...]
    ppermute x4 -> x8, starting transfers between devices: 8.86 us -> 18.4 us  [moved(): return lax.ppermute(value, ('row', 'col'), pairs)]
    ppermute x4 -> x8, waiting for transfers between devices: 19.2 us -> 12.5 us  [moved(): return lax.ppermute(value, ('row', 'col'), pairs)]
    unnamed x10 -> x8, local copies, waits for them, and re-layouts: 1.57 us -> 3.98 us
  transfers between devices with their start and end apart: 4 -> 8, of which waited for: 3 -> 2; matrix products, arithmetic and copies ran while one was open for 0% -> 0% of each run, Pallas kernels for 0% -> 0%
where the time goes in v2:
time: 90.6 us; the launch traced here: 90.2 us
  Pallas kernels  33 us (36%)
  blocking collectives  20.7 us (23%)
  starting transfers between devices  18.4 us (20%)
  waiting for transfers between devices  12.5 us (14%)
  local copies, waits for them, and re-layouts  3.99 us (4%)
    pallas_call x1, Pallas kernels, per_device(): pl.pallas_call(first_kernel, out_shape=[plane] * 5 + [field] * 5 + [shape...  23.5 us
    all_gather x1, blocking collectives, per_device(): every_sum = lax.all_gather(sums, ('row', 'col'))  20.7 us
    ppermute x8, starting transfers between devices, moved(): return lax.ppermute(value, ('row', 'col'), pairs)  18.4 us
    ppermute x8, waiting for transfers between devices, moved(): return lax.ppermute(value, ('row', 'col'), pairs)  12.5 us
    pallas_call x1, Pallas kernels, per_device(): pl.pallas_call(second_kernel, out_shape=field, in_specs=[in_vmem] * 5, ou...  6.64 us
    unnamed x8, local copies, waits for them, and re-layouts  3.98 us
    pallas_call x1, Pallas kernels, per_device(): pl.pallas_call(third_kernel, out_shape=[shaped(chans, rows, cols)] * 3, i...  2.11 us
  transfers between devices with their start and end apart: 8, of which 2 were waited for; matrix products, arithmetic and copies ran while one was open for 0% of the time, Pallas kernels for 0%

profile of v2, /device:TPU:0, one launch (start us, length us, event | category | flops | bytes accessed | tf_op | source)
XLA Modules:
  0.0 90.2 jit_solution(6126256129051820662)
XLA Ops:
  0.6 0.8 convert_multiply_fusion
  1.4 0.1 add_convert_fusion.flags_ref
  1.5 0.0 copy-start
  1.5 1.1 %copy-done = f32[3,64,1024]{2,1,0:T(8,128)S(1)} copy-done((f32[3,64,1024]{2,1,0:T(8,128)S(1)}, f32[3,64,1024]{2,1,0:T(8,128)}, u32[]{:S(2)}) %copy-start) | copy-done | bytes 786456
  2.6 0.0 copy-start.1
  2.6 0.9 %copy-done.1 = f32[64,1024]{1,0:T(8,128)S(1)} copy-done((f32[64,1024]{1,0:T(8,128)S(1)}, f32[64,1024]{1,0:T(8,128)}, u32[]{:S(2)}) %copy-start.1) | copy-done | bytes 262168
  3.6 0.0 copy-start.2
  3.6 0.9 %copy-done.2 = s32[64,1024]{1,0:T(8,128)S(1)} copy-done((s32[64,1024]{1,0:T(8,128)S(1)}, s32[64,1024]{1,0:T(8,128)}, u32[]{:S(2)}) %copy-start.2) | copy-done | bytes 262168
  4.5 0.0 copy-start.3
  4.5 0.9 %copy-done.3 = s32[64,1024]{1,0:T(8,128)S(1)} copy-done((s32[64,1024]{1,0:T(8,128)S(1)}, s32[64,1024]{1,0:T(8,128)}, u32[]{:S(2)}) %copy-start.3) | copy-done | bytes 262168
  5.5 0.7 shard_map.76
  6.2 5.0 %collective-permute-start = (f32[6,24,1024]{2,1,0:T(8,128)S(1)}, f32[6,24,1024]{2,1,0:T(8,128)S(1)}, u32[]{:S(2)}, u32[]{:S(2)}) collective-permute-start(f32[6,24,1024]{2,1,0:T(8,128)S(1)} %get-tuple-element.22), channel_id=1, source_target_pairs={{0,4},{1,5},{2,6},{3,7},{4,8},{5,9},{6,10},{7,11},{8,12},{9,13},{1... | collective-permute-start | bytes 1769480 | tf_op jit(solution)/shard_map/ppermute | solution.py:405
  11.2 1.3 %collective-permute-start.1 = (f32[6,24,1024]{2,1,0:T(8,128)S(1)}, f32[6,24,1024]{2,1,0:T(8,128)S(1)}, u32[]{:S(2)}, u32[]{:S(2)}) collective-permute-start(f32[6,24,1024]{2,1,0:T(8,128)S(1)} %get-tuple-element.23), channel_id=1, source_target_pairs={{4,0},{5,1},{6,2},{7,3},{8,4},{9,5},{10,6},{11,7},{12,8},{13,9},{1... | collective-permute-start | bytes 1769480 | tf_op jit(solution)/shard_map/ppermute | solution.py:405
  12.5 3.4 %collective-permute-start.4 = (f32[2,24,128]{2,1,0:T(8,128)S(1)}, f32[2,24,128]{2,1,0:T(8,128)S(1)}, u32[]{:S(2)}, u32[]{:S(2)}) collective-permute-start(f32[2,24,128]{2,1,0:T(8,128)S(1)} %get-tuple-element.26), channel_id=1, source_target_pairs={{0,5},{1,6},{2,7},{4,9},{5,10},{6,11},{8,13},{9,14},{10,15},{16,21... | collective-permute-start | bytes 73736 | tf_op jit(solution)/shard_map/ppermute | solution.py:405
  15.9 0.7 collective-permute-start.5
  16.6 4.8 %collective-permute-start.2 = (f32[2,64,128]{2,1,0:T(8,128)S(1)}, f32[2,64,128]{2,1,0:T(8,128)S(1)}, u32[]{:S(2)}, u32[]{:S(2)}) collective-permute-start(f32[2,64,128]{2,1,0:T(8,128)S(1)} %get-tuple-element.24), channel_id=1, source_target_pairs={{0,1},{1,2},{2,3},{4,5},{5,6},{6,7},{8,9},{9,10},{10,11},{12,13},{... | collective-permute-start | bytes 196616 | tf_op jit(solution)/shard_map/ppermute | solution.py:405
  21.4 3.1 %collective-permute-done.4.top_before_ref = f32[2,24,128]{2,1,0:T(8,128)S(1)} collective-permute-done((f32[2,24,128]{2,1,0:T(8,128)S(1)}, f32[2,24,128]{2,1,0:T(8,128)S(1)}, u32[]{:S(2)}, u32[]{:S(2)}) %collective-permute-start.4) | collective-permute-done | bytes 24608 | tf_op jit(solution)/shard_map/ppermute | solution.py:405
  24.5 1.3 %collective-permute-start.3 = (f32[2,64,128]{2,1,0:T(8,128)S(1)}, f32[2,64,128]{2,1,0:T(8,128)S(1)}, u32[]{:S(2)}, u32[]{:S(2)}) collective-permute-start(f32[2,64,128]{2,1,0:T(8,128)S(1)} %get-tuple-element.25), channel_id=1, source_target_pairs={{1,0},{2,1},{3,2},{5,4},{6,5},{7,6},{9,8},{10,9},{11,10},{13,12},{... | collective-permute-start | bytes 196616 | tf_op jit(solution)/shard_map/ppermute | solution.py:405
  25.8 0.0 collective-permute-done.5.top_after_ref
  25.8 0.7 collective-permute-start.6
  26.5 0.0 collective-permute-done.6.bottom_before_ref
  26.5 1.3 %collective-permute-start.7 = (f32[2,24,128]{2,1,0:T(8,128)S(1)}, f32[2,24,128]{2,1,0:T(8,128)S(1)}, u32[]{:S(2)}, u32[]{:S(2)}) collective-permute-start(f32[2,24,128]{2,1,0:T(8,128)S(1)} %get-tuple-element.29), channel_id=1, source_target_pairs={{5,0},{6,1},{7,2},{9,4},{10,5},{11,6},{13,8},{14,9},{15,10},{21,16... | collective-permute-start | bytes 73736 | tf_op jit(solution)/shard_map/ppermute | solution.py:405
  27.8 9.4 %collective-permute-done.7.bottom_after_ref = f32[2,24,128]{2,1,0:T(8,128)S(1)} collective-permute-done((f32[2,24,128]{2,1,0:T(8,128)S(1)}, f32[2,24,128]{2,1,0:T(8,128)S(1)}, u32[]{:S(2)}, u32[]{:S(2)}) %collective-permute-start.7) | collective-permute-done | bytes 24608 | tf_op jit(solution)/shard_map/ppermute | solution.py:405
  37.2 0.0 collective-permute-done.2.before_ref
  37.2 0.0 collective-permute-done.3.after_ref
  37.2 0.0 collective-permute-done.top_ref
  37.2 0.0 collective-permute-done.1.bottom_ref
  37.2 23.5 %shard_map.77 = (f32[9,128,128]{2,1,0:T(8,128)S(1)}, f32[9,128,128]{2,1,0:T(8,128)S(1)}, f32[9,128,128]{2,1,0:T(8,128)S(1)}, f32[9,128,128]{2,1,0:T(8,128)S(1)},...) custom-call(s32[2]{0:T(128)S(1)} %add_convert_fusion.flags_ref, ...), custom_call_target="tpu_custom_call" | custom-call | tf_op jit(solution)/shard_map/pallas_call | solution.py:423
  60.7 20.7 %all-gather = f32[128,128]{1,0:T(8,128)S(1)} all-gather(f32[8,128]{1,0:T(8,128)S(1)} %get-tuple-element.30), channel_id=2, replica_groups=mesh['band'=2,'row'=4,'col'=4] {'row','col'}, dimensions={0}, use_global_device_ids=true | all-gather | bytes 69632 | tf_op jit(solution)/shard_map/all_gather | solution.py:432
  81.4 6.6 %shard_map.78.f2_ref = f32[3,9,128,128]{3,2,1,0:T(8,128)S(1)} custom-call(f32[9,128,128]{2,1,0:T(8,128)S(1)} %get-tuple-element.37.right_ref, f32[9,128,128]{2,1,0:T(8,128)S(1)} %get-tuple-element.38.left_ref, f32[9,128,128]{2,1,0:T(8,128)S(1)} %get-tuple-element.39.down_ref, f32[9,128,128]{2,1,0:T(8,128)S(1)} %get-tuple-element.40.up_ref, ...), custom_call_target="tpu_custom_call" | custom-call | flops 1000000000 | bytes 10000000 | tf_op jit(solution)/shard_map/pallas_call | solution.py:433
  88.1 2.1 %shard_map.79 = (f32[3,64,1024]{2,1,0:T(8,128)}, f32[3,64,1024]{2,1,0:T(8,128)}, f32[3,64,1024]{2,1,0:T(8,128)}) custom-call(f32[16,8,128]{2,1,0:T(8,128)S(1)} %bitcast.9, f32[9,128,128]{2,1,0:T(8,128)S(1)} %get-tuple-element.31.diag_ref, f32[3,9,128,128]{3,2,1,0:T(8,128)S(1)} %get-tuple-element.32.g0_ref, f32[3,9,128,128]{3,2,1,0:T(8,128)S(1)} %get-tuple-element.33.z0_ref, ...), custom_call_target="tpu_custom_call" | custom-call | tf_op jit(solution)/shard_map/pallas_call | solution.py:442
  (1 shorter events, 0.0 us)
Async XLA Ops:
  1.5 1.1 %copy-start = (f32[3,64,1024]{2,1,0:T(8,128)S(1)}, f32[3,64,1024]{2,1,0:T(8,128)}, u32[]{:S(2)}) copy-start(f32[3,64,1024]{2,1,0:T(8,128)} %src_ref.3) | copy-start | bytes 2359300
  2.6 0.9 %copy-start.1 = (f32[64,1024]{1,0:T(8,128)S(1)}, f32[64,1024]{1,0:T(8,128)}, u32[]{:S(2)}) copy-start(f32[64,1024]{1,0:T(8,128)} %weight_ref.3) | copy-start | bytes 786436
  3.6 0.9 %copy-start.2 = (s32[64,1024]{1,0:T(8,128)S(1)}, s32[64,1024]{1,0:T(8,128)}, u32[]{:S(2)}) copy-start(s32[64,1024]{1,0:T(8,128)} %seam_right_ref.3) | copy-start | bytes 786436
  4.5 0.9 %copy-start.3 = (s32[64,1024]{1,0:T(8,128)S(1)}, s32[64,1024]{1,0:T(8,128)}, u32[]{:S(2)}) copy-start(s32[64,1024]{1,0:T(8,128)} %seam_down_ref.3) | copy-start | bytes 786436
  6.2 31.0 %collective-permute-start = (f32[6,24,1024]{2,1,0:T(8,128)S(1)}, f32[6,24,1024]{2,1,0:T(8,128)S(1)}, u32[]{:S(2)}, u32[]{:S(2)}) collective-permute-start(f32[6,24,1024]{2,1,0:T(8,128)S(1)} %get-tuple-element.22), channel_id=1, source_target_pairs={{0,4},{1,5},{2,6},{3,7},{4,8},{5,9},{6,10},{7,11},{8,12},{9,13},{1... | collective-permute-start | bytes 1769480 | tf_op jit(solution)/shard_map/ppermute | solution.py:405
  11.2 26.0 %collective-permute-start.1 = (f32[6,24,1024]{2,1,0:T(8,128)S(1)}, f32[6,24,1024]{2,1,0:T(8,128)S(1)}, u32[]{:S(2)}, u32[]{:S(2)}) collective-permute-start(f32[6,24,1024]{2,1,0:T(8,128)S(1)} %get-tuple-element.23), channel_id=1, source_target_pairs={{4,0},{5,1},{6,2},{7,3},{8,4},{9,5},{10,6},{11,7},{12,8},{13,9},{1... | collective-permute-start | bytes 1769480 | tf_op jit(solution)/shard_map/ppermute | solution.py:405
  12.5 12.0 %collective-permute-start.4 = (f32[2,24,128]{2,1,0:T(8,128)S(1)}, f32[2,24,128]{2,1,0:T(8,128)S(1)}, u32[]{:S(2)}, u32[]{:S(2)}) collective-permute-start(f32[2,24,128]{2,1,0:T(8,128)S(1)} %get-tuple-element.26), channel_id=1, source_target_pairs={{0,5},{1,6},{2,7},{4,9},{5,10},{6,11},{8,13},{9,14},{10,15},{16,21... | collective-permute-start | bytes 73736 | tf_op jit(solution)/shard_map/ppermute | solution.py:405
  15.9 9.9 %collective-permute-start.5 = (f32[2,24,128]{2,1,0:T(8,128)S(1)}, f32[2,24,128]{2,1,0:T(8,128)S(1)}, u32[]{:S(2)}, u32[]{:S(2)}) collective-permute-start(f32[2,24,128]{2,1,0:T(8,128)S(1)} %get-tuple-element.27), channel_id=1, source_target_pairs={{1,4},{2,5},{3,6},{5,8},{6,9},{7,10},{9,12},{10,13},{11,14},{17,20... | collective-permute-start | bytes 73736 | tf_op jit(solution)/shard_map/ppermute | solution.py:405
  16.6 20.6 %collective-permute-start.2 = (f32[2,64,128]{2,1,0:T(8,128)S(1)}, f32[2,64,128]{2,1,0:T(8,128)S(1)}, u32[]{:S(2)}, u32[]{:S(2)}) collective-permute-start(f32[2,64,128]{2,1,0:T(8,128)S(1)} %get-tuple-element.24), channel_id=1, source_target_pairs={{0,1},{1,2},{2,3},{4,5},{5,6},{6,7},{8,9},{9,10},{10,11},{12,13},{... | collective-permute-start | bytes 196616 | tf_op jit(solution)/shard_map/ppermute | solution.py:405
  24.5 12.7 %collective-permute-start.3 = (f32[2,64,128]{2,1,0:T(8,128)S(1)}, f32[2,64,128]{2,1,0:T(8,128)S(1)}, u32[]{:S(2)}, u32[]{:S(2)}) collective-permute-start(f32[2,64,128]{2,1,0:T(8,128)S(1)} %get-tuple-element.25), channel_id=1, source_target_pairs={{1,0},{2,1},{3,2},{5,4},{6,5},{7,6},{9,8},{10,9},{11,10},{13,12},{... | collective-permute-start | bytes 196616 | tf_op jit(solution)/shard_map/ppermute | solution.py:405
  25.8 0.7 collective-permute-start.6
  26.5 10.7 %collective-permute-start.7 = (f32[2,24,128]{2,1,0:T(8,128)S(1)}, f32[2,24,128]{2,1,0:T(8,128)S(1)}, u32[]{:S(2)}, u32[]{:S(2)}) collective-permute-start(f32[2,24,128]{2,1,0:T(8,128)S(1)} %get-tuple-element.29), channel_id=1, source_target_pairs={{5,0},{6,1},{7,2},{9,4},{10,5},{11,6},{13,8},{14,9},{15,10},{21,16... | collective-permute-start | bytes 73736 | tf_op jit(solution)/shard_map/ppermute | solution.py:405

commit v3 on v0

v3 whole, which is shorter than its diff:
```python
import jax
import jax.numpy as jnp
from jax import lax
from jax.experimental import pallas as pl
from jax.experimental.pallas import tpu as pltpu
from jax.sharding import PartitionSpec as P

TILE = 256
SWEEPS = 8
SUBS = 8
LANES = 128
HALO = 24
SLOT = 32
SLOTS = LANES // SLOT

seam_damping = 0.8
offset_unit = 32.0
spectrum_low = 0.08
spectrum_high = 2.0
MIX = 2.4

VMEM_LIMIT = 28 * 1024 * 1024


def chebyshev_polynomial():
    centre = (spectrum_high + spectrum_low) / 2.0
    radius = (spectrum_high - spectrum_low) / 2.0
    sigma = centre / radius
    size = SWEEPS
    update = [1.0 / centre] + [0.0] * (size - 1)
    smoothed = list(update)
    rho = 1.0 / sigma
    for _ in range(SWEEPS - 1):
        remainder = [-s for s in smoothed]
        remainder[0] += 1.0
        for k in range(size - 1):
            remainder[k + 1] += smoothed[k]
        following = 1.0 / (2.0 * sigma - rho)
        update = [following * rho * u + 2.0 * following / radius * r for u, r in zip(update, remainder)]
        smoothed = [s + u for s, u in zip(smoothed, update)]
        rho = following
    return smoothed


def lane_index():
    return lax.broadcasted_iota(jnp.int32, (SUBS, LANES), 1)


def own_kernel(
    flags_ref, shift_ref, src_hbm, weight_hbm, seam_right_hbm, seam_down_hbm,
    own_ref, first_ref, last_ref,
    src_ref, weight_ref, seam_right_ref, seam_down_ref, sems,
):
    chans, rows, cols = src_ref.shape
    own_tiles = cols // LANES
    copies = [pltpu.make_async_copy(src_hbm.at[c], src_ref.at[c], sems.at[c]) for c in range(chans)]
    for k, (there, here) in enumerate(
        ((weight_hbm, weight_ref), (seam_right_hbm, seam_right_ref), (seam_down_hbm, seam_down_ref))
    ):
        copies.append(pltpu.make_async_copy(there, here, sems.at[chans + k]))
    for copy in copies:
        copy.start()
    for copy in copies:
        copy.wait()
    lane = lane_index()
    sub = lax.broadcasted_iota(jnp.int32, (SUBS, LANES), 0)
    last_row = jnp.where(flags_ref[0] == 1, rows - 1, -1)
    last_lane = jnp.where(flags_ref[1] == 1, LANES - 1, -1)

    def body(t, carry):
        at = pl.multiple_of(SUBS * t, SUBS)
        here = pl.ds(at, SUBS)
        for j in range(own_tiles):
            there = pl.ds(j * LANES, LANES)
            planes = [src_ref[c, here, there] + shift_ref[c, j * LANES // TILE] for c in range(chans)]
            planes.append(weight_ref[here, there])
            to_right = 1.0 - seam_damping * seam_right_ref[here, there].astype(jnp.float32)
            if j == own_tiles - 1:
                to_right = jnp.where(lane == last_lane, 0.0, to_right)
            to_down = 1.0 - seam_damping * seam_down_ref[here, there].astype(jnp.float32)
            planes += [to_right, jnp.where(at + sub == last_row, 0.0, to_down)]
            for p, plane in enumerate(planes):
                own_ref[p, j, here, :] = plane
            for side, start, cols_ref in ((0, 0, first_ref), (own_tiles - 1, LANES - SLOT, last_ref)):
                if j != side:
                    continue
                packed = [None] * (-(-len(planes) // SLOTS))
                for p, plane in enumerate(planes):
                    slot = p % SLOTS
                    by = (slot * SLOT - start) % LANES
                    moved = pltpu.roll(plane, by, 1) if by else plane
                    k = p // SLOTS
                    packed[k] = moved if slot == 0 else jnp.where(lane < slot * SLOT, packed[k], moved)
                for k, value in enumerate(packed):
                    cols_ref[k, here, :] = value
        return carry

    lax.fori_loop(0, rows // SUBS, body, 0)


def spread(b_right_ref, b_down_ref, z_ref, c, emit):
    tiles, height = z_ref.shape[1:3]
    steps = height // SUBS
    lane = lane_index()
    first, last = (lane == 0, lane == LANES - 1)

    def at(i):
        return pl.ds(i * SUBS, SUBS)

    def z_at(i, j):
        return z_ref[c, j, at(i), :]

    from_above = [pltpu.roll(b_down_ref[j, at(steps - 1), :] * z_at(steps - 1, j), 1, 0) for j in range(tiles)]
    centre = [z_at(0, j) for j in range(tiles)]
    wrapped = [pltpu.roll(v, SUBS - 1, 0) for v in centre]
    for i in range(steps):
        below = [z_at(i + 1, j) for j in range(tiles)] if i + 1 < steps else wrapped
        ahead_first = ahead_now = pltpu.roll(centre[0], LANES - 1, 1)
        b_last = b_right_ref[tiles - 1, at(i), :]
        pushed_before = pltpu.roll(b_last * centre[tiles - 1], 1, 1)
        for j in range(tiles):
            b_right = b_right_ref[j, at(i), :] if j + 1 < tiles else b_last
            b_down = b_down_ref[j, at(i), :]
            ahead_next = pltpu.roll(centre[j + 1], LANES - 1, 1) if j + 1 < tiles else ahead_first
            pushed_now = pltpu.roll(b_right * centre[j], 1, 1)
            to_right = jnp.where(last, ahead_next, ahead_now)
            from_left = jnp.where(first, pushed_before, pushed_now)
            moved = (b_right * to_right + from_left) + (b_down * below[j] + from_above[j])
            from_above[j] = b_down * centre[j]
            emit(i, j, centre[j], moved)
            ahead_now, pushed_before = ahead_next, pushed_now
        centre = below


def precondition(b_right_ref, b_down_ref, g_ref, z_ref, work_ref, c):
    poly = chebyshev_polynomial()
    degree = SWEEPS - 1

    def at(i):
        return pl.ds(i * SUBS, SUBS)

    def first(i, j, centre, moved):
        z_ref[c, j, at(i), :] = poly[degree] * moved + poly[degree - 1] * centre

    spread(b_right_ref, b_down_ref, g_ref, c, first)

    def pair(k, carry):
        adds = []
        for half in range(2):
            value = jnp.float32(poly[half])
            for later in range(1, (degree - 1) // 2):
                value = jnp.where(k == (degree - 1) // 2 - 1 - later, jnp.float32(poly[2 * later + half]), value)
            adds.append(value)

        def one(target, add):
            def emit(i, j, centre, moved):
                target[c, j, at(i), :] = moved + add * g_ref[c, j, at(i), :]

            return emit

        spread(b_right_ref, b_down_ref, z_ref, c, one(work_ref, adds[1]))
        spread(b_right_ref, b_down_ref, work_ref, c, one(z_ref, adds[0]))
        return carry

    lax.fori_loop(0, (degree - 1) // 2, pair, 0)


def own_bounds(steps, rows, i):
    return -(-(HALO - i) // steps), (HALO + rows - 1 - i) // steps


def next_residual(b_right_ref, b_down_ref, g_ref, z_ref, next_ref, c, rows):
    tiles, height = g_ref.shape[1:3]
    steps = height // SUBS
    sums = {}

    def emit(i, j, centre, moved):
        at = pl.ds(i * SUBS, SUBS)
        g = g_ref[c, j, at, :]
        following = g - MIX * (centre - moved)
        next_ref[c, j, at, :] = following
        if j + 1 < tiles:
            bounds = own_bounds(steps, rows, i)
            now = (g * centre, following * centre)
            before = sums.get(bounds)
            sums[bounds] = now if before is None else (before[0] + now[0], before[1] + now[1])

    spread(b_right_ref, b_down_ref, z_ref, c, emit)
    sub = lax.broadcasted_iota(jnp.int32, (SUBS, LANES), 0)
    total = [jnp.zeros((SUBS, LANES), jnp.float32)] * 2
    for (low, high), parts in sums.items():
        inside = jnp.logical_and(sub >= low, sub <= high)
        total = [t + jnp.where(inside, p, 0.0) for t, p in zip(total, parts)]
    return total


def first_kernel(
    own_ref, top_ref, bottom_ref, before_ref, after_ref,
    b_right_ref, b_down_ref, scale_ref, root_ref, g0_ref, z0_ref, g1_ref, f1_ref, g2_ref, sums_ref,
    natural, work_ref,
):
    planes, own_tiles, rows = own_ref.shape[:3]
    chans = planes - 3
    tiles = own_tiles + 1
    height = rows + 2 * HALO
    steps = height // SUBS
    packs = before_ref.shape[0]
    lane = lane_index()

    def copy_own(t, carry):
        here = pl.ds(pl.multiple_of(SUBS * t, SUBS), SUBS)
        there = pl.ds(pl.multiple_of(HALO + SUBS * t, SUBS), SUBS)
        for p in range(planes):
            for j in range(own_tiles):
                natural[p, j, there, :] = own_ref[p, j, here, :]
        return carry

    lax.fori_loop(0, rows // SUBS, copy_own, 0)
    main = planes * own_tiles * HALO
    for slab, start in ((top_ref, 0), (bottom_ref, HALO + rows)):
        for p in range(planes):
            for j in range(own_tiles):
                at = (p * own_tiles + j) * HALO
                natural[p, j, start:start + HALO, :] = slab[at:at + HALO, :]

    def unpack(p, lefts, rights):
        slot = p % SLOTS
        if slot != SLOTS - 1:
            lefts = pltpu.roll(lefts, LANES - SLOT - slot * SLOT, 1)
        if slot:
            rights = pltpu.roll(rights, LANES - slot * SLOT, 1)
        return jnp.where(lane < SLOT, rights, jnp.where(lane >= LANES - SLOT, lefts, 0.0))

    def side_own(t, carry):
        here = pl.ds(pl.multiple_of(SUBS * t, SUBS), SUBS)
        there = pl.ds(pl.multiple_of(HALO + SUBS * t, SUBS), SUBS)
        for p in range(planes):
            natural[p, own_tiles, there, :] = unpack(p, before_ref[p // SLOTS, here, :], after_ref[p // SLOTS, here, :])
        return carry

    lax.fori_loop(0, rows // SUBS, side_own, 0)
    for slab, start in ((top_ref, 0), (bottom_ref, HALO + rows)):
        for t in range(HALO // SUBS):
            for p in range(planes):
                at = main + (p // SLOTS) * HALO + t * SUBS
                lefts = slab[at:at + SUBS, :]
                at += packs * HALO
                rights = slab[at:at + SUBS, :]
                natural[p, own_tiles, start + t * SUBS:start + (t + 1) * SUBS, :] = unpack(p, lefts, rights)

    def at(i):
        return pl.ds(i * SUBS, SUBS)

    def interleaved(p, i, j):
        return natural[p, j, pl.ds(i, SUBS, stride=steps), :]

    to_up = [pltpu.roll(interleaved(chans + 2, steps - 1, j), 1, 0) for j in range(tiles)]
    for i in range(steps):
        to_right = [interleaved(chans + 1, i, j) for j in range(tiles)]
        behind = [pltpu.roll(v, 1, 1) for v in to_right]
        for j in range(tiles):
            to_left = jnp.where(lane == 0, behind[(j - 1) % tiles], behind[j])
            to_down = interleaved(chans + 2, i, j)
            diag = interleaved(chans, i, j) + to_right[j] + to_left + to_down + to_up[j]
            inside = diag > 0.0
            safe = jnp.where(inside, diag, 1.0)
            guess = lax.rsqrt(safe)
            scale = guess * (1.5 - 0.5 * safe * guess * guess)
            scale_ref[j, at(i), :] = jnp.where(inside, scale, 0.0)
            root_ref[j, at(i), :] = safe * scale
            to_up[j] = to_down
    wrapped = [pltpu.roll(scale_ref[j, at(0), :], SUBS - 1, 0) for j in range(tiles)]
    for i in range(steps):
        scale = [scale_ref[j, at(i), :] for j in range(tiles)]
        ahead = [pltpu.roll(v, LANES - 1, 1) for v in scale]
        for j in range(tiles):
            right_scale = jnp.where(lane == LANES - 1, ahead[(j + 1) % tiles], ahead[j])
            b_right_ref[j, at(i), :] = interleaved(chans + 1, i, j) * scale[j] * right_scale
            down_scale = scale_ref[j, at(i + 1), :] if i + 1 < steps else wrapped[j]
            b_down_ref[j, at(i), :] = interleaved(chans + 2, i, j) * scale[j] * down_scale
            for c in range(chans):
                g0_ref[c, j, at(i), :] = interleaved(c, i, j) * scale[j]

    def channel(c, carry):
        precondition(b_right_ref, b_down_ref, g0_ref, z0_ref, work_ref, c)
        sum0, sum1 = next_residual(b_right_ref, b_down_ref, g0_ref, z0_ref, g1_ref, c, rows)
        precondition(b_right_ref, b_down_ref, g1_ref, f1_ref, work_ref, c)
        sum2, sum3 = next_residual(b_right_ref, b_down_ref, g1_ref, f1_ref, g2_ref, c, rows)
        return tuple(a + b for a, b in zip(carry, (sum0, sum1, sum2, sum3)))

    zero = jnp.zeros((SUBS, LANES), jnp.float32)
    parts = lax.fori_loop(0, chans, channel, (zero,) * 4)
    sub = lax.broadcasted_iota(jnp.int32, (SUBS, LANES), 0)
    sums = zero
    for k, part in enumerate(parts):
        sums = jnp.where(sub == k, jnp.sum(part), sums)
    sums_ref[...] = sums


def second_kernel(b_right_ref, b_down_ref, g2_ref, f2_ref, work_ref):
    def channel(c, carry):
        precondition(b_right_ref, b_down_ref, g2_ref, f2_ref, work_ref, c)
        return carry

    lax.fori_loop(0, g2_ref.shape[0], channel, 0)


def combine(n0, n1, n2, n3):
    gap = n0 - n1
    keep = -n1 / gap
    step = n0 / gap
    beta = (n0 * n2 - n1 * n1) / (gap * gap)
    along = keep + beta
    curvature = along * along * gap + 2.0 * along * step * (n1 - n2) + step * step * (n2 - n3)
    scaled = n0 * beta / curvature
    first_size = step * MIX
    second_size = scaled * MIX
    x0 = first_size + second_size * along
    x1 = second_size * step
    r0 = keep - scaled * along
    r1 = step + scaled * (along - step)
    r2 = scaled * step
    return x0, x1, r0, r1, r2


def third_kernel(
    sums_ref, scale_ref, root_ref, g0_ref, z0_ref, g1_ref, f1_ref, g2_ref, f2_ref,
    solution_ref, residual_ref, smoothed_ref,
    natural,
):
    chans, rows, cols = solution_ref.shape
    own_tiles = cols // LANES
    steps = scale_ref.shape[1] // SUBS
    x0, x1, r0, r1, r2 = combine(*[jnp.broadcast_to(sums_ref[k:k + 1, :], (SUBS, LANES)) for k in range(4)])
    outs = (solution_ref, residual_ref, smoothed_ref)

    def channel(c, carry):
        for j in range(own_tiles):
            for i in range(steps):
                at = pl.ds(i * SUBS, SUBS)
                scale = scale_ref[j, at, :]
                root = root_ref[j, at, :]
                g0, g1, g2, z0, f1, f2 = [
                    ref[c, j, at, :] for ref in (g0_ref, g1_ref, g2_ref, z0_ref, f1_ref, f2_ref)
                ]
                there = pl.ds(i, SUBS, stride=steps)
                natural[0, j, there, :] = scale * (x0 * z0 + x1 * f1)
                natural[1, j, there, :] = root * (r0 * g0 + r1 * g1 + r2 * g2)
                natural[2, j, there, :] = scale * (r0 * z0 + r1 * f1 + r2 * f2)
        for k, ref in enumerate(outs):
            for j in range(own_tiles):
                ref[c, :, j * LANES:(j + 1) * LANES] = natural[k, j, HALO:HALO + rows, :]
        return carry

    lax.fori_loop(0, chans, channel, 0)


def sum_over(value, axis):
    size = lax.axis_size(axis)
    if size & (size - 1):
        return lax.psum(value, axis)
    step = 1
    while step < size:
        value = value + lax.ppermute(value, axis, [(i, i ^ step) for i in range(size)])
        step *= 2
    return value


def per_device(source, weight, seam_right, seam_down, offsets):
    chans, rows, cols = source.shape
    row_axis, col_axis = lax.axis_size("row"), lax.axis_size("col")
    row_at, col_at = lax.axis_index("row"), lax.axis_index("col")
    flags = jnp.stack([row_at == row_axis - 1, col_at == col_axis - 1]).astype(jnp.int32)
    per_tile = cols // TILE
    shift = lax.dynamic_slice(
        offsets, (row_at * rows // TILE, col_at * per_tile, 0), (1, per_tile, chans)
    )[0].T.astype(jnp.float32) / offset_unit

    in_vmem = pl.BlockSpec(memory_space=pltpu.VMEM)
    in_smem = pl.BlockSpec(memory_space=pltpu.SMEM)
    anywhere = pl.BlockSpec(memory_space=pl.ANY)
    params = pltpu.CompilerParams(vmem_limit_bytes=VMEM_LIMIT)

    def shaped(*shape):
        return jax.ShapeDtypeStruct(shape, jnp.float32)

    planes = chans + 3
    own_tiles = cols // LANES
    packs = -(-planes // SLOTS)
    own, first_cols, last_cols = pl.pallas_call(
        own_kernel,
        out_shape=[shaped(planes, own_tiles, rows, LANES)] + [shaped(packs, rows, LANES)] * 2,
        in_specs=[in_smem] * 2 + [anywhere] * 4,
        out_specs=[in_vmem] * 3,
        scratch_shapes=[
            pltpu.VMEM(source.shape, jnp.float32),
            pltpu.VMEM(weight.shape, jnp.float32),
            pltpu.VMEM(weight.shape, jnp.int32),
            pltpu.VMEM(weight.shape, jnp.int32),
            pltpu.SemaphoreType.DMA((planes,)),
        ],
        compiler_params=params,
    )(flags, shift, source, weight, seam_right, seam_down)

    onward = [(i, i + 1) for i in range(col_axis - 1)]
    back = [(j, i) for i, j in onward]
    before = lax.ppermute(last_cols, "col", onward)
    after = lax.ppermute(first_cols, "col", back)

    def slab(low, high):
        parts = [own[:, :, low:high], before[:, low:high], after[:, low:high]]
        return jnp.concatenate([part.reshape(-1, LANES) for part in parts], axis=0)

    down = [(i, i + 1) for i in range(row_axis - 1)]
    up = [(j, i) for i, j in down]
    top = lax.ppermute(slab(rows - HALO, rows), "row", down)
    bottom = lax.ppermute(slab(0, HALO), "row", up)

    tiles = own_tiles + 1
    height = rows + 2 * HALO
    plane = shaped(tiles, height, LANES)
    field = shaped(chans, tiles, height, LANES)
    work = pltpu.VMEM(field.shape, jnp.float32)
    b_right, b_down, scale, root, g0, z0, g1, f1, g2, sums = pl.pallas_call(
        first_kernel,
        out_shape=[plane] * 4 + [field] * 5 + [shaped(SUBS, LANES)],
        in_specs=[in_vmem] * 5,
        out_specs=[in_vmem] * 10,
        scratch_shapes=[pltpu.VMEM((planes, tiles, height, LANES), jnp.float32), work],
        compiler_params=params,
    )(own, top, bottom, before, after)

    total = sum_over(sum_over(sums, "col"), "row")
    f2 = pl.pallas_call(
        second_kernel,
        out_shape=field,
        in_specs=[in_vmem] * 3,
        out_specs=in_vmem,
        scratch_shapes=[work],
        compiler_params=params,
        cost_estimate=pl.CostEstimate(flops=10**9, bytes_accessed=10**7, transcendentals=0),
    )(b_right, b_down, g2)
    return pl.pallas_call(
        third_kernel,
        out_shape=[shaped(chans, rows, cols)] * 3,
        in_specs=[in_vmem] * 9,
        out_specs=[in_vmem] * 3,
        scratch_shapes=[pltpu.VMEM((3, own_tiles, height, LANES), jnp.float32)],
        compiler_params=params,
    )(total, scale, root, g0, z0, g1, f1, g2, f2)


def solution(mesh):
    placed = (
        P(None, ("band", "row"), "col"),
        P(("band", "row"), "col"),
        P(("band", "row"), "col"),
        P(("band", "row"), "col"),
        P("band", None, None),
    )
    return jax.shard_map(
        per_device,
        mesh=mesh,
        in_specs=placed,
        out_specs=(
            P(None, ("band", "row"), "col"),
            P(None, ("band", "row"), "col"),
            P(None, ("band", "row"), "col"),
        ),
        check_vma=False,
    )
```

time: 518 us -> 76.2 us (0.15); the launches traced: 510 us -> 75.9 us
  starting transfers between devices: 291 us -> 14.2 us
  blocking collectives: 108 us -> 0 us
  other arithmetic: 50.1 us -> 0.93 us
  Pallas kernels: 0 us -> 29.4 us
  waiting for transfers between devices: 52.2 us -> 26.4 us
  between operations: 6.61 us -> 0.76 us
    ppermute x94 -> x8, starting transfers between devices: 291 us -> 14.2 us  [the longest x4 5.73 us: sum_over(): lax.ppermute(value, axis, [(i, i ^ step) for i in range(size)])]
    psum x3 -> x0, blocking collectives: 108 us -> none  [the longest x2 76.7 us: inner_sum(): return lax.psum(jnp.sum(residual * smoothed), ('row', 'col'))]
    add x23 -> x4, other arithmetic: 36.4 us -> 0.01 us  [sum_over(): value + lax.ppermute(value, axis, [(i, i ^ step) for i in range(size)])]
    pallas_call x0 -> x4, Pallas kernels: none -> 29.4 us  [the longest x1 18.2 us: per_device(): pl.pallas_call(first_kernel, out_shape=[plane] * 4 + [field] * 5 + [shape...]
    ppermute x94 -> x8, waiting for transfers between devices: 52.2 us -> 26.4 us  [the longest x1 11.3 us: per_device(): top = lax.ppermute(slab(rows - HALO, rows), 'row', down)]
    reduce_sum x3 -> x0, other arithmetic: 6.81 us -> none  [the longest x2 4.56 us: per_device(): jnp.sum(direction * applied)]
  transfers between devices with their start and end apart: 94 -> 8, of which waited for: 46 -> 6; matrix products, arithmetic and copies ran while one was open for 0% -> 0% of each run, Pallas kernels for 0% -> 9%
where the time goes in v3:
time: 76.2 us; the launch traced here: 75.9 us
  Pallas kernels  29.4 us (39%)
  waiting for transfers between devices  26.4 us (35%)
  starting transfers between devices  14.2 us (19%)
  local copies, waits for them, and re-layouts  4.11 us (5%)
  other arithmetic  0.93 us (1%)
    pallas_call x1, Pallas kernels, per_device(): pl.pallas_call(first_kernel, out_shape=[plane] * 4 + [field] * 5 + [shape...  18.2 us
    ppermute x1, waiting for transfers between devices, per_device(): top = lax.ppermute(slab(rows - HALO, rows), 'row', down)  11.3 us
    pallas_call x1, Pallas kernels, per_device(): pl.pallas_call(second_kernel, out_shape=field, in_specs=[in_vmem] * 3, ou...  7.05 us
    ppermute x4, waiting for transfers between devices, sum_over(): lax.ppermute(value, axis, [(i, i ^ step) for i in range(size)])  6.5 us
    ppermute x4, starting transfers between devices, sum_over(): lax.ppermute(value, axis, [(i, i ^ step) for i in range(size)])  5.73 us
    ppermute x1, waiting for transfers between devices, per_device(): bottom = lax.ppermute(slab(0, HALO), 'row', up)  4.77 us
    unnamed x8, local copies, waits for them, and re-layouts  3.98 us
    ppermute x1, waiting for transfers between devices, per_device(): after = lax.ppermute(first_cols, 'col', back)  3.81 us
  transfers between devices with their start and end apart: 8, of which 6 were waited for; matrix products, arithmetic and copies ran while one was open for 0% of the time, Pallas kernels for 9%

profile of v3, /device:TPU:0, one launch (start us, length us, event | category | flops | bytes accessed | tf_op | source)
XLA Modules:
  0.0 75.9 jit_solution(14009581580051392428)
XLA Ops:
  0.6 0.8 %convert_multiply_fusion = f32[1,4,3]{1,0,2:T(1,128)S(1)} fusion(s32[1,16,3]{1,0,2:T(1,128)} %param.9, s32[]{:T(128)S(6)} %select_n.7), kind=kLoop, calls=%fused_computation.4 | loop fusion | flops 24 | bytes 100 | tf_op jit(solution)/shard_map/div | solution.py:375
  1.4 0.1 add_convert_fusion.flags_ref
  1.5 0.0 copy-start
  1.5 1.1 %copy-done = f32[3,64,1024]{2,1,0:T(8,128)S(1)} copy-done((f32[3,64,1024]{2,1,0:T(8,128)S(1)}, f32[3,64,1024]{2,1,0:T(8,128)}, u32[]{:S(2)}) %copy-start) | copy-done | bytes 786456
  2.6 0.0 copy-start.1
  2.6 0.9 %copy-done.1 = f32[64,1024]{1,0:T(8,128)S(1)} copy-done((f32[64,1024]{1,0:T(8,128)S(1)}, f32[64,1024]{1,0:T(8,128)}, u32[]{:S(2)}) %copy-start.1) | copy-done | bytes 262168
  3.6 0.0 copy-start.2
  3.6 0.9 %copy-done.2 = s32[64,1024]{1,0:T(8,128)S(1)} copy-done((s32[64,1024]{1,0:T(8,128)S(1)}, s32[64,1024]{1,0:T(8,128)}, u32[]{:S(2)}) %copy-start.2) | copy-done | bytes 262168
  4.5 0.0 copy-start.3
  4.5 0.9 %copy-done.3 = s32[64,1024]{1,0:T(8,128)S(1)} copy-done((s32[64,1024]{1,0:T(8,128)S(1)}, s32[64,1024]{1,0:T(8,128)}, u32[]{:S(2)}) %copy-start.3) | copy-done | bytes 262168
  5.5 1.5 %shard_map.76 = (f32[6,8,64,128]{3,2,1,0:T(8,128)S(1)}, f32[2,64,128]{2,1,0:T(8,128)S(1)}, f32[2,64,128]{2,1,0:T(8,128)S(1)}) custom-call(s32[2]{0:T(128)S(1)} %add_convert_fusion.flags_ref, f32[3,4]{1,0:T(4,128)S(1)} %bitcast.14, f32[3,64,1024]{2,1,0:T(8,128)S(1)} %copy-done, f32[64,1024]{1,0:T(8,128)S(1)} %copy-done.1, s32[64,1024]{1,0:T(8,128)S(1)} %copy-done.2, ...), custom_call_target="tpu_custom_call" | custom-call | tf_op jit(solution)/shard_map/pallas_call | solution.py:390
  7.0 2.4 %collective-permute-start = (f32[2,64,128]{2,1,0:T(8,128)S(1)}, f32[2,64,128]{2,1,0:T(8,128)S(1)}, u32[]{:S(2)}, u32[]{:S(2)}) collective-permute-start(f32[2,64,128]{2,1,0:T(8,128)S(1)} %get-tuple-element.17), channel_id=1, source_target_pairs={{0,1},{1,2},{2,3},{4,5},{5,6},{6,7},{8,9},{9,10},{10,11},{12,13},{... | collective-permute-start | bytes 196616 | tf_op jit(solution)/shard_map/ppermute | solution.py:407
  9.4 1.3 %collective-permute-start.1 = (f32[2,64,128]{2,1,0:T(8,128)S(1)}, f32[2,64,128]{2,1,0:T(8,128)S(1)}, u32[]{:S(2)}, u32[]{:S(2)}) collective-permute-start(f32[2,64,128]{2,1,0:T(8,128)S(1)} %get-tuple-element.18), channel_id=1, source_target_pairs={{1,0},{2,1},{3,2},{5,4},{6,5},{7,6},{9,8},{10,9},{11,10},{13,12},{... | collective-permute-start | bytes 196616 | tf_op jit(solution)/shard_map/ppermute | solution.py:408
  10.7 0.1 fusion
  10.8 0.0 collective-permute-done.before_ref
  10.8 3.8 %collective-permute-done.1.after_ref = f32[2,64,128]{2,1,0:T(8,128)S(1)} collective-permute-done((f32[2,64,128]{2,1,0:T(8,128)S(1)}, f32[2,64,128]{2,1,0:T(8,128)S(1)}, u32[]{:S(2)}, u32[]{:S(2)}) %collective-permute-start.1) | collective-permute-done | bytes 65568 | tf_op jit(solution)/shard_map/ppermute | solution.py:408
  14.7 3.5 %collective-permute-start.2 = (f32[1248,128]{1,0:T(8,128)S(1)}, f32[1248,128]{1,0:T(8,128)S(1)}, u32[]{:S(2)}, u32[]{:S(2)}) collective-permute-start(f32[1248,128]{1,0:T(8,128)S(1)} %pad_maximum_fusion), channel_id=1, source_target_pairs={{0,4},{4,8},{8,12},{1,5},{5,9},{9,13},{2,6},{6,10},{10,14},{3,7},{... | collective-permute-start | bytes 1916936 | tf_op jit(solution)/shard_map/ppermute | solution.py:416
  18.3 1.3 %collective-permute-start.3 = (f32[1248,128]{1,0:T(8,128)S(1)}, f32[1248,128]{1,0:T(8,128)S(1)}, u32[]{:S(2)}, u32[]{:S(2)}) collective-permute-start(f32[1248,128]{1,0:T(8,128)S(1)} %pad_maximum_fusion.1), channel_id=1, source_target_pairs={{4,0},{8,4},{12,8},{5,1},{9,5},{13,9},{6,2},{10,6},{14,10},{7,3},{... | collective-permute-start | bytes 1916936 | tf_op jit(solution)/shard_map/ppermute | solution.py:417
  19.6 11.3 %collective-permute-done.2.top_ref = f32[1248,128]{1,0:T(8,128)S(1)} collective-permute-done((f32[1248,128]{1,0:T(8,128)S(1)}, f32[1248,128]{1,0:T(8,128)S(1)}, u32[]{:S(2)}, u32[]{:S(2)}) %collective-permute-start.2) | collective-permute-done | bytes 639008 | tf_op jit(solution)/shard_map/ppermute | solution.py:416
  30.9 4.8 %collective-permute-done.3.bottom_ref = f32[1248,128]{1,0:T(8,128)S(1)} collective-permute-done((f32[1248,128]{1,0:T(8,128)S(1)}, f32[1248,128]{1,0:T(8,128)S(1)}, u32[]{:S(2)}, u32[]{:S(2)}) %collective-permute-start.3) | collective-permute-done | bytes 639008 | tf_op jit(solution)/shard_map/ppermute | solution.py:417
  35.7 18.2 %shard_map.77 = (f32[9,112,128]{2,1,0:T(8,128)S(1)}, f32[9,112,128]{2,1,0:T(8,128)S(1)}, f32[9,112,128]{2,1,0:T(8,128)S(1)}, f32[9,112,128]{2,1,0:T(8,128)S(1)},...) custom-call(f32[6,8,64,128]{3,2,1,0:T(8,128)S(1)} %get-tuple-element, ...), custom_call_target="tpu_custom_call" | custom-call | tf_op jit(solution)/shard_map/pallas_call | solution.py:424
  53.9 1.6 %collective-permute-start.4 = (f32[8,128]{1,0:T(8,128)S(1)}, f32[8,128]{1,0:T(8,128)S(1)}, u32[]{:S(2)}, u32[]{:S(2)}) collective-permute-start(f32[8,128]{1,0:T(8,128)S(1)} %get-tuple-element.19), channel_id=1, source_target_pairs={{0,1},{1,0},{2,3},{3,2},{4,5},{5,4},{6,7},{7,6},{8,9},{9,8},{10,11... | collective-permute-start | bytes 12296 | tf_op jit(solution)/shard_map/ppermute | solution.py:364
  55.6 0.8 %collective-permute-done.4 = f32[8,128]{1,0:T(8,128)S(1)} collective-permute-done((f32[8,128]{1,0:T(8,128)S(1)}, f32[8,128]{1,0:T(8,128)S(1)}, u32[]{:S(2)}, u32[]{:S(2)}) %collective-permute-start.4) | collective-permute-done | bytes 4128 | tf_op jit(solution)/shard_map/ppermute | solution.py:364
  56.4 0.0 collective-permute-start.5
  56.4 3.6 %collective-permute-done.5 = f32[8,128]{1,0:T(8,128)S(1)} collective-permute-done((f32[8,128]{1,0:T(8,128)S(1)}, f32[8,128]{1,0:T(8,128)S(1)}, u32[]{:S(2)}, u32[]{:S(2)}) %collective-permute-start.5) | collective-permute-done | bytes 4128 | tf_op jit(solution)/shard_map/ppermute | solution.py:364
  60.0 1.5 %collective-permute-start.6 = (f32[8,128]{1,0:T(8,128)S(1)}, f32[8,128]{1,0:T(8,128)S(1)}, u32[]{:S(2)}, u32[]{:S(2)}) collective-permute-start(f32[8,128]{1,0:T(8,128)S(1)} %add.19), channel_id=1, source_target_pairs={{0,4},{4,0},{8,12},{12,8},{1,5},{5,1},{9,13},{13,9},{2,6},{6,2},{1... | collective-permute-start | bytes 12296 | tf_op jit(solution)/shard_map/ppermute | solution.py:364
  61.5 2.1 %collective-permute-done.6 = f32[8,128]{1,0:T(8,128)S(1)} collective-permute-done((f32[8,128]{1,0:T(8,128)S(1)}, f32[8,128]{1,0:T(8,128)S(1)}, u32[]{:S(2)}, u32[]{:S(2)}) %collective-permute-start.6) | collective-permute-done | bytes 4128 | tf_op jit(solution)/shard_map/ppermute | solution.py:364
  63.6 2.6 %collective-permute-start.7 = (f32[8,128]{1,0:T(8,128)S(1)}, f32[8,128]{1,0:T(8,128)S(1)}, u32[]{:S(2)}, u32[]{:S(2)}) collective-permute-start(f32[8,128]{1,0:T(8,128)S(1)} %add.20), channel_id=1, source_target_pairs={{0,8},{4,12},{8,0},{12,4},{1,9},{5,13},{9,1},{13,5},{2,10},{6,14},... | collective-permute-start | bytes 12296 | tf_op jit(solution)/shard_map/ppermute | solution.py:364
  66.2 7.1 %shard_map.78.f2_ref = f32[3,9,112,128]{3,2,1,0:T(8,128)S(1)} custom-call(f32[9,112,128]{2,1,0:T(8,128)S(1)} %get-tuple-element.27.b_right_ref, f32[9,112,128]{2,1,0:T(8,128)S(1)} %get-tuple-element.28.b_down_ref, f32[3,9,112,128]{3,2,1,0:T(8,128)S(1)} %get-tuple-element.26.g2_ref), custom_call_target="tpu_custom_call" | custom-call | flops 1000000000 | bytes 10000000 | tf_op jit(solution)/shard_map/pallas_call | solution.py:434
  73.2 0.0 collective-permute-done.7
  73.2 2.6 %shard_map.79 = (f32[3,64,1024]{2,1,0:T(8,128)}, f32[3,64,1024]{2,1,0:T(8,128)}, f32[3,64,1024]{2,1,0:T(8,128)}) custom-call(f32[8,128]{1,0:T(8,128)S(1)} %add.21.sums_ref, f32[9,112,128]{2,1,0:T(8,128)S(1)} %get-tuple-element.20.scale_ref, f32[9,112,128]{2,1,0:T(8,128)S(1)} %get-tuple-element.21.root_ref, f32[3,9,112,128]{3,2,1,0:T(8,128)S(1)} %get-tuple-element.22.g0_ref, ...), custom_call_target="tpu_custom_call" | custom-call | tf_op jit(solution)/shard_map/pallas_call | solution.py:443
  (9 shorter events, 0.1 us)
Async XLA Ops:
  1.5 1.1 %copy-start = (f32[3,64,1024]{2,1,0:T(8,128)S(1)}, f32[3,64,1024]{2,1,0:T(8,128)}, u32[]{:S(2)}) copy-start(f32[3,64,1024]{2,1,0:T(8,128)} %src_hbm.1) | copy-start | bytes 2359300
  2.6 0.9 %copy-start.1 = (f32[64,1024]{1,0:T(8,128)S(1)}, f32[64,1024]{1,0:T(8,128)}, u32[]{:S(2)}) copy-start(f32[64,1024]{1,0:T(8,128)} %weight_hbm.1) | copy-start | bytes 786436
  3.6 0.9 %copy-start.2 = (s32[64,1024]{1,0:T(8,128)S(1)}, s32[64,1024]{1,0:T(8,128)}, u32[]{:S(2)}) copy-start(s32[64,1024]{1,0:T(8,128)} %seam_right_hbm.1) | copy-start | bytes 786436
  4.5 0.9 %copy-start.3 = (s32[64,1024]{1,0:T(8,128)S(1)}, s32[64,1024]{1,0:T(8,128)}, u32[]{:S(2)}) copy-start(s32[64,1024]{1,0:T(8,128)} %seam_down_hbm.1) | copy-start | bytes 786436
  7.0 3.8 %collective-permute-start = (f32[2,64,128]{2,1,0:T(8,128)S(1)}, f32[2,64,128]{2,1,0:T(8,128)S(1)}, u32[]{:S(2)}, u32[]{:S(2)}) collective-permute-start(f32[2,64,128]{2,1,0:T(8,128)S(1)} %get-tuple-element.17), channel_id=1, source_target_pairs={{0,1},{1,2},{2,3},{4,5},{5,6},{6,7},{8,9},{9,10},{10,11},{12,13},{... | collective-permute-start | bytes 196616 | tf_op jit(solution)/shard_map/ppermute | solution.py:407
  9.4 5.3 %collective-permute-start.1 = (f32[2,64,128]{2,1,0:T(8,128)S(1)}, f32[2,64,128]{2,1,0:T(8,128)S(1)}, u32[]{:S(2)}, u32[]{:S(2)}) collective-permute-start(f32[2,64,128]{2,1,0:T(8,128)S(1)} %get-tuple-element.18), channel_id=1, source_target_pairs={{1,0},{2,1},{3,2},{5,4},{6,5},{7,6},{9,8},{10,9},{11,10},{13,12},{... | collective-permute-start | bytes 196616 | tf_op jit(solution)/shard_map/ppermute | solution.py:408
  14.7 16.2 %collective-permute-start.2 = (f32[1248,128]{1,0:T(8,128)S(1)}, f32[1248,128]{1,0:T(8,128)S(1)}, u32[]{:S(2)}, u32[]{:S(2)}) collective-permute-start(f32[1248,128]{1,0:T(8,128)S(1)} %pad_maximum_fusion), channel_id=1, source_target_pairs={{0,4},{4,8},{8,12},{1,5},{5,9},{9,13},{2,6},{6,10},{10,14},{3,7},{... | collective-permute-start | bytes 1916936 | tf_op jit(solution)/shard_map/ppermute | solution.py:416
  18.3 17.4 %collective-permute-start.3 = (f32[1248,128]{1,0:T(8,128)S(1)}, f32[1248,128]{1,0:T(8,128)S(1)}, u32[]{:S(2)}, u32[]{:S(2)}) collective-permute-start(f32[1248,128]{1,0:T(8,128)S(1)} %pad_maximum_fusion.1), channel_id=1, source_target_pairs={{4,0},{8,4},{12,8},{5,1},{9,5},{13,9},{6,2},{10,6},{14,10},{7,3},{... | collective-permute-start | bytes 1916936 | tf_op jit(solution)/shard_map/ppermute | solution.py:417
  53.9 2.5 %collective-permute-start.4 = (f32[8,128]{1,0:T(8,128)S(1)}, f32[8,128]{1,0:T(8,128)S(1)}, u32[]{:S(2)}, u32[]{:S(2)}) collective-permute-start(f32[8,128]{1,0:T(8,128)S(1)} %get-tuple-element.19), channel_id=1, source_target_pairs={{0,1},{1,0},{2,3},{3,2},{4,5},{5,4},{6,7},{7,6},{8,9},{9,8},{10,11... | collective-permute-start | bytes 12296 | tf_op jit(solution)/shard_map/ppermute | solution.py:364
  56.4 3.6 %collective-permute-start.5 = (f32[8,128]{1,0:T(8,128)S(1)}, f32[8,128]{1,0:T(8,128)S(1)}, u32[]{:S(2)}, u32[]{:S(2)}) collective-permute-start(f32[8,128]{1,0:T(8,128)S(1)} %add.18), channel_id=1, source_target_pairs={{0,2},{1,3},{2,0},{3,1},{4,6},{5,7},{6,4},{7,5},{8,10},{9,11},{10,... | collective-permute-start | bytes 12296 | tf_op jit(solution)/shard_map/ppermute | solution.py:364
  60.0 3.6 %collective-permute-start.6 = (f32[8,128]{1,0:T(8,128)S(1)}, f32[8,128]{1,0:T(8,128)S(1)}, u32[]{:S(2)}, u32[]{:S(2)}) collective-permute-start(f32[8,128]{1,0:T(8,128)S(1)} %add.19), channel_id=1, source_target_pairs={{0,4},{4,0},{8,12},{12,8},{1,5},{5,1},{9,13},{13,9},{2,6},{6,2},{1... | collective-permute-start | bytes 12296 | tf_op jit(solution)/shard_map/ppermute | solution.py:364
  63.6 9.6 %collective-permute-start.7 = (f32[8,128]{1,0:T(8,128)S(1)}, f32[8,128]{1,0:T(8,128)S(1)}, u32[]{:S(2)}, u32[]{:S(2)}) collective-permute-start(f32[8,128]{1,0:T(8,128)S(1)} %add.20), channel_id=1, source_target_pairs={{0,8},{4,12},{8,0},{12,4},{1,9},{5,13},{9,1},{13,5},{2,10},{6,14},... | collective-permute-start | bytes 12296 | tf_op jit(solution)/shard_map/ppermute | solution.py:364

commit v4 on v3

v4 whole, which is shorter than its diff:
```python
import functools

import jax
import jax.numpy as jnp
from jax import lax
from jax.experimental import pallas as pl
from jax.experimental.pallas import tpu as pltpu
from jax.sharding import PartitionSpec as P

TILE = 256
SWEEPS = 8
SUBS = 8
LANES = 128
HALO = 24
SLOT = 32
SLOTS = LANES // SLOT
WAYS = 3

seam_damping = 0.8
offset_unit = 32.0
spectrum_low = 0.08
spectrum_high = 2.0
MIX = 2.4

VMEM_LIMIT = 28 * 1024 * 1024


def chebyshev_polynomial():
    centre = (spectrum_high + spectrum_low) / 2.0
    radius = (spectrum_high - spectrum_low) / 2.0
    sigma = centre / radius
    size = SWEEPS
    update = [1.0 / centre] + [0.0] * (size - 1)
    smoothed = list(update)
    rho = 1.0 / sigma
    for _ in range(SWEEPS - 1):
        remainder = [-s for s in smoothed]
        remainder[0] += 1.0
        for k in range(size - 1):
            remainder[k + 1] += smoothed[k]
        following = 1.0 / (2.0 * sigma - rho)
        update = [following * rho * u + 2.0 * following / radius * r for u, r in zip(update, remainder)]
        smoothed = [s + u for s, u in zip(smoothed, update)]
        rho = following
    return smoothed


def lane_index():
    return lax.broadcasted_iota(jnp.int32, (SUBS, LANES), 1)


def own_kernel(
    place_ref, offsets_ref, src_hbm, weight_hbm, seam_right_hbm, seam_down_hbm,
    own_ref, first_ref, last_ref,
    src_ref, weight_ref, seam_right_ref, seam_down_ref, sems,
):
    chans, rows, cols = src_ref.shape
    own_tiles = cols // LANES
    copies = [pltpu.make_async_copy(src_hbm.at[c], src_ref.at[c], sems.at[c]) for c in range(chans)]
    for k, (there, here) in enumerate(
        ((weight_hbm, weight_ref), (seam_right_hbm, seam_right_ref), (seam_down_hbm, seam_down_ref))
    ):
        copies.append(pltpu.make_async_copy(there, here, sems.at[chans + k]))
    for copy in copies:
        copy.start()
    lane = lane_index()
    sub = lax.broadcasted_iota(jnp.int32, (SUBS, LANES), 0)
    last_row, last_lane, tile_at = place_ref[0], place_ref[1], place_ref[2]
    shift = [
        [
            jnp.broadcast_to(offsets_ref[tile_at + k * chans + c], (SUBS, LANES)).astype(jnp.float32) / offset_unit
            for k in range(cols // TILE)
        ]
        for c in range(chans)
    ]
    for copy in copies:
        copy.wait()

    def body(t, carry):
        at = pl.multiple_of(SUBS * t, SUBS)
        here = pl.ds(at, SUBS)
        for j in range(own_tiles):
            there = pl.ds(j * LANES, LANES)
            planes = [src_ref[c, here, there] + shift[c][j * LANES // TILE] for c in range(chans)]
            planes.append(weight_ref[here, there])
            to_right = 1.0 - seam_damping * seam_right_ref[here, there].astype(jnp.float32)
            if j == own_tiles - 1:
                to_right = jnp.where(lane == last_lane, 0.0, to_right)
            to_down = 1.0 - seam_damping * seam_down_ref[here, there].astype(jnp.float32)
            planes += [to_right, jnp.where(at + sub == last_row, 0.0, to_down)]
            for p, plane in enumerate(planes):
                own_ref[p, j, here, :] = plane
            for side, start, cols_ref in ((0, 0, first_ref), (own_tiles - 1, LANES - SLOT, last_ref)):
                if j != side:
                    continue
                packed = [None] * (-(-len(planes) // SLOTS))
                for p, plane in enumerate(planes):
                    slot = p % SLOTS
                    by = (slot * SLOT - start) % LANES
                    moved = pltpu.roll(plane, by, 1) if by else plane
                    k = p // SLOTS
                    packed[k] = moved if slot == 0 else jnp.where(lane < slot * SLOT, packed[k], moved)
                for k, value in enumerate(packed):
                    cols_ref[k, here, :] = value
        return carry

    lax.fori_loop(0, rows // SUBS, body, 0)


def unpack(p, lefts, rights):
    lane = lane_index()
    slot = p % SLOTS
    if slot != SLOTS - 1:
        lefts = pltpu.roll(lefts, LANES - SLOT - slot * SLOT, 1)
    if slot:
        rights = pltpu.roll(rights, LANES - slot * SLOT, 1)
    return jnp.where(lane < SLOT, rights, jnp.where(lane >= LANES - SLOT, lefts, 0.0))


def ways_of(tiles):
    return WAYS if tiles % WAYS == 0 else 1


def take(value, index):
    return jnp.take_along_axis(value, index, axis=1)


def deal(values):
    ways = ways_of(len(values))
    lane = lane_index()
    out = []
    for g in range(0, len(values), ways):
        for m in range(ways):
            place = ways * lane + m
            result = None
            for t in range(ways):
                part = take(values[g + t], place % LANES) if ways > 1 else values[g + t]
                result = part if result is None else jnp.where(place >= t * LANES, part, result)
            out.append(result)
    return out


def gather_back(values, t):
    ways = ways_of(len(values))
    if ways == 1:
        return values[t]
    lane = lane_index()
    group = t // ways * ways
    place = (t % ways) * LANES + lane
    result = None
    for m in range(ways):
        part = take(values[group + m], place // ways)
        result = part if result is None else jnp.where(place % ways == m, part, result)
    return result


def own_dealt_kernel(own_ref, before_ref, after_ref, dealt_ref):
    planes, own_tiles, rows = own_ref.shape[:3]

    def body(t, carry):
        here = pl.ds(pl.multiple_of(SUBS * t, SUBS), SUBS)
        for p in range(planes):
            values = [own_ref[p, j, here, :] for j in range(own_tiles)]
            values.append(unpack(p, before_ref[p // SLOTS, here, :], after_ref[p // SLOTS, here, :]))
            for j, value in enumerate(deal(values)):
                dealt_ref[p, j, here, :] = value
        return carry

    lax.fori_loop(0, rows // SUBS, body, 0)


def rightward(values):
    tiles = len(values)
    ways = ways_of(tiles)
    last = lane_index() == LANES - 1
    ahead = {g: pltpu.roll(values[g], LANES - 1, 1) for g in range(0, tiles, ways)}
    out = []
    for j in range(tiles):
        if j % ways + 1 < ways:
            out.append(values[j + 1])
        else:
            g = j - ways + 1
            out.append(jnp.where(last, ahead[(g + ways) % tiles], ahead[g]))
    return out


def leftward(values):
    tiles = len(values)
    ways = ways_of(tiles)
    first = lane_index() == 0
    behind = {g: pltpu.roll(values[g + ways - 1], 1, 1) for g in range(0, tiles, ways)}
    out = []
    for j in range(tiles):
        if j % ways:
            out.append(values[j - 1])
        else:
            out.append(jnp.where(first, behind[(j - ways) % tiles], behind[j]))
    return out


def spread(b_right_ref, b_down_ref, z_ref, c, emit):
    tiles, height = z_ref.shape[1:3]
    steps = height // SUBS

    def at(i):
        return pl.ds(i * SUBS, SUBS)

    def z_at(i, j):
        return z_ref[c, j, at(i), :]

    from_above = [pltpu.roll(b_down_ref[j, at(steps - 1), :] * z_at(steps - 1, j), 1, 0) for j in range(tiles)]
    centre = [z_at(0, j) for j in range(tiles)]
    wrapped = [pltpu.roll(v, SUBS - 1, 0) for v in centre]
    for i in range(steps):
        below = [z_at(i + 1, j) for j in range(tiles)] if i + 1 < steps else wrapped
        b_right = [b_right_ref[j, at(i), :] for j in range(tiles)]
        to_right = rightward(centre)
        from_left = leftward([b * v for b, v in zip(b_right, centre)])
        for j in range(tiles):
            b_down = b_down_ref[j, at(i), :]
            moved = (b_right[j] * to_right[j] + from_left[j]) + (b_down * below[j] + from_above[j])
            from_above[j] = b_down * centre[j]
            emit(i, j, centre[j], moved)
        centre = below


def precondition(b_right_ref, b_down_ref, g_ref, z_ref, work_ref, c):
    poly = chebyshev_polynomial()
    degree = SWEEPS - 1

    def at(i):
        return pl.ds(i * SUBS, SUBS)

    def first(i, j, centre, moved):
        z_ref[c, j, at(i), :] = poly[degree] * moved + poly[degree - 1] * centre

    spread(b_right_ref, b_down_ref, g_ref, c, first)

    def pair(k, carry):
        adds = []
        for half in range(2):
            value = jnp.float32(poly[half])
            for later in range(1, (degree - 1) // 2):
                value = jnp.where(k == (degree - 1) // 2 - 1 - later, jnp.float32(poly[2 * later + half]), value)
            adds.append(value)

        def one(target, add):
            def emit(i, j, centre, moved):
                target[c, j, at(i), :] = moved + add * g_ref[c, j, at(i), :]

            return emit

        spread(b_right_ref, b_down_ref, z_ref, c, one(work_ref, adds[1]))
        spread(b_right_ref, b_down_ref, work_ref, c, one(z_ref, adds[0]))
        return carry

    lax.fori_loop(0, (degree - 1) // 2, pair, 0)


def next_residual(b_right_ref, b_down_ref, g_ref, z_ref, next_ref, c, own_of):
    height = g_ref.shape[2]
    steps = height // SUBS
    sums = {}

    def emit(i, j, centre, moved):
        at = pl.ds(i * SUBS, SUBS)
        g = g_ref[c, j, at, :]
        following = g - MIX * (centre - moved)
        next_ref[c, j, at, :] = following
        key = own_of(i, j)
        now = (g * centre, following * centre)
        before = sums.get(key)
        sums[key] = now if before is None else (before[0] + now[0], before[1] + now[1])

    spread(b_right_ref, b_down_ref, z_ref, c, emit)
    sub = lax.broadcasted_iota(jnp.int32, (SUBS, LANES), 0)
    lane = lane_index()
    total = [jnp.zeros((SUBS, LANES), jnp.float32)] * 2
    for (low, high, lanes), parts in sums.items():
        inside = jnp.logical_and(jnp.logical_and(sub >= low, sub <= high), lane < lanes)
        total = [t + jnp.where(inside, p, 0.0) for t, p in zip(total, parts)]
    return total


def first_kernel(
    dealt_ref, top_ref, bottom_ref, top_corners_ref, bottom_corners_ref,
    b_right_ref, b_down_ref, scale_ref, root_ref, g0_ref, z0_ref, g1_ref, f1_ref, g2_ref, sums_ref,
    natural, work_ref,
):
    planes, tiles, rows = dealt_ref.shape[:3]
    chans = planes - 3
    own_tiles = tiles - 1
    height = rows + 2 * HALO
    steps = height // SUBS
    packs = -(-planes // SLOTS)

    def copy_own(t, carry):
        here = pl.ds(pl.multiple_of(SUBS * t, SUBS), SUBS)
        there = pl.ds(pl.multiple_of(HALO + SUBS * t, SUBS), SUBS)
        for p in range(planes):
            for j in range(tiles):
                natural[p, j, there, :] = dealt_ref[p, j, here, :]
        return carry

    lax.fori_loop(0, rows // SUBS, copy_own, 0)

    def deal_edge(t, carry):
        for slab, corners, start in ((top_ref, top_corners_ref, 0), (bottom_ref, bottom_corners_ref, HALO + rows)):
            there = pl.ds(pl.multiple_of(start + SUBS * t, SUBS), SUBS)
            for p in range(planes):

                def rows_at(k):
                    return pl.ds(pl.multiple_of(k * HALO + SUBS * t, SUBS), SUBS)

                values = [slab[rows_at(p * own_tiles + j), :] for j in range(own_tiles)]
                values.append(
                    unpack(p, corners[rows_at(p // SLOTS), :], corners[rows_at(packs + p // SLOTS), :])
                )
                for j, value in enumerate(deal(values)):
                    natural[p, j, there, :] = value
        return carry

    lax.fori_loop(0, HALO // SUBS, deal_edge, 0)

    def at(i):
        return pl.ds(i * SUBS, SUBS)

    def interleaved(p, i, j):
        return natural[p, j, pl.ds(i, SUBS, stride=steps), :]

    to_up = [pltpu.roll(interleaved(chans + 2, steps - 1, j), 1, 0) for j in range(tiles)]
    for i in range(steps):
        to_right = [interleaved(chans + 1, i, j) for j in range(tiles)]
        to_left = leftward(to_right)
        for j in range(tiles):
            to_down = interleaved(chans + 2, i, j)
            diag = interleaved(chans, i, j) + to_right[j] + to_left[j] + to_down + to_up[j]
            inside = diag > 0.0
            safe = jnp.where(inside, diag, 1.0)
            guess = lax.rsqrt(safe)
            scale = guess * (1.5 - 0.5 * safe * guess * guess)
            scale_ref[j, at(i), :] = jnp.where(inside, scale, 0.0)
            root_ref[j, at(i), :] = safe * scale
            to_up[j] = to_down
    wrapped = [pltpu.roll(scale_ref[j, at(0), :], SUBS - 1, 0) for j in range(tiles)]
    for i in range(steps):
        scale = [scale_ref[j, at(i), :] for j in range(tiles)]
        right_scale = rightward(scale)
        for j in range(tiles):
            b_right_ref[j, at(i), :] = interleaved(chans + 1, i, j) * scale[j] * right_scale[j]
            down_scale = scale_ref[j, at(i + 1), :] if i + 1 < steps else wrapped[j]
            b_down_ref[j, at(i), :] = interleaved(chans + 2, i, j) * scale[j] * down_scale
            for c in range(chans):
                g0_ref[c, j, at(i), :] = interleaved(c, i, j) * scale[j]

    ways = ways_of(tiles)

    def own_of(i, j):
        low, high = -(-(HALO - i) // steps), (HALO + rows - 1 - i) // steps
        left = own_tiles * LANES - j // ways * ways * LANES - j % ways
        return low, high, min(LANES, max(0, -(-left // ways)))

    def channel(c, carry):
        precondition(b_right_ref, b_down_ref, g0_ref, z0_ref, work_ref, c)
        sum0, sum1 = next_residual(b_right_ref, b_down_ref, g0_ref, z0_ref, g1_ref, c, own_of)
        precondition(b_right_ref, b_down_ref, g1_ref, f1_ref, work_ref, c)
        sum2, sum3 = next_residual(b_right_ref, b_down_ref, g1_ref, f1_ref, g2_ref, c, own_of)
        return tuple(a + b for a, b in zip(carry, (sum0, sum1, sum2, sum3)))

    zero = jnp.zeros((SUBS, LANES), jnp.float32)
    parts = lax.fori_loop(0, chans, channel, (zero,) * 4)
    sub = lax.broadcasted_iota(jnp.int32, (SUBS, LANES), 0)
    sums = zero
    for k, part in enumerate(parts):
        sums = jnp.where(sub == k, jnp.sum(part), sums)
    sums_ref[...] = sums


def second_kernel(
    c, b_right_ref, b_down_ref, scale_ref, root_ref, g0_ref, z0_ref, g1_ref, f1_ref, g2_ref,
    fields_ref, f2_ref, work_ref, natural,
):
    rows, cols = fields_ref.shape[1:]
    tiles, height = scale_ref.shape[:2]
    steps = height // SUBS

    def at(i):
        return pl.ds(i * SUBS, SUBS)

    for j in range(tiles):
        for i in range(steps):
            work_ref[0, j, at(i), :] = g2_ref[c, j, at(i), :]
    precondition(b_right_ref, b_down_ref, work_ref.at[pl.ds(0, 1)], f2_ref, work_ref.at[pl.ds(1, 1)], 0)
    sources = ((g0_ref, c, root_ref), (g1_ref, c, root_ref), (g2_ref, c, root_ref),
               (z0_ref, c, scale_ref), (f1_ref, c, scale_ref), (f2_ref, 0, scale_ref))
    for k, (ref, channel, factor_ref) in enumerate(sources):
        for j in range(tiles):
            for i in range(steps):
                natural[j, pl.ds(i, SUBS, stride=steps), :] = ref[channel, j, at(i), :] * factor_ref[j, at(i), :]

        def body(t, carry, k=k):
            there = pl.ds(pl.multiple_of(HALO + SUBS * t, SUBS), SUBS)
            here = pl.ds(pl.multiple_of(SUBS * t, SUBS), SUBS)
            values = [natural[j, there, :] for j in range(tiles)]
            for j in range(cols // LANES):
                fields_ref[k, here, j * LANES:(j + 1) * LANES] = gather_back(values, j)
            return carry

        lax.fori_loop(0, rows // SUBS, body, 0)


def combine(n0, n1, n2, n3):
    gap = n0 - n1
    keep = -n1 / gap
    step = n0 / gap
    beta = (n0 * n2 - n1 * n1) / (gap * gap)
    along = keep + beta
    curvature = along * along * gap + 2.0 * along * step * (n1 - n2) + step * step * (n2 - n3)
    scaled = n0 * beta / curvature
    first_size = step * MIX
    second_size = scaled * MIX
    x0 = first_size + second_size * along
    x1 = second_size * step
    r0 = keep - scaled * along
    r1 = step + scaled * (along - step)
    r2 = scaled * step
    return x0, x1, r0, r1, r2


def third_kernel(sums_ref, *refs):
    *field_refs, solution_ref, residual_ref, smoothed_ref = refs
    rows, cols = solution_ref.shape[1:]
    x0, x1, r0, r1, r2 = combine(*[jnp.broadcast_to(sums_ref[k:k + 1, :], (SUBS, LANES)) for k in range(4)])

    def body(t, carry):
        here = pl.ds(pl.multiple_of(SUBS * t, SUBS), SUBS)
        for c, fields in enumerate(field_refs):
            for j in range(cols // LANES):
                there = pl.ds(j * LANES, LANES)
                e0, e1, e2, z0, f1, f2 = [fields[k, here, there] for k in range(6)]
                solution_ref[c, here, there] = x0 * z0 + x1 * f1
                residual_ref[c, here, there] = r0 * e0 + r1 * e1 + r2 * e2
                smoothed_ref[c, here, there] = r0 * z0 + r1 * f1 + r2 * f2
        return carry

    lax.fori_loop(0, rows // SUBS, body, 0)


def sum_over(value, axis):
    size = lax.axis_size(axis)
    if size & (size - 1):
        return lax.psum(value, axis)
    step = 1
    while step < size:
        value = value + lax.ppermute(value, axis, [(i, i ^ step) for i in range(size)])
        step *= 2
    return value


def per_device(source, weight, seam_right, seam_down, offsets):
    chans, rows, cols = source.shape
    row_axis, col_axis = lax.axis_size("row"), lax.axis_size("col")
    row_at, col_at = lax.axis_index("row"), lax.axis_index("col")
    tile_at = (row_at * rows // TILE * offsets.shape[1] + col_at * (cols // TILE)) * chans
    place = jnp.stack(
        [jnp.where(row_at == row_axis - 1, rows - 1, -1), jnp.where(col_at == col_axis - 1, LANES - 1, -1), tile_at]
    ).astype(jnp.int32)

    in_vmem = pl.BlockSpec(memory_space=pltpu.VMEM)
    in_smem = pl.BlockSpec(memory_space=pltpu.SMEM)
    in_hbm = pl.BlockSpec(memory_space=pltpu.HBM)
    params = pltpu.CompilerParams(vmem_limit_bytes=VMEM_LIMIT)

    def shaped(*shape):
        return jax.ShapeDtypeStruct(shape, jnp.float32)

    def scratch(*shape):
        return pltpu.VMEM(shape, jnp.float32)

    planes = chans + 3
    own_tiles = cols // LANES
    tiles = own_tiles + 1
    packs = -(-planes // SLOTS)
    own, first_cols, last_cols = pl.pallas_call(
        own_kernel,
        out_shape=[shaped(planes, own_tiles, rows, LANES)] + [shaped(packs, rows, LANES)] * 2,
        in_specs=[in_smem] * 2 + [in_hbm] * 4,
        out_specs=[in_vmem] * 3,
        scratch_shapes=[
            scratch(*source.shape),
            scratch(*weight.shape),
            pltpu.VMEM(weight.shape, jnp.int32),
            pltpu.VMEM(weight.shape, jnp.int32),
            pltpu.SemaphoreType.DMA((planes,)),
        ],
        compiler_params=params,
    )(place, offsets.reshape(-1), source, weight, seam_right, seam_down)

    down = [(i, i + 1) for i in range(row_axis - 1)]
    up = [(j, i) for i, j in down]
    onward = [(i, i + 1) for i in range(col_axis - 1)]
    back = [(j, i) for i, j in onward]
    top = lax.ppermute(own[:, :, rows - HALO:].reshape(-1, LANES), "row", down)
    bottom = lax.ppermute(own[:, :, :HALO].reshape(-1, LANES), "row", up)
    before = lax.ppermute(last_cols, "col", onward)
    after = lax.ppermute(first_cols, "col", back)

    def corners(low, high):
        parts = [before[:, low:high], after[:, low:high]]
        return jnp.concatenate([part.reshape(-1, LANES) for part in parts], axis=0)

    top_corners = lax.ppermute(corners(rows - HALO, rows), "row", down)
    bottom_corners = lax.ppermute(corners(0, HALO), "row", up)
    dealt = pl.pallas_call(
        own_dealt_kernel,
        out_shape=shaped(planes, tiles, rows, LANES),
        in_specs=[in_vmem] * 3,
        out_specs=in_vmem,
        compiler_params=params,
        cost_estimate=pl.CostEstimate(flops=10**8, bytes_accessed=5 * 10**6, transcendentals=0),
    )(own, before, after)

    height = rows + 2 * HALO
    plane = shaped(tiles, height, LANES)
    field = shaped(chans, tiles, height, LANES)
    *basis, sums = pl.pallas_call(
        first_kernel,
        out_shape=[plane] * 4 + [field] * 5 + [shaped(SUBS, LANES)],
        in_specs=[in_vmem] * 5,
        out_specs=[in_vmem] * 10,
        scratch_shapes=[scratch(planes, tiles, height, LANES), scratch(*field.shape)],
        compiler_params=params,
    )(dealt, top, bottom, top_corners, bottom_corners)

    total = sum_over(sum_over(sums, "col"), "row")
    fields = [
        pl.pallas_call(
            functools.partial(second_kernel, c),
            out_shape=shaped(6, rows, cols),
            in_specs=[in_vmem] * 9,
            out_specs=in_vmem,
            scratch_shapes=[
                scratch(1, tiles, height, LANES), scratch(2, tiles, height, LANES), scratch(tiles, height, LANES)
            ],
            compiler_params=params,
            cost_estimate=pl.CostEstimate(flops=10**8, bytes_accessed=10**7, transcendentals=0),
        )(*basis)
        for c in range(chans)
    ]
    return pl.pallas_call(
        third_kernel,
        out_shape=[shaped(chans, rows, cols)] * 3,
        in_specs=[in_vmem] * (1 + chans),
        out_specs=[in_vmem] * 3,
        compiler_params=params,
    )(total, *fields)


def solution(mesh):
    placed = (
        P(None, ("band", "row"), "col"),
        P(("band", "row"), "col"),
        P(("band", "row"), "col"),
        P(("band", "row"), "col"),
        P("band", None, None),
    )
    return jax.shard_map(
        per_device,
        mesh=mesh,
        in_specs=placed,
        out_specs=(
            P(None, ("band", "row"), "col"),
            P(None, ("band", "row"), "col"),
            P(None, ("band", "row"), "col"),
        ),
        check_vma=False,
    )
```

time: 76.2 us -> 80.1 us (1.051)
  waiting for transfers between devices: 26.4 us -> 7.57 us
  Pallas kernels: 29.4 us -> 45.3 us
  starting transfers between devices: 14.2 us -> 21 us
  local copies, waits for them, and re-layouts: 4.11 us -> 4.95 us
  other arithmetic: 0.93 us -> 0.11 us
    pallas_call x1 -> x4, Pallas kernels: 7.05 us -> 26.6 us  [the longest x3 22.6 us: per_device(): pl.pallas_call(functools.partial(second_kernel, c), out_shape=shaped(6, r...]
    ppermute x2 -> x4, waiting for transfers between devices: 16.1 us -> 6.73 us  [the longest x1 4.75 us: per_device(): bottom_corners = lax.ppermute(corners(0, HALO), 'row', up)]
    ppermute x2 -> x4, starting transfers between devices: 4.81 us -> 11.5 us  [the longest x1 4.55 us: per_device(): top_corners = lax.ppermute(corners(rows - HALO, rows), 'row', down)]
    ppermute x4, waiting for transfers between devices: 6.5 us -> 0.83 us  [sum_over(): lax.ppermute(value, axis, [(i, i ^ step) for i in range(size)])]
    ppermute x1, waiting for transfers between devices: 3.81 us -> 0.01 us  [per_device(): after = lax.ppermute(first_cols, 'col', back)]
    pallas_call x1, Pallas kernels: 18.2 us -> 15.3 us  [per_device(): pl.pallas_call(first_kernel, out_shape=[plane] * 4 + [field] * 5 + [shape...]
    unnamed x8 -> x9, local copies, waits for them, and re-layouts: 3.98 us -> 4.74 us
  transfers between devices with their start and end apart: 8 -> 10, of which waited for: 6 -> 3; matrix products, arithmetic and copies ran while one was open for 0% -> 0% of each run, Pallas kernels for 9% -> 33%
where the time goes in v4:
time: 80.1 us; the launch traced here: 79.7 us
  Pallas kernels  45.3 us (57%)
  starting transfers between devices  21 us (26%)
  waiting for transfers between devices  7.57 us (9%)
  local copies, waits for them, and re-layouts  4.95 us (6%)
  between operations  0.87 us (1%)
    pallas_call x3, Pallas kernels, per_device(): pl.pallas_call(functools.partial(second_kernel, c), out_shape=shaped(6, r...  22.6 us
    pallas_call x1, Pallas kernels, per_device(): pl.pallas_call(first_kernel, out_shape=[plane] * 4 + [field] * 5 + [shape...  15.3 us
    ppermute x4, starting transfers between devices, sum_over(): lax.ppermute(value, axis, [(i, i ^ step) for i in range(size)])  5.82 us
    ppermute x1, waiting for transfers between devices, per_device(): bottom_corners = lax.ppermute(corners(0, HALO), 'row', up)  4.75 us
    unnamed x9, local copies, waits for them, and re-layouts  4.74 us
    ppermute x1, starting transfers between devices, per_device(): top_corners = lax.ppermute(corners(rows - HALO, rows), 'row', down)  4.55 us
    ppermute x1, starting transfers between devices, per_device(): top = lax.ppermute(own[:, :, rows - HALO:].reshape(-1, LANES), 'row', down)  4.35 us
    pallas_call x1, Pallas kernels, per_device(): pl.pallas_call(own_dealt_kernel, out_shape=shaped(planes, tiles, rows, LA...  4.02 us
  transfers between devices with their start and end apart: 10, of which 3 were waited for; matrix products, arithmetic and copies ran while one was open for 0% of the time, Pallas kernels for 33%

profile of v4, /device:TPU:0, one launch (start us, length us, event | category | flops | bytes accessed | tf_op | source)
XLA Modules:
  0.0 79.7 jit_solution(2504009474761982054)
XLA Ops:
  0.7 0.8 copy.9
  1.4 0.1 reshape.27.offsets_ref
  1.5 0.1 pad_add_fusion.place_ref
  1.6 1.1 %copy-done = f32[3,64,1024]{2,1,0:T(8,128)S(1)} copy-done((f32[3,64,1024]{2,1,0:T(8,128)S(1)}, f32[3,64,1024]{2,1,0:T(8,128)}, u32[]{:S(2)}) %copy-start) | copy-done | bytes 786456
  2.7 0.9 %copy-done.1 = f32[64,1024]{1,0:T(8,128)S(1)} copy-done((f32[64,1024]{1,0:T(8,128)S(1)}, f32[64,1024]{1,0:T(8,128)}, u32[]{:S(2)}) %copy-start.1) | copy-done | bytes 262168
  3.7 0.9 %copy-done.2 = s32[64,1024]{1,0:T(8,128)S(1)} copy-done((s32[64,1024]{1,0:T(8,128)S(1)}, s32[64,1024]{1,0:T(8,128)}, u32[]{:S(2)}) %copy-start.2) | copy-done | bytes 262168
  4.6 0.9 %copy-done.3 = s32[64,1024]{1,0:T(8,128)S(1)} copy-done((s32[64,1024]{1,0:T(8,128)S(1)}, s32[64,1024]{1,0:T(8,128)}, u32[]{:S(2)}) %copy-start.3) | copy-done | bytes 262168
  5.6 1.5 %shard_map.76 = (f32[6,8,64,128]{3,2,1,0:T(8,128)S(1)}, f32[2,64,128]{2,1,0:T(8,128)S(1)}, f32[2,64,128]{2,1,0:T(8,128)S(1)}) custom-call(s32[3]{0:T(128)S(1)} %pad_add_fusion.place_ref, s32[48]{0:T(128)S(1)} %reshape.27.offsets_ref, f32[3,64,1024]{2,1,0:T(8,128)S(1)} %copy-done, f32[64,1024]{1,0:T(8,128)S(1)} %copy-done.1, s32[64,1024]{1,0:T(8,128)S(1)} %copy-done.2, ...), custom_call_target="tpu_custom_call" | custom-call | tf_op jit(solution)/shard_map/pallas_call | solution.py:484
  7.1 2.4 %collective-permute-start = (f32[2,64,128]{2,1,0:T(8,128)S(1)}, f32[2,64,128]{2,1,0:T(8,128)S(1)}, u32[]{:S(2)}, u32[]{:S(2)}) collective-permute-start(f32[2,64,128]{2,1,0:T(8,128)S(1)} %get-tuple-element.17), channel_id=1, source_target_pairs={{0,1},{1,2},{2,3},{4,5},{5,6},{6,7},{8,9},{9,10},{10,11},{12,13},{... | collective-permute-start | bytes 196616 | tf_op jit(solution)/shard_map/ppermute | solution.py:505
  9.5 1.3 %collective-permute-start.1 = (f32[2,64,128]{2,1,0:T(8,128)S(1)}, f32[2,64,128]{2,1,0:T(8,128)S(1)}, u32[]{:S(2)}, u32[]{:S(2)}) collective-permute-start(f32[2,64,128]{2,1,0:T(8,128)S(1)} %get-tuple-element.18), channel_id=1, source_target_pairs={{1,0},{2,1},{3,2},{5,4},{6,5},{7,6},{9,8},{10,9},{11,10},{13,12},{... | collective-permute-start | bytes 196616 | tf_op jit(solution)/shard_map/ppermute | solution.py:506
  10.8 0.1 fusion
  10.9 4.3 %collective-permute-start.2 = (f32[1152,128]{1,0:T(8,128)S(1)}, f32[1152,128]{1,0:T(8,128)S(1)}, u32[]{:S(2)}, u32[]{:S(2)}) collective-permute-start(f32[1152,128]{1,0:T(8,128)S(1)} %bitcast.10), channel_id=1, source_target_pairs={{0,4},{4,8},{8,12},{1,5},{5,9},{9,13},{2,6},{6,10},{10,14},{3,7},{... | collective-permute-start | bytes 1769480 | tf_op jit(solution)/shard_map/ppermute | solution.py:503
  15.2 1.3 %collective-permute-start.3 = (f32[1152,128]{1,0:T(8,128)S(1)}, f32[1152,128]{1,0:T(8,128)S(1)}, u32[]{:S(2)}, u32[]{:S(2)}) collective-permute-start(f32[1152,128]{1,0:T(8,128)S(1)} %bitcast.9), channel_id=1, source_target_pairs={{4,0},{8,4},{12,8},{5,1},{9,5},{13,9},{6,2},{10,6},{14,10},{7,3},{... | collective-permute-start | bytes 1769480 | tf_op jit(solution)/shard_map/ppermute | solution.py:504
  16.5 0.0 collective-permute-done.before_ref
  16.6 0.0 collective-permute-done.1.after_ref
  16.6 4.5 %collective-permute-start.4 = (f32[96,128]{1,0:T(8,128)S(1)}, f32[96,128]{1,0:T(8,128)S(1)}, u32[]{:S(2)}, u32[]{:S(2)}) collective-permute-start(f32[96,128]{1,0:T(8,128)S(1)} %pad_maximum_fusion), channel_id=1, source_target_pairs={{0,4},{4,8},{8,12},{1,5},{5,9},{9,13},{2,6},{6,10},{10,14},{3,7},{... | collective-permute-start | bytes 147464 | tf_op jit(solution)/shard_map/ppermute | solution.py:512
  21.2 1.3 %collective-permute-start.5 = (f32[96,128]{1,0:T(8,128)S(1)}, f32[96,128]{1,0:T(8,128)S(1)}, u32[]{:S(2)}, u32[]{:S(2)}) collective-permute-start(f32[96,128]{1,0:T(8,128)S(1)} %pad_maximum_fusion.1), channel_id=1, source_target_pairs={{4,0},{8,4},{12,8},{5,1},{9,5},{13,9},{6,2},{10,6},{14,10},{7,3},{... | collective-permute-start | bytes 147464 | tf_op jit(solution)/shard_map/ppermute | solution.py:513
  22.5 4.0 %shard_map.77.dealt_ref = f32[6,9,64,128]{3,2,1,0:T(8,128)S(1)} custom-call(f32[6,8,64,128]{3,2,1,0:T(8,128)S(1)} %get-tuple-element.16.own_ref, f32[2,64,128]{2,1,0:T(8,128)S(1)} %collective-permute-done.before_ref, f32[2,64,128]{2,1,0:T(8,128)S(1)} %collective-permute-done.1.after_ref), custom_call_target="tpu_custom_call" | custom-call | flops 100000000 | bytes 5000000 | tf_op jit(solution)/shard_map/pallas_call | solution.py:514
  26.5 2.0 %collective-permute-done.4.top_corners_ref = f32[96,128]{1,0:T(8,128)S(1)} collective-permute-done((f32[96,128]{1,0:T(8,128)S(1)}, f32[96,128]{1,0:T(8,128)S(1)}, u32[]{:S(2)}, u32[]{:S(2)}) %collective-permute-start.4) | collective-permute-done | bytes 49184 | tf_op jit(solution)/shard_map/ppermute | solution.py:512
  28.5 4.8 %collective-permute-done.5.bottom_corners_ref = f32[96,128]{1,0:T(8,128)S(1)} collective-permute-done((f32[96,128]{1,0:T(8,128)S(1)}, f32[96,128]{1,0:T(8,128)S(1)}, u32[]{:S(2)}, u32[]{:S(2)}) %collective-permute-start.5) | collective-permute-done | bytes 49184 | tf_op jit(solution)/shard_map/ppermute | solution.py:513
  33.2 15.3 %shard_map.78 = (f32[9,112,128]{2,1,0:T(8,128)S(1)}, f32[9,112,128]{2,1,0:T(8,128)S(1)}, f32[9,112,128]{2,1,0:T(8,128)S(1)}, f32[9,112,128]{2,1,0:T(8,128)S(1)},...) custom-call(f32[6,9,64,128]{3,2,1,0:T(8,128)S(1)} %shard_map.77.deal, ...), custom_call_target="tpu_custom_call" | custom-call | tf_op jit(solution)/shard_map/pallas_call | solution.py:526
  48.6 1.1 %collective-permute-start.6 = (f32[8,128]{1,0:T(8,128)S(1)}, f32[8,128]{1,0:T(8,128)S(1)}, u32[]{:S(2)}, u32[]{:S(2)}) collective-permute-start(f32[8,128]{1,0:T(8,128)S(1)} %get-tuple-element.19), channel_id=1, source_target_pairs={{0,1},{1,0},{2,3},{3,2},{4,5},{5,4},{6,7},{7,6},{8,9},{9,8},{10,11... | collective-permute-start | bytes 12296 | tf_op jit(solution)/shard_map/ppermute | solution.py:455
  49.6 0.8 %collective-permute-done.6 = f32[8,128]{1,0:T(8,128)S(1)} collective-permute-done((f32[8,128]{1,0:T(8,128)S(1)}, f32[8,128]{1,0:T(8,128)S(1)}, u32[]{:S(2)}, u32[]{:S(2)}) %collective-permute-start.6) | collective-permute-done | bytes 4128 | tf_op jit(solution)/shard_map/ppermute | solution.py:455
  50.4 2.1 %collective-permute-start.7 = (f32[8,128]{1,0:T(8,128)S(1)}, f32[8,128]{1,0:T(8,128)S(1)}, u32[]{:S(2)}, u32[]{:S(2)}) collective-permute-start(f32[8,128]{1,0:T(8,128)S(1)} %add.17), channel_id=1, source_target_pairs={{0,2},{1,3},{2,0},{3,1},{4,6},{5,7},{6,4},{7,5},{8,10},{9,11},{10,... | collective-permute-start | bytes 12296 | tf_op jit(solution)/shard_map/ppermute | solution.py:455
  52.5 7.5 %shard_map.81.refs_2_ = f32[6,64,1024]{2,1,0:T(8,128)S(1)} custom-call(f32[9,112,128]{2,1,0:T(8,128)S(1)} %get-tuple-element.20.b_right_ref, f32[9,112,128]{2,1,0:T(8,128)S(1)} %get-tuple-element.21.b_down_ref, f32[9,112,128]{2,1,0:T(8,128)S(1)} %get-tuple-element.22.scale_ref, f32[9,112,128]{2,1,0:T(8,128)S(1)} %get-tuple-element.23.root_ref, ...), custom_call_target="tpu_custom_call" | custom-call | flops 100000000 | bytes 10000000 | tf_op jit(solution)/shard_map/pallas_call | solution.py:537
  60.1 1.6 %collective-permute-start.8 = (f32[8,128]{1,0:T(8,128)S(1)}, f32[8,128]{1,0:T(8,128)S(1)}, u32[]{:S(2)}, u32[]{:S(2)}) collective-permute-start(f32[8,128]{1,0:T(8,128)S(1)} %add.18), channel_id=1, source_target_pairs={{0,4},{4,0},{8,12},{12,8},{1,5},{5,1},{9,13},{13,9},{2,6},{6,2},{1... | collective-permute-start | bytes 12296 | tf_op jit(solution)/shard_map/ppermute | solution.py:455
  61.7 7.5 %shard_map.80.refs_1_ = f32[6,64,1024]{2,1,0:T(8,128)S(1)} custom-call(f32[9,112,128]{2,1,0:T(8,128)S(1)} %get-tuple-element.20.b_right_ref, f32[9,112,128]{2,1,0:T(8,128)S(1)} %get-tuple-element.21.b_down_ref, f32[9,112,128]{2,1,0:T(8,128)S(1)} %get-tuple-element.22.scale_ref, f32[9,112,128]{2,1,0:T(8,128)S(1)} %get-tuple-element.23.root_ref, ...), custom_call_target="tpu_custom_call" | custom-call | flops 100000000 | bytes 10000000 | tf_op jit(solution)/shard_map/pallas_call | solution.py:537
  69.2 0.0 collective-permute-done.8
  69.2 1.1 %collective-permute-start.9 = (f32[8,128]{1,0:T(8,128)S(1)}, f32[8,128]{1,0:T(8,128)S(1)}, u32[]{:S(2)}, u32[]{:S(2)}) collective-permute-start(f32[8,128]{1,0:T(8,128)S(1)} %add.19), channel_id=1, source_target_pairs={{0,8},{4,12},{8,0},{12,4},{1,9},{5,13},{9,1},{13,5},{2,10},{6,14},... | collective-permute-start | bytes 12296 | tf_op jit(solution)/shard_map/ppermute | solution.py:455
  70.3 7.5 %shard_map.79.refs_0_ = f32[6,64,1024]{2,1,0:T(8,128)S(1)} custom-call(f32[9,112,128]{2,1,0:T(8,128)S(1)} %get-tuple-element.20.b_right_ref, f32[9,112,128]{2,1,0:T(8,128)S(1)} %get-tuple-element.21.b_down_ref, f32[9,112,128]{2,1,0:T(8,128)S(1)} %get-tuple-element.22.scale_ref, f32[9,112,128]{2,1,0:T(8,128)S(1)} %get-tuple-element.23.root_ref, ...), custom_call_target="tpu_custom_call" | custom-call | flops 100000000 | bytes 10000000 | tf_op jit(solution)/shard_map/pallas_call | solution.py:537
  77.9 0.0 collective-permute-done.9
  77.9 1.8 %shard_map.82 = (f32[3,64,1024]{2,1,0:T(8,128)}, f32[3,64,1024]{2,1,0:T(8,128)}, f32[3,64,1024]{2,1,0:T(8,128)}) custom-call(f32[8,128]{1,0:T(8,128)S(1)} %add.20.sums_ref, f32[6,64,1024]{2,1,0:T(8,128)S(1)} %shard_map.79.refs_0_, f32[6,64,1024]{2,1,0:T(8,128)S(1)} %shard_map.80.refs_1_, f32[6,64,1024]{2,1,0:T(8,128)S(1)} %shard_map.81.refs_2_), custom_call_target="tpu_custom_call" | custom-call | tf_op jit(solution)/shard_map/pallas_call | solution.py:550
  (15 shorter events, 0.1 us)
Async XLA Ops:
  1.6 1.1 %copy-start = (f32[3,64,1024]{2,1,0:T(8,128)S(1)}, f32[3,64,1024]{2,1,0:T(8,128)}, u32[]{:S(2)}) copy-start(f32[3,64,1024]{2,1,0:T(8,128)} %src_hbm.1) | copy-start | bytes 2359300
  2.7 0.9 %copy-start.1 = (f32[64,1024]{1,0:T(8,128)S(1)}, f32[64,1024]{1,0:T(8,128)}, u32[]{:S(2)}) copy-start(f32[64,1024]{1,0:T(8,128)} %weight_hbm.1) | copy-start | bytes 786436
  3.7 0.9 %copy-start.2 = (s32[64,1024]{1,0:T(8,128)S(1)}, s32[64,1024]{1,0:T(8,128)}, u32[]{:S(2)}) copy-start(s32[64,1024]{1,0:T(8,128)} %seam_right_hbm.1) | copy-start | bytes 786436
  4.6 0.9 %copy-start.3 = (s32[64,1024]{1,0:T(8,128)S(1)}, s32[64,1024]{1,0:T(8,128)}, u32[]{:S(2)}) copy-start(s32[64,1024]{1,0:T(8,128)} %seam_down_hbm.1) | copy-start | bytes 786436
  7.1 9.4 %collective-permute-start = (f32[2,64,128]{2,1,0:T(8,128)S(1)}, f32[2,64,128]{2,1,0:T(8,128)S(1)}, u32[]{:S(2)}, u32[]{:S(2)}) collective-permute-start(f32[2,64,128]{2,1,0:T(8,128)S(1)} %get-tuple-element.17), channel_id=1, source_target_pairs={{0,1},{1,2},{2,3},{4,5},{5,6},{6,7},{8,9},{9,10},{10,11},{12,13},{... | collective-permute-start | bytes 196616 | tf_op jit(solution)/shard_map/ppermute | solution.py:505
  9.5 7.1 %collective-permute-start.1 = (f32[2,64,128]{2,1,0:T(8,128)S(1)}, f32[2,64,128]{2,1,0:T(8,128)S(1)}, u32[]{:S(2)}, u32[]{:S(2)}) collective-permute-start(f32[2,64,128]{2,1,0:T(8,128)S(1)} %get-tuple-element.18), channel_id=1, source_target_pairs={{1,0},{2,1},{3,2},{5,4},{6,5},{7,6},{9,8},{10,9},{11,10},{13,12},{... | collective-permute-start | bytes 196616 | tf_op jit(solution)/shard_map/ppermute | solution.py:506
  10.9 22.3 %collective-permute-start.2 = (f32[1152,128]{1,0:T(8,128)S(1)}, f32[1152,128]{1,0:T(8,128)S(1)}, u32[]{:S(2)}, u32[]{:S(2)}) collective-permute-start(f32[1152,128]{1,0:T(8,128)S(1)} %bitcast.10), channel_id=1, source_target_pairs={{0,4},{4,8},{8,12},{1,5},{5,9},{9,13},{2,6},{6,10},{10,14},{3,7},{... | collective-permute-start | bytes 1769480 | tf_op jit(solution)/shard_map/ppermute | solution.py:503
  15.2 18.0 %collective-permute-start.3 = (f32[1152,128]{1,0:T(8,128)S(1)}, f32[1152,128]{1,0:T(8,128)S(1)}, u32[]{:S(2)}, u32[]{:S(2)}) collective-permute-start(f32[1152,128]{1,0:T(8,128)S(1)} %bitcast.9), channel_id=1, source_target_pairs={{4,0},{8,4},{12,8},{5,1},{9,5},{13,9},{6,2},{10,6},{14,10},{7,3},{... | collective-permute-start | bytes 1769480 | tf_op jit(solution)/shard_map/ppermute | solution.py:504
  16.6 11.9 %collective-permute-start.4 = (f32[96,128]{1,0:T(8,128)S(1)}, f32[96,128]{1,0:T(8,128)S(1)}, u32[]{:S(2)}, u32[]{:S(2)}) collective-permute-start(f32[96,128]{1,0:T(8,128)S(1)} %pad_maximum_fusion), channel_id=1, source_target_pairs={{0,4},{4,8},{8,12},{1,5},{5,9},{9,13},{2,6},{6,10},{10,14},{3,7},{... | collective-permute-start | bytes 147464 | tf_op jit(solution)/shard_map/ppermute | solution.py:512
  21.2 12.0 %collective-permute-start.5 = (f32[96,128]{1,0:T(8,128)S(1)}, f32[96,128]{1,0:T(8,128)S(1)}, u32[]{:S(2)}, u32[]{:S(2)}) collective-permute-start(f32[96,128]{1,0:T(8,128)S(1)} %pad_maximum_fusion.1), channel_id=1, source_target_pairs={{4,0},{8,4},{12,8},{5,1},{9,5},{13,9},{6,2},{10,6},{14,10},{7,3},{... | collective-permute-start | bytes 147464 | tf_op jit(solution)/shard_map/ppermute | solution.py:513
  48.6 1.9 %collective-permute-start.6 = (f32[8,128]{1,0:T(8,128)S(1)}, f32[8,128]{1,0:T(8,128)S(1)}, u32[]{:S(2)}, u32[]{:S(2)}) collective-permute-start(f32[8,128]{1,0:T(8,128)S(1)} %get-tuple-element.19), channel_id=1, source_target_pairs={{0,1},{1,0},{2,3},{3,2},{4,5},{5,4},{6,7},{7,6},{8,9},{9,8},{10,11... | collective-permute-start | bytes 12296 | tf_op jit(solution)/shard_map/ppermute | solution.py:455
  50.4 9.6 %collective-permute-start.7 = (f32[8,128]{1,0:T(8,128)S(1)}, f32[8,128]{1,0:T(8,128)S(1)}, u32[]{:S(2)}, u32[]{:S(2)}) collective-permute-start(f32[8,128]{1,0:T(8,128)S(1)} %add.17), channel_id=1, source_target_pairs={{0,2},{1,3},{2,0},{3,1},{4,6},{5,7},{6,4},{7,5},{8,10},{9,11},{10,... | collective-permute-start | bytes 12296 | tf_op jit(solution)/shard_map/ppermute | solution.py:455
  60.1 9.1 %collective-permute-start.8 = (f32[8,128]{1,0:T(8,128)S(1)}, f32[8,128]{1,0:T(8,128)S(1)}, u32[]{:S(2)}, u32[]{:S(2)}) collective-permute-start(f32[8,128]{1,0:T(8,128)S(1)} %add.18), channel_id=1, source_target_pairs={{0,4},{4,0},{8,12},{12,8},{1,5},{5,1},{9,13},{13,9},{2,6},{6,2},{1... | collective-permute-start | bytes 12296 | tf_op jit(solution)/shard_map/ppermute | solution.py:455
  69.2 8.6 %collective-permute-start.9 = (f32[8,128]{1,0:T(8,128)S(1)}, f32[8,128]{1,0:T(8,128)S(1)}, u32[]{:S(2)}, u32[]{:S(2)}) collective-permute-start(f32[8,128]{1,0:T(8,128)S(1)} %add.19), channel_id=1, source_target_pairs={{0,8},{4,12},{8,0},{12,4},{1,9},{5,13},{9,1},{13,5},{2,10},{6,14},... | collective-permute-start | bytes 12296 | tf_op jit(solution)/shard_map/ppermute | solution.py:455

commit v5 on v4

--- a/solution.py
+++ b/solution.py
@@ -66,9 +66,10 @@
     lane = lane_index()
     sub = lax.broadcasted_iota(jnp.int32, (SUBS, LANES), 0)
     last_row, last_lane, tile_at = place_ref[0], place_ref[1], place_ref[2]
+    tiles_all = offsets_ref.shape[0] // chans
     shift = [
         [
-            jnp.broadcast_to(offsets_ref[tile_at + k * chans + c], (SUBS, LANES)).astype(jnp.float32) / offset_unit
+            jnp.broadcast_to(offsets_ref[c * tiles_all + tile_at + k], (SUBS, LANES)).astype(jnp.float32) / offset_unit
             for k in range(cols // TILE)
         ]
         for c in range(chans)
@@ -108,7 +109,7 @@
 
 
 def unpack(p, lefts, rights):
-    lane = lane_index()
+    lane = lax.broadcasted_iota(jnp.int32, lefts.shape, 1)
     slot = p % SLOTS
     if slot != SLOTS - 1:
         lefts = pltpu.roll(lefts, LANES - SLOT - slot * SLOT, 1)
@@ -121,52 +122,58 @@
     return WAYS if tiles % WAYS == 0 else 1
 
 
-def take(value, index):
-    return jnp.take_along_axis(value, index, axis=1)
-
-
-def deal(values):
-    ways = ways_of(len(values))
-    lane = lane_index()
-    out = []
-    for g in range(0, len(values), ways):
+def exact_parts(value):
+    high = value.astype(jnp.bfloat16)
+    rest = value - high.astype(jnp.float32)
+    middle = rest.astype(jnp.bfloat16)
+    low = (rest - middle.astype(jnp.float32)).astype(jnp.bfloat16)
+    return jnp.concatenate([high, middle, low], axis=0)
+
+
+def permuted(value, index):
+    rows = value.shape[0]
+    out = jnp.dot(exact_parts(value), index, preferred_element_type=jnp.float32)
+    return (out[:rows] + out[rows:2 * rows]) + out[2 * rows:]
+
+
+def dealing(ways):
+    size = ways * LANES
+    column = lax.broadcasted_iota(jnp.int32, (size, size), 0)
+    place = lax.broadcasted_iota(jnp.int32, (size, size), 1)
+    return jnp.where(column == ways * (place % LANES) + place // LANES, 1.0, 0.0).astype(jnp.bfloat16)
+
+
+def undealing(ways):
+    size = ways * LANES
+    column = lax.broadcasted_iota(jnp.int32, (size, size), 1)
+    place = lax.broadcasted_iota(jnp.int32, (size, size), 0)
+    return jnp.where(column == ways * (place % LANES) + place // LANES, 1.0, 0.0).astype(jnp.bfloat16)
+
+
+def deal(tile_of, tiles, emit):
+    ways = ways_of(tiles)
+    matrix = dealing(ways) if ways > 1 else None
+    for g in range(0, tiles, ways):
+        if ways == 1:
+            emit(g, tile_of(g))
+            continue
+        value = permuted(jnp.concatenate([tile_of(g + m) for m in range(ways)], axis=1), matrix)
         for m in range(ways):
-            place = ways * lane + m
-            result = None
-            for t in range(ways):
-                part = take(values[g + t], place % LANES) if ways > 1 else values[g + t]
-                result = part if result is None else jnp.where(place >= t * LANES, part, result)
-            out.append(result)
-    return out
-
-
-def gather_back(values, t):
-    ways = ways_of(len(values))
-    if ways == 1:
-        return values[t]
-    lane = lane_index()
-    group = t // ways * ways
-    place = (t % ways) * LANES + lane
-    result = None
-    for m in range(ways):
-        part = take(values[group + m], place // ways)
-        result = part if result is None else jnp.where(place % ways == m, part, result)
-    return result
+            emit(g + m, value[:, m * LANES:(m + 1) * LANES])
 
 
 def own_dealt_kernel(own_ref, before_ref, after_ref, dealt_ref):
     planes, own_tiles, rows = own_ref.shape[:3]
 
-    def body(t, carry):
-        here = pl.ds(pl.multiple_of(SUBS * t, SUBS), SUBS)
-        for p in range(planes):
-            values = [own_ref[p, j, here, :] for j in range(own_tiles)]
-            values.append(unpack(p, before_ref[p // SLOTS, here, :], after_ref[p // SLOTS, here, :]))
-            for j, value in enumerate(deal(values)):
-                dealt_ref[p, j, here, :] = value
-        return carry
-
-    lax.fori_loop(0, rows // SUBS, body, 0)
+    def tile_of(j):
+        if j < own_tiles:
+            return own_ref[:, j].reshape(planes * rows, LANES)
+        return jnp.concatenate([unpack(p, before_ref[p // SLOTS], after_ref[p // SLOTS]) for p in range(planes)], axis=0)
+
+    def emit(j, value):
+        dealt_ref[:, j] = value.reshape(planes, rows, LANES)
+
+    deal(tile_of, own_tiles + 1, emit)
 
 
 def rightward(values):
@@ -198,33 +205,48 @@
     return out
 
 
-def spread(b_right_ref, b_down_ref, z_ref, c, emit):
-    tiles, height = z_ref.shape[1:3]
+def spread(b_right_ref, b_down_ref, z_ref, emit):
+    tiles, height = z_ref.shape[:2]
     steps = height // SUBS
+    ways = ways_of(tiles)
+    lane = lane_index()
+    first, last = (lane == 0, lane == LANES - 1)
 
     def at(i):
         return pl.ds(i * SUBS, SUBS)
 
-    def z_at(i, j):
-        return z_ref[c, j, at(i), :]
-
-    from_above = [pltpu.roll(b_down_ref[j, at(steps - 1), :] * z_at(steps - 1, j), 1, 0) for j in range(tiles)]
-    centre = [z_at(0, j) for j in range(tiles)]
+    from_above = [pltpu.roll(b_down_ref[j, at(steps - 1), :] * z_ref[j, at(steps - 1), :], 1, 0) for j in range(tiles)]
+    centre = [z_ref[j, at(0), :] for j in range(tiles)]
     wrapped = [pltpu.roll(v, SUBS - 1, 0) for v in centre]
     for i in range(steps):
-        below = [z_at(i + 1, j) for j in range(tiles)] if i + 1 < steps else wrapped
-        b_right = [b_right_ref[j, at(i), :] for j in range(tiles)]
-        to_right = rightward(centre)
-        from_left = leftward([b * v for b, v in zip(b_right, centre)])
+        pushed_out = {
+            g: pltpu.roll(b_right_ref[g + ways - 1, at(i), :] * centre[g + ways - 1], 1, 1)
+            for g in range(0, tiles, ways)
+        }
+        ahead = {g: pltpu.roll(centre[g], LANES - 1, 1) for g in range(0, tiles, ways)}
+        pushed = None
+        below = []
         for j in range(tiles):
+            g = j // ways * ways
+            b_right = b_right_ref[j, at(i), :]
             b_down = b_down_ref[j, at(i), :]
-            moved = (b_right[j] * to_right[j] + from_left[j]) + (b_down * below[j] + from_above[j])
+            below.append(z_ref[j, at(i + 1), :] if i + 1 < steps else wrapped[j])
+            if j == g:
+                from_left = jnp.where(first, pushed_out[(g - ways) % tiles], pushed_out[g])
+            else:
+                from_left = pushed
+            if j + 1 < g + ways:
+                to_right = centre[j + 1]
+                pushed = b_right * centre[j]
+            else:
+                to_right = jnp.where(last, ahead[(g + ways) % tiles], ahead[g])
+            moved = (b_right * to_right + from_left) + (b_down * below[j] + from_above[j])
             from_above[j] = b_down * centre[j]
             emit(i, j, centre[j], moved)
         centre = below
 
 
-def precondition(b_right_ref, b_down_ref, g_ref, z_ref, work_ref, c):
+def precondition(b_right_ref, b_down_ref, g_ref, z_ref, work_ref):
     poly = chebyshev_polynomial()
     degree = SWEEPS - 1
 
@@ -232,9 +254,9 @@
         return pl.ds(i * SUBS, SUBS)
 
     def first(i, j, centre, moved):
-        z_ref[c, j, at(i), :] = poly[degree] * moved + poly[degree - 1] * centre
-
-    spread(b_right_ref, b_down_ref, g_ref, c, first)
+        z_ref[j, at(i), :] = poly[degree] * moved + poly[degree - 1] * centre
+
+    spread(b_right_ref, b_down_ref, g_ref, first)
 
     def pair(k, carry):
         adds = []
@@ -246,33 +268,33 @@
 
         def one(target, add):
             def emit(i, j, centre, moved):
-                target[c, j, at(i), :] = moved + add * g_ref[c, j, at(i), :]
+                target[j, at(i), :] = moved + add * g_ref[j, at(i), :]
 
             return emit
 
-        spread(b_right_ref, b_down_ref, z_ref, c, one(work_ref, adds[1]))
-        spread(b_right_ref, b_down_ref, work_ref, c, one(z_ref, adds[0]))
+        spread(b_right_ref, b_down_ref, z_ref, one(work_ref, adds[1]))
+        spread(b_right_ref, b_down_ref, work_ref, one(z_ref, adds[0]))
         return carry
 
     lax.fori_loop(0, (degree - 1) // 2, pair, 0)
 
 
-def next_residual(b_right_ref, b_down_ref, g_ref, z_ref, next_ref, c, own_of):
-    height = g_ref.shape[2]
+def next_residual(b_right_ref, b_down_ref, g_ref, z_ref, next_ref, own_of):
+    height = g_ref.shape[1]
     steps = height // SUBS
     sums = {}
 
     def emit(i, j, centre, moved):
         at = pl.ds(i * SUBS, SUBS)
-        g = g_ref[c, j, at, :]
+        g = g_ref[j, at, :]
         following = g - MIX * (centre - moved)
-        next_ref[c, j, at, :] = following
+        next_ref[j, at, :] = following
         key = own_of(i, j)
         now = (g * centre, following * centre)
         before = sums.get(key)
         sums[key] = now if before is None else (before[0] + now[0], before[1] + now[1])
 
-    spread(b_right_ref, b_down_ref, z_ref, c, emit)
+    spread(b_right_ref, b_down_ref, z_ref, emit)
     sub = lax.broadcasted_iota(jnp.int32, (SUBS, LANES), 0)
     lane = lane_index()
     total = [jnp.zeros((SUBS, LANES), jnp.float32)] * 2
@@ -292,7 +314,6 @@
     own_tiles = tiles - 1
     height = rows + 2 * HALO
     steps = height // SUBS
-    packs = -(-planes // SLOTS)
 
     def copy_own(t, carry):
         here = pl.ds(pl.multiple_of(SUBS * t, SUBS), SUBS)
@@ -304,23 +325,22 @@
 
     lax.fori_loop(0, rows // SUBS, copy_own, 0)
 
-    def deal_edge(t, carry):
-        for slab, corners, start in ((top_ref, top_corners_ref, 0), (bottom_ref, bottom_corners_ref, HALO + rows)):
-            there = pl.ds(pl.multiple_of(start + SUBS * t, SUBS), SUBS)
+    def edge_tile(j):
+        parts = []
+        for slab, corners in ((top_ref, top_corners_ref), (bottom_ref, bottom_corners_ref)):
+            if j < own_tiles:
+                parts.append(slab[:, j].reshape(planes * HALO, LANES))
+                continue
             for p in range(planes):
-
-                def rows_at(k):
-                    return pl.ds(pl.multiple_of(k * HALO + SUBS * t, SUBS), SUBS)
-
-                values = [slab[rows_at(p * own_tiles + j), :] for j in range(own_tiles)]
-                values.append(
-                    unpack(p, corners[rows_at(p // SLOTS), :], corners[rows_at(packs + p // SLOTS), :])
-                )
-                for j, value in enumerate(deal(values)):
-                    natural[p, j, there, :] = value
-        return carry
-
-    lax.fori_loop(0, HALO // SUBS, deal_edge, 0)
+                parts.append(unpack(p, corners[0, p // SLOTS], corners[1, p // SLOTS]))
+        return jnp.concatenate(parts, axis=0)
+
+    def put_edge(j, value):
+        value = value.reshape(2, planes, HALO, LANES)
+        natural[:, j, 0:HALO, :] = value[0]
+        natural[:, j, HALO + rows:height, :] = value[1]
+
+    deal(edge_tile, tiles, put_edge)
 
     def at(i):
         return pl.ds(i * SUBS, SUBS)
@@ -361,10 +381,11 @@
         return low, high, min(LANES, max(0, -(-left // ways)))
 
     def channel(c, carry):
-        precondition(b_right_ref, b_down_ref, g0_ref, z0_ref, work_ref, c)
-        sum0, sum1 = next_residual(b_right_ref, b_down_ref, g0_ref, z0_ref, g1_ref, c, own_of)
-        precondition(b_right_ref, b_down_ref, g1_ref, f1_ref, work_ref, c)
-        sum2, sum3 = next_residual(b_right_ref, b_down_ref, g1_ref, f1_ref, g2_ref, c, own_of)
+        g0, z0, g1, f1, g2 = [ref.at[c] for ref in (g0_ref, z0_ref, g1_ref, f1_ref, g2_ref)]
+        precondition(b_right_ref, b_down_ref, g0, z0, work_ref)
+        sum0, sum1 = next_residual(b_right_ref, b_down_ref, g0, z0, g1, own_of)
+        precondition(b_right_ref, b_down_ref, g1, f1, work_ref)
+        sum2, sum3 = next_residual(b_right_ref, b_down_ref, g1, f1, g2, own_of)
         return tuple(a + b for a, b in zip(carry, (sum0, sum1, sum2, sum3)))
 
     zero = jnp.zeros((SUBS, LANES), jnp.float32)
@@ -376,37 +397,8 @@
     sums_ref[...] = sums
 
 
-def second_kernel(
-    c, b_right_ref, b_down_ref, scale_ref, root_ref, g0_ref, z0_ref, g1_ref, f1_ref, g2_ref,
-    fields_ref, f2_ref, work_ref, natural,
-):
-    rows, cols = fields_ref.shape[1:]
-    tiles, height = scale_ref.shape[:2]
-    steps = height // SUBS
-
-    def at(i):
-        return pl.ds(i * SUBS, SUBS)
-
-    for j in range(tiles):
-        for i in range(steps):
-            work_ref[0, j, at(i), :] = g2_ref[c, j, at(i), :]
-    precondition(b_right_ref, b_down_ref, work_ref.at[pl.ds(0, 1)], f2_ref, work_ref.at[pl.ds(1, 1)], 0)
-    sources = ((g0_ref, c, root_ref), (g1_ref, c, root_ref), (g2_ref, c, root_ref),
-               (z0_ref, c, scale_ref), (f1_ref, c, scale_ref), (f2_ref, 0, scale_ref))
-    for k, (ref, channel, factor_ref) in enumerate(sources):
-        for j in range(tiles):
-            for i in range(steps):
-                natural[j, pl.ds(i, SUBS, stride=steps), :] = ref[channel, j, at(i), :] * factor_ref[j, at(i), :]
-
-        def body(t, carry, k=k):
-            there = pl.ds(pl.multiple_of(HALO + SUBS * t, SUBS), SUBS)
-            here = pl.ds(pl.multiple_of(SUBS * t, SUBS), SUBS)
-            values = [natural[j, there, :] for j in range(tiles)]
-            for j in range(cols // LANES):
-                fields_ref[k, here, j * LANES:(j + 1) * LANES] = gather_back(values, j)
-            return carry
-
-        lax.fori_loop(0, rows // SUBS, body, 0)
+def second_kernel(c, b_right_ref, b_down_ref, g2_ref, f2_ref, work_ref):
+    precondition(b_right_ref, b_down_ref, g2_ref.at[c], f2_ref, work_ref)
 
 
 def combine(n0, n1, n2, n3):
@@ -427,23 +419,39 @@
     return x0, x1, r0, r1, r2
 
 
-def third_kernel(sums_ref, *refs):
-    *field_refs, solution_ref, residual_ref, smoothed_ref = refs
+def third_kernel(
+    sums_ref, scale_ref, root_ref, g0_ref, z0_ref, g1_ref, f1_ref, g2_ref, *refs
+):
+    *f2_refs, solution_ref, residual_ref, smoothed_ref, natural = refs
     rows, cols = solution_ref.shape[1:]
+    own_tiles = cols // LANES
+    tiles, height = scale_ref.shape[:2]
+    steps = height // SUBS
+    ways = ways_of(tiles)
     x0, x1, r0, r1, r2 = combine(*[jnp.broadcast_to(sums_ref[k:k + 1, :], (SUBS, LANES)) for k in range(4)])
-
-    def body(t, carry):
-        here = pl.ds(pl.multiple_of(SUBS * t, SUBS), SUBS)
-        for c, fields in enumerate(field_refs):
-            for j in range(cols // LANES):
-                there = pl.ds(j * LANES, LANES)
-                e0, e1, e2, z0, f1, f2 = [fields[k, here, there] for k in range(6)]
-                solution_ref[c, here, there] = x0 * z0 + x1 * f1
-                residual_ref[c, here, there] = r0 * e0 + r1 * e1 + r2 * e2
-                smoothed_ref[c, here, there] = r0 * z0 + r1 * f1 + r2 * f2
-        return carry
-
-    lax.fori_loop(0, rows // SUBS, body, 0)
+    matrix = undealing(ways) if ways > 1 else None
+    outs = (solution_ref, residual_ref, smoothed_ref)
+    for c, f2_ref in enumerate(f2_refs):
+        for j in range(tiles):
+            for i in range(steps):
+                at = pl.ds(i * SUBS, SUBS)
+                scale = scale_ref[j, at, :]
+                root = root_ref[j, at, :]
+                g0, g1, g2, z0, f1 = [ref[c, j, at, :] for ref in (g0_ref, g1_ref, g2_ref, z0_ref, f1_ref)]
+                f2 = f2_ref[j, at, :]
+                there = pl.ds(i, SUBS, stride=steps)
+                natural[c, 0, j, there, :] = scale * (x0 * z0 + x1 * f1)
+                natural[c, 1, j, there, :] = root * (r0 * g0 + r1 * g1 + r2 * g2)
+                natural[c, 2, j, there, :] = scale * (r0 * z0 + r1 * f1 + r2 * f2)
+        for g in range(0, own_tiles, ways):
+            value = jnp.concatenate(
+                [natural[c, :, g + m, HALO:HALO + rows, :].reshape(3 * rows, LANES) for m in range(ways)], axis=1
+            )
+            width = min(ways, own_tiles - g) * LANES
+            if ways > 1:
+                value = permuted(value, matrix[:, :width])
+            for k, ref in enumerate(outs):
+                ref[c, :, g * LANES:g * LANES + width] = value[k * rows:(k + 1) * rows]
 
 
 def sum_over(value, axis):
@@ -461,7 +469,7 @@
     chans, rows, cols = source.shape
     row_axis, col_axis = lax.axis_size("row"), lax.axis_size("col")
     row_at, col_at = lax.axis_index("row"), lax.axis_index("col")
-    tile_at = (row_at * rows // TILE * offsets.shape[1] + col_at * (cols // TILE)) * chans
+    tile_at = lax.div(row_at * rows, TILE) * offsets.shape[1] + col_at * (cols // TILE)
     place = jnp.stack(
         [jnp.where(row_at == row_axis - 1, rows - 1, -1), jnp.where(col_at == col_axis - 1, LANES - 1, -1), tile_at]
     ).astype(jnp.int32)
@@ -494,20 +502,23 @@
             pltpu.SemaphoreType.DMA((planes,)),
         ],
         compiler_params=params,
-    )(place, offsets.reshape(-1), source, weight, seam_right, seam_down)
+    )(
+        place,
+        offsets.transpose(2, 0, 1).reshape(-1),
+        *[pltpu.with_memory_space_constraint(v, pltpu.HBM) for v in (source, weight, seam_right, seam_down)],
+    )
 
     down = [(i, i + 1) for i in range(row_axis - 1)]
     up = [(j, i) for i, j in down]
     onward = [(i, i + 1) for i in range(col_axis - 1)]
     back = [(j, i) for i, j in onward]
-    top = lax.ppermute(own[:, :, rows - HALO:].reshape(-1, LANES), "row", down)
-    bottom = lax.ppermute(own[:, :, :HALO].reshape(-1, LANES), "row", up)
+    top = lax.ppermute(own[:, :, rows - HALO:], "row", down)
+    bottom = lax.ppermute(own[:, :, :HALO], "row", up)
     before = lax.ppermute(last_cols, "col", onward)
     after = lax.ppermute(first_cols, "col", back)
 
     def corners(low, high):
-        parts = [before[:, low:high], after[:, low:high]]
-        return jnp.concatenate([part.reshape(-1, LANES) for part in parts], axis=0)
+        return jnp.stack([before[:, low:high], after[:, low:high]])
 
     top_corners = lax.ppermute(corners(rows - HALO, rows), "row", down)
     bottom_corners = lax.ppermute(corners(0, HALO), "row", up)
@@ -528,32 +539,32 @@
         out_shape=[plane] * 4 + [field] * 5 + [shaped(SUBS, LANES)],
         in_specs=[in_vmem] * 5,
         out_specs=[in_vmem] * 10,
-        scratch_shapes=[scratch(planes, tiles, height, LANES), scratch(*field.shape)],
+        scratch_shapes=[scratch(planes, tiles, height, LANES), scratch(*plane.shape)],
         compiler_params=params,
     )(dealt, top, bottom, top_corners, bottom_corners)
 
     total = sum_over(sum_over(sums, "col"), "row")
-    fields = [
+    b_right, b_down, scale, root, g0, z0, g1, f1, g2 = basis
+    f2 = [
         pl.pallas_call(
             functools.partial(second_kernel, c),
-            out_shape=shaped(6, rows, cols),
-            in_specs=[in_vmem] * 9,
+            out_shape=plane,
+            in_specs=[in_vmem] * 3,
             out_specs=in_vmem,
-            scratch_shapes=[
-                scratch(1, tiles, height, LANES), scratch(2, tiles, height, LANES), scratch(tiles, height, LANES)
-            ],
+            scratch_shapes=[scratch(*plane.shape)],
             compiler_params=params,
             cost_estimate=pl.CostEstimate(flops=10**8, bytes_accessed=10**7, transcendentals=0),
-        )(*basis)
+        )(b_right, b_down, g2)
         for c in range(chans)
     ]
     return pl.pallas_call(
         third_kernel,
         out_shape=[shaped(chans, rows, cols)] * 3,
-        in_specs=[in_vmem] * (1 + chans),
+        in_specs=[in_vmem] * (8 + chans),
         out_specs=[in_vmem] * 3,
+        scratch_shapes=[scratch(chans, 3, tiles, height, LANES)],
         compiler_params=params,
-    )(total, *fields)
+    )(total, scale, root, g0, z0, g1, f1, g2, *f2)
 
 
 def solution(mesh):

time: 80.1 us -> 60 us (0.75)
  Pallas kernels: 45.3 us -> 25.9 us
  local copies, waits for them, and re-layouts: 4.95 us -> 0.89 us
  starting transfers between devices: 21 us -> 24.7 us
    pallas_call x3, Pallas kernels: 22.6 us -> 4.14 us  [per_device(): pl.pallas_call(functools.partial(second_kernel, c), out_shape=plane, in_s...]
    ppermute x1, waiting for transfers between devices: 4.75 us -> 0.01 us  [per_device(): bottom_corners = lax.ppermute(corners(0, HALO), 'row', up)]
    unnamed x9 -> x2, local copies, waits for them, and re-layouts: 4.74 us -> 0.67 us
    ppermute x1, waiting for transfers between devices: 1.97 us -> 5.97 us  [per_device(): top_corners = lax.ppermute(corners(rows - HALO, rows), 'row', down)]
    ppermute x4, starting transfers between devices: 5.82 us -> 9.56 us  [sum_over(): lax.ppermute(value, axis, [(i, i ^ step) for i in range(size)])]
    pallas_call x1, Pallas kernels: 1.81 us -> 4.31 us  [per_device(): pl.pallas_call(third_kernel, out_shape=[shaped(chans, rows, cols)] * 3, i...]
    pallas_call x1, Pallas kernels: 15.3 us -> 12.9 us  [per_device(): pl.pallas_call(first_kernel, out_shape=[plane] * 4 + [field] * 5 + [shape...]
    pallas_call x1, Pallas kernels: 4.02 us -> 1.81 us  [per_device(): pl.pallas_call(own_dealt_kernel, out_shape=shaped(planes, tiles, rows, LA...]
  transfers between devices with their start and end apart: 10 -> 10, of which waited for: 3 -> 5; matrix products, arithmetic and copies ran while one was open for 0% -> 0% of each run, Pallas kernels for 33% -> 10%
where the time goes in v5:
time: 60 us; the launch traced here: 59.8 us
  Pallas kernels  25.9 us (43%)
  starting transfers between devices  24.7 us (41%)
  waiting for transfers between devices  7.41 us (12%)
  local copies, waits for them, and re-layouts  0.89 us (1%)
  between operations  0.8 us (1%)
    pallas_call x1, Pallas kernels, per_device(): pl.pallas_call(first_kernel, out_shape=[plane] * 4 + [field] * 5 + [shape...  12.9 us
    ppermute x4, starting transfers between devices, sum_over(): lax.ppermute(value, axis, [(i, i ^ step) for i in range(size)])  9.56 us
    ppermute x1, waiting for transfers between devices, per_device(): top_corners = lax.ppermute(corners(rows - HALO, rows), 'row', down)  5.97 us
    ppermute x1, starting transfers between devices, per_device(): top = lax.ppermute(own[:, :, rows - HALO:], 'row', down)  4.98 us
    pallas_call x1, Pallas kernels, per_device(): pl.pallas_call(third_kernel, out_shape=[shaped(chans, rows, cols)] * 3, i...  4.31 us
    pallas_call x3, Pallas kernels, per_device(): pl.pallas_call(functools.partial(second_kernel, c), out_shape=plane, in_s...  4.14 us
    ppermute x1, starting transfers between devices, per_device(): top_corners = lax.ppermute(corners(rows - HALO, rows), 'row', down)  3.89 us
    pallas_call x1, Pallas kernels, per_device(): pl.pallas_call(own_kernel, out_shape=[shaped(planes, own_tiles, rows, LAN...  2.73 us
  transfers between devices with their start and end apart: 10, of which 5 were waited for; matrix products, arithmetic and copies ran while one was open for 0% of the time, Pallas kernels for 10%

profile of v5, /device:TPU:0, one launch (start us, length us, event | category | flops | bytes accessed | tf_op | source)
XLA Modules:
  0.0 59.8 jit_solution(10486411889754814306)
XLA Ops:
  0.6 0.0 copy-start
  0.7 0.7 %copy-done = s32[1,16,3]{1,0,2:T(1,128)S(1)} copy-done((s32[1,16,3]{1,0,2:T(1,128)S(1)}, s32[1,16,3]{1,0,2:T(1,128)}, u32[]{:S(2)}) %copy-start) | copy-done | bytes 216
  1.3 0.1 reshape.9.offsets_ref
  1.4 0.1 pad_add_fusion.place_ref
  1.5 2.7 %shard_map.76 = (f32[6,8,64,128]{3,2,1,0:T(8,128)S(1)}, f32[2,64,128]{2,1,0:T(8,128)S(1)}, f32[2,64,128]{2,1,0:T(8,128)S(1)}) custom-call(s32[3]{0:T(128)S(1)} %pad_add_fusion.place_ref, s32[48]{0:T(128)S(1)} %reshape.9.offsets_ref, f32[3,64,1024]{2,1,0:T(8,128)} %src_hbm.1, f32[64,1024]{1,0:T(8,128)} %weight_hbm.1, s32[64,1024]{1,0:T(8,128)} %seam_right_hbm.1, ...), custom_call_target="tpu_custom_call" | custom-call | tf_op jit(solution)/shard_map/pallas_call | solution.py:492
  4.2 2.4 %collective-permute-start = (f32[2,64,128]{2,1,0:T(8,128)S(1)}, f32[2,64,128]{2,1,0:T(8,128)S(1)}, u32[]{:S(2)}, u32[]{:S(2)}) collective-permute-start(f32[2,64,128]{2,1,0:T(8,128)S(1)} %get-tuple-element.17), channel_id=1, source_target_pairs={{0,1},{1,2},{2,3},{4,5},{5,6},{6,7},{8,9},{9,10},{10,11},{12,13},{... | collective-permute-start | bytes 196616 | tf_op jit(solution)/shard_map/ppermute | solution.py:517
  6.6 1.3 %collective-permute-start.1 = (f32[2,64,128]{2,1,0:T(8,128)S(1)}, f32[2,64,128]{2,1,0:T(8,128)S(1)}, u32[]{:S(2)}, u32[]{:S(2)}) collective-permute-start(f32[2,64,128]{2,1,0:T(8,128)S(1)} %get-tuple-element.18), channel_id=1, source_target_pairs={{1,0},{2,1},{3,2},{5,4},{6,5},{7,6},{9,8},{10,9},{11,10},{13,12},{... | collective-permute-start | bytes 196616 | tf_op jit(solution)/shard_map/ppermute | solution.py:518
  7.9 0.1 fusion
  8.0 1.3 %collective-permute-start.3 = (f32[6,8,24,128]{3,2,1,0:T(8,128)S(1)}, f32[6,8,24,128]{3,2,1,0:T(8,128)S(1)}, u32[]{:S(2)}, u32[]{:S(2)}) collective-permute-start(f32[6,8,24,128]{3,2,1,0:T(8,128)S(1)} %get-tuple-element.29), channel_id=1, source_target_pairs={{4,0},{8,4},{12,8},{5,1},{9,5},{13,9},{6,2},{10,6},{14,10},{7,3},{... | collective-permute-start | bytes 1769480 | tf_op jit(solution)/shard_map/ppermute | solution.py:516
  9.3 5.0 %collective-permute-start.2 = (f32[6,8,24,128]{3,2,1,0:T(8,128)S(1)}, f32[6,8,24,128]{3,2,1,0:T(8,128)S(1)}, u32[]{:S(2)}, u32[]{:S(2)}) collective-permute-start(f32[6,8,24,128]{3,2,1,0:T(8,128)S(1)} %get-tuple-element.30), channel_id=1, source_target_pairs={{0,4},{4,8},{8,12},{1,5},{5,9},{9,13},{2,6},{6,10},{10,14},{3,7},{... | collective-permute-start | bytes 1769480 | tf_op jit(solution)/shard_map/ppermute | solution.py:515
  14.3 0.0 collective-permute-done.before_ref
  14.3 0.0 collective-permute-done.1.after_ref
  14.4 3.9 %collective-permute-start.4 = (f32[2,2,24,128]{3,2,1,0:T(8,128)S(1)}, f32[2,2,24,128]{3,2,1,0:T(8,128)S(1)}, u32[]{:S(2)}, u32[]{:S(2)}) collective-permute-start(f32[2,2,24,128]{3,2,1,0:T(8,128)S(1)} %pad_maximum_fusion), channel_id=1, source_target_pairs={{0,4},{4,8},{8,12},{1,5},{5,9},{9,13},{2,6},{6,10},{10,14},{3,7},{... | collective-permute-start | bytes 147464 | tf_op jit(solution)/shard_map/ppermute | solution.py:523
  18.3 1.3 %collective-permute-start.5 = (f32[2,2,24,128]{3,2,1,0:T(8,128)S(1)}, f32[2,2,24,128]{3,2,1,0:T(8,128)S(1)}, u32[]{:S(2)}, u32[]{:S(2)}) collective-permute-start(f32[2,2,24,128]{3,2,1,0:T(8,128)S(1)} %pad_maximum_fusion.1), channel_id=1, source_target_pairs={{4,0},{8,4},{12,8},{5,1},{9,5},{13,9},{6,2},{10,6},{14,10},{7,3},{... | collective-permute-start | bytes 147464 | tf_op jit(solution)/shard_map/ppermute | solution.py:524
  19.6 1.8 %shard_map.77.dealt_ref = f32[6,9,64,128]{3,2,1,0:T(8,128)S(1)} custom-call(f32[6,8,64,128]{3,2,1,0:T(8,128)S(1)} %get-tuple-element.16.own_ref, f32[2,64,128]{2,1,0:T(8,128)S(1)} %collective-permute-done.before_ref, f32[2,64,128]{2,1,0:T(8,128)S(1)} %collective-permute-done.1.after_ref), custom_call_target="tpu_custom_call" | custom-call | flops 100000000 | bytes 5000000 | tf_op jit(solution)/shard_map/pallas_call | solution.py:525
  21.4 6.0 %collective-permute-done.4.top_corners_ref = f32[2,2,24,128]{3,2,1,0:T(8,128)S(1)} collective-permute-done((f32[2,2,24,128]{3,2,1,0:T(8,128)S(1)}, f32[2,2,24,128]{3,2,1,0:T(8,128)S(1)}, u32[]{:S(2)}, u32[]{:S(2)}) %collective-permute-start.4) | collective-permute-done | bytes 49184 | tf_op jit(solution)/shard_map/ppermute | solution.py:523
  27.4 0.0 collective-permute-done.5.bottom_corners_ref
  27.4 0.0 collective-permute-done.3.bottom_ref
  27.4 0.0 collective-permute-done.2.top_ref
  27.4 12.9 %shard_map.78 = (f32[9,112,128]{2,1,0:T(8,128)S(1)}, f32[9,112,128]{2,1,0:T(8,128)S(1)}, f32[9,112,128]{2,1,0:T(8,128)S(1)}, f32[9,112,128]{2,1,0:T(8,128)S(1)},...) custom-call(f32[6,9,64,128]{3,2,1,0:T(8,128)S(1)} %shard_map.77.deal, ...), custom_call_target="tpu_custom_call" | custom-call | tf_op jit(solution)/shard_map/pallas_call | solution.py:537
  40.3 1.8 %collective-permute-start.6 = (f32[8,128]{1,0:T(8,128)S(1)}, f32[8,128]{1,0:T(8,128)S(1)}, u32[]{:S(2)}, u32[]{:S(2)}) collective-permute-start(f32[8,128]{1,0:T(8,128)S(1)} %get-tuple-element.19), channel_id=1, source_target_pairs={{0,1},{1,0},{2,3},{3,2},{4,5},{5,4},{6,7},{7,6},{8,9},{9,8},{10,11... | collective-permute-start | bytes 12296 | tf_op jit(solution)/shard_map/ppermute | solution.py:463
  42.1 0.8 %collective-permute-done.6 = f32[8,128]{1,0:T(8,128)S(1)} collective-permute-done((f32[8,128]{1,0:T(8,128)S(1)}, f32[8,128]{1,0:T(8,128)S(1)}, u32[]{:S(2)}, u32[]{:S(2)}) %collective-permute-start.6) | collective-permute-done | bytes 4128 | tf_op jit(solution)/shard_map/ppermute | solution.py:463
  43.0 2.2 %collective-permute-start.7 = (f32[8,128]{1,0:T(8,128)S(1)}, f32[8,128]{1,0:T(8,128)S(1)}, u32[]{:S(2)}, u32[]{:S(2)}) collective-permute-start(f32[8,128]{1,0:T(8,128)S(1)} %add.16), channel_id=1, source_target_pairs={{0,2},{1,3},{2,0},{3,1},{4,6},{5,7},{6,4},{7,5},{8,10},{9,11},{10,... | collective-permute-start | bytes 12296 | tf_op jit(solution)/shard_map/ppermute | solution.py:463
  45.2 1.4 %shard_map.81.refs_2_ = f32[9,112,128]{2,1,0:T(8,128)S(1)} custom-call(f32[9,112,128]{2,1,0:T(8,128)S(1)} %get-tuple-element.27.b_right_ref, f32[9,112,128]{2,1,0:T(8,128)S(1)} %get-tuple-element.28.b_down_ref, f32[3,9,112,128]{3,2,1,0:T(8,128)S(1)} %get-tuple-element.26.g2_ref), custom_call_target="tpu_custom_call" | custom-call | flops 100000000 | bytes 10000000 | tf_op jit(solution)/shard_map/pallas_call | solution.py:549
  46.6 0.2 collective-permute-done.7
  46.8 2.5 %collective-permute-start.8 = (f32[8,128]{1,0:T(8,128)S(1)}, f32[8,128]{1,0:T(8,128)S(1)}, u32[]{:S(2)}, u32[]{:S(2)}) collective-permute-start(f32[8,128]{1,0:T(8,128)S(1)} %add.17), channel_id=1, source_target_pairs={{0,4},{4,0},{8,12},{12,8},{1,5},{5,1},{9,13},{13,9},{2,6},{6,2},{1... | collective-permute-start | bytes 12296 | tf_op jit(solution)/shard_map/ppermute | solution.py:463
  49.2 1.3 %shard_map.80.refs_1_ = f32[9,112,128]{2,1,0:T(8,128)S(1)} custom-call(f32[9,112,128]{2,1,0:T(8,128)S(1)} %get-tuple-element.27.b_right_ref, f32[9,112,128]{2,1,0:T(8,128)S(1)} %get-tuple-element.28.b_down_ref, f32[3,9,112,128]{3,2,1,0:T(8,128)S(1)} %get-tuple-element.26.g2_ref), custom_call_target="tpu_custom_call" | custom-call | flops 100000000 | bytes 10000000 | tf_op jit(solution)/shard_map/pallas_call | solution.py:549
  50.5 0.3 collective-permute-done.8
  50.8 3.0 %collective-permute-start.9 = (f32[8,128]{1,0:T(8,128)S(1)}, f32[8,128]{1,0:T(8,128)S(1)}, u32[]{:S(2)}, u32[]{:S(2)}) collective-permute-start(f32[8,128]{1,0:T(8,128)S(1)} %add.18), channel_id=1, source_target_pairs={{0,8},{4,12},{8,0},{12,4},{1,9},{5,13},{9,1},{13,5},{2,10},{6,14},... | collective-permute-start | bytes 12296 | tf_op jit(solution)/shard_map/ppermute | solution.py:463
  53.9 1.4 %shard_map.79.refs_0_ = f32[9,112,128]{2,1,0:T(8,128)S(1)} custom-call(f32[9,112,128]{2,1,0:T(8,128)S(1)} %get-tuple-element.27.b_right_ref, f32[9,112,128]{2,1,0:T(8,128)S(1)} %get-tuple-element.28.b_down_ref, f32[3,9,112,128]{3,2,1,0:T(8,128)S(1)} %get-tuple-element.26.g2_ref), custom_call_target="tpu_custom_call" | custom-call | flops 100000000 | bytes 10000000 | tf_op jit(solution)/shard_map/pallas_call | solution.py:549
  55.3 0.1 collective-permute-done.9
  55.4 4.3 %shard_map.82 = (f32[3,64,1024]{2,1,0:T(8,128)}, f32[3,64,1024]{2,1,0:T(8,128)}, f32[3,64,1024]{2,1,0:T(8,128)}) custom-call(f32[8,128]{1,0:T(8,128)S(1)} %add.19.sums_ref, f32[9,112,128]{2,1,0:T(8,128)S(1)} %get-tuple-element.20.scale_ref, f32[9,112,128]{2,1,0:T(8,128)S(1)} %get-tuple-element.21.root_ref, f32[3,9,112,128]{3,2,1,0:T(8,128)S(1)} %get-tuple-element.22.g0_ref, ...), custom_call_target="tpu_custom_call" | custom-call | tf_op jit(solution)/shard_map/pallas_call | solution.py:560
  (9 shorter events, 0.1 us)
Async XLA Ops:
  0.6 0.7 %copy-start = (s32[1,16,3]{1,0,2:T(1,128)S(1)}, s32[1,16,3]{1,0,2:T(1,128)}, u32[]{:S(2)}) copy-start(s32[1,16,3]{1,0,2:T(1,128)} %param.9) | copy-start | bytes 580
  4.2 10.1 %collective-permute-start = (f32[2,64,128]{2,1,0:T(8,128)S(1)}, f32[2,64,128]{2,1,0:T(8,128)S(1)}, u32[]{:S(2)}, u32[]{:S(2)}) collective-permute-start(f32[2,64,128]{2,1,0:T(8,128)S(1)} %get-tuple-element.17), channel_id=1, source_target_pairs={{0,1},{1,2},{2,3},{4,5},{5,6},{6,7},{8,9},{9,10},{10,11},{12,13},{... | collective-permute-start | bytes 196616 | tf_op jit(solution)/shard_map/ppermute | solution.py:517
  6.6 7.7 %collective-permute-start.1 = (f32[2,64,128]{2,1,0:T(8,128)S(1)}, f32[2,64,128]{2,1,0:T(8,128)S(1)}, u32[]{:S(2)}, u32[]{:S(2)}) collective-permute-start(f32[2,64,128]{2,1,0:T(8,128)S(1)} %get-tuple-element.18), channel_id=1, source_target_pairs={{1,0},{2,1},{3,2},{5,4},{6,5},{7,6},{9,8},{10,9},{11,10},{13,12},{... | collective-permute-start | bytes 196616 | tf_op jit(solution)/shard_map/ppermute | solution.py:518
  8.0 19.4 %collective-permute-start.3 = (f32[6,8,24,128]{3,2,1,0:T(8,128)S(1)}, f32[6,8,24,128]{3,2,1,0:T(8,128)S(1)}, u32[]{:S(2)}, u32[]{:S(2)}) collective-permute-start(f32[6,8,24,128]{3,2,1,0:T(8,128)S(1)} %get-tuple-element.29), channel_id=1, source_target_pairs={{4,0},{8,4},{12,8},{5,1},{9,5},{13,9},{6,2},{10,6},{14,10},{7,3},{... | collective-permute-start | bytes 1769480 | tf_op jit(solution)/shard_map/ppermute | solution.py:516
  9.3 18.1 %collective-permute-start.2 = (f32[6,8,24,128]{3,2,1,0:T(8,128)S(1)}, f32[6,8,24,128]{3,2,1,0:T(8,128)S(1)}, u32[]{:S(2)}, u32[]{:S(2)}) collective-permute-start(f32[6,8,24,128]{3,2,1,0:T(8,128)S(1)} %get-tuple-element.30), channel_id=1, source_target_pairs={{0,4},{4,8},{8,12},{1,5},{5,9},{9,13},{2,6},{6,10},{10,14},{3,7},{... | collective-permute-start | bytes 1769480 | tf_op jit(solution)/shard_map/ppermute | solution.py:515
  14.4 13.0 %collective-permute-start.4 = (f32[2,2,24,128]{3,2,1,0:T(8,128)S(1)}, f32[2,2,24,128]{3,2,1,0:T(8,128)S(1)}, u32[]{:S(2)}, u32[]{:S(2)}) collective-permute-start(f32[2,2,24,128]{3,2,1,0:T(8,128)S(1)} %pad_maximum_fusion), channel_id=1, source_target_pairs={{0,4},{4,8},{8,12},{1,5},{5,9},{9,13},{2,6},{6,10},{10,14},{3,7},{... | collective-permute-start | bytes 147464 | tf_op jit(solution)/shard_map/ppermute | solution.py:523
  18.3 9.1 %collective-permute-start.5 = (f32[2,2,24,128]{3,2,1,0:T(8,128)S(1)}, f32[2,2,24,128]{3,2,1,0:T(8,128)S(1)}, u32[]{:S(2)}, u32[]{:S(2)}) collective-permute-start(f32[2,2,24,128]{3,2,1,0:T(8,128)S(1)} %pad_maximum_fusion.1), channel_id=1, source_target_pairs={{4,0},{8,4},{12,8},{5,1},{9,5},{13,9},{6,2},{10,6},{14,10},{7,3},{... | collective-permute-start | bytes 147464 | tf_op jit(solution)/shard_map/ppermute | solution.py:524
  40.3 2.7 %collective-permute-start.6 = (f32[8,128]{1,0:T(8,128)S(1)}, f32[8,128]{1,0:T(8,128)S(1)}, u32[]{:S(2)}, u32[]{:S(2)}) collective-permute-start(f32[8,128]{1,0:T(8,128)S(1)} %get-tuple-element.19), channel_id=1, source_target_pairs={{0,1},{1,0},{2,3},{3,2},{4,5},{5,4},{6,7},{7,6},{8,9},{9,8},{10,11... | collective-permute-start | bytes 12296 | tf_op jit(solution)/shard_map/ppermute | solution.py:463
  43.0 3.8 %collective-permute-start.7 = (f32[8,128]{1,0:T(8,128)S(1)}, f32[8,128]{1,0:T(8,128)S(1)}, u32[]{:S(2)}, u32[]{:S(2)}) collective-permute-start(f32[8,128]{1,0:T(8,128)S(1)} %add.16), channel_id=1, source_target_pairs={{0,2},{1,3},{2,0},{3,1},{4,6},{5,7},{6,4},{7,5},{8,10},{9,11},{10,... | collective-permute-start | bytes 12296 | tf_op jit(solution)/shard_map/ppermute | solution.py:463
  46.8 4.1 %collective-permute-start.8 = (f32[8,128]{1,0:T(8,128)S(1)}, f32[8,128]{1,0:T(8,128)S(1)}, u32[]{:S(2)}, u32[]{:S(2)}) collective-permute-start(f32[8,128]{1,0:T(8,128)S(1)} %add.17), channel_id=1, source_target_pairs={{0,4},{4,0},{8,12},{12,8},{1,5},{5,1},{9,13},{13,9},{2,6},{6,2},{1... | collective-permute-start | bytes 12296 | tf_op jit(solution)/shard_map/ppermute | solution.py:463
  50.8 4.6 %collective-permute-start.9 = (f32[8,128]{1,0:T(8,128)S(1)}, f32[8,128]{1,0:T(8,128)S(1)}, u32[]{:S(2)}, u32[]{:S(2)}) collective-permute-start(f32[8,128]{1,0:T(8,128)S(1)} %add.18), channel_id=1, source_target_pairs={{0,8},{4,12},{8,0},{12,4},{1,9},{5,13},{9,1},{13,5},{2,10},{6,14},... | collective-permute-start | bytes 12296 | tf_op jit(solution)/shard_map/ppermute | solution.py:463

commit v6 on v5

--- a/solution.py
+++ b/solution.py
@@ -51,7 +51,7 @@
 
 def own_kernel(
     place_ref, offsets_ref, src_hbm, weight_hbm, seam_right_hbm, seam_down_hbm,
-    own_ref, first_ref, last_ref,
+    own_ref, first_swap_ref, second_swap_ref,
     src_ref, weight_ref, seam_right_ref, seam_down_ref, sems,
 ):
     chans, rows, cols = src_ref.shape
@@ -65,11 +65,11 @@
         copy.start()
     lane = lane_index()
     sub = lax.broadcasted_iota(jnp.int32, (SUBS, LANES), 0)
-    last_row, last_lane, tile_at = place_ref[0], place_ref[1], place_ref[2]
-    tiles_all = offsets_ref.shape[0] // chans
+    last_row, last_lane, tile_row, tile_at = [place_ref[k] for k in range(4)]
+    odd = place_ref[5] == 1
     shift = [
         [
-            jnp.broadcast_to(offsets_ref[c * tiles_all + tile_at + k], (SUBS, LANES)).astype(jnp.float32) / offset_unit
+            jnp.broadcast_to(offsets_ref[c, tile_row, tile_at + k], (SUBS, LANES)).astype(jnp.float32) / offset_unit
             for k in range(cols // TILE)
         ]
         for c in range(chans)
@@ -80,6 +80,7 @@
     def body(t, carry):
         at = pl.multiple_of(SUBS * t, SUBS)
         here = pl.ds(at, SUBS)
+        ends_of = {}
         for j in range(own_tiles):
             there = pl.ds(j * LANES, LANES)
             planes = [src_ref[c, here, there] + shift[c][j * LANES // TILE] for c in range(chans)]
@@ -91,18 +92,21 @@
             planes += [to_right, jnp.where(at + sub == last_row, 0.0, to_down)]
             for p, plane in enumerate(planes):
                 own_ref[p, j, here, :] = plane
-            for side, start, cols_ref in ((0, 0, first_ref), (own_tiles - 1, LANES - SLOT, last_ref)):
-                if j != side:
-                    continue
-                packed = [None] * (-(-len(planes) // SLOTS))
-                for p, plane in enumerate(planes):
-                    slot = p % SLOTS
-                    by = (slot * SLOT - start) % LANES
-                    moved = pltpu.roll(plane, by, 1) if by else plane
-                    k = p // SLOTS
-                    packed[k] = moved if slot == 0 else jnp.where(lane < slot * SLOT, packed[k], moved)
-                for k, value in enumerate(packed):
-                    cols_ref[k, here, :] = value
+            if j in (0, own_tiles - 1):
+                ends_of[j] = planes
+        ends = []
+        for start, planes in ((0, ends_of[0]), (LANES - SLOT, ends_of[own_tiles - 1])):
+            packed = [None] * (-(-len(planes) // SLOTS))
+            for p, plane in enumerate(planes):
+                slot = p % SLOTS
+                by = (slot * SLOT - start) % LANES
+                moved = pltpu.roll(plane, by, 1) if by else plane
+                k = p // SLOTS
+                packed[k] = moved if slot == 0 else jnp.where(lane < slot * SLOT, packed[k], moved)
+            ends.append(packed)
+        for k, (low, high) in enumerate(zip(*ends)):
+            first_swap_ref[k, here, :] = jnp.where(odd, low, high)
+            second_swap_ref[k, here, :] = jnp.where(odd, high, low)
         return carry
 
     lax.fori_loop(0, rows // SUBS, body, 0)
@@ -305,7 +309,7 @@
 
 
 def first_kernel(
-    dealt_ref, top_ref, bottom_ref, top_corners_ref, bottom_corners_ref,
+    place_ref, dealt_ref, first_rows_ref, second_rows_ref, first_corners_ref, second_corners_ref,
     b_right_ref, b_down_ref, scale_ref, root_ref, g0_ref, z0_ref, g1_ref, f1_ref, g2_ref, sums_ref,
     natural, work_ref,
 ):
@@ -325,15 +329,17 @@
 
     lax.fori_loop(0, rows // SUBS, copy_own, 0)
 
+    odd = place_ref[4] == 1
+
     def edge_tile(j):
-        parts = []
-        for slab, corners in ((top_ref, top_corners_ref), (bottom_ref, bottom_corners_ref)):
-            if j < own_tiles:
-                parts.append(slab[:, j].reshape(planes * HALO, LANES))
-                continue
-            for p in range(planes):
-                parts.append(unpack(p, corners[0, p // SLOTS], corners[1, p // SLOTS]))
-        return jnp.concatenate(parts, axis=0)
+        if j < own_tiles:
+            first, second = [ref[:, j].reshape(planes * HALO, LANES) for ref in (first_rows_ref, second_rows_ref)]
+        else:
+            first, second = [
+                jnp.concatenate([unpack(p, ref[0, p // SLOTS], ref[1, p // SLOTS]) for p in range(planes)], axis=0)
+                for ref in (first_corners_ref, second_corners_ref)
+            ]
+        return jnp.concatenate([jnp.where(odd, first, second), jnp.where(odd, second, first)], axis=0)
 
     def put_edge(j, value):
         value = value.reshape(2, planes, HALO, LANES)
@@ -422,15 +428,16 @@
 def third_kernel(
     sums_ref, scale_ref, root_ref, g0_ref, z0_ref, g1_ref, f1_ref, g2_ref, *refs
 ):
-    *f2_refs, solution_ref, residual_ref, smoothed_ref, natural = refs
-    rows, cols = solution_ref.shape[1:]
+    *f2_refs, solution_hbm, residual_hbm, smoothed_hbm, natural, done, sems = refs
+    rows, cols = solution_hbm.shape[1:]
     own_tiles = cols // LANES
     tiles, height = scale_ref.shape[:2]
     steps = height // SUBS
     ways = ways_of(tiles)
     x0, x1, r0, r1, r2 = combine(*[jnp.broadcast_to(sums_ref[k:k + 1, :], (SUBS, LANES)) for k in range(4)])
     matrix = undealing(ways) if ways > 1 else None
-    outs = (solution_ref, residual_ref, smoothed_ref)
+    outs = (solution_hbm, residual_hbm, smoothed_hbm)
+    copies = []
     for c, f2_ref in enumerate(f2_refs):
         for j in range(tiles):
             for i in range(steps):
@@ -450,8 +457,13 @@
             width = min(ways, own_tiles - g) * LANES
             if ways > 1:
                 value = permuted(value, matrix[:, :width])
-            for k, ref in enumerate(outs):
-                ref[c, :, g * LANES:g * LANES + width] = value[k * rows:(k + 1) * rows]
+            for k in range(len(outs)):
+                done[c, k, :, g * LANES:g * LANES + width] = value[k * rows:(k + 1) * rows]
+        for k, ref in enumerate(outs):
+            copies.append(pltpu.make_async_copy(done.at[c, k], ref.at[c], sems.at[c, k]))
+            copies[-1].start()
+    for copy in copies:
+        copy.wait()
 
 
 def sum_over(value, axis):
@@ -469,9 +481,16 @@
     chans, rows, cols = source.shape
     row_axis, col_axis = lax.axis_size("row"), lax.axis_size("col")
     row_at, col_at = lax.axis_index("row"), lax.axis_index("col")
-    tile_at = lax.div(row_at * rows, TILE) * offsets.shape[1] + col_at * (cols // TILE)
+    odd_row, odd_col = lax.rem(row_at, 2), lax.rem(col_at, 2)
     place = jnp.stack(
-        [jnp.where(row_at == row_axis - 1, rows - 1, -1), jnp.where(col_at == col_axis - 1, LANES - 1, -1), tile_at]
+        [
+            jnp.where(row_at == row_axis - 1, rows - 1, -1),
+            jnp.where(col_at == col_axis - 1, LANES - 1, -1),
+            lax.div(row_at * rows, TILE),
+            col_at * (cols // TILE),
+            odd_row,
+            odd_col,
+        ]
     ).astype(jnp.int32)
 
     in_vmem = pl.BlockSpec(memory_space=pltpu.VMEM)
@@ -489,7 +508,7 @@
     own_tiles = cols // LANES
     tiles = own_tiles + 1
     packs = -(-planes // SLOTS)
-    own, first_cols, last_cols = pl.pallas_call(
+    own, first_cols, second_cols = pl.pallas_call(
         own_kernel,
         out_shape=[shaped(planes, own_tiles, rows, LANES)] + [shaped(packs, rows, LANES)] * 2,
         in_specs=[in_smem] * 2 + [in_hbm] * 4,
@@ -504,24 +523,25 @@
         compiler_params=params,
     )(
         place,
-        offsets.transpose(2, 0, 1).reshape(-1),
+        offsets.transpose(2, 0, 1),
         *[pltpu.with_memory_space_constraint(v, pltpu.HBM) for v in (source, weight, seam_right, seam_down)],
     )
 
-    down = [(i, i + 1) for i in range(row_axis - 1)]
-    up = [(j, i) for i, j in down]
-    onward = [(i, i + 1) for i in range(col_axis - 1)]
-    back = [(j, i) for i, j in onward]
-    top = lax.ppermute(own[:, :, rows - HALO:], "row", down)
-    bottom = lax.ppermute(own[:, :, :HALO], "row", up)
-    before = lax.ppermute(last_cols, "col", onward)
-    after = lax.ppermute(first_cols, "col", back)
-
-    def corners(low, high):
-        return jnp.stack([before[:, low:high], after[:, low:high]])
-
-    top_corners = lax.ppermute(corners(rows - HALO, rows), "row", down)
-    bottom_corners = lax.ppermute(corners(0, HALO), "row", up)
+    def swap(first, second, axis):
+        size = lax.axis_size(axis)
+        pairs = [[(i, i + 1) for i in range(start, size - 1, 2)] for start in range(2)]
+        pairs = [some + [(j, i) for i, j in some] for some in pairs]
+        return [lax.ppermute(value, axis, some) for value, some in zip((first, second), pairs)]
+
+    def ends_of_rows(value):
+        high = (1 - odd_row) * (rows - HALO)
+        return [lax.dynamic_slice_in_dim(value, at, HALO, axis=2) for at in (high, rows - HALO - high)]
+
+    first_rows, second_rows = swap(*ends_of_rows(own), "row")
+    first_cols, second_cols = swap(first_cols, second_cols, "col")
+    before = jnp.where(odd_col == 1, first_cols, second_cols)
+    after = jnp.where(odd_col == 1, second_cols, first_cols)
+    first_corners, second_corners = swap(*ends_of_rows(jnp.stack([before, after])), "row")
     dealt = pl.pallas_call(
         own_dealt_kernel,
         out_shape=shaped(planes, tiles, rows, LANES),
@@ -537,11 +557,11 @@
     *basis, sums = pl.pallas_call(
         first_kernel,
         out_shape=[plane] * 4 + [field] * 5 + [shaped(SUBS, LANES)],
-        in_specs=[in_vmem] * 5,
+        in_specs=[in_smem] + [in_vmem] * 5,
         out_specs=[in_vmem] * 10,
         scratch_shapes=[scratch(planes, tiles, height, LANES), scratch(*plane.shape)],
         compiler_params=params,
-    )(dealt, top, bottom, top_corners, bottom_corners)
+    )(place, dealt, first_rows, second_rows, first_corners, second_corners)
 
     total = sum_over(sum_over(sums, "col"), "row")
     b_right, b_down, scale, root, g0, z0, g1, f1, g2 = basis
@@ -561,8 +581,12 @@
         third_kernel,
         out_shape=[shaped(chans, rows, cols)] * 3,
         in_specs=[in_vmem] * (8 + chans),
-        out_specs=[in_vmem] * 3,
-        scratch_shapes=[scratch(chans, 3, tiles, height, LANES)],
+        out_specs=[pl.BlockSpec(memory_space=pltpu.HBM)] * 3,
+        scratch_shapes=[
+            scratch(chans, 3, tiles, height, LANES),
+            scratch(chans, 3, rows, cols),
+            pltpu.SemaphoreType.DMA((chans, 3)),
+        ],
         compiler_params=params,
     )(total, scale, root, g0, z0, g1, f1, g2, *f2)
 

time: 60 us -> 56.4 us (0.940)
  starting transfers between devices: 24.7 us -> 15.3 us
  waiting for transfers between devices: 7.41 us -> 11.1 us
  local copies, waits for them, and re-layouts: 0.89 us -> 1.72 us
  other arithmetic: 0.1 us -> 0.88 us
    ppermute x6, starting transfers between devices: 15.1 us -> 10.4 us  [swap(): lax.ppermute(value, axis, some)]
    ppermute x4, starting transfers between devices: 9.56 us -> 4.93 us  [sum_over(): lax.ppermute(value, axis, [(i, i ^ step) for i in range(size)])]
    ppermute x4, waiting for transfers between devices: 1.42 us -> 3.52 us  [sum_over(): lax.ppermute(value, axis, [(i, i ^ step) for i in range(size)])]
    ppermute x6, waiting for transfers between devices: 5.99 us -> 7.62 us  [swap(): lax.ppermute(value, axis, some)]
    dynamic_slice x0 -> x1, local copies, waits for them, and re-layouts: none -> 0.95 us  [ends_of_rows(): lax.dynamic_slice_in_dim(value, at, HALO, axis=2)]
    select_n x0 -> x1, other arithmetic: none -> 0.85 us  [per_device(): after = jnp.where(odd_col == 1, second_cols, first_cols)]
  transfers between devices with their start and end apart: 10 -> 10, of which waited for: 5 -> 5; matrix products, arithmetic and copies ran while one was open for 0% -> 2% of each run, Pallas kernels for 10% -> 11%
where the time goes in v6:
time: 56.4 us; the launch traced here: 56.1 us
  Pallas kernels  26.3 us (47%)
  starting transfers between devices  15.3 us (27%)
  waiting for transfers between devices  11.1 us (20%)
  local copies, waits for them, and re-layouts  1.72 us (3%)
  other arithmetic  0.88 us (2%)
  between operations  0.75 us (1%)
    pallas_call x1, Pallas kernels, per_device(): pl.pallas_call(first_kernel, out_shape=[plane] * 4 + [field] * 5 + [shape...  13.4 us
    ppermute x6, starting transfers between devices, swap(): lax.ppermute(value, axis, some)  10.4 us
    ppermute x6, waiting for transfers between devices, swap(): lax.ppermute(value, axis, some)  7.62 us
    ppermute x4, starting transfers between devices, sum_over(): lax.ppermute(value, axis, [(i, i ^ step) for i in range(size)])  4.93 us
    pallas_call x3, Pallas kernels, per_device(): pl.pallas_call(functools.partial(second_kernel, c), out_shape=plane, in_s...  4.48 us
    pallas_call x1, Pallas kernels, per_device(): pl.pallas_call(third_kernel, out_shape=[shaped(chans, rows, cols)] * 3, i...  3.92 us
    ppermute x4, waiting for transfers between devices, sum_over(): lax.ppermute(value, axis, [(i, i ^ step) for i in range(size)])  3.52 us
    pallas_call x1, Pallas kernels, per_device(): pl.pallas_call(own_kernel, out_shape=[shaped(planes, own_tiles, rows, LAN...  2.74 us
  transfers between devices with their start and end apart: 10, of which 5 were waited for; matrix products, arithmetic and copies ran while one was open for 2% of the time, Pallas kernels for 11%

profile of v6, /device:TPU:0, one launch (start us, length us, event | category | flops | bytes accessed | tf_op | source)
XLA Modules:
  0.0 56.1 jit_solution(10721907489710764264)
XLA Ops:
  0.7 0.1 stack.36.place_ref
  0.7 0.0 copy-start
  0.7 0.7 %copy-done = s32[1,16,3]{1,0,2:T(1,128)S(1)} copy-done((s32[1,16,3]{1,0,2:T(1,128)S(1)}, s32[1,16,3]{1,0,2:T(1,128)}, u32[]{:S(2)}) %copy-start) | copy-done | bytes 216
  1.4 2.7 %shard_map.76 = (f32[6,8,64,128]{3,2,1,0:T(8,128)S(1)}, f32[2,64,128]{2,1,0:T(8,128)S(1)}, f32[2,64,128]{2,1,0:T(8,128)S(1)}) custom-call(s32[6]{0:T(128)S(1)} %stack.36.place_ref, s32[3,1,16]{2,1,0:T(1,128)S(1)} %bitcast.11, f32[3,64,1024]{2,1,0:T(8,128)} %src_hbm.1, f32[64,1024]{1,0:T(8,128)} %weight_hbm.1, s32[64,1024]{1,0:T(8,128)} %seam_right_hbm.1, ...), custom_call_target="tpu_custom_call" | custom-call | tf_op jit(solution)/shard_map/pallas_call | solution.py:511
  4.2 1.0 %constant_dynamic-slice_fusion = (f32[6,8,24,128]{3,2,1,0:T(8,128)}, f32[6,8,24,128]{3,2,1,0:T(8,128)S(1)}) fusion(f32[6,8,64,128]{3,2,1,0:T(8,128)S(1)} %get-tuple-element.16.own_ref, s32[]{:T(128)S(6)} %select_n.33, s32[]{:T(128)S(6)} %select_n.32), kind=kLoop, calls=%fused_computation.8 | loop fusion | bytes 2359304 | tf_op jit(solution)/shard_map/dynamic_slice | solution.py:538
  5.1 0.7 %collective-permute-start.3 = (f32[6,8,24,128]{3,2,1,0:T(8,128)}, f32[6,8,24,128]{3,2,1,0:T(8,128)S(1)}, u32[]{:S(2)}, u32[]{:S(2)}) collective-permute-start(f32[6,8,24,128]{3,2,1,0:T(8,128)} %get-tuple-element.29), channel_id=1, source_target_pairs={{4,8},{8,4},{5,9},{9,5},{6,10},{10,6},{7,11},{11,7},{20,24},{24,20... | collective-permute-start | bytes 1769480 | tf_op jit(solution)/shard_map/ppermute | solution.py:534
  5.8 5.9 %collective-permute-start.2 = (f32[6,8,24,128]{3,2,1,0:T(8,128)S(1)}, f32[6,8,24,128]{3,2,1,0:T(8,128)S(1)}, u32[]{:S(2)}, u32[]{:S(2)}) collective-permute-start(f32[6,8,24,128]{3,2,1,0:T(8,128)S(1)} %get-tuple-element.30), channel_id=1, source_target_pairs={{0,4},{8,12},{4,0},{12,8},{1,5},{9,13},{5,1},{13,9},{2,6},{10,14},... | collective-permute-start | bytes 1769480 | tf_op jit(solution)/shard_map/ppermute | solution.py:534
  11.7 0.0 collective-permute-start
  11.7 1.3 %collective-permute-start.1 = (f32[2,64,128]{2,1,0:T(8,128)S(1)}, f32[2,64,128]{2,1,0:T(8,128)}, u32[]{:S(2)}, u32[]{:S(2)}) collective-permute-start(f32[2,64,128]{2,1,0:T(8,128)S(1)} %get-tuple-element.18), channel_id=1, source_target_pairs={{1,2},{2,1},{5,6},{6,5},{9,10},{10,9},{13,14},{14,13},{17,18},{18,... | collective-permute-start | bytes 196616 | tf_op jit(solution)/shard_map/ppermute | solution.py:534
  13.0 0.0 collective-permute-done
  13.0 0.0 collective-permute-done.1
  13.0 0.9 %broadcast_select_fusion = (f32[2,64,128]{2,1,0:T(8,128)S(1)}, f32[2,64,128]{2,1,0:T(8,128)S(1)}) fusion(f32[2,64,128]{2,1,0:T(8,128)} %collective-permute-done.1, f32[2,64,128]{2,1,0:T(8,128)S(1)} %collective-permute-done, pred[]{:T(512)S(6)} %eq.12), kind=kLoop, calls=%fused_computation.6 | loop fusion | flops 32768 | bytes 262145 | tf_op jit(solution)/shard_map/jit(_where)/select_n | solution.py:543
  13.9 0.7 %collective-permute-start.5 = (f32[2,2,24,128]{3,2,1,0:T(8,128)S(1)}, f32[2,2,24,128]{3,2,1,0:T(8,128)S(1)}, u32[]{:S(2)}, u32[]{:S(2)}) collective-permute-start(f32[2,2,24,128]{3,2,1,0:T(8,128)S(1)} %get-tuple-element.31), channel_id=1, source_target_pairs={{4,8},{8,4},{5,9},{9,5},{6,10},{10,6},{7,11},{11,7},{20,24},{24,20... | collective-permute-start | bytes 147464 | tf_op jit(solution)/shard_map/ppermute | solution.py:534
  14.5 1.9 %collective-permute-start.4 = (f32[2,2,24,128]{3,2,1,0:T(8,128)S(1)}, f32[2,2,24,128]{3,2,1,0:T(8,128)S(1)}, u32[]{:S(2)}, u32[]{:S(2)}) collective-permute-start(f32[2,2,24,128]{3,2,1,0:T(8,128)S(1)} %get-tuple-element.32), channel_id=1, source_target_pairs={{0,4},{8,12},{4,0},{12,8},{1,5},{9,13},{5,1},{13,9},{2,6},{10,14},... | collective-permute-start | bytes 147464 | tf_op jit(solution)/shard_map/ppermute | solution.py:534
  16.4 1.8 %shard_map.77.dealt_ref = f32[6,9,64,128]{3,2,1,0:T(8,128)S(1)} custom-call(f32[6,8,64,128]{3,2,1,0:T(8,128)S(1)} %get-tuple-element.16.own_ref, f32[2,64,128]{2,1,0:T(8,128)S(1)} %get-tuple-element.34.before_ref, f32[2,64,128]{2,1,0:T(8,128)S(1)} %get-tuple-element.33.after_ref), custom_call_target="tpu_custom_call" | custom-call | flops 100000000 | bytes 5000000 | tf_op jit(solution)/shard_map/pallas_call | solution.py:545
  18.2 0.0 collective-permute-done.5.second_corners_ref
  18.2 7.6 %collective-permute-done.4.first_corners_ref = f32[2,2,24,128]{3,2,1,0:T(8,128)S(1)} collective-permute-done((f32[2,2,24,128]{3,2,1,0:T(8,128)S(1)}, f32[2,2,24,128]{3,2,1,0:T(8,128)S(1)}, u32[]{:S(2)}, u32[]{:S(2)}) %collective-permute-start.4) | collective-permute-done | bytes 49184 | tf_op jit(solution)/shard_map/ppermute | solution.py:534
  25.8 0.0 collective-permute-done.3.second_rows_ref
  25.8 0.0 collective-permute-done.2.first_rows_ref
  25.8 13.4 %shard_map.78 = (f32[9,112,128]{2,1,0:T(8,128)S(1)}, f32[9,112,128]{2,1,0:T(8,128)S(1)}, f32[9,112,128]{2,1,0:T(8,128)S(1)}, f32[9,112,128]{2,1,0:T(8,128)S(1)},...) custom-call(s32[6]{0:T(128)S(1)} %stack.36.place_ref, ...), custom_call_target="tpu_custom_call" | custom-call | tf_op jit(solution)/shard_map/pallas_call | solution.py:557
  39.2 0.1 collective-permute-start.6
  39.3 1.2 %collective-permute-done.6 = f32[8,128]{1,0:T(8,128)S(1)} collective-permute-done((f32[8,128]{1,0:T(8,128)S(1)}, f32[8,128]{1,0:T(8,128)S(1)}, u32[]{:S(2)}, u32[]{:S(2)}) %collective-permute-start.6) | collective-permute-done | bytes 4128 | tf_op jit(solution)/shard_map/ppermute | solution.py:475
  40.5 1.5 %collective-permute-start.7 = (f32[8,128]{1,0:T(8,128)S(1)}, f32[8,128]{1,0:T(8,128)S(1)}, u32[]{:S(2)}, u32[]{:S(2)}) collective-permute-start(f32[8,128]{1,0:T(8,128)S(1)} %add.23), channel_id=1, source_target_pairs={{0,2},{1,3},{2,0},{3,1},{4,6},{5,7},{6,4},{7,5},{8,10},{9,11},{10,... | collective-permute-start | bytes 12296 | tf_op jit(solution)/shard_map/ppermute | solution.py:475
  41.9 1.5 %shard_map.81.refs_2_ = f32[9,112,128]{2,1,0:T(8,128)S(1)} custom-call(f32[9,112,128]{2,1,0:T(8,128)S(1)} %get-tuple-element.27.b_right_ref, f32[9,112,128]{2,1,0:T(8,128)S(1)} %get-tuple-element.28.b_down_ref, f32[3,9,112,128]{3,2,1,0:T(8,128)S(1)} %get-tuple-element.26.g2_ref), custom_call_target="tpu_custom_call" | custom-call | flops 100000000 | bytes 10000000 | tf_op jit(solution)/shard_map/pallas_call | solution.py:569
  43.5 0.6 %collective-permute-done.7 = f32[8,128]{1,0:T(8,128)S(1)} collective-permute-done((f32[8,128]{1,0:T(8,128)S(1)}, f32[8,128]{1,0:T(8,128)S(1)}, u32[]{:S(2)}, u32[]{:S(2)}) %collective-permute-start.7) | collective-permute-done | bytes 4128 | tf_op jit(solution)/shard_map/ppermute | solution.py:475
  44.1 1.7 %collective-permute-start.8 = (f32[8,128]{1,0:T(8,128)S(1)}, f32[8,128]{1,0:T(8,128)S(1)}, u32[]{:S(2)}, u32[]{:S(2)}) collective-permute-start(f32[8,128]{1,0:T(8,128)S(1)} %add.24), channel_id=1, source_target_pairs={{0,4},{4,0},{8,12},{12,8},{1,5},{5,1},{9,13},{13,9},{2,6},{6,2},{1... | collective-permute-start | bytes 12296 | tf_op jit(solution)/shard_map/ppermute | solution.py:475
  45.8 1.4 %shard_map.80.refs_1_ = f32[9,112,128]{2,1,0:T(8,128)S(1)} custom-call(f32[9,112,128]{2,1,0:T(8,128)S(1)} %get-tuple-element.27.b_right_ref, f32[9,112,128]{2,1,0:T(8,128)S(1)} %get-tuple-element.28.b_down_ref, f32[3,9,112,128]{3,2,1,0:T(8,128)S(1)} %get-tuple-element.26.g2_ref), custom_call_target="tpu_custom_call" | custom-call | flops 100000000 | bytes 10000000 | tf_op jit(solution)/shard_map/pallas_call | solution.py:569
  47.3 0.4 collective-permute-done.8
  47.7 1.6 %collective-permute-start.9 = (f32[8,128]{1,0:T(8,128)S(1)}, f32[8,128]{1,0:T(8,128)S(1)}, u32[]{:S(2)}, u32[]{:S(2)}) collective-permute-start(f32[8,128]{1,0:T(8,128)S(1)} %add.25), channel_id=1, source_target_pairs={{0,8},{4,12},{8,0},{12,4},{1,9},{5,13},{9,1},{13,5},{2,10},{6,14},... | collective-permute-start | bytes 12296 | tf_op jit(solution)/shard_map/ppermute | solution.py:475
  49.3 1.5 %shard_map.79.refs_0_ = f32[9,112,128]{2,1,0:T(8,128)S(1)} custom-call(f32[9,112,128]{2,1,0:T(8,128)S(1)} %get-tuple-element.27.b_right_ref, f32[9,112,128]{2,1,0:T(8,128)S(1)} %get-tuple-element.28.b_down_ref, f32[3,9,112,128]{3,2,1,0:T(8,128)S(1)} %get-tuple-element.26.g2_ref), custom_call_target="tpu_custom_call" | custom-call | flops 100000000 | bytes 10000000 | tf_op jit(solution)/shard_map/pallas_call | solution.py:569
  50.8 1.4 %collective-permute-done.9 = f32[8,128]{1,0:T(8,128)S(1)} collective-permute-done((f32[8,128]{1,0:T(8,128)S(1)}, f32[8,128]{1,0:T(8,128)S(1)}, u32[]{:S(2)}, u32[]{:S(2)}) %collective-permute-start.9) | collective-permute-done | bytes 4128 | tf_op jit(solution)/shard_map/ppermute | solution.py:475
  52.2 3.9 %shard_map.82 = (f32[3,64,1024]{2,1,0:T(8,128)}, f32[3,64,1024]{2,1,0:T(8,128)}, f32[3,64,1024]{2,1,0:T(8,128)}) custom-call(f32[8,128]{1,0:T(8,128)S(1)} %add.26.sums_ref, f32[9,112,128]{2,1,0:T(8,128)S(1)} %get-tuple-element.20.scale_ref, f32[9,112,128]{2,1,0:T(8,128)S(1)} %get-tuple-element.21.root_ref, f32[3,9,112,128]{3,2,1,0:T(8,128)S(1)} %get-tuple-element.22.g0_ref, ...), custom_call_target="tpu_custom_call" | custom-call | tf_op jit(solution)/shard_map/pallas_call | solution.py:580
  (5 shorter events, 0.0 us)
Async XLA Ops:
  0.7 0.7 %copy-start = (s32[1,16,3]{1,0,2:T(1,128)S(1)}, s32[1,16,3]{1,0,2:T(1,128)}, u32[]{:S(2)}) copy-start(s32[1,16,3]{1,0,2:T(1,128)} %param.9) | copy-start | bytes 580
  5.1 20.7 %collective-permute-start.3 = (f32[6,8,24,128]{3,2,1,0:T(8,128)}, f32[6,8,24,128]{3,2,1,0:T(8,128)S(1)}, u32[]{:S(2)}, u32[]{:S(2)}) collective-permute-start(f32[6,8,24,128]{3,2,1,0:T(8,128)} %get-tuple-element.29), channel_id=1, source_target_pairs={{4,8},{8,4},{5,9},{9,5},{6,10},{10,6},{7,11},{11,7},{20,24},{24,20... | collective-permute-start | bytes 1769480 | tf_op jit(solution)/shard_map/ppermute | solution.py:534
  5.8 20.0 %collective-permute-start.2 = (f32[6,8,24,128]{3,2,1,0:T(8,128)S(1)}, f32[6,8,24,128]{3,2,1,0:T(8,128)S(1)}, u32[]{:S(2)}, u32[]{:S(2)}) collective-permute-start(f32[6,8,24,128]{3,2,1,0:T(8,128)S(1)} %get-tuple-element.30), channel_id=1, source_target_pairs={{0,4},{8,12},{4,0},{12,8},{1,5},{9,13},{5,1},{13,9},{2,6},{10,14},... | collective-permute-start | bytes 1769480 | tf_op jit(solution)/shard_map/ppermute | solution.py:534
  11.7 1.3 %collective-permute-start = (f32[2,64,128]{2,1,0:T(8,128)S(1)}, f32[2,64,128]{2,1,0:T(8,128)S(1)}, u32[]{:S(2)}, u32[]{:S(2)}) collective-permute-start(f32[2,64,128]{2,1,0:T(8,128)S(1)} %get-tuple-element.17), channel_id=1, source_target_pairs={{0,1},{2,3},{1,0},{3,2},{4,5},{6,7},{5,4},{7,6},{8,9},{10,11},{9,8... | collective-permute-start | bytes 196616 | tf_op jit(solution)/shard_map/ppermute | solution.py:534
  11.7 1.3 %collective-permute-start.1 = (f32[2,64,128]{2,1,0:T(8,128)S(1)}, f32[2,64,128]{2,1,0:T(8,128)}, u32[]{:S(2)}, u32[]{:S(2)}) collective-permute-start(f32[2,64,128]{2,1,0:T(8,128)S(1)} %get-tuple-element.18), channel_id=1, source_target_pairs={{1,2},{2,1},{5,6},{6,5},{9,10},{10,9},{13,14},{14,13},{17,18},{18,... | collective-permute-start | bytes 196616 | tf_op jit(solution)/shard_map/ppermute | solution.py:534
  13.9 4.3 %collective-permute-start.5 = (f32[2,2,24,128]{3,2,1,0:T(8,128)S(1)}, f32[2,2,24,128]{3,2,1,0:T(8,128)S(1)}, u32[]{:S(2)}, u32[]{:S(2)}) collective-permute-start(f32[2,2,24,128]{3,2,1,0:T(8,128)S(1)} %get-tuple-element.31), channel_id=1, source_target_pairs={{4,8},{8,4},{5,9},{9,5},{6,10},{10,6},{7,11},{11,7},{20,24},{24,20... | collective-permute-start | bytes 147464 | tf_op jit(solution)/shard_map/ppermute | solution.py:534
  14.5 11.3 %collective-permute-start.4 = (f32[2,2,24,128]{3,2,1,0:T(8,128)S(1)}, f32[2,2,24,128]{3,2,1,0:T(8,128)S(1)}, u32[]{:S(2)}, u32[]{:S(2)}) collective-permute-start(f32[2,2,24,128]{3,2,1,0:T(8,128)S(1)} %get-tuple-element.32), channel_id=1, source_target_pairs={{0,4},{8,12},{4,0},{12,8},{1,5},{9,13},{5,1},{13,9},{2,6},{10,14},... | collective-permute-start | bytes 147464 | tf_op jit(solution)/shard_map/ppermute | solution.py:534
  39.2 1.2 %collective-permute-start.6 = (f32[8,128]{1,0:T(8,128)S(1)}, f32[8,128]{1,0:T(8,128)S(1)}, u32[]{:S(2)}, u32[]{:S(2)}) collective-permute-start(f32[8,128]{1,0:T(8,128)S(1)} %get-tuple-element.19), channel_id=1, source_target_pairs={{0,1},{1,0},{2,3},{3,2},{4,5},{5,4},{6,7},{7,6},{8,9},{9,8},{10,11... | collective-permute-start | bytes 12296 | tf_op jit(solution)/shard_map/ppermute | solution.py:475
  40.5 3.6 %collective-permute-start.7 = (f32[8,128]{1,0:T(8,128)S(1)}, f32[8,128]{1,0:T(8,128)S(1)}, u32[]{:S(2)}, u32[]{:S(2)}) collective-permute-start(f32[8,128]{1,0:T(8,128)S(1)} %add.23), channel_id=1, source_target_pairs={{0,2},{1,3},{2,0},{3,1},{4,6},{5,7},{6,4},{7,5},{8,10},{9,11},{10,... | collective-permute-start | bytes 12296 | tf_op jit(solution)/shard_map/ppermute | solution.py:475
  44.1 3.6 %collective-permute-start.8 = (f32[8,128]{1,0:T(8,128)S(1)}, f32[8,128]{1,0:T(8,128)S(1)}, u32[]{:S(2)}, u32[]{:S(2)}) collective-permute-start(f32[8,128]{1,0:T(8,128)S(1)} %add.24), channel_id=1, source_target_pairs={{0,4},{4,0},{8,12},{12,8},{1,5},{5,1},{9,13},{13,9},{2,6},{6,2},{1... | collective-permute-start | bytes 12296 | tf_op jit(solution)/shard_map/ppermute | solution.py:475
  47.7 4.5 %collective-permute-start.9 = (f32[8,128]{1,0:T(8,128)S(1)}, f32[8,128]{1,0:T(8,128)S(1)}, u32[]{:S(2)}, u32[]{:S(2)}) collective-permute-start(f32[8,128]{1,0:T(8,128)S(1)} %add.25), channel_id=1, source_target_pairs={{0,8},{4,12},{8,0},{12,4},{1,9},{5,13},{9,1},{13,5},{2,10},{6,14},... | collective-permute-start | bytes 12296 | tf_op jit(solution)/shard_map/ppermute | solution.py:475

commit v7 on v6

--- a/solution.py
+++ b/solution.py
@@ -49,67 +49,108 @@
     return lax.broadcasted_iota(jnp.int32, (SUBS, LANES), 1)
 
 
+def pack(planes, start):
+    lane = lane_index()
+    packed = [None] * (-(-len(planes) // SLOTS))
+    for p, plane in enumerate(planes):
+        slot = p % SLOTS
+        by = (slot * SLOT - start) % LANES
+        moved = pltpu.roll(plane, by, 1) if by else plane
+        k = p // SLOTS
+        packed[k] = moved if slot == 0 else jnp.where(lane < slot * SLOT, packed[k], moved)
+    return packed
+
+
 def own_kernel(
     place_ref, offsets_ref, src_hbm, weight_hbm, seam_right_hbm, seam_down_hbm,
-    own_ref, first_swap_ref, second_swap_ref,
+    own_ref, first_rows_ref, second_rows_ref, first_cols_ref, second_cols_ref,
     src_ref, weight_ref, seam_right_ref, seam_down_ref, sems,
 ):
     chans, rows, cols = src_ref.shape
     own_tiles = cols // LANES
-    copies = [pltpu.make_async_copy(src_hbm.at[c], src_ref.at[c], sems.at[c]) for c in range(chans)]
-    for k, (there, here) in enumerate(
-        ((weight_hbm, weight_ref), (seam_right_hbm, seam_right_ref), (seam_down_hbm, seam_down_ref))
-    ):
-        copies.append(pltpu.make_async_copy(there, here, sems.at[chans + k]))
+    moves = [(weight_hbm, weight_ref), (seam_right_hbm, seam_right_ref), (seam_down_hbm, seam_down_ref)]
+    moves += [(src_hbm.at[c], src_ref.at[c]) for c in range(chans)]
+    copies = [pltpu.make_async_copy(there, here, sems.at[k]) for k, (there, here) in enumerate(moves)]
     for copy in copies:
         copy.start()
     lane = lane_index()
     sub = lax.broadcasted_iota(jnp.int32, (SUBS, LANES), 0)
     last_row, last_lane, tile_row, tile_at = [place_ref[k] for k in range(4)]
-    odd = place_ref[5] == 1
-    shift = [
-        [
+    odd_row, odd_col = (place_ref[4] == 1, place_ref[5] == 1)
+
+    def over_own(plane, value_of):
+        def body(t, carry):
+            at = pl.multiple_of(SUBS * t, SUBS)
+            for j in range(own_tiles):
+                own_ref[plane, j, pl.ds(at, SUBS), :] = value_of(at, j)
+            return carry
+
+        lax.fori_loop(0, rows // SUBS, body, 0)
+
+    def tile(ref, at, j):
+        return ref[pl.ds(at, SUBS), pl.ds(j * LANES, LANES)]
+
+    def to_right(at, j):
+        value = 1.0 - seam_damping * tile(seam_right_ref, at, j).astype(jnp.float32)
+        return jnp.where(lane == last_lane, 0.0, value) if j == own_tiles - 1 else value
+
+    def to_down(at, j):
+        value = 1.0 - seam_damping * tile(seam_down_ref, at, j).astype(jnp.float32)
+        return jnp.where(at + sub == last_row, 0.0, value)
+
+    copies[0].wait()
+    over_own(chans, lambda at, j: tile(weight_ref, at, j))
+    copies[1].wait()
+    over_own(chans + 1, to_right)
+    copies[2].wait()
+    over_own(chans + 2, to_down)
+    for c in range(chans):
+        shift = [
             jnp.broadcast_to(offsets_ref[c, tile_row, tile_at + k], (SUBS, LANES)).astype(jnp.float32) / offset_unit
             for k in range(cols // TILE)
         ]
-        for c in range(chans)
-    ]
-    for copy in copies:
-        copy.wait()
-
-    def body(t, carry):
-        at = pl.multiple_of(SUBS * t, SUBS)
-        here = pl.ds(at, SUBS)
-        ends_of = {}
-        for j in range(own_tiles):
-            there = pl.ds(j * LANES, LANES)
-            planes = [src_ref[c, here, there] + shift[c][j * LANES // TILE] for c in range(chans)]
-            planes.append(weight_ref[here, there])
-            to_right = 1.0 - seam_damping * seam_right_ref[here, there].astype(jnp.float32)
-            if j == own_tiles - 1:
-                to_right = jnp.where(lane == last_lane, 0.0, to_right)
-            to_down = 1.0 - seam_damping * seam_down_ref[here, there].astype(jnp.float32)
-            planes += [to_right, jnp.where(at + sub == last_row, 0.0, to_down)]
-            for p, plane in enumerate(planes):
-                own_ref[p, j, here, :] = plane
-            if j in (0, own_tiles - 1):
-                ends_of[j] = planes
-        ends = []
-        for start, planes in ((0, ends_of[0]), (LANES - SLOT, ends_of[own_tiles - 1])):
-            packed = [None] * (-(-len(planes) // SLOTS))
-            for p, plane in enumerate(planes):
-                slot = p % SLOTS
-                by = (slot * SLOT - start) % LANES
-                moved = pltpu.roll(plane, by, 1) if by else plane
-                k = p // SLOTS
-                packed[k] = moved if slot == 0 else jnp.where(lane < slot * SLOT, packed[k], moved)
-            ends.append(packed)
-        for k, (low, high) in enumerate(zip(*ends)):
-            first_swap_ref[k, here, :] = jnp.where(odd, low, high)
-            second_swap_ref[k, here, :] = jnp.where(odd, high, low)
+        copies[3 + c].wait()
+        over_own(c, lambda at, j, c=c, shift=shift: tile(src_ref.at[c], at, j) + shift[j * LANES // TILE])
+
+    planes = range(chans + 3)
+    low, high = pl.ds(0, HALO), pl.ds(rows - HALO, HALO)
+    for ref, odd, even in ((first_rows_ref, low, high), (second_rows_ref, high, low)):
+
+        @pl.when(odd_row)
+        def _(ref=ref, odd=odd):
+            for p in planes:
+                ref[p] = own_ref[p, :, odd, :]
+
+        @pl.when(jnp.logical_not(odd_row))
+        def _(ref=ref, even=even):
+            for p in planes:
+                ref[p] = own_ref[p, :, even, :]
+
+    def columns(t, carry):
+        here = pl.ds(pl.multiple_of(SUBS * t, SUBS), SUBS)
+        left = pack([own_ref[p, 0, here, :] for p in planes], 0)
+        right = pack([own_ref[p, own_tiles - 1, here, :] for p in planes], LANES - SLOT)
+        for k, (a, b) in enumerate(zip(left, right)):
+            first_cols_ref[k, here, :] = jnp.where(odd_col, a, b)
+            second_cols_ref[k, here, :] = jnp.where(odd_col, b, a)
         return carry
 
-    lax.fori_loop(0, rows // SUBS, body, 0)
+    lax.fori_loop(0, rows // SUBS, columns, 0)
+
+
+def corners_kernel(place_ref, first_ref, second_ref, first_out, second_out):
+    rows = first_ref.shape[1]
+    odd_row, odd_col = (place_ref[4] == 1, place_ref[5] == 1)
+    for k in range(first_ref.shape[0]):
+        for low in range(0, HALO, SUBS):
+            lows = [ref[k, low:low + SUBS, :] for ref in (first_ref, second_ref)]
+            at = rows - HALO + low
+            highs = [ref[k, at:at + SUBS, :] for ref in (first_ref, second_ref)]
+            for side in range(2):
+                near = jnp.where(odd_col, lows[side], lows[1 - side])
+                far = jnp.where(odd_col, highs[side], highs[1 - side])
+                first_out[side, k, low:low + SUBS, :] = jnp.where(odd_row, near, far)
+                second_out[side, k, low:low + SUBS, :] = jnp.where(odd_row, far, near)
 
 
 def unpack(p, lefts, rights):
@@ -126,18 +167,23 @@
     return WAYS if tiles % WAYS == 0 else 1
 
 
-def exact_parts(value):
-    high = value.astype(jnp.bfloat16)
-    rest = value - high.astype(jnp.float32)
-    middle = rest.astype(jnp.bfloat16)
-    low = (rest - middle.astype(jnp.float32)).astype(jnp.bfloat16)
-    return jnp.concatenate([high, middle, low], axis=0)
-
-
-def permuted(value, index):
+def split(value, count):
+    parts = []
+    for k in range(count):
+        part = value.astype(jnp.bfloat16)
+        parts.append(part)
+        if k + 1 < count:
+            value = value - part.astype(jnp.float32)
+    return jnp.concatenate(parts, axis=0)
+
+
+def permuted(value, index, count):
     rows = value.shape[0]
-    out = jnp.dot(exact_parts(value), index, preferred_element_type=jnp.float32)
-    return (out[:rows] + out[rows:2 * rows]) + out[2 * rows:]
+    out = jnp.dot(split(value, count), index, preferred_element_type=jnp.float32)
+    total = out[:rows]
+    for k in range(1, count):
+        total = total + out[k * rows:(k + 1) * rows]
+    return total
 
 
 def dealing(ways):
@@ -161,18 +207,23 @@
         if ways == 1:
             emit(g, tile_of(g))
             continue
-        value = permuted(jnp.concatenate([tile_of(g + m) for m in range(ways)], axis=1), matrix)
+        value = permuted(jnp.concatenate([tile_of(g + m) for m in range(ways)], axis=1), matrix, 3)
         for m in range(ways):
             emit(g + m, value[:, m * LANES:(m + 1) * LANES])
 
 
-def own_dealt_kernel(own_ref, before_ref, after_ref, dealt_ref):
+def own_dealt_kernel(place_ref, own_ref, first_ref, second_ref, dealt_ref):
     planes, own_tiles, rows = own_ref.shape[:3]
+    odd = place_ref[5] == 1
 
     def tile_of(j):
         if j < own_tiles:
             return own_ref[:, j].reshape(planes * rows, LANES)
-        return jnp.concatenate([unpack(p, before_ref[p // SLOTS], after_ref[p // SLOTS]) for p in range(planes)], axis=0)
+        parts = []
+        for p in range(planes):
+            first, second = first_ref[p // SLOTS], second_ref[p // SLOTS]
+            parts.append(unpack(p, jnp.where(odd, first, second), jnp.where(odd, second, first)))
+        return jnp.concatenate(parts, axis=0)
 
     def emit(j, value):
         dealt_ref[:, j] = value.reshape(planes, rows, LANES)
@@ -456,7 +507,7 @@
             )
             width = min(ways, own_tiles - g) * LANES
             if ways > 1:
-                value = permuted(value, matrix[:, :width])
+                value = permuted(value, matrix[:, :width], 2)
             for k in range(len(outs)):
                 done[c, k, :, g * LANES:g * LANES + width] = value[k * rows:(k + 1) * rows]
         for k, ref in enumerate(outs):
@@ -508,11 +559,13 @@
     own_tiles = cols // LANES
     tiles = own_tiles + 1
     packs = -(-planes // SLOTS)
-    own, first_cols, second_cols = pl.pallas_call(
+    own, first_rows, second_rows, first_cols, second_cols = pl.pallas_call(
         own_kernel,
-        out_shape=[shaped(planes, own_tiles, rows, LANES)] + [shaped(packs, rows, LANES)] * 2,
+        out_shape=[shaped(planes, own_tiles, rows, LANES)]
+        + [shaped(planes, own_tiles, HALO, LANES)] * 2
+        + [shaped(packs, rows, LANES)] * 2,
         in_specs=[in_smem] * 2 + [in_hbm] * 4,
-        out_specs=[in_vmem] * 3,
+        out_specs=[in_vmem] * 5,
         scratch_shapes=[
             scratch(*source.shape),
             scratch(*weight.shape),
@@ -533,23 +586,24 @@
         pairs = [some + [(j, i) for i, j in some] for some in pairs]
         return [lax.ppermute(value, axis, some) for value, some in zip((first, second), pairs)]
 
-    def ends_of_rows(value):
-        high = (1 - odd_row) * (rows - HALO)
-        return [lax.dynamic_slice_in_dim(value, at, HALO, axis=2) for at in (high, rows - HALO - high)]
-
-    first_rows, second_rows = swap(*ends_of_rows(own), "row")
+    first_rows, second_rows = swap(first_rows, second_rows, "row")
     first_cols, second_cols = swap(first_cols, second_cols, "col")
-    before = jnp.where(odd_col == 1, first_cols, second_cols)
-    after = jnp.where(odd_col == 1, second_cols, first_cols)
-    first_corners, second_corners = swap(*ends_of_rows(jnp.stack([before, after])), "row")
+    corners = pl.pallas_call(
+        corners_kernel,
+        out_shape=[shaped(2, packs, HALO, LANES)] * 2,
+        in_specs=[in_smem] + [in_vmem] * 2,
+        out_specs=[in_vmem] * 2,
+        compiler_params=params,
+    )(place, first_cols, second_cols)
+    first_corners, second_corners = swap(*corners, "row")
     dealt = pl.pallas_call(
         own_dealt_kernel,
         out_shape=shaped(planes, tiles, rows, LANES),
-        in_specs=[in_vmem] * 3,
+        in_specs=[in_smem] + [in_vmem] * 3,
         out_specs=in_vmem,
         compiler_params=params,
         cost_estimate=pl.CostEstimate(flops=10**8, bytes_accessed=5 * 10**6, transcendentals=0),
-    )(own, before, after)
+    )(place, own, first_cols, second_cols)
 
     height = rows + 2 * HALO
     plane = shaped(tiles, height, LANES)

time: 56.4 us -> 54.4 us (0.965)
  waiting for transfers between devices: 11.1 us -> 6.55 us
  starting transfers between devices: 15.3 us -> 19.4 us
  local copies, waits for them, and re-layouts: 1.72 us -> 0.77 us
  other arithmetic: 0.88 us -> 0.01 us
    ppermute x4, starting transfers between devices: 4.93 us -> 9.83 us  [sum_over(): lax.ppermute(value, axis, [(i, i ^ step) for i in range(size)])]
    ppermute x6, waiting for transfers between devices: 7.62 us -> 4.93 us  [swap(): lax.ppermute(value, axis, some)]
    ppermute x4, waiting for transfers between devices: 3.52 us -> 1.62 us  [sum_over(): lax.ppermute(value, axis, [(i, i ^ step) for i in range(size)])]
    dynamic_slice x1 -> x0, local copies, waits for them, and re-layouts: 0.95 us -> none  [ends_of_rows(): lax.dynamic_slice_in_dim(value, at, HALO, axis=2)]
    select_n x1 -> x0, other arithmetic: 0.85 us -> none  [per_device(): after = jnp.where(odd_col == 1, second_cols, first_cols)]
    pallas_call x1, Pallas kernels: 3.92 us -> 3.15 us  [per_device(): pl.pallas_call(third_kernel, out_shape=[shaped(chans, rows, cols)] * 3, i...]
    ppermute x6, starting transfers between devices: 10.4 us -> 9.59 us  [swap(): lax.ppermute(value, axis, some)]
    pallas_call x1, Pallas kernels: 1.78 us -> 2.35 us  [per_device(): pl.pallas_call(own_dealt_kernel, out_shape=shaped(planes, tiles, rows, LA...]
  transfers between devices with their start and end apart: 10 -> 10, of which waited for: 5 -> 6; matrix products, arithmetic and copies ran while one was open for 2% -> 0% of each run, Pallas kernels for 11% -> 14%
where the time goes in v7:
time: 54.4 us; the launch traced here: 54.2 us
  Pallas kernels  26.7 us (49%)
  starting transfers between devices  19.4 us (36%)
  waiting for transfers between devices  6.55 us (12%)
  local copies, waits for them, and re-layouts  0.77 us (1%)
  between operations  0.74 us (1%)
    pallas_call x1, Pallas kernels, per_device(): pl.pallas_call(first_kernel, out_shape=[plane] * 4 + [field] * 5 + [shape...  13.4 us
    ppermute x4, starting transfers between devices, sum_over(): lax.ppermute(value, axis, [(i, i ^ step) for i in range(size)])  9.83 us
    ppermute x6, starting transfers between devices, swap(): lax.ppermute(value, axis, some)  9.59 us
    ppermute x6, waiting for transfers between devices, swap(): lax.ppermute(value, axis, some)  4.93 us
    pallas_call x3, Pallas kernels, per_device(): pl.pallas_call(functools.partial(second_kernel, c), out_shape=plane, in_s...  4.48 us
    pallas_call x1, Pallas kernels, per_device(): pl.pallas_call(third_kernel, out_shape=[shaped(chans, rows, cols)] * 3, i...  3.15 us
    pallas_call x1, Pallas kernels, per_device(): pl.pallas_call(own_kernel, out_shape=[shaped(planes, own_tiles, rows, LAN...  2.71 us
    pallas_call x1, Pallas kernels, per_device(): pl.pallas_call(own_dealt_kernel, out_shape=shaped(planes, tiles, rows, LA...  2.35 us
  transfers between devices with their start and end apart: 10, of which 6 were waited for; matrix products, arithmetic and copies ran while one was open for 0% of the time, Pallas kernels for 14%

profile of v7, /device:TPU:0, one launch (start us, length us, event | category | flops | bytes accessed | tf_op | source)
XLA Modules:
  0.0 54.2 jit_solution(15658676551329947526)
XLA Ops:
  0.6 0.1 stack.27.place_ref
  0.7 0.0 copy-start
  0.7 0.7 %copy-done = s32[1,16,3]{1,0,2:T(1,128)S(1)} copy-done((s32[1,16,3]{1,0,2:T(1,128)S(1)}, s32[1,16,3]{1,0,2:T(1,128)}, u32[]{:S(2)}) %copy-start) | copy-done | bytes 216
  1.4 2.7 %shard_map.76 = (f32[6,8,64,128]{3,2,1,0:T(8,128)S(1)}, f32[6,8,24,128]{3,2,1,0:T(8,128)S(1)}, f32[6,8,24,128]{3,2,1,0:T(8,128)S(1)}, f32[2,64,128]{2,1,0:T(8,128)S(1)}, f32[2,64,128]{2,1,0:T(8,128)S(1)}) custom-call(s32[6]{0:T(128)S(1)} %stack.27.place_ref, s32[3,1,16]{2,1,0:T(1,128)S(1)} %bitcast.7, f32[3,64,1024]{2,1,0:T(8,128)} %src_hbm.1, ...), custom_call_target="tpu_custom_call" | custom-call | tf_op jit(solution)/shard_map/pallas_call | solution.py:562
  4.1 3.1 %collective-permute-start.2 = (f32[6,8,24,128]{3,2,1,0:T(8,128)S(1)}, f32[6,8,24,128]{3,2,1,0:T(8,128)S(1)}, u32[]{:S(2)}, u32[]{:S(2)}) collective-permute-start(f32[6,8,24,128]{3,2,1,0:T(8,128)S(1)} %get-tuple-element.23), channel_id=1, source_target_pairs={{0,4},{8,12},{4,0},{12,8},{1,5},{9,13},{5,1},{13,9},{2,6},{10,14},... | collective-permute-start | bytes 1769480 | tf_op jit(solution)/shard_map/ppermute | solution.py:587
  7.2 0.7 %collective-permute-start.3 = (f32[6,8,24,128]{3,2,1,0:T(8,128)S(1)}, f32[6,8,24,128]{3,2,1,0:T(8,128)S(1)}, u32[]{:S(2)}, u32[]{:S(2)}) collective-permute-start(f32[6,8,24,128]{3,2,1,0:T(8,128)S(1)} %get-tuple-element.24), channel_id=1, source_target_pairs={{4,8},{8,4},{5,9},{9,5},{6,10},{10,6},{7,11},{11,7},{20,24},{24,20... | collective-permute-start | bytes 1769480 | tf_op jit(solution)/shard_map/ppermute | solution.py:587
  7.9 0.1 collective-permute-start
  8.0 0.7 %collective-permute-start.1 = (f32[2,64,128]{2,1,0:T(8,128)S(1)}, f32[2,64,128]{2,1,0:T(8,128)S(1)}, u32[]{:S(2)}, u32[]{:S(2)}) collective-permute-start(f32[2,64,128]{2,1,0:T(8,128)S(1)} %get-tuple-element.22), channel_id=1, source_target_pairs={{1,2},{2,1},{5,6},{6,5},{9,10},{10,9},{13,14},{14,13},{17,18},{18,... | collective-permute-start | bytes 196616 | tf_op jit(solution)/shard_map/ppermute | solution.py:587
  8.7 0.6 %collective-permute-done.first_ref = f32[2,64,128]{2,1,0:T(8,128)S(1)} collective-permute-done((f32[2,64,128]{2,1,0:T(8,128)S(1)}, f32[2,64,128]{2,1,0:T(8,128)S(1)}, u32[]{:S(2)}, u32[]{:S(2)}) %collective-permute-start) | collective-permute-done | bytes 65568 | tf_op jit(solution)/shard_map/ppermute | solution.py:587
  9.2 0.0 collective-permute-done.1.second_ref
  9.2 0.6 %shard_map.78 = (f32[2,2,24,128]{3,2,1,0:T(8,128)S(1)}, f32[2,2,24,128]{3,2,1,0:T(8,128)S(1)}) custom-call(s32[6]{0:T(128)S(1)} %stack.27.place_ref, f32[2,64,128]{2,1,0:T(8,128)S(1)} %collective-permute-done.first_ref, f32[2,64,128]{2,1,0:T(8,128)S(1)} %collective-permute-done.1.second_ref), custom_call_target="tpu_custom_call" | custom-call | tf_op jit(solution)/shard_map/pallas_call | solution.py:591
  9.8 4.4 %collective-permute-start.4 = (f32[2,2,24,128]{3,2,1,0:T(8,128)S(1)}, f32[2,2,24,128]{3,2,1,0:T(8,128)S(1)}, u32[]{:S(2)}, u32[]{:S(2)}) collective-permute-start(f32[2,2,24,128]{3,2,1,0:T(8,128)S(1)} %get-tuple-element.25), channel_id=1, source_target_pairs={{0,4},{8,12},{4,0},{12,8},{1,5},{9,13},{5,1},{13,9},{2,6},{10,14},... | collective-permute-start | bytes 147464 | tf_op jit(solution)/shard_map/ppermute | solution.py:587
  14.2 0.7 %collective-permute-start.5 = (f32[2,2,24,128]{3,2,1,0:T(8,128)S(1)}, f32[2,2,24,128]{3,2,1,0:T(8,128)S(1)}, u32[]{:S(2)}, u32[]{:S(2)}) collective-permute-start(f32[2,2,24,128]{3,2,1,0:T(8,128)S(1)} %get-tuple-element.26), channel_id=1, source_target_pairs={{4,8},{8,4},{5,9},{9,5},{6,10},{10,6},{7,11},{11,7},{20,24},{24,20... | collective-permute-start | bytes 147464 | tf_op jit(solution)/shard_map/ppermute | solution.py:587
  14.9 2.3 %shard_map.77.dealt_ref = f32[6,9,64,128]{3,2,1,0:T(8,128)S(1)} custom-call(s32[6]{0:T(128)S(1)} %stack.27.place_ref, f32[6,8,64,128]{3,2,1,0:T(8,128)S(1)} %get-tuple-element.20.own_ref, f32[2,64,128]{2,1,0:T(8,128)S(1)} %collective-permute-done.first_ref, f32[2,64,128]{2,1,0:T(8,128)S(1)} %collective-permute-done.1.second_ref), custom_call_target="tpu_custom_call" | custom-call | flops 100000000 | bytes 5000000 | tf_op jit(solution)/shard_map/pallas_call | solution.py:599
  17.3 4.4 %collective-permute-done.4.first_corners_ref = f32[2,2,24,128]{3,2,1,0:T(8,128)S(1)} collective-permute-done((f32[2,2,24,128]{3,2,1,0:T(8,128)S(1)}, f32[2,2,24,128]{3,2,1,0:T(8,128)S(1)}, u32[]{:S(2)}, u32[]{:S(2)}) %collective-permute-start.4) | collective-permute-done | bytes 49184 | tf_op jit(solution)/shard_map/ppermute | solution.py:587
  21.6 0.0 collective-permute-done.5.second_corners_ref
  21.6 0.0 collective-permute-done.2.first_rows_ref
  21.6 0.0 collective-permute-done.3.second_rows_ref
  21.6 13.4 %shard_map.79 = (f32[9,112,128]{2,1,0:T(8,128)S(1)}, f32[9,112,128]{2,1,0:T(8,128)S(1)}, f32[9,112,128]{2,1,0:T(8,128)S(1)}, f32[9,112,128]{2,1,0:T(8,128)S(1)},...) custom-call(s32[6]{0:T(128)S(1)} %stack.27.place_ref, ...), custom_call_target="tpu_custom_call" | custom-call | tf_op jit(solution)/shard_map/pallas_call | solution.py:611
  35.0 0.6 %collective-permute-start.6 = (f32[8,128]{1,0:T(8,128)S(1)}, f32[8,128]{1,0:T(8,128)S(1)}, u32[]{:S(2)}, u32[]{:S(2)}) collective-permute-start(f32[8,128]{1,0:T(8,128)S(1)} %get-tuple-element.27), channel_id=1, source_target_pairs={{0,1},{1,0},{2,3},{3,2},{4,5},{5,4},{6,7},{7,6},{8,9},{9,8},{10,11... | collective-permute-start | bytes 12296 | tf_op jit(solution)/shard_map/ppermute | solution.py:526
  35.6 0.8 %collective-permute-done.6 = f32[8,128]{1,0:T(8,128)S(1)} collective-permute-done((f32[8,128]{1,0:T(8,128)S(1)}, f32[8,128]{1,0:T(8,128)S(1)}, u32[]{:S(2)}, u32[]{:S(2)}) %collective-permute-start.6) | collective-permute-done | bytes 4128 | tf_op jit(solution)/shard_map/ppermute | solution.py:526
  36.4 1.5 %collective-permute-start.7 = (f32[8,128]{1,0:T(8,128)S(1)}, f32[8,128]{1,0:T(8,128)S(1)}, u32[]{:S(2)}, u32[]{:S(2)}) collective-permute-start(f32[8,128]{1,0:T(8,128)S(1)} %add.12), channel_id=1, source_target_pairs={{0,2},{1,3},{2,0},{3,1},{4,6},{5,7},{6,4},{7,5},{8,10},{9,11},{10,... | collective-permute-start | bytes 12296 | tf_op jit(solution)/shard_map/ppermute | solution.py:526
  37.9 1.5 %shard_map.82.refs_2_ = f32[9,112,128]{2,1,0:T(8,128)S(1)} custom-call(f32[9,112,128]{2,1,0:T(8,128)S(1)} %get-tuple-element.35.b_right_ref, f32[9,112,128]{2,1,0:T(8,128)S(1)} %get-tuple-element.36.b_down_ref, f32[3,9,112,128]{3,2,1,0:T(8,128)S(1)} %get-tuple-element.34.g2_ref), custom_call_target="tpu_custom_call" | custom-call | flops 100000000 | bytes 10000000 | tf_op jit(solution)/shard_map/pallas_call | solution.py:623
  39.4 0.6 %collective-permute-done.7 = f32[8,128]{1,0:T(8,128)S(1)} collective-permute-done((f32[8,128]{1,0:T(8,128)S(1)}, f32[8,128]{1,0:T(8,128)S(1)}, u32[]{:S(2)}, u32[]{:S(2)}) %collective-permute-start.7) | collective-permute-done | bytes 4128 | tf_op jit(solution)/shard_map/ppermute | solution.py:526
  40.1 4.6 %collective-permute-start.8 = (f32[8,128]{1,0:T(8,128)S(1)}, f32[8,128]{1,0:T(8,128)S(1)}, u32[]{:S(2)}, u32[]{:S(2)}) collective-permute-start(f32[8,128]{1,0:T(8,128)S(1)} %add.13), channel_id=1, source_target_pairs={{0,4},{4,0},{8,12},{12,8},{1,5},{5,1},{9,13},{13,9},{2,6},{6,2},{1... | collective-permute-start | bytes 12296 | tf_op jit(solution)/shard_map/ppermute | solution.py:526
  44.6 1.4 %shard_map.81.refs_1_ = f32[9,112,128]{2,1,0:T(8,128)S(1)} custom-call(f32[9,112,128]{2,1,0:T(8,128)S(1)} %get-tuple-element.35.b_right_ref, f32[9,112,128]{2,1,0:T(8,128)S(1)} %get-tuple-element.36.b_down_ref, f32[3,9,112,128]{3,2,1,0:T(8,128)S(1)} %get-tuple-element.34.g2_ref), custom_call_target="tpu_custom_call" | custom-call | flops 100000000 | bytes 10000000 | tf_op jit(solution)/shard_map/pallas_call | solution.py:623
  46.1 0.1 collective-permute-done.8
  46.2 3.2 %collective-permute-start.9 = (f32[8,128]{1,0:T(8,128)S(1)}, f32[8,128]{1,0:T(8,128)S(1)}, u32[]{:S(2)}, u32[]{:S(2)}) collective-permute-start(f32[8,128]{1,0:T(8,128)S(1)} %add.14), channel_id=1, source_target_pairs={{0,8},{4,12},{8,0},{12,4},{1,9},{5,13},{9,1},{13,5},{2,10},{6,14},... | collective-permute-start | bytes 12296 | tf_op jit(solution)/shard_map/ppermute | solution.py:526
  49.4 1.5 %shard_map.80.refs_0_ = f32[9,112,128]{2,1,0:T(8,128)S(1)} custom-call(f32[9,112,128]{2,1,0:T(8,128)S(1)} %get-tuple-element.35.b_right_ref, f32[9,112,128]{2,1,0:T(8,128)S(1)} %get-tuple-element.36.b_down_ref, f32[3,9,112,128]{3,2,1,0:T(8,128)S(1)} %get-tuple-element.34.g2_ref), custom_call_target="tpu_custom_call" | custom-call | flops 100000000 | bytes 10000000 | tf_op jit(solution)/shard_map/pallas_call | solution.py:623
  50.9 0.1 collective-permute-done.9
  51.0 3.1 %shard_map.83 = (f32[3,64,1024]{2,1,0:T(8,128)}, f32[3,64,1024]{2,1,0:T(8,128)}, f32[3,64,1024]{2,1,0:T(8,128)}) custom-call(f32[8,128]{1,0:T(8,128)S(1)} %add.15.sums_ref, f32[9,112,128]{2,1,0:T(8,128)S(1)} %get-tuple-element.28.scale_ref, f32[9,112,128]{2,1,0:T(8,128)S(1)} %get-tuple-element.29.root_ref, f32[3,9,112,128]{3,2,1,0:T(8,128)S(1)} %get-tuple-element.30.g0_ref, ...), custom_call_target="tpu_custom_call" | custom-call | tf_op jit(solution)/shard_map/pallas_call | solution.py:634
  (4 shorter events, 0.0 us)
Async XLA Ops:
  0.7 0.7 %copy-start = (s32[1,16,3]{1,0,2:T(1,128)S(1)}, s32[1,16,3]{1,0,2:T(1,128)}, u32[]{:S(2)}) copy-start(s32[1,16,3]{1,0,2:T(1,128)} %param.9) | copy-start | bytes 580
  4.1 17.5 %collective-permute-start.2 = (f32[6,8,24,128]{3,2,1,0:T(8,128)S(1)}, f32[6,8,24,128]{3,2,1,0:T(8,128)S(1)}, u32[]{:S(2)}, u32[]{:S(2)}) collective-permute-start(f32[6,8,24,128]{3,2,1,0:T(8,128)S(1)} %get-tuple-element.23), channel_id=1, source_target_pairs={{0,4},{8,12},{4,0},{12,8},{1,5},{9,13},{5,1},{13,9},{2,6},{10,14},... | collective-permute-start | bytes 1769480 | tf_op jit(solution)/shard_map/ppermute | solution.py:587
  7.2 14.4 %collective-permute-start.3 = (f32[6,8,24,128]{3,2,1,0:T(8,128)S(1)}, f32[6,8,24,128]{3,2,1,0:T(8,128)S(1)}, u32[]{:S(2)}, u32[]{:S(2)}) collective-permute-start(f32[6,8,24,128]{3,2,1,0:T(8,128)S(1)} %get-tuple-element.24), channel_id=1, source_target_pairs={{4,8},{8,4},{5,9},{9,5},{6,10},{10,6},{7,11},{11,7},{20,24},{24,20... | collective-permute-start | bytes 1769480 | tf_op jit(solution)/shard_map/ppermute | solution.py:587
  7.9 1.3 %collective-permute-start = (f32[2,64,128]{2,1,0:T(8,128)S(1)}, f32[2,64,128]{2,1,0:T(8,128)S(1)}, u32[]{:S(2)}, u32[]{:S(2)}) collective-permute-start(f32[2,64,128]{2,1,0:T(8,128)S(1)} %get-tuple-element.21), channel_id=1, source_target_pairs={{0,1},{2,3},{1,0},{3,2},{4,5},{6,7},{5,4},{7,6},{8,9},{10,11},{9,8... | collective-permute-start | bytes 196616 | tf_op jit(solution)/shard_map/ppermute | solution.py:587
  8.0 1.2 %collective-permute-start.1 = (f32[2,64,128]{2,1,0:T(8,128)S(1)}, f32[2,64,128]{2,1,0:T(8,128)S(1)}, u32[]{:S(2)}, u32[]{:S(2)}) collective-permute-start(f32[2,64,128]{2,1,0:T(8,128)S(1)} %get-tuple-element.22), channel_id=1, source_target_pairs={{1,2},{2,1},{5,6},{6,5},{9,10},{10,9},{13,14},{14,13},{17,18},{18,... | collective-permute-start | bytes 196616 | tf_op jit(solution)/shard_map/ppermute | solution.py:587
  9.8 11.8 %collective-permute-start.4 = (f32[2,2,24,128]{3,2,1,0:T(8,128)S(1)}, f32[2,2,24,128]{3,2,1,0:T(8,128)S(1)}, u32[]{:S(2)}, u32[]{:S(2)}) collective-permute-start(f32[2,2,24,128]{3,2,1,0:T(8,128)S(1)} %get-tuple-element.25), channel_id=1, source_target_pairs={{0,4},{8,12},{4,0},{12,8},{1,5},{9,13},{5,1},{13,9},{2,6},{10,14},... | collective-permute-start | bytes 147464 | tf_op jit(solution)/shard_map/ppermute | solution.py:587
  14.2 7.4 %collective-permute-start.5 = (f32[2,2,24,128]{3,2,1,0:T(8,128)S(1)}, f32[2,2,24,128]{3,2,1,0:T(8,128)S(1)}, u32[]{:S(2)}, u32[]{:S(2)}) collective-permute-start(f32[2,2,24,128]{3,2,1,0:T(8,128)S(1)} %get-tuple-element.26), channel_id=1, source_target_pairs={{4,8},{8,4},{5,9},{9,5},{6,10},{10,6},{7,11},{11,7},{20,24},{24,20... | collective-permute-start | bytes 147464 | tf_op jit(solution)/shard_map/ppermute | solution.py:587
  35.0 1.4 %collective-permute-start.6 = (f32[8,128]{1,0:T(8,128)S(1)}, f32[8,128]{1,0:T(8,128)S(1)}, u32[]{:S(2)}, u32[]{:S(2)}) collective-permute-start(f32[8,128]{1,0:T(8,128)S(1)} %get-tuple-element.27), channel_id=1, source_target_pairs={{0,1},{1,0},{2,3},{3,2},{4,5},{5,4},{6,7},{7,6},{8,9},{9,8},{10,11... | collective-permute-start | bytes 12296 | tf_op jit(solution)/shard_map/ppermute | solution.py:526
  36.4 3.6 %collective-permute-start.7 = (f32[8,128]{1,0:T(8,128)S(1)}, f32[8,128]{1,0:T(8,128)S(1)}, u32[]{:S(2)}, u32[]{:S(2)}) collective-permute-start(f32[8,128]{1,0:T(8,128)S(1)} %add.12), channel_id=1, source_target_pairs={{0,2},{1,3},{2,0},{3,1},{4,6},{5,7},{6,4},{7,5},{8,10},{9,11},{10,... | collective-permute-start | bytes 12296 | tf_op jit(solution)/shard_map/ppermute | solution.py:526
  40.1 6.2 %collective-permute-start.8 = (f32[8,128]{1,0:T(8,128)S(1)}, f32[8,128]{1,0:T(8,128)S(1)}, u32[]{:S(2)}, u32[]{:S(2)}) collective-permute-start(f32[8,128]{1,0:T(8,128)S(1)} %add.13), channel_id=1, source_target_pairs={{0,4},{4,0},{8,12},{12,8},{1,5},{5,1},{9,13},{13,9},{2,6},{6,2},{1... | collective-permute-start | bytes 12296 | tf_op jit(solution)/shard_map/ppermute | solution.py:526
  46.2 4.8 %collective-permute-start.9 = (f32[8,128]{1,0:T(8,128)S(1)}, f32[8,128]{1,0:T(8,128)S(1)}, u32[]{:S(2)}, u32[]{:S(2)}) collective-permute-start(f32[8,128]{1,0:T(8,128)S(1)} %add.14), channel_id=1, source_target_pairs={{0,8},{4,12},{8,0},{12,4},{1,9},{5,13},{9,1},{13,5},{2,10},{6,14},... | collective-permute-start | bytes 12296 | tf_op jit(solution)/shard_map/ppermute | solution.py:526

commit v8 on v7

--- a/solution.py
+++ b/solution.py
@@ -11,7 +11,8 @@
 SWEEPS = 8
 SUBS = 8
 LANES = 128
-HALO = 24
+HALO = 16
+LATE = 8
 SLOT = 32
 SLOTS = LANES // SLOT
 WAYS = 3
@@ -50,7 +51,7 @@
 
 
 def pack(planes, start):
-    lane = lane_index()
+    lane = lax.broadcasted_iota(jnp.int32, planes[0].shape, 1)
     packed = [None] * (-(-len(planes) // SLOTS))
     for p, plane in enumerate(planes):
         slot = p % SLOTS
@@ -73,82 +74,89 @@
     copies = [pltpu.make_async_copy(there, here, sems.at[k]) for k, (there, here) in enumerate(moves)]
     for copy in copies:
         copy.start()
-    lane = lane_index()
+    row = lax.broadcasted_iota(jnp.int32, (rows, LANES), 0)
+    lane = lax.broadcasted_iota(jnp.int32, (rows, LANES), 1)
     sub = lax.broadcasted_iota(jnp.int32, (SUBS, LANES), 0)
     last_row, last_lane, tile_row, tile_at = [place_ref[k] for k in range(4)]
     odd_row, odd_col = (place_ref[4] == 1, place_ref[5] == 1)
 
-    def over_own(plane, value_of):
-        def body(t, carry):
-            at = pl.multiple_of(SUBS * t, SUBS)
-            for j in range(own_tiles):
-                own_ref[plane, j, pl.ds(at, SUBS), :] = value_of(at, j)
-            return carry
-
-        lax.fori_loop(0, rows // SUBS, body, 0)
-
-    def tile(ref, at, j):
-        return ref[pl.ds(at, SUBS), pl.ds(j * LANES, LANES)]
-
-    def to_right(at, j):
-        value = 1.0 - seam_damping * tile(seam_right_ref, at, j).astype(jnp.float32)
-        return jnp.where(lane == last_lane, 0.0, value) if j == own_tiles - 1 else value
-
-    def to_down(at, j):
-        value = 1.0 - seam_damping * tile(seam_down_ref, at, j).astype(jnp.float32)
-        return jnp.where(at + sub == last_row, 0.0, value)
+    def tile(ref, j):
+        return ref[:, j * LANES:(j + 1) * LANES]
 
     copies[0].wait()
-    over_own(chans, lambda at, j: tile(weight_ref, at, j))
+    for j in range(own_tiles):
+        own_ref[chans, j] = tile(weight_ref, j)
     copies[1].wait()
-    over_own(chans + 1, to_right)
+    for j in range(own_tiles):
+        value = 1.0 - seam_damping * tile(seam_right_ref, j).astype(jnp.float32)
+        own_ref[chans + 1, j] = jnp.where(lane == last_lane, 0.0, value) if j == own_tiles - 1 else value
     copies[2].wait()
-    over_own(chans + 2, to_down)
+    for j in range(own_tiles):
+        value = 1.0 - seam_damping * tile(seam_down_ref, j).astype(jnp.float32)
+        own_ref[chans + 2, j] = jnp.where(row == last_row, 0.0, value)
     for c in range(chans):
         shift = [
-            jnp.broadcast_to(offsets_ref[c, tile_row, tile_at + k], (SUBS, LANES)).astype(jnp.float32) / offset_unit
+            jnp.broadcast_to(offsets_ref[c, tile_row, tile_at + k], (rows, LANES)).astype(jnp.float32) / offset_unit
             for k in range(cols // TILE)
         ]
         copies[3 + c].wait()
-        over_own(c, lambda at, j, c=c, shift=shift: tile(src_ref.at[c], at, j) + shift[j * LANES // TILE])
+        for j in range(own_tiles):
+            own_ref[c, j] = tile(src_ref.at[c], j) + shift[j * LANES // TILE]
 
     planes = range(chans + 3)
-    low, high = pl.ds(0, HALO), pl.ds(rows - HALO, HALO)
-    for ref, odd, even in ((first_rows_ref, low, high), (second_rows_ref, high, low)):
-
-        @pl.when(odd_row)
-        def _(ref=ref, odd=odd):
-            for p in planes:
-                ref[p] = own_ref[p, :, odd, :]
-
-        @pl.when(jnp.logical_not(odd_row))
-        def _(ref=ref, even=even):
-            for p in planes:
-                ref[p] = own_ref[p, :, even, :]
-
-    def columns(t, carry):
-        here = pl.ds(pl.multiple_of(SUBS * t, SUBS), SUBS)
-        left = pack([own_ref[p, 0, here, :] for p in planes], 0)
-        right = pack([own_ref[p, own_tiles - 1, here, :] for p in planes], LANES - SLOT)
-        for k, (a, b) in enumerate(zip(left, right)):
-            first_cols_ref[k, here, :] = jnp.where(odd_col, a, b)
-            second_cols_ref[k, here, :] = jnp.where(odd_col, b, a)
-        return carry
-
-    lax.fori_loop(0, rows // SUBS, columns, 0)
-
-
-def corners_kernel(place_ref, first_ref, second_ref, first_out, second_out):
+
+    def low_rows(ref):
+        for p in planes:
+            ref[p] = own_ref[p, :, 0:HALO, :]
+
+    def high_rows(ref):
+        at = rows - HALO
+        for p in planes:
+            ref[p] = own_ref[p, :, at:rows, :]
+        for j in range(own_tiles):
+            above = jnp.where(sub == 0, own_ref[chans + 2, j, at - 1:at, :], 0.0)
+            ref[chans, j, 0:SUBS, :] = own_ref[chans, j, at:at + SUBS, :] + above
+
+    @pl.when(odd_row)
+    def _():
+        low_rows(first_rows_ref)
+        high_rows(second_rows_ref)
+
+    @pl.when(jnp.logical_not(odd_row))
+    def _():
+        high_rows(first_rows_ref)
+        low_rows(second_rows_ref)
+
+    left = pack([own_ref[p, 0] for p in planes], 0)
+    right = pack([own_ref[p, own_tiles - 1] for p in planes], LANES - SLOT)
+    for k, (a, b) in enumerate(zip(left, right)):
+        first_cols_ref[k] = jnp.where(odd_col, a, b)
+        second_cols_ref[k] = jnp.where(odd_col, b, a)
+
+
+def corners_kernel(chans, place_ref, first_ref, second_ref, first_out, second_out):
     rows = first_ref.shape[1]
     odd_row, odd_col = (place_ref[4] == 1, place_ref[5] == 1)
-    for k in range(first_ref.shape[0]):
-        for low in range(0, HALO, SUBS):
-            lows = [ref[k, low:low + SUBS, :] for ref in (first_ref, second_ref)]
-            at = rows - HALO + low
-            highs = [ref[k, at:at + SUBS, :] for ref in (first_ref, second_ref)]
-            for side in range(2):
-                near = jnp.where(odd_col, lows[side], lows[1 - side])
-                far = jnp.where(odd_col, highs[side], highs[1 - side])
+    sub = lax.broadcasted_iota(jnp.int32, (SUBS, LANES), 0)
+    lane = lane_index()
+    weight, down = chans, chans + 2
+    slot = weight % SLOTS
+    at = rows - HALO
+    for side, (odd, even) in enumerate(((first_ref, second_ref), (second_ref, first_ref))):
+
+        def tile(k, low, count=SUBS, odd=odd, even=even):
+            return jnp.where(odd_col, odd[k, low:low + count, :], even[k, low:low + count, :])
+
+        above = jnp.broadcast_to(tile(down // SLOTS, at - 1, 1), (SUBS, LANES))
+        above = pltpu.roll(above, (slot - down % SLOTS) % SLOTS * SLOT, 1)
+        own_slot = jnp.logical_and(lane >= slot * SLOT, lane < (slot + 1) * SLOT)
+        above = jnp.where(jnp.logical_and(sub == 0, own_slot), above, 0.0)
+        for k in range(first_ref.shape[0]):
+            for low in range(0, HALO, SUBS):
+                near = tile(k, low)
+                far = tile(k, at + low)
+                if low == 0 and k == weight // SLOTS:
+                    far = far + above
                 first_out[side, k, low:low + SUBS, :] = jnp.where(odd_row, near, far)
                 second_out[side, k, low:low + SUBS, :] = jnp.where(odd_row, far, near)
 
@@ -200,10 +208,9 @@
     return jnp.where(column == ways * (place % LANES) + place // LANES, 1.0, 0.0).astype(jnp.bfloat16)
 
 
-def deal(tile_of, tiles, emit):
-    ways = ways_of(tiles)
+def deal(tile_of, low, high, ways, emit):
     matrix = dealing(ways) if ways > 1 else None
-    for g in range(0, tiles, ways):
+    for g in range(low, high, ways):
         if ways == 1:
             emit(g, tile_of(g))
             continue
@@ -212,8 +219,19 @@
             emit(g + m, value[:, m * LANES:(m + 1) * LANES])
 
 
-def own_dealt_kernel(place_ref, own_ref, first_ref, second_ref, dealt_ref):
+def inner_dealt_kernel(own_ref, dealt_ref):
     planes, own_tiles, rows = own_ref.shape[:3]
+
+    def emit(j, value):
+        dealt_ref[:, j] = value.reshape(planes, rows, LANES)
+
+    deal(lambda j: own_ref[:, j].reshape(planes * rows, LANES), 0, dealt_ref.shape[1], ways_of(own_tiles + 1), emit)
+
+
+def outer_dealt_kernel(place_ref, own_ref, first_ref, second_ref, dealt_ref):
+    planes, own_tiles, rows = own_ref.shape[:3]
+    tiles = own_tiles + 1
+    low = tiles - dealt_ref.shape[1]
     odd = place_ref[5] == 1
 
     def tile_of(j):
@@ -226,9 +244,9 @@
         return jnp.concatenate(parts, axis=0)
 
     def emit(j, value):
-        dealt_ref[:, j] = value.reshape(planes, rows, LANES)
-
-    deal(tile_of, own_tiles + 1, emit)
+        dealt_ref[:, j - low] = value.reshape(planes, rows, LANES)
+
+    deal(tile_of, low, tiles, ways_of(tiles), emit)
 
 
 def rightward(values):
@@ -360,26 +378,21 @@
 
 
 def first_kernel(
-    place_ref, dealt_ref, first_rows_ref, second_rows_ref, first_corners_ref, second_corners_ref,
+    place_ref, inner_ref, outer_ref, first_rows_ref, second_rows_ref, first_corners_ref, second_corners_ref,
     b_right_ref, b_down_ref, scale_ref, root_ref, g0_ref, z0_ref, g1_ref, f1_ref, g2_ref, sums_ref,
+    first_late_ref, second_late_ref,
     natural, work_ref,
 ):
-    planes, tiles, rows = dealt_ref.shape[:3]
+    planes, inner, rows = inner_ref.shape[:3]
+    tiles = inner + outer_ref.shape[1]
     chans = planes - 3
     own_tiles = tiles - 1
     height = rows + 2 * HALO
     steps = height // SUBS
 
-    def copy_own(t, carry):
-        here = pl.ds(pl.multiple_of(SUBS * t, SUBS), SUBS)
-        there = pl.ds(pl.multiple_of(HALO + SUBS * t, SUBS), SUBS)
-        for p in range(planes):
-            for j in range(tiles):
-                natural[p, j, there, :] = dealt_ref[p, j, here, :]
-        return carry
-
-    lax.fori_loop(0, rows // SUBS, copy_own, 0)
-
+    for p in range(planes):
+        for j in range(tiles):
+            natural[p, j, HALO:HALO + rows, :] = inner_ref[p, j] if j < inner else outer_ref[p, j - inner]
     odd = place_ref[4] == 1
 
     def edge_tile(j):
@@ -397,7 +410,7 @@
         natural[:, j, 0:HALO, :] = value[0]
         natural[:, j, HALO + rows:height, :] = value[1]
 
-    deal(edge_tile, tiles, put_edge)
+    deal(edge_tile, 0, tiles, ways_of(tiles), put_edge)
 
     def at(i):
         return pl.ds(i * SUBS, SUBS)
@@ -405,7 +418,10 @@
     def interleaved(p, i, j):
         return natural[p, j, pl.ds(i, SUBS, stride=steps), :]
 
-    to_up = [pltpu.roll(interleaved(chans + 2, steps - 1, j), 1, 0) for j in range(tiles)]
+    sub = lax.broadcasted_iota(jnp.int32, (SUBS, LANES), 0)
+    to_up = [
+        jnp.where(sub == 0, 0.0, pltpu.roll(interleaved(chans + 2, steps - 1, j), 1, 0)) for j in range(tiles)
+    ]
     for i in range(steps):
         to_right = [interleaved(chans + 1, i, j) for j in range(tiles)]
         to_left = leftward(to_right)
@@ -447,15 +463,44 @@
 
     zero = jnp.zeros((SUBS, LANES), jnp.float32)
     parts = lax.fori_loop(0, chans, channel, (zero,) * 4)
-    sub = lax.broadcasted_iota(jnp.int32, (SUBS, LANES), 0)
     sums = zero
     for k, part in enumerate(parts):
         sums = jnp.where(sub == k, jnp.sum(part), sums)
     sums_ref[...] = sums
 
-
-def second_kernel(c, b_right_ref, b_down_ref, g2_ref, f2_ref, work_ref):
-    precondition(b_right_ref, b_down_ref, g2_ref.at[c], f2_ref, work_ref)
+    def edge(c, j, at):
+        s, i = divmod(HALO + at, steps)
+        return g2_ref[c, j, pl.ds(i * SUBS + s, LATE, stride=SUBS), :]
+
+    for c in range(chans):
+        for j in range(tiles):
+            low, high = edge(c, j, 0), edge(c, j, rows - LATE)
+            first_late_ref[c, j] = jnp.where(odd, low, high)
+            second_late_ref[c, j] = jnp.where(odd, high, low)
+
+
+def second_kernel(
+    c, place_ref, first_late_ref, second_late_ref, b_right_ref, b_down_ref, g2_ref, f2_ref, g_ref, work_ref
+):
+    tiles, height = b_right_ref.shape[:2]
+    rows = height - 2 * HALO
+    steps = height // SUBS
+    odd = place_ref[4] == 1
+    sub = lax.broadcasted_iota(jnp.int32, (SUBS, LANES), 0)
+    halo = {i: [] for i in range(steps)}
+    for k in range(LATE):
+        for top, at in ((True, HALO - LATE + k), (False, HALO + rows + k)):
+            s, i = divmod(at, steps)
+            halo[i].append((s, top, k))
+    for j in range(tiles):
+        for i in range(steps):
+            value = g2_ref[c, j, i * SUBS:(i + 1) * SUBS, :]
+            for s, top, k in halo[i]:
+                first, second = [ref[c, j, k:k + 1, :] for ref in (first_late_ref, second_late_ref)]
+                row = jnp.where(odd, first, second) if top else jnp.where(odd, second, first)
+                value = jnp.where(sub == s, row, value)
+            g_ref[j, i * SUBS:(i + 1) * SUBS, :] = value
+    precondition(b_right_ref, b_down_ref, g_ref, f2_ref, work_ref)
 
 
 def combine(n0, n1, n2, n3):
@@ -517,15 +562,22 @@
         copy.wait()
 
 
-def sum_over(value, axis):
-    size = lax.axis_size(axis)
-    if size & (size - 1):
-        return lax.psum(value, axis)
-    step = 1
-    while step < size:
-        value = value + lax.ppermute(value, axis, [(i, i ^ step) for i in range(size)])
-        step *= 2
-    return value
+def sum_over(value, axes, beside):
+    steps = []
+    for axis in axes:
+        size = lax.axis_size(axis)
+        if size & (size - 1):
+            value = lax.psum(value, axis)
+            continue
+        steps += [(axis, [(i, i ^ (1 << k)) for i in range(size)]) for k in range(size.bit_length() - 1)]
+    done = []
+    for k, (axis, pairs) in enumerate(steps):
+        other = lax.ppermute(value, axis, pairs)
+        if len(steps) - k <= len(beside):
+            value, array = lax.optimization_barrier((value, beside[len(done)]))
+            done.append(array)
+        value = value + other
+    return value, done + list(beside[len(done):])
 
 
 def per_device(source, weight, seam_right, seam_down, offsets):
@@ -589,48 +641,60 @@
     first_rows, second_rows = swap(first_rows, second_rows, "row")
     first_cols, second_cols = swap(first_cols, second_cols, "col")
     corners = pl.pallas_call(
-        corners_kernel,
+        functools.partial(corners_kernel, chans),
         out_shape=[shaped(2, packs, HALO, LANES)] * 2,
         in_specs=[in_smem] + [in_vmem] * 2,
         out_specs=[in_vmem] * 2,
         compiler_params=params,
     )(place, first_cols, second_cols)
     first_corners, second_corners = swap(*corners, "row")
-    dealt = pl.pallas_call(
-        own_dealt_kernel,
-        out_shape=shaped(planes, tiles, rows, LANES),
+    ways = ways_of(tiles)
+    inner = pl.pallas_call(
+        inner_dealt_kernel,
+        out_shape=shaped(planes, tiles - ways, rows, LANES),
+        in_specs=[in_vmem],
+        out_specs=in_vmem,
+        compiler_params=params,
+        cost_estimate=pl.CostEstimate(flops=10**8, bytes_accessed=4 * 10**6, transcendentals=0),
+    )(own)
+    outer = pl.pallas_call(
+        outer_dealt_kernel,
+        out_shape=shaped(planes, ways, rows, LANES),
         in_specs=[in_smem] + [in_vmem] * 3,
         out_specs=in_vmem,
         compiler_params=params,
-        cost_estimate=pl.CostEstimate(flops=10**8, bytes_accessed=5 * 10**6, transcendentals=0),
+        cost_estimate=pl.CostEstimate(flops=10**8, bytes_accessed=2 * 10**6, transcendentals=0),
     )(place, own, first_cols, second_cols)
 
     height = rows + 2 * HALO
     plane = shaped(tiles, height, LANES)
     field = shaped(chans, tiles, height, LANES)
-    *basis, sums = pl.pallas_call(
+    late = shaped(chans, tiles, LATE, LANES)
+    *basis, sums, first_late, second_late = pl.pallas_call(
         first_kernel,
-        out_shape=[plane] * 4 + [field] * 5 + [shaped(SUBS, LANES)],
-        in_specs=[in_smem] + [in_vmem] * 5,
-        out_specs=[in_vmem] * 10,
+        out_shape=[plane] * 4 + [field] * 5 + [shaped(SUBS, LANES)] + [late] * 2,
+        in_specs=[in_smem] + [in_vmem] * 6,
+        out_specs=[in_vmem] * 12,
         scratch_shapes=[scratch(planes, tiles, height, LANES), scratch(*plane.shape)],
         compiler_params=params,
-    )(place, dealt, first_rows, second_rows, first_corners, second_corners)
-
-    total = sum_over(sum_over(sums, "col"), "row")
+    )(place, inner, outer, first_rows, second_rows, first_corners, second_corners)
+
+    first_late, second_late = swap(first_late, second_late, "row")
+
     b_right, b_down, scale, root, g0, z0, g1, f1, g2 = basis
     f2 = [
         pl.pallas_call(
             functools.partial(second_kernel, c),
             out_shape=plane,
-            in_specs=[in_vmem] * 3,
+            in_specs=[in_smem] + [in_vmem] * 5,
             out_specs=in_vmem,
-            scratch_shapes=[scratch(*plane.shape)],
+            scratch_shapes=[scratch(*plane.shape)] * 2,
             compiler_params=params,
             cost_estimate=pl.CostEstimate(flops=10**8, bytes_accessed=10**7, transcendentals=0),
-        )(b_right, b_down, g2)
+        )(place, first_late, second_late, b_right, b_down, g2)
         for c in range(chans)
     ]
+    total, f2 = sum_over(sums, ("col", "row"), f2)
     return pl.pallas_call(
         third_kernel,
         out_shape=[shaped(chans, rows, cols)] * 3,

time: 54.4 us -> 52.7 us (0.969)
  waiting for transfers between devices: 6.55 us -> 1.68 us
  starting transfers between devices: 19.4 us -> 23.5 us
  Pallas kernels: 26.7 us -> 25.7 us
    ppermute x6 -> x8, starting transfers between devices: 9.59 us -> 14.2 us  [swap(): lax.ppermute(value, axis, some)]
    ppermute x6 -> x8, waiting for transfers between devices: 4.93 us -> 0.59 us  [swap(): lax.ppermute(value, axis, some)]
    pallas_call x1, Pallas kernels: 13.4 us -> 11.6 us  [per_device(): pl.pallas_call(first_kernel, out_shape=[plane] * 4 + [field] * 5 + [shape...]
    pallas_call x3, Pallas kernels: 4.48 us -> 5.88 us  [per_device(): pl.pallas_call(functools.partial(second_kernel, c), out_shape=plane, in_s...]
    ppermute x4, starting transfers between devices: 9.83 us -> 9.28 us  [sum_over(): other = lax.ppermute(value, axis, pairs)]
    pallas_call x2 -> x3, Pallas kernels: 2.91 us -> 3.17 us  [the longest x1 1.3 us: per_device(): pl.pallas_call(outer_dealt_kernel, out_shape=shaped(planes, ways, rows, L...]
  transfers between devices with their start and end apart: 10 -> 12, of which waited for: 6 -> 3; matrix products, arithmetic and copies ran while one was open for 0% -> 0% of each run, Pallas kernels for 14% -> 17%
where the time goes in v8:
time: 52.7 us; the launch traced here: 52.5 us
  Pallas kernels  25.7 us (49%)
  starting transfers between devices  23.5 us (45%)
  waiting for transfers between devices  1.68 us (3%)
  between operations  0.8 us (2%)
  local copies, waits for them, and re-layouts  0.77 us (1%)
    ppermute x8, starting transfers between devices, swap(): lax.ppermute(value, axis, some)  14.2 us
    pallas_call x1, Pallas kernels, per_device(): pl.pallas_call(first_kernel, out_shape=[plane] * 4 + [field] * 5 + [shape...  11.6 us
    ppermute x4, starting transfers between devices, sum_over(): other = lax.ppermute(value, axis, pairs)  9.28 us
    pallas_call x3, Pallas kernels, per_device(): pl.pallas_call(functools.partial(second_kernel, c), out_shape=plane, in_s...  5.88 us
    pallas_call x1, Pallas kernels, per_device(): pl.pallas_call(third_kernel, out_shape=[shaped(chans, rows, cols)] * 3, i...  2.85 us
    pallas_call x1, Pallas kernels, per_device(): pl.pallas_call(own_kernel, out_shape=[shaped(planes, own_tiles, rows, LAN...  2.18 us
    pallas_call x1, Pallas kernels, per_device(): pl.pallas_call(outer_dealt_kernel, out_shape=shaped(planes, ways, rows, L...  1.3 us
    pallas_call x1, Pallas kernels, per_device(): pl.pallas_call(inner_dealt_kernel, out_shape=shaped(planes, tiles - ways,...  1.25 us
  transfers between devices with their start and end apart: 12, of which 3 were waited for; matrix products, arithmetic and copies ran while one was open for 0% of the time, Pallas kernels for 17%

profile of v8, /device:TPU:0, one launch (start us, length us, event | category | flops | bytes accessed | tf_op | source)
XLA Modules:
  0.0 52.5 jit_solution(5902290087987891510)
XLA Ops:
  0.6 0.1 stack.27.place_ref
  0.7 0.7 %copy-done = s32[1,16,3]{1,0,2:T(1,128)S(1)} copy-done((s32[1,16,3]{1,0,2:T(1,128)S(1)}, s32[1,16,3]{1,0,2:T(1,128)}, u32[]{:S(2)}) %copy-start) | copy-done | bytes 216
  1.4 2.2 %shard_map.76 = (f32[6,8,64,128]{3,2,1,0:T(8,128)S(1)}, f32[6,8,16,128]{3,2,1,0:T(8,128)S(1)}, f32[6,8,16,128]{3,2,1,0:T(8,128)S(1)}, f32[2,64,128]{2,1,0:T(8,128)S(1)}, f32[2,64,128]{2,1,0:T(8,128)S(1)}) custom-call(s32[6]{0:T(128)S(1)} %stack.27.place_ref, s32[3,1,16]{2,1,0:T(1,128)S(1)} %bitcast.7, f32[3,64,1024]{2,1,0:T(8,128)} %src_hbm.1, ...), custom_call_target="tpu_custom_call" | custom-call | tf_op jit(solution)/shard_map/pallas_call | solution.py:614
  3.6 3.1 %collective-permute-start.2 = (f32[6,8,16,128]{3,2,1,0:T(8,128)S(1)}, f32[6,8,16,128]{3,2,1,0:T(8,128)S(1)}, u32[]{:S(2)}, u32[]{:S(2)}) collective-permute-start(f32[6,8,16,128]{3,2,1,0:T(8,128)S(1)} %get-tuple-element.31), channel_id=1, source_target_pairs={{0,4},{8,12},{4,0},{12,8},{1,5},{9,13},{5,1},{13,9},{2,6},{10,14},... | collective-permute-start | bytes 1179656 | tf_op jit(solution)/shard_map/ppermute | solution.py:639
  6.7 0.7 %collective-permute-start.3 = (f32[6,8,16,128]{3,2,1,0:T(8,128)S(1)}, f32[6,8,16,128]{3,2,1,0:T(8,128)S(1)}, u32[]{:S(2)}, u32[]{:S(2)}) collective-permute-start(f32[6,8,16,128]{3,2,1,0:T(8,128)S(1)} %get-tuple-element.32), channel_id=1, source_target_pairs={{4,8},{8,4},{5,9},{9,5},{6,10},{10,6},{7,11},{11,7},{20,24},{24,20... | collective-permute-start | bytes 1179656 | tf_op jit(solution)/shard_map/ppermute | solution.py:639
  7.4 0.1 collective-permute-start
  7.4 0.7 %collective-permute-start.1 = (f32[2,64,128]{2,1,0:T(8,128)S(1)}, f32[2,64,128]{2,1,0:T(8,128)S(1)}, u32[]{:S(2)}, u32[]{:S(2)}) collective-permute-start(f32[2,64,128]{2,1,0:T(8,128)S(1)} %get-tuple-element.30), channel_id=1, source_target_pairs={{1,2},{2,1},{5,6},{6,5},{9,10},{10,9},{13,14},{14,13},{17,18},{18,... | collective-permute-start | bytes 196616 | tf_op jit(solution)/shard_map/ppermute | solution.py:639
  8.1 0.6 %collective-permute-done.first_ref = f32[2,64,128]{2,1,0:T(8,128)S(1)} collective-permute-done((f32[2,64,128]{2,1,0:T(8,128)S(1)}, f32[2,64,128]{2,1,0:T(8,128)S(1)}, u32[]{:S(2)}, u32[]{:S(2)}) %collective-permute-start) | collective-permute-done | bytes 65568 | tf_op jit(solution)/shard_map/ppermute | solution.py:639
  8.7 0.6 %shard_map.79 = (f32[2,2,16,128]{3,2,1,0:T(8,128)S(1)}, f32[2,2,16,128]{3,2,1,0:T(8,128)S(1)}) custom-call(s32[6]{0:T(128)S(1)} %stack.27.place_ref, f32[2,64,128]{2,1,0:T(8,128)S(1)} %collective-permute-done.first_ref, f32[2,64,128]{2,1,0:T(8,128)S(1)} %collective-permute-done.1.second_ref), custom_call_target="tpu_custom_call" | custom-call | tf_op jit(solution)/shard_map/pallas_call | solution.py:643
  9.3 4.4 %collective-permute-start.4 = (f32[2,2,16,128]{3,2,1,0:T(8,128)S(1)}, f32[2,2,16,128]{3,2,1,0:T(8,128)S(1)}, u32[]{:S(2)}, u32[]{:S(2)}) collective-permute-start(f32[2,2,16,128]{3,2,1,0:T(8,128)S(1)} %get-tuple-element.33), channel_id=1, source_target_pairs={{0,4},{8,12},{4,0},{12,8},{1,5},{9,13},{5,1},{13,9},{2,6},{10,14},... | collective-permute-start | bytes 98312 | tf_op jit(solution)/shard_map/ppermute | solution.py:639
  13.7 0.7 %collective-permute-start.5 = (f32[2,2,16,128]{3,2,1,0:T(8,128)S(1)}, f32[2,2,16,128]{3,2,1,0:T(8,128)S(1)}, u32[]{:S(2)}, u32[]{:S(2)}) collective-permute-start(f32[2,2,16,128]{3,2,1,0:T(8,128)S(1)} %get-tuple-element.34), channel_id=1, source_target_pairs={{4,8},{8,4},{5,9},{9,5},{6,10},{10,6},{7,11},{11,7},{20,24},{24,20... | collective-permute-start | bytes 98312 | tf_op jit(solution)/shard_map/ppermute | solution.py:639
  14.4 1.3 %shard_map.77.inner_ref = f32[6,6,64,128]{3,2,1,0:T(8,128)S(1)} custom-call(f32[6,8,64,128]{3,2,1,0:T(8,128)S(1)} %get-tuple-element.28.own_ref), custom_call_target="tpu_custom_call" | custom-call | flops 100000000 | bytes 4000000 | tf_op jit(solution)/shard_map/pallas_call | solution.py:652
  15.6 1.3 %shard_map.78.outer_ref = f32[6,3,64,128]{3,2,1,0:T(8,128)S(1)} custom-call(s32[6]{0:T(128)S(1)} %stack.27.place_ref, f32[6,8,64,128]{3,2,1,0:T(8,128)S(1)} %get-tuple-element.28.own_ref, f32[2,64,128]{2,1,0:T(8,128)S(1)} %collective-permute-done.first_ref, f32[2,64,128]{2,1,0:T(8,128)S(1)} %collective-permute-done.1.second_ref), custom_call_target="tpu_custom_call" | custom-call | flops 100000000 | bytes 2000000 | tf_op jit(solution)/shard_map/pallas_call | solution.py:660
  16.9 0.0 collective-permute-done.4.first_corners_ref
  17.0 0.0 collective-permute-done.3.second_rows_ref
  17.0 11.6 %shard_map.80 = (f32[9,96,128]{2,1,0:T(8,128)S(1)}, f32[9,96,128]{2,1,0:T(8,128)S(1)}, f32[9,96,128]{2,1,0:T(8,128)S(1)}, f32[9,96,128]{2,1,0:T(8,128)S(1)}, f32...) custom-call(s32[6]{0:T(128)S(1)} %stack.27.place_ref, ...), custom_call_target="tpu_custom_call" | custom-call | tf_op jit(solution)/shard_map/pallas_call | solution.py:673
  28.6 4.0 %collective-permute-start.7 = (f32[3,9,8,128]{3,2,1,0:T(8,128)S(1)}, f32[3,9,8,128]{3,2,1,0:T(8,128)S(1)}, u32[]{:S(2)}, u32[]{:S(2)}) collective-permute-start(f32[3,9,8,128]{3,2,1,0:T(8,128)S(1)} %get-tuple-element.36), channel_id=1, source_target_pairs={{0,4},{8,12},{4,0},{12,8},{1,5},{9,13},{5,1},{13,9},{2,6},{10,14},... | collective-permute-start | bytes 331784 | tf_op jit(solution)/shard_map/ppermute | solution.py:639
  32.6 0.7 %collective-permute-start.8 = (f32[3,9,8,128]{3,2,1,0:T(8,128)S(1)}, f32[3,9,8,128]{3,2,1,0:T(8,128)S(1)}, u32[]{:S(2)}, u32[]{:S(2)}) collective-permute-start(f32[3,9,8,128]{3,2,1,0:T(8,128)S(1)} %get-tuple-element.37), channel_id=1, source_target_pairs={{4,8},{8,4},{5,9},{9,5},{6,10},{10,6},{7,11},{11,7},{20,24},{24,20... | collective-permute-start | bytes 331784 | tf_op jit(solution)/shard_map/ppermute | solution.py:639
  33.3 2.4 %collective-permute-start.6 = (f32[8,128]{1,0:T(8,128)S(1)}, f32[8,128]{1,0:T(8,128)S(1)}, u32[]{:S(2)}, u32[]{:S(2)}) collective-permute-start(f32[8,128]{1,0:T(8,128)S(1)} %get-tuple-element.35), channel_id=1, source_target_pairs={{0,1},{1,0},{2,3},{3,2},{4,5},{5,4},{6,7},{7,6},{8,9},{9,8},{10,11... | collective-permute-start | bytes 12296 | tf_op jit(solution)/shard_map/ppermute | solution.py:575
  35.6 0.8 %collective-permute-done.6 = f32[8,128]{1,0:T(8,128)S(1)} collective-permute-done((f32[8,128]{1,0:T(8,128)S(1)}, f32[8,128]{1,0:T(8,128)S(1)}, u32[]{:S(2)}, u32[]{:S(2)}) %collective-permute-start.6) | collective-permute-done | bytes 4128 | tf_op jit(solution)/shard_map/ppermute | solution.py:575
  36.5 2.5 %collective-permute-start.9 = (f32[8,128]{1,0:T(8,128)S(1)}, f32[8,128]{1,0:T(8,128)S(1)}, u32[]{:S(2)}, u32[]{:S(2)}) collective-permute-start(f32[8,128]{1,0:T(8,128)S(1)} %add.12), channel_id=1, source_target_pairs={{0,2},{1,3},{2,0},{3,1},{4,6},{5,7},{6,4},{7,5},{8,10},{9,11},{10,... | collective-permute-start | bytes 12296 | tf_op jit(solution)/shard_map/ppermute | solution.py:575
  39.0 0.0 collective-permute-done.7.first_late_ref
  39.0 0.0 collective-permute-done.8.second_late_ref
  39.0 2.0 %shard_map.81.refs_0_ = f32[9,96,128]{2,1,0:T(8,128)S(1)} custom-call(s32[6]{0:T(128)S(1)} %stack.27.place_ref, f32[3,9,8,128]{3,2,1,0:T(8,128)S(1)} %collective-permute-done.7.first_late_ref, f32[3,9,8,128]{3,2,1,0:T(8,128)S(1)} %collective-permute-done.8.second_late_ref, f32[9,96,128]{2,1,0:T(8,128)S(1)} %get-tuple-element.38.b_right_ref, ...), custom_call_target="tpu_custom_call" | custom-call | flops 100000000 | bytes 10000000 | tf_op jit(solution)/shard_map/pallas_call | solution.py:686
  41.0 0.0 collective-permute-done.9
  41.0 2.1 %collective-permute-start.10 = (f32[8,128]{1,0:T(8,128)S(1)}, f32[8,128]{1,0:T(8,128)S(1)}, u32[]{:S(2)}, u32[]{:S(2)}) collective-permute-start(f32[8,128]{1,0:T(8,128)S(1)} %add.13), channel_id=1, source_target_pairs={{0,4},{4,0},{8,12},{12,8},{1,5},{5,1},{9,13},{13,9},{2,6},{6,2},{1... | collective-permute-start | bytes 12296 | tf_op jit(solution)/shard_map/ppermute | solution.py:575
  43.1 1.9 %shard_map.82.refs_1_ = f32[9,96,128]{2,1,0:T(8,128)S(1)} custom-call(s32[6]{0:T(128)S(1)} %stack.27.place_ref, f32[3,9,8,128]{3,2,1,0:T(8,128)S(1)} %collective-permute-done.7.first_late_ref, f32[3,9,8,128]{3,2,1,0:T(8,128)S(1)} %collective-permute-done.8.second_late_ref, f32[9,96,128]{2,1,0:T(8,128)S(1)} %get-tuple-element.38.b_right_ref, ...), custom_call_target="tpu_custom_call" | custom-call | flops 100000000 | bytes 10000000 | tf_op jit(solution)/shard_map/pallas_call | solution.py:686
  45.0 0.0 collective-permute-done.10
  45.0 2.4 %collective-permute-start.11 = (f32[8,128]{1,0:T(8,128)S(1)}, f32[8,128]{1,0:T(8,128)S(1)}, u32[]{:S(2)}, u32[]{:S(2)}) collective-permute-start(f32[8,128]{1,0:T(8,128)S(1)} %add.14), channel_id=1, source_target_pairs={{0,8},{4,12},{8,0},{12,4},{1,9},{5,13},{9,1},{13,5},{2,10},{6,14},... | collective-permute-start | bytes 12296 | tf_op jit(solution)/shard_map/ppermute | solution.py:575
  47.4 1.9 %shard_map.83.refs_2_ = f32[9,96,128]{2,1,0:T(8,128)S(1)} custom-call(s32[6]{0:T(128)S(1)} %stack.27.place_ref, f32[3,9,8,128]{3,2,1,0:T(8,128)S(1)} %collective-permute-done.7.first_late_ref, f32[3,9,8,128]{3,2,1,0:T(8,128)S(1)} %collective-permute-done.8.second_late_ref, f32[9,96,128]{2,1,0:T(8,128)S(1)} %get-tuple-element.38.b_right_ref, ...), custom_call_target="tpu_custom_call" | custom-call | flops 100000000 | bytes 10000000 | tf_op jit(solution)/shard_map/pallas_call | solution.py:686
  49.3 0.3 collective-permute-done.11
  49.6 2.8 %shard_map.84 = (f32[3,64,1024]{2,1,0:T(8,128)}, f32[3,64,1024]{2,1,0:T(8,128)}, f32[3,64,1024]{2,1,0:T(8,128)}) custom-call(f32[8,128]{1,0:T(8,128)S(1)} %add.15.sums_ref, f32[9,96,128]{2,1,0:T(8,128)S(1)} %get-tuple-element.44.scale_ref, f32[9,96,128]{2,1,0:T(8,128)S(1)} %get-tuple-element.45.root_ref, f32[3,9,96,128]{3,2,1,0:T(8,128)S(1)} %get-tuple-element.46.g0_ref, ...), custom_call_target="tpu_custom_call" | custom-call | tf_op jit(solution)/shard_map/pallas_call | solution.py:698
  (8 shorter events, 0.0 us)
Async XLA Ops:
  0.7 0.7 %copy-start = (s32[1,16,3]{1,0,2:T(1,128)S(1)}, s32[1,16,3]{1,0,2:T(1,128)}, u32[]{:S(2)}) copy-start(s32[1,16,3]{1,0,2:T(1,128)} %param.9) | copy-start | bytes 580
  3.6 13.3 %collective-permute-start.2 = (f32[6,8,16,128]{3,2,1,0:T(8,128)S(1)}, f32[6,8,16,128]{3,2,1,0:T(8,128)S(1)}, u32[]{:S(2)}, u32[]{:S(2)}) collective-permute-start(f32[6,8,16,128]{3,2,1,0:T(8,128)S(1)} %get-tuple-element.31), channel_id=1, source_target_pairs={{0,4},{8,12},{4,0},{12,8},{1,5},{9,13},{5,1},{13,9},{2,6},{10,14},... | collective-permute-start | bytes 1179656 | tf_op jit(solution)/shard_map/ppermute | solution.py:639
  6.7 10.3 %collective-permute-start.3 = (f32[6,8,16,128]{3,2,1,0:T(8,128)S(1)}, f32[6,8,16,128]{3,2,1,0:T(8,128)S(1)}, u32[]{:S(2)}, u32[]{:S(2)}) collective-permute-start(f32[6,8,16,128]{3,2,1,0:T(8,128)S(1)} %get-tuple-element.32), channel_id=1, source_target_pairs={{4,8},{8,4},{5,9},{9,5},{6,10},{10,6},{7,11},{11,7},{20,24},{24,20... | collective-permute-start | bytes 1179656 | tf_op jit(solution)/shard_map/ppermute | solution.py:639
  7.4 1.3 %collective-permute-start = (f32[2,64,128]{2,1,0:T(8,128)S(1)}, f32[2,64,128]{2,1,0:T(8,128)S(1)}, u32[]{:S(2)}, u32[]{:S(2)}) collective-permute-start(f32[2,64,128]{2,1,0:T(8,128)S(1)} %get-tuple-element.29), channel_id=1, source_target_pairs={{0,1},{2,3},{1,0},{3,2},{4,5},{6,7},{5,4},{7,6},{8,9},{10,11},{9,8... | collective-permute-start | bytes 196616 | tf_op jit(solution)/shard_map/ppermute | solution.py:639
  7.4 1.2 %collective-permute-start.1 = (f32[2,64,128]{2,1,0:T(8,128)S(1)}, f32[2,64,128]{2,1,0:T(8,128)S(1)}, u32[]{:S(2)}, u32[]{:S(2)}) collective-permute-start(f32[2,64,128]{2,1,0:T(8,128)S(1)} %get-tuple-element.30), channel_id=1, source_target_pairs={{1,2},{2,1},{5,6},{6,5},{9,10},{10,9},{13,14},{14,13},{17,18},{18,... | collective-permute-start | bytes 196616 | tf_op jit(solution)/shard_map/ppermute | solution.py:639
  9.3 7.6 %collective-permute-start.4 = (f32[2,2,16,128]{3,2,1,0:T(8,128)S(1)}, f32[2,2,16,128]{3,2,1,0:T(8,128)S(1)}, u32[]{:S(2)}, u32[]{:S(2)}) collective-permute-start(f32[2,2,16,128]{3,2,1,0:T(8,128)S(1)} %get-tuple-element.33), channel_id=1, source_target_pairs={{0,4},{8,12},{4,0},{12,8},{1,5},{9,13},{5,1},{13,9},{2,6},{10,14},... | collective-permute-start | bytes 98312 | tf_op jit(solution)/shard_map/ppermute | solution.py:639
  13.7 3.2 %collective-permute-start.5 = (f32[2,2,16,128]{3,2,1,0:T(8,128)S(1)}, f32[2,2,16,128]{3,2,1,0:T(8,128)S(1)}, u32[]{:S(2)}, u32[]{:S(2)}) collective-permute-start(f32[2,2,16,128]{3,2,1,0:T(8,128)S(1)} %get-tuple-element.34), channel_id=1, source_target_pairs={{4,8},{8,4},{5,9},{9,5},{6,10},{10,6},{7,11},{11,7},{20,24},{24,20... | collective-permute-start | bytes 98312 | tf_op jit(solution)/shard_map/ppermute | solution.py:639
  28.6 10.4 %collective-permute-start.7 = (f32[3,9,8,128]{3,2,1,0:T(8,128)S(1)}, f32[3,9,8,128]{3,2,1,0:T(8,128)S(1)}, u32[]{:S(2)}, u32[]{:S(2)}) collective-permute-start(f32[3,9,8,128]{3,2,1,0:T(8,128)S(1)} %get-tuple-element.36), channel_id=1, source_target_pairs={{0,4},{8,12},{4,0},{12,8},{1,5},{9,13},{5,1},{13,9},{2,6},{10,14},... | collective-permute-start | bytes 331784 | tf_op jit(solution)/shard_map/ppermute | solution.py:639
  32.6 6.3 %collective-permute-start.8 = (f32[3,9,8,128]{3,2,1,0:T(8,128)S(1)}, f32[3,9,8,128]{3,2,1,0:T(8,128)S(1)}, u32[]{:S(2)}, u32[]{:S(2)}) collective-permute-start(f32[3,9,8,128]{3,2,1,0:T(8,128)S(1)} %get-tuple-element.37), channel_id=1, source_target_pairs={{4,8},{8,4},{5,9},{9,5},{6,10},{10,6},{7,11},{11,7},{20,24},{24,20... | collective-permute-start | bytes 331784 | tf_op jit(solution)/shard_map/ppermute | solution.py:639
  33.3 3.2 %collective-permute-start.6 = (f32[8,128]{1,0:T(8,128)S(1)}, f32[8,128]{1,0:T(8,128)S(1)}, u32[]{:S(2)}, u32[]{:S(2)}) collective-permute-start(f32[8,128]{1,0:T(8,128)S(1)} %get-tuple-element.35), channel_id=1, source_target_pairs={{0,1},{1,0},{2,3},{3,2},{4,5},{5,4},{6,7},{7,6},{8,9},{9,8},{10,11... | collective-permute-start | bytes 12296 | tf_op jit(solution)/shard_map/ppermute | solution.py:575
  36.5 4.5 %collective-permute-start.9 = (f32[8,128]{1,0:T(8,128)S(1)}, f32[8,128]{1,0:T(8,128)S(1)}, u32[]{:S(2)}, u32[]{:S(2)}) collective-permute-start(f32[8,128]{1,0:T(8,128)S(1)} %add.12), channel_id=1, source_target_pairs={{0,2},{1,3},{2,0},{3,1},{4,6},{5,7},{6,4},{7,5},{8,10},{9,11},{10,... | collective-permute-start | bytes 12296 | tf_op jit(solution)/shard_map/ppermute | solution.py:575
  41.0 4.0 %collective-permute-start.10 = (f32[8,128]{1,0:T(8,128)S(1)}, f32[8,128]{1,0:T(8,128)S(1)}, u32[]{:S(2)}, u32[]{:S(2)}) collective-permute-start(f32[8,128]{1,0:T(8,128)S(1)} %add.13), channel_id=1, source_target_pairs={{0,4},{4,0},{8,12},{12,8},{1,5},{5,1},{9,13},{13,9},{2,6},{6,2},{1... | collective-permute-start | bytes 12296 | tf_op jit(solution)/shard_map/ppermute | solution.py:575
  45.0 4.6 %collective-permute-start.11 = (f32[8,128]{1,0:T(8,128)S(1)}, f32[8,128]{1,0:T(8,128)S(1)}, u32[]{:S(2)}, u32[]{:S(2)}) collective-permute-start(f32[8,128]{1,0:T(8,128)S(1)} %add.14), channel_id=1, source_target_pairs={{0,8},{4,12},{8,0},{12,4},{1,9},{5,13},{9,1},{13,5},{2,10},{6,14},... | collective-permute-start | bytes 12296 | tf_op jit(solution)/shard_map/ppermute | solution.py:575

commit v9 on v8

--- a/solution.py
+++ b/solution.py
@@ -63,14 +63,14 @@
 
 
 def own_kernel(
-    place_ref, offsets_ref, src_hbm, weight_hbm, seam_right_hbm, seam_down_hbm,
+    place_ref, offsets_hbm, src_hbm, weight_hbm, seam_right_hbm, seam_down_hbm,
     own_ref, first_rows_ref, second_rows_ref, first_cols_ref, second_cols_ref,
-    src_ref, weight_ref, seam_right_ref, seam_down_ref, sems,
+    offsets_ref, src_ref, weight_ref, seam_right_ref, seam_down_ref, sems,
 ):
     chans, rows, cols = src_ref.shape
     own_tiles = cols // LANES
     moves = [(weight_hbm, weight_ref), (seam_right_hbm, seam_right_ref), (seam_down_hbm, seam_down_ref)]
-    moves += [(src_hbm.at[c], src_ref.at[c]) for c in range(chans)]
+    moves += [(src_hbm.at[c], src_ref.at[c]) for c in range(chans)] + [(offsets_hbm, offsets_ref)]
     copies = [pltpu.make_async_copy(there, here, sems.at[k]) for k, (there, here) in enumerate(moves)]
     for copy in copies:
         copy.start()
@@ -94,6 +94,7 @@
     for j in range(own_tiles):
         value = 1.0 - seam_damping * tile(seam_down_ref, j).astype(jnp.float32)
         own_ref[chans + 2, j] = jnp.where(row == last_row, 0.0, value)
+    copies[-1].wait()
     for c in range(chans):
         shift = [
             jnp.broadcast_to(offsets_ref[c, tile_row, tile_at + k], (rows, LANES)).astype(jnp.float32) / offset_unit
@@ -486,20 +487,16 @@
     rows = height - 2 * HALO
     steps = height // SUBS
     odd = place_ref[4] == 1
-    sub = lax.broadcasted_iota(jnp.int32, (SUBS, LANES), 0)
-    halo = {i: [] for i in range(steps)}
-    for k in range(LATE):
-        for top, at in ((True, HALO - LATE + k), (False, HALO + rows + k)):
-            s, i = divmod(at, steps)
-            halo[i].append((s, top, k))
     for j in range(tiles):
-        for i in range(steps):
-            value = g2_ref[c, j, i * SUBS:(i + 1) * SUBS, :]
-            for s, top, k in halo[i]:
-                first, second = [ref[c, j, k:k + 1, :] for ref in (first_late_ref, second_late_ref)]
-                row = jnp.where(odd, first, second) if top else jnp.where(odd, second, first)
-                value = jnp.where(sub == s, row, value)
-            g_ref[j, i * SUBS:(i + 1) * SUBS, :] = value
+        g_ref[j] = g2_ref[c, j]
+        first, second = first_late_ref[c, j], second_late_ref[c, j]
+        for value, at in ((jnp.where(odd, first, second), HALO - LATE), (jnp.where(odd, second, first), HALO + rows)):
+            done = 0
+            while done < LATE:
+                s, i = divmod(at + done, steps)
+                count = min(LATE - done, steps - i)
+                g_ref[j, pl.ds(i * SUBS + s, count, stride=SUBS), :] = value[done:done + count]
+                done += count
     precondition(b_right_ref, b_down_ref, g_ref, f2_ref, work_ref)
 
 
@@ -616,38 +613,34 @@
         out_shape=[shaped(planes, own_tiles, rows, LANES)]
         + [shaped(planes, own_tiles, HALO, LANES)] * 2
         + [shaped(packs, rows, LANES)] * 2,
-        in_specs=[in_smem] * 2 + [in_hbm] * 4,
+        in_specs=[in_smem] + [in_hbm] * 5,
         out_specs=[in_vmem] * 5,
         scratch_shapes=[
+            pltpu.SMEM((chans,) + offsets.shape[:2], jnp.int32),
             scratch(*source.shape),
             scratch(*weight.shape),
             pltpu.VMEM(weight.shape, jnp.int32),
             pltpu.VMEM(weight.shape, jnp.int32),
-            pltpu.SemaphoreType.DMA((planes,)),
+            pltpu.SemaphoreType.DMA((planes + 1,)),
         ],
         compiler_params=params,
     )(
         place,
-        offsets.transpose(2, 0, 1),
-        *[pltpu.with_memory_space_constraint(v, pltpu.HBM) for v in (source, weight, seam_right, seam_down)],
+        *[
+            pltpu.with_memory_space_constraint(v, pltpu.HBM)
+            for v in (offsets.transpose(2, 0, 1), source, weight, seam_right, seam_down)
+        ],
     )
 
     def swap(first, second, axis):
         size = lax.axis_size(axis)
-        pairs = [[(i, i + 1) for i in range(start, size - 1, 2)] for start in range(2)]
-        pairs = [some + [(j, i) for i, j in some] for some in pairs]
-        return [lax.ppermute(value, axis, some) for value, some in zip((first, second), pairs)]
-
-    first_rows, second_rows = swap(first_rows, second_rows, "row")
-    first_cols, second_cols = swap(first_cols, second_cols, "col")
-    corners = pl.pallas_call(
-        functools.partial(corners_kernel, chans),
-        out_shape=[shaped(2, packs, HALO, LANES)] * 2,
-        in_specs=[in_smem] + [in_vmem] * 2,
-        out_specs=[in_vmem] * 2,
-        compiler_params=params,
-    )(place, first_cols, second_cols)
-    first_corners, second_corners = swap(*corners, "row")
+        received = []
+        for start, value in enumerate((first, second)):
+            pairs = [(i, i + 1) for i in range(start, size - 1, 2)]
+            pairs += [(j, i) for i, j in pairs]
+            received.append(None if value is None else lax.ppermute(value, axis, pairs))
+        return received
+
     ways = ways_of(tiles)
     inner = pl.pallas_call(
         inner_dealt_kernel,
@@ -657,6 +650,20 @@
         compiler_params=params,
         cost_estimate=pl.CostEstimate(flops=10**8, bytes_accessed=4 * 10**6, transcendentals=0),
     )(own)
+    first_rows, _ = swap(first_rows, None, "row")
+    first_cols, second_cols = swap(first_cols, second_cols, "col")
+    first_cols, second_cols, second_rows, inner = lax.optimization_barrier(
+        (first_cols, second_cols, second_rows, inner)
+    )
+    _, second_rows = swap(None, second_rows, "row")
+    corners = pl.pallas_call(
+        functools.partial(corners_kernel, chans),
+        out_shape=[shaped(2, packs, HALO, LANES)] * 2,
+        in_specs=[in_smem] + [in_vmem] * 2,
+        out_specs=[in_vmem] * 2,
+        compiler_params=params,
+    )(place, first_cols, second_cols)
+    first_corners, second_corners = swap(*corners, "row")
     outer = pl.pallas_call(
         outer_dealt_kernel,
         out_shape=shaped(planes, ways, rows, LANES),

time: 52.7 us -> 53.5 us (1.015)
  starting transfers between devices: 23.5 us -> 25 us
  local copies, waits for them, and re-layouts: 0.77 us -> 0.08 us
    ppermute x8, starting transfers between devices: 14.2 us -> 15.7 us  [swap(): received.append(None if value is None else lax.ppermute(value, axis, pairs))]
    unnamed x2 -> x0, local copies, waits for them, and re-layouts: 0.68 us -> none
where the time goes in v9:
time: 53.5 us; the launch traced here: 53.3 us
  Pallas kernels  26.1 us (49%)
  starting transfers between devices  25 us (47%)
  waiting for transfers between devices  1.35 us (3%)
  between operations  0.78 us (1%)
    ppermute x8, starting transfers between devices, swap(): received.append(None if value is None else lax.ppermute(value, axis, pairs))  15.7 us
    pallas_call x1, Pallas kernels, per_device(): pl.pallas_call(first_kernel, out_shape=[plane] * 4 + [field] * 5 + [shape...  12 us
    ppermute x4, starting transfers between devices, sum_over(): other = lax.ppermute(value, axis, pairs)  9.27 us
    pallas_call x3, Pallas kernels, per_device(): pl.pallas_call(functools.partial(second_kernel, c), out_shape=plane, in_s...  5.84 us
    pallas_call x1, Pallas kernels, per_device(): pl.pallas_call(third_kernel, out_shape=[shaped(chans, rows, cols)] * 3, i...  2.93 us
    pallas_call x1, Pallas kernels, per_device(): pl.pallas_call(own_kernel, out_shape=[shaped(planes, own_tiles, rows, LAN...  2.17 us
    pallas_call x1, Pallas kernels, per_device(): pl.pallas_call(outer_dealt_kernel, out_shape=shaped(planes, ways, rows, L...  1.3 us
    pallas_call x1, Pallas kernels, per_device(): pl.pallas_call(inner_dealt_kernel, out_shape=shaped(planes, tiles - ways,...  1.25 us
  transfers between devices with their start and end apart: 12, of which 3 were waited for; matrix products, arithmetic and copies ran while one was open for 0% of the time, Pallas kernels for 17%

profile of v9, /device:TPU:0, one launch (start us, length us, event | category | flops | bytes accessed | tf_op | source)
XLA Modules:
  0.0 53.3 jit_solution(3530925252743919769)
XLA Ops:
  0.6 0.1 stack.27.place_ref
  0.7 2.2 %shard_map.76 = (f32[6,8,64,128]{3,2,1,0:T(8,128)S(1)}, f32[6,8,16,128]{3,2,1,0:T(8,128)S(1)}, f32[6,8,16,128]{3,2,1,0:T(8,128)S(1)}, f32[2,64,128]{2,1,0:T(8,128)S(1)}, f32[2,64,128]{2,1,0:T(8,128)S(1)}) custom-call(s32[6]{0:T(128)S(1)} %stack.27.place_ref, s32[3,1,16]{2,1,0:T(1,128)} %bitcast.7, f32[3,64,1024]{2,1,0:T(8,128)} %src_hbm.1, ...), custom_call_target="tpu_custom_call" | custom-call | tf_op jit(solution)/shard_map/pallas_call | solution.py:611
  2.9 0.5 collective-permute-start
  3.4 0.7 %collective-permute-start.1 = (f32[2,64,128]{2,1,0:T(8,128)S(1)}, f32[2,64,128]{2,1,0:T(8,128)S(1)}, u32[]{:S(2)}, u32[]{:S(2)}) collective-permute-start(f32[2,64,128]{2,1,0:T(8,128)S(1)} %get-tuple-element.33), channel_id=1, source_target_pairs={{1,2},{2,1},{5,6},{6,5},{9,10},{10,9},{13,14},{14,13},{17,18},{18,... | collective-permute-start | bytes 196616 | tf_op jit(solution)/shard_map/ppermute | solution.py:641
  4.1 2.7 %collective-permute-start.2 = (f32[6,8,16,128]{3,2,1,0:T(8,128)S(1)}, f32[6,8,16,128]{3,2,1,0:T(8,128)S(1)}, u32[]{:S(2)}, u32[]{:S(2)}) collective-permute-start(f32[6,8,16,128]{3,2,1,0:T(8,128)S(1)} %get-tuple-element.39), channel_id=1, source_target_pairs={{0,4},{8,12},{4,0},{12,8},{1,5},{9,13},{5,1},{13,9},{2,6},{10,14},... | collective-permute-start | bytes 1179656 | tf_op jit(solution)/shard_map/ppermute | solution.py:641
  6.7 1.2 %shard_map.77.inner_ref = f32[6,6,64,128]{3,2,1,0:T(8,128)S(1)} custom-call(f32[6,8,64,128]{3,2,1,0:T(8,128)S(1)} %get-tuple-element.35.own_ref), custom_call_target="tpu_custom_call" | custom-call | flops 100000000 | bytes 4000000 | tf_op jit(solution)/shard_map/pallas_call | solution.py:645
  8.0 0.0 collective-permute-done.first_ref
  8.0 0.0 collective-permute-done.1.second_ref
  8.0 0.7 %collective-permute-start.3 = (f32[6,8,16,128]{3,2,1,0:T(8,128)S(1)}, f32[6,8,16,128]{3,2,1,0:T(8,128)S(1)}, u32[]{:S(2)}, u32[]{:S(2)}) collective-permute-start(f32[6,8,16,128]{3,2,1,0:T(8,128)S(1)} %get-tuple-element.40), channel_id=1, source_target_pairs={{4,8},{8,4},{5,9},{9,5},{6,10},{10,6},{7,11},{11,7},{20,24},{24,20... | collective-permute-start | bytes 1179656 | tf_op jit(solution)/shard_map/ppermute | solution.py:641
  8.7 0.6 %shard_map.79 = (f32[2,2,16,128]{3,2,1,0:T(8,128)S(1)}, f32[2,2,16,128]{3,2,1,0:T(8,128)S(1)}) custom-call(s32[6]{0:T(128)S(1)} %stack.27.place_ref, f32[2,64,128]{2,1,0:T(8,128)S(1)} %collective-permute-done.first_ref, f32[2,64,128]{2,1,0:T(8,128)S(1)} %collective-permute-done.1.second_ref), custom_call_target="tpu_custom_call" | custom-call | tf_op jit(solution)/shard_map/pallas_call | solution.py:659
  9.3 4.4 %collective-permute-start.4 = (f32[2,2,16,128]{3,2,1,0:T(8,128)S(1)}, f32[2,2,16,128]{3,2,1,0:T(8,128)S(1)}, u32[]{:S(2)}, u32[]{:S(2)}) collective-permute-start(f32[2,2,16,128]{3,2,1,0:T(8,128)S(1)} %get-tuple-element.41), channel_id=1, source_target_pairs={{0,4},{8,12},{4,0},{12,8},{1,5},{9,13},{5,1},{13,9},{2,6},{10,14},... | collective-permute-start | bytes 98312 | tf_op jit(solution)/shard_map/ppermute | solution.py:641
  13.7 0.7 %collective-permute-start.5 = (f32[2,2,16,128]{3,2,1,0:T(8,128)S(1)}, f32[2,2,16,128]{3,2,1,0:T(8,128)S(1)}, u32[]{:S(2)}, u32[]{:S(2)}) collective-permute-start(f32[2,2,16,128]{3,2,1,0:T(8,128)S(1)} %get-tuple-element.42), channel_id=1, source_target_pairs={{4,8},{8,4},{5,9},{9,5},{6,10},{10,6},{7,11},{11,7},{20,24},{24,20... | collective-permute-start | bytes 98312 | tf_op jit(solution)/shard_map/ppermute | solution.py:641
  14.4 1.3 %shard_map.78.outer_ref = f32[6,3,64,128]{3,2,1,0:T(8,128)S(1)} custom-call(s32[6]{0:T(128)S(1)} %stack.27.place_ref, f32[6,8,64,128]{3,2,1,0:T(8,128)S(1)} %get-tuple-element.35.own_ref, f32[2,64,128]{2,1,0:T(8,128)S(1)} %collective-permute-done.first_ref, f32[2,64,128]{2,1,0:T(8,128)S(1)} %collective-permute-done.1.second_ref), custom_call_target="tpu_custom_call" | custom-call | flops 100000000 | bytes 2000000 | tf_op jit(solution)/shard_map/pallas_call | solution.py:667
  15.7 0.3 collective-permute-done.4.first_corners_ref
  16.0 0.0 collective-permute-done.5.second_corners_ref
  16.0 0.0 collective-permute-done.2.first_rows_ref
  16.1 0.0 collective-permute-done.3.second_rows_ref
  16.1 12.0 %shard_map.80 = (f32[9,96,128]{2,1,0:T(8,128)S(1)}, f32[9,96,128]{2,1,0:T(8,128)S(1)}, f32[9,96,128]{2,1,0:T(8,128)S(1)}, f32[9,96,128]{2,1,0:T(8,128)S(1)}, f32...) custom-call(s32[6]{0:T(128)S(1)} %stack.27.place_ref, ...), custom_call_target="tpu_custom_call" | custom-call | tf_op jit(solution)/shard_map/pallas_call | solution.py:680
  28.1 5.5 %collective-permute-start.7 = (f32[3,9,8,128]{3,2,1,0:T(8,128)S(1)}, f32[3,9,8,128]{3,2,1,0:T(8,128)S(1)}, u32[]{:S(2)}, u32[]{:S(2)}) collective-permute-start(f32[3,9,8,128]{3,2,1,0:T(8,128)S(1)} %get-tuple-element.44), channel_id=1, source_target_pairs={{0,4},{8,12},{4,0},{12,8},{1,5},{9,13},{5,1},{13,9},{2,6},{10,14},... | collective-permute-start | bytes 331784 | tf_op jit(solution)/shard_map/ppermute | solution.py:641
  33.6 0.7 %collective-permute-start.8 = (f32[3,9,8,128]{3,2,1,0:T(8,128)S(1)}, f32[3,9,8,128]{3,2,1,0:T(8,128)S(1)}, u32[]{:S(2)}, u32[]{:S(2)}) collective-permute-start(f32[3,9,8,128]{3,2,1,0:T(8,128)S(1)} %get-tuple-element.45), channel_id=1, source_target_pairs={{4,8},{8,4},{5,9},{9,5},{6,10},{10,6},{7,11},{11,7},{20,24},{24,20... | collective-permute-start | bytes 331784 | tf_op jit(solution)/shard_map/ppermute | solution.py:641
  34.2 1.9 %collective-permute-start.6 = (f32[8,128]{1,0:T(8,128)S(1)}, f32[8,128]{1,0:T(8,128)S(1)}, u32[]{:S(2)}, u32[]{:S(2)}) collective-permute-start(f32[8,128]{1,0:T(8,128)S(1)} %get-tuple-element.43), channel_id=1, source_target_pairs={{0,1},{1,0},{2,3},{3,2},{4,5},{5,4},{6,7},{7,6},{8,9},{9,8},{10,11... | collective-permute-start | bytes 12296 | tf_op jit(solution)/shard_map/ppermute | solution.py:572
  36.1 0.8 %collective-permute-done.6 = f32[8,128]{1,0:T(8,128)S(1)} collective-permute-done((f32[8,128]{1,0:T(8,128)S(1)}, f32[8,128]{1,0:T(8,128)S(1)}, u32[]{:S(2)}, u32[]{:S(2)}) %collective-permute-start.6) | collective-permute-done | bytes 4128 | tf_op jit(solution)/shard_map/ppermute | solution.py:572
  37.0 1.8 %collective-permute-start.9 = (f32[8,128]{1,0:T(8,128)S(1)}, f32[8,128]{1,0:T(8,128)S(1)}, u32[]{:S(2)}, u32[]{:S(2)}) collective-permute-start(f32[8,128]{1,0:T(8,128)S(1)} %add.12), channel_id=1, source_target_pairs={{0,2},{1,3},{2,0},{3,1},{4,6},{5,7},{6,4},{7,5},{8,10},{9,11},{10,... | collective-permute-start | bytes 12296 | tf_op jit(solution)/shard_map/ppermute | solution.py:572
  38.8 0.0 collective-permute-done.7.first_late_ref
  38.8 0.0 collective-permute-done.8.second_late_ref
  38.8 1.9 %shard_map.81.refs_0_ = f32[9,96,128]{2,1,0:T(8,128)S(1)} custom-call(s32[6]{0:T(128)S(1)} %stack.27.place_ref, f32[3,9,8,128]{3,2,1,0:T(8,128)S(1)} %collective-permute-done.7.first_late_ref, f32[3,9,8,128]{3,2,1,0:T(8,128)S(1)} %collective-permute-done.8.second_late_ref, f32[9,96,128]{2,1,0:T(8,128)S(1)} %get-tuple-element.46.b_right_ref, ...), custom_call_target="tpu_custom_call" | custom-call | flops 100000000 | bytes 10000000 | tf_op jit(solution)/shard_map/pallas_call | solution.py:693
  40.7 3.1 %collective-permute-start.10 = (f32[8,128]{1,0:T(8,128)S(1)}, f32[8,128]{1,0:T(8,128)S(1)}, u32[]{:S(2)}, u32[]{:S(2)}) collective-permute-start(f32[8,128]{1,0:T(8,128)S(1)} %add.13), channel_id=1, source_target_pairs={{0,4},{4,0},{8,12},{12,8},{1,5},{5,1},{9,13},{13,9},{2,6},{6,2},{1... | collective-permute-start | bytes 12296 | tf_op jit(solution)/shard_map/ppermute | solution.py:572
  43.8 1.9 %shard_map.82.refs_1_ = f32[9,96,128]{2,1,0:T(8,128)S(1)} custom-call(s32[6]{0:T(128)S(1)} %stack.27.place_ref, f32[3,9,8,128]{3,2,1,0:T(8,128)S(1)} %collective-permute-done.7.first_late_ref, f32[3,9,8,128]{3,2,1,0:T(8,128)S(1)} %collective-permute-done.8.second_late_ref, f32[9,96,128]{2,1,0:T(8,128)S(1)} %get-tuple-element.46.b_right_ref, ...), custom_call_target="tpu_custom_call" | custom-call | flops 100000000 | bytes 10000000 | tf_op jit(solution)/shard_map/pallas_call | solution.py:693
  45.8 2.5 %collective-permute-start.11 = (f32[8,128]{1,0:T(8,128)S(1)}, f32[8,128]{1,0:T(8,128)S(1)}, u32[]{:S(2)}, u32[]{:S(2)}) collective-permute-start(f32[8,128]{1,0:T(8,128)S(1)} %add.14), channel_id=1, source_target_pairs={{0,8},{4,12},{8,0},{12,4},{1,9},{5,13},{9,1},{13,5},{2,10},{6,14},... | collective-permute-start | bytes 12296 | tf_op jit(solution)/shard_map/ppermute | solution.py:572
  48.3 1.9 %shard_map.83.refs_2_ = f32[9,96,128]{2,1,0:T(8,128)S(1)} custom-call(s32[6]{0:T(128)S(1)} %stack.27.place_ref, f32[3,9,8,128]{3,2,1,0:T(8,128)S(1)} %collective-permute-done.7.first_late_ref, f32[3,9,8,128]{3,2,1,0:T(8,128)S(1)} %collective-permute-done.8.second_late_ref, f32[9,96,128]{2,1,0:T(8,128)S(1)} %get-tuple-element.46.b_right_ref, ...), custom_call_target="tpu_custom_call" | custom-call | flops 100000000 | bytes 10000000 | tf_op jit(solution)/shard_map/pallas_call | solution.py:693
  50.2 0.2 collective-permute-done.11
  50.4 2.9 %shard_map.84 = (f32[3,64,1024]{2,1,0:T(8,128)}, f32[3,64,1024]{2,1,0:T(8,128)}, f32[3,64,1024]{2,1,0:T(8,128)}) custom-call(f32[8,128]{1,0:T(8,128)S(1)} %add.15.sums_ref, f32[9,96,128]{2,1,0:T(8,128)S(1)} %get-tuple-element.52.scale_ref, f32[9,96,128]{2,1,0:T(8,128)S(1)} %get-tuple-element.53.root_ref, f32[3,9,96,128]{3,2,1,0:T(8,128)S(1)} %get-tuple-element.54.g0_ref, ...), custom_call_target="tpu_custom_call" | custom-call | tf_op jit(solution)/shard_map/pallas_call | solution.py:705
  (6 shorter events, 0.0 us)
Async XLA Ops:
  2.9 5.1 %collective-permute-start = (f32[2,64,128]{2,1,0:T(8,128)S(1)}, f32[2,64,128]{2,1,0:T(8,128)S(1)}, u32[]{:S(2)}, u32[]{:S(2)}) collective-permute-start(f32[2,64,128]{2,1,0:T(8,128)S(1)} %get-tuple-element.32), channel_id=1, source_target_pairs={{0,1},{2,3},{1,0},{3,2},{4,5},{6,7},{5,4},{7,6},{8,9},{10,11},{9,8... | collective-permute-start | bytes 196616 | tf_op jit(solution)/shard_map/ppermute | solution.py:641
  3.4 4.6 %collective-permute-start.1 = (f32[2,64,128]{2,1,0:T(8,128)S(1)}, f32[2,64,128]{2,1,0:T(8,128)S(1)}, u32[]{:S(2)}, u32[]{:S(2)}) collective-permute-start(f32[2,64,128]{2,1,0:T(8,128)S(1)} %get-tuple-element.33), channel_id=1, source_target_pairs={{1,2},{2,1},{5,6},{6,5},{9,10},{10,9},{13,14},{14,13},{17,18},{18,... | collective-permute-start | bytes 196616 | tf_op jit(solution)/shard_map/ppermute | solution.py:641
  4.1 12.0 %collective-permute-start.2 = (f32[6,8,16,128]{3,2,1,0:T(8,128)S(1)}, f32[6,8,16,128]{3,2,1,0:T(8,128)S(1)}, u32[]{:S(2)}, u32[]{:S(2)}) collective-permute-start(f32[6,8,16,128]{3,2,1,0:T(8,128)S(1)} %get-tuple-element.39), channel_id=1, source_target_pairs={{0,4},{8,12},{4,0},{12,8},{1,5},{9,13},{5,1},{13,9},{2,6},{10,14},... | collective-permute-start | bytes 1179656 | tf_op jit(solution)/shard_map/ppermute | solution.py:641
  8.0 8.0 %collective-permute-start.3 = (f32[6,8,16,128]{3,2,1,0:T(8,128)S(1)}, f32[6,8,16,128]{3,2,1,0:T(8,128)S(1)}, u32[]{:S(2)}, u32[]{:S(2)}) collective-permute-start(f32[6,8,16,128]{3,2,1,0:T(8,128)S(1)} %get-tuple-element.40), channel_id=1, source_target_pairs={{4,8},{8,4},{5,9},{9,5},{6,10},{10,6},{7,11},{11,7},{20,24},{24,20... | collective-permute-start | bytes 1179656 | tf_op jit(solution)/shard_map/ppermute | solution.py:641
  9.3 6.7 %collective-permute-start.4 = (f32[2,2,16,128]{3,2,1,0:T(8,128)S(1)}, f32[2,2,16,128]{3,2,1,0:T(8,128)S(1)}, u32[]{:S(2)}, u32[]{:S(2)}) collective-permute-start(f32[2,2,16,128]{3,2,1,0:T(8,128)S(1)} %get-tuple-element.41), channel_id=1, source_target_pairs={{0,4},{8,12},{4,0},{12,8},{1,5},{9,13},{5,1},{13,9},{2,6},{10,14},... | collective-permute-start | bytes 98312 | tf_op jit(solution)/shard_map/ppermute | solution.py:641
  13.7 2.3 %collective-permute-start.5 = (f32[2,2,16,128]{3,2,1,0:T(8,128)S(1)}, f32[2,2,16,128]{3,2,1,0:T(8,128)S(1)}, u32[]{:S(2)}, u32[]{:S(2)}) collective-permute-start(f32[2,2,16,128]{3,2,1,0:T(8,128)S(1)} %get-tuple-element.42), channel_id=1, source_target_pairs={{4,8},{8,4},{5,9},{9,5},{6,10},{10,6},{7,11},{11,7},{20,24},{24,20... | collective-permute-start | bytes 98312 | tf_op jit(solution)/shard_map/ppermute | solution.py:641
  28.1 10.7 %collective-permute-start.7 = (f32[3,9,8,128]{3,2,1,0:T(8,128)S(1)}, f32[3,9,8,128]{3,2,1,0:T(8,128)S(1)}, u32[]{:S(2)}, u32[]{:S(2)}) collective-permute-start(f32[3,9,8,128]{3,2,1,0:T(8,128)S(1)} %get-tuple-element.44), channel_id=1, source_target_pairs={{0,4},{8,12},{4,0},{12,8},{1,5},{9,13},{5,1},{13,9},{2,6},{10,14},... | collective-permute-start | bytes 331784 | tf_op jit(solution)/shard_map/ppermute | solution.py:641
  33.6 5.2 %collective-permute-start.8 = (f32[3,9,8,128]{3,2,1,0:T(8,128)S(1)}, f32[3,9,8,128]{3,2,1,0:T(8,128)S(1)}, u32[]{:S(2)}, u32[]{:S(2)}) collective-permute-start(f32[3,9,8,128]{3,2,1,0:T(8,128)S(1)} %get-tuple-element.45), channel_id=1, source_target_pairs={{4,8},{8,4},{5,9},{9,5},{6,10},{10,6},{7,11},{11,7},{20,24},{24,20... | collective-permute-start | bytes 331784 | tf_op jit(solution)/shard_map/ppermute | solution.py:641
  34.2 2.7 %collective-permute-start.6 = (f32[8,128]{1,0:T(8,128)S(1)}, f32[8,128]{1,0:T(8,128)S(1)}, u32[]{:S(2)}, u32[]{:S(2)}) collective-permute-start(f32[8,128]{1,0:T(8,128)S(1)} %get-tuple-element.43), channel_id=1, source_target_pairs={{0,1},{1,0},{2,3},{3,2},{4,5},{5,4},{6,7},{7,6},{8,9},{9,8},{10,11... | collective-permute-start | bytes 12296 | tf_op jit(solution)/shard_map/ppermute | solution.py:572
  37.0 3.8 %collective-permute-start.9 = (f32[8,128]{1,0:T(8,128)S(1)}, f32[8,128]{1,0:T(8,128)S(1)}, u32[]{:S(2)}, u32[]{:S(2)}) collective-permute-start(f32[8,128]{1,0:T(8,128)S(1)} %add.12), channel_id=1, source_target_pairs={{0,2},{1,3},{2,0},{3,1},{4,6},{5,7},{6,4},{7,5},{8,10},{9,11},{10,... | collective-permute-start | bytes 12296 | tf_op jit(solution)/shard_map/ppermute | solution.py:572
  40.7 5.1 %collective-permute-start.10 = (f32[8,128]{1,0:T(8,128)S(1)}, f32[8,128]{1,0:T(8,128)S(1)}, u32[]{:S(2)}, u32[]{:S(2)}) collective-permute-start(f32[8,128]{1,0:T(8,128)S(1)} %add.13), channel_id=1, source_target_pairs={{0,4},{4,0},{8,12},{12,8},{1,5},{5,1},{9,13},{13,9},{2,6},{6,2},{1... | collective-permute-start | bytes 12296 | tf_op jit(solution)/shard_map/ppermute | solution.py:572
  45.8 4.6 %collective-permute-start.11 = (f32[8,128]{1,0:T(8,128)S(1)}, f32[8,128]{1,0:T(8,128)S(1)}, u32[]{:S(2)}, u32[]{:S(2)}) collective-permute-start(f32[8,128]{1,0:T(8,128)S(1)} %add.14), channel_id=1, source_target_pairs={{0,8},{4,12},{8,0},{12,4},{1,9},{5,13},{9,1},{13,5},{2,10},{6,14},... | collective-permute-start | bytes 12296 | tf_op jit(solution)/shard_map/ppermute | solution.py:572

commit v10 on v9

--- a/solution.py
+++ b/solution.py
@@ -50,6 +50,10 @@
     return lax.broadcasted_iota(jnp.int32, (SUBS, LANES), 1)
 
 
+def odd(axis):
+    return lax.rem(lax.axis_index(axis), 2) == 1
+
+
 def pack(planes, start):
     lane = lax.broadcasted_iota(jnp.int32, planes[0].shape, 1)
     packed = [None] * (-(-len(planes) // SLOTS))
@@ -63,7 +67,7 @@
 
 
 def own_kernel(
-    place_ref, offsets_hbm, src_hbm, weight_hbm, seam_right_hbm, seam_down_hbm,
+    offsets_hbm, src_hbm, weight_hbm, seam_right_hbm, seam_down_hbm,
     own_ref, first_rows_ref, second_rows_ref, first_cols_ref, second_cols_ref,
     offsets_ref, src_ref, weight_ref, seam_right_ref, seam_down_ref, sems,
 ):
@@ -77,8 +81,11 @@
     row = lax.broadcasted_iota(jnp.int32, (rows, LANES), 0)
     lane = lax.broadcasted_iota(jnp.int32, (rows, LANES), 1)
     sub = lax.broadcasted_iota(jnp.int32, (SUBS, LANES), 0)
-    last_row, last_lane, tile_row, tile_at = [place_ref[k] for k in range(4)]
-    odd_row, odd_col = (place_ref[4] == 1, place_ref[5] == 1)
+    row_at, col_at = lax.axis_index("row"), lax.axis_index("col")
+    last_row = jnp.where(row_at == lax.axis_size("row") - 1, rows - 1, -1)
+    last_lane = jnp.where(col_at == lax.axis_size("col") - 1, LANES - 1, -1)
+    tile_row, tile_at = lax.div(row_at * rows, TILE), col_at * (cols // TILE)
+    odd_row, odd_col = odd("row"), odd("col")
 
     def tile(ref, j):
         return ref[:, j * LANES:(j + 1) * LANES]
@@ -135,18 +142,18 @@
         second_cols_ref[k] = jnp.where(odd_col, b, a)
 
 
-def corners_kernel(chans, place_ref, first_ref, second_ref, first_out, second_out):
+def corners_kernel(chans, first_ref, second_ref, first_out, second_out):
     rows = first_ref.shape[1]
-    odd_row, odd_col = (place_ref[4] == 1, place_ref[5] == 1)
+    odd_row, odd_col = odd("row"), odd("col")
     sub = lax.broadcasted_iota(jnp.int32, (SUBS, LANES), 0)
     lane = lane_index()
     weight, down = chans, chans + 2
     slot = weight % SLOTS
     at = rows - HALO
-    for side, (odd, even) in enumerate(((first_ref, second_ref), (second_ref, first_ref))):
-
-        def tile(k, low, count=SUBS, odd=odd, even=even):
-            return jnp.where(odd_col, odd[k, low:low + count, :], even[k, low:low + count, :])
+    for side, (in_odd, in_even) in enumerate(((first_ref, second_ref), (second_ref, first_ref))):
+
+        def tile(k, low, count=SUBS, in_odd=in_odd, in_even=in_even):
+            return jnp.where(odd_col, in_odd[k, low:low + count, :], in_even[k, low:low + count, :])
 
         above = jnp.broadcast_to(tile(down // SLOTS, at - 1, 1), (SUBS, LANES))
         above = pltpu.roll(above, (slot - down % SLOTS) % SLOTS * SLOT, 1)
@@ -229,11 +236,11 @@
     deal(lambda j: own_ref[:, j].reshape(planes * rows, LANES), 0, dealt_ref.shape[1], ways_of(own_tiles + 1), emit)
 
 
-def outer_dealt_kernel(place_ref, own_ref, first_ref, second_ref, dealt_ref):
+def outer_dealt_kernel(own_ref, first_ref, second_ref, dealt_ref):
     planes, own_tiles, rows = own_ref.shape[:3]
     tiles = own_tiles + 1
     low = tiles - dealt_ref.shape[1]
-    odd = place_ref[5] == 1
+    odd_col = odd("col")
 
     def tile_of(j):
         if j < own_tiles:
@@ -241,7 +248,7 @@
         parts = []
         for p in range(planes):
             first, second = first_ref[p // SLOTS], second_ref[p // SLOTS]
-            parts.append(unpack(p, jnp.where(odd, first, second), jnp.where(odd, second, first)))
+            parts.append(unpack(p, jnp.where(odd_col, first, second), jnp.where(odd_col, second, first)))
         return jnp.concatenate(parts, axis=0)
 
     def emit(j, value):
@@ -379,7 +386,7 @@
 
 
 def first_kernel(
-    place_ref, inner_ref, outer_ref, first_rows_ref, second_rows_ref, first_corners_ref, second_corners_ref,
+    inner_ref, outer_ref, first_rows_ref, second_rows_ref, first_corners_ref, second_corners_ref,
     b_right_ref, b_down_ref, scale_ref, root_ref, g0_ref, z0_ref, g1_ref, f1_ref, g2_ref, sums_ref,
     first_late_ref, second_late_ref,
     natural, work_ref,
@@ -394,7 +401,7 @@
     for p in range(planes):
         for j in range(tiles):
             natural[p, j, HALO:HALO + rows, :] = inner_ref[p, j] if j < inner else outer_ref[p, j - inner]
-    odd = place_ref[4] == 1
+    odd_row = odd("row")
 
     def edge_tile(j):
         if j < own_tiles:
@@ -404,7 +411,7 @@
                 jnp.concatenate([unpack(p, ref[0, p // SLOTS], ref[1, p // SLOTS]) for p in range(planes)], axis=0)
                 for ref in (first_corners_ref, second_corners_ref)
             ]
-        return jnp.concatenate([jnp.where(odd, first, second), jnp.where(odd, second, first)], axis=0)
+        return jnp.concatenate([jnp.where(odd_row, first, second), jnp.where(odd_row, second, first)], axis=0)
 
     def put_edge(j, value):
         value = value.reshape(2, planes, HALO, LANES)
@@ -476,21 +483,21 @@
     for c in range(chans):
         for j in range(tiles):
             low, high = edge(c, j, 0), edge(c, j, rows - LATE)
-            first_late_ref[c, j] = jnp.where(odd, low, high)
-            second_late_ref[c, j] = jnp.where(odd, high, low)
+            first_late_ref[c, j] = jnp.where(odd_row, low, high)
+            second_late_ref[c, j] = jnp.where(odd_row, high, low)
 
 
 def second_kernel(
-    c, place_ref, first_late_ref, second_late_ref, b_right_ref, b_down_ref, g2_ref, f2_ref, g_ref, work_ref
+    c, first_late_ref, second_late_ref, b_right_ref, b_down_ref, g2_ref, f2_ref, g_ref, work_ref
 ):
     tiles, height = b_right_ref.shape[:2]
     rows = height - 2 * HALO
     steps = height // SUBS
-    odd = place_ref[4] == 1
+    odd_row = odd("row")
     for j in range(tiles):
         g_ref[j] = g2_ref[c, j]
         first, second = first_late_ref[c, j], second_late_ref[c, j]
-        for value, at in ((jnp.where(odd, first, second), HALO - LATE), (jnp.where(odd, second, first), HALO + rows)):
+        for value, at in ((jnp.where(odd_row, first, second), HALO - LATE), (jnp.where(odd_row, second, first), HALO + rows)):
             done = 0
             while done < LATE:
                 s, i = divmod(at + done, steps)
@@ -579,22 +586,7 @@
 
 def per_device(source, weight, seam_right, seam_down, offsets):
     chans, rows, cols = source.shape
-    row_axis, col_axis = lax.axis_size("row"), lax.axis_size("col")
-    row_at, col_at = lax.axis_index("row"), lax.axis_index("col")
-    odd_row, odd_col = lax.rem(row_at, 2), lax.rem(col_at, 2)
-    place = jnp.stack(
-        [
-            jnp.where(row_at == row_axis - 1, rows - 1, -1),
-            jnp.where(col_at == col_axis - 1, LANES - 1, -1),
-            lax.div(row_at * rows, TILE),
-            col_at * (cols // TILE),
-            odd_row,
-            odd_col,
-        ]
-    ).astype(jnp.int32)
-
     in_vmem = pl.BlockSpec(memory_space=pltpu.VMEM)
-    in_smem = pl.BlockSpec(memory_space=pltpu.SMEM)
     in_hbm = pl.BlockSpec(memory_space=pltpu.HBM)
     params = pltpu.CompilerParams(vmem_limit_bytes=VMEM_LIMIT)
 
@@ -613,7 +605,7 @@
         out_shape=[shaped(planes, own_tiles, rows, LANES)]
         + [shaped(planes, own_tiles, HALO, LANES)] * 2
         + [shaped(packs, rows, LANES)] * 2,
-        in_specs=[in_smem] + [in_hbm] * 5,
+        in_specs=[in_hbm] * 5,
         out_specs=[in_vmem] * 5,
         scratch_shapes=[
             pltpu.SMEM((chans,) + offsets.shape[:2], jnp.int32),
@@ -625,7 +617,6 @@
         ],
         compiler_params=params,
     )(
-        place,
         *[
             pltpu.with_memory_space_constraint(v, pltpu.HBM)
             for v in (offsets.transpose(2, 0, 1), source, weight, seam_right, seam_down)
@@ -634,12 +625,9 @@
 
     def swap(first, second, axis):
         size = lax.axis_size(axis)
-        received = []
-        for start, value in enumerate((first, second)):
-            pairs = [(i, i + 1) for i in range(start, size - 1, 2)]
-            pairs += [(j, i) for i, j in pairs]
-            received.append(None if value is None else lax.ppermute(value, axis, pairs))
-        return received
+        pairs = [[(i, i + 1) for i in range(start, size - 1, 2)] for start in range(2)]
+        pairs = [some + [(j, i) for i, j in some] for some in pairs]
+        return [lax.ppermute(value, axis, some) for value, some in zip((first, second), pairs)]
 
     ways = ways_of(tiles)
     inner = pl.pallas_call(
@@ -650,28 +638,25 @@
         compiler_params=params,
         cost_estimate=pl.CostEstimate(flops=10**8, bytes_accessed=4 * 10**6, transcendentals=0),
     )(own)
-    first_rows, _ = swap(first_rows, None, "row")
+    first_rows, second_rows = swap(first_rows, second_rows, "row")
     first_cols, second_cols = swap(first_cols, second_cols, "col")
-    first_cols, second_cols, second_rows, inner = lax.optimization_barrier(
-        (first_cols, second_cols, second_rows, inner)
-    )
-    _, second_rows = swap(None, second_rows, "row")
+    first_cols, second_cols, inner = lax.optimization_barrier((first_cols, second_cols, inner))
     corners = pl.pallas_call(
         functools.partial(corners_kernel, chans),
         out_shape=[shaped(2, packs, HALO, LANES)] * 2,
-        in_specs=[in_smem] + [in_vmem] * 2,
+        in_specs=[in_vmem] * 2,
         out_specs=[in_vmem] * 2,
         compiler_params=params,
-    )(place, first_cols, second_cols)
+    )(first_cols, second_cols)
     first_corners, second_corners = swap(*corners, "row")
     outer = pl.pallas_call(
         outer_dealt_kernel,
         out_shape=shaped(planes, ways, rows, LANES),
-        in_specs=[in_smem] + [in_vmem] * 3,
+        in_specs=[in_vmem] * 3,
         out_specs=in_vmem,
         compiler_params=params,
         cost_estimate=pl.CostEstimate(flops=10**8, bytes_accessed=2 * 10**6, transcendentals=0),
-    )(place, own, first_cols, second_cols)
+    )(own, first_cols, second_cols)
 
     height = rows + 2 * HALO
     plane = shaped(tiles, height, LANES)
@@ -680,11 +665,11 @@
     *basis, sums, first_late, second_late = pl.pallas_call(
         first_kernel,
         out_shape=[plane] * 4 + [field] * 5 + [shaped(SUBS, LANES)] + [late] * 2,
-        in_specs=[in_smem] + [in_vmem] * 6,
+        in_specs=[in_vmem] * 6,
         out_specs=[in_vmem] * 12,
         scratch_shapes=[scratch(planes, tiles, height, LANES), scratch(*plane.shape)],
         compiler_params=params,
-    )(place, inner, outer, first_rows, second_rows, first_corners, second_corners)
+    )(inner, outer, first_rows, second_rows, first_corners, second_corners)
 
     first_late, second_late = swap(first_late, second_late, "row")
 
@@ -693,12 +678,12 @@
         pl.pallas_call(
             functools.partial(second_kernel, c),
             out_shape=plane,
-            in_specs=[in_smem] + [in_vmem] * 5,
+            in_specs=[in_vmem] * 5,
             out_specs=in_vmem,
             scratch_shapes=[scratch(*plane.shape)] * 2,
             compiler_params=params,
             cost_estimate=pl.CostEstimate(flops=10**8, bytes_accessed=10**7, transcendentals=0),
-        )(place, first_late, second_late, b_right, b_down, g2)
+        )(first_late, second_late, b_right, b_down, g2)
         for c in range(chans)
     ]
     total, f2 = sum_over(sums, ("col", "row"), f2)

time: 53.5 us -> 50.1 us (0.936)
  Pallas kernels: 26.1 us -> 22.6 us
  starting transfers between devices: 25 us -> 23.4 us
  waiting for transfers between devices: 1.35 us -> 2.9 us
    pallas_call x3, Pallas kernels: 5.84 us -> 4.36 us  [per_device(): pl.pallas_call(functools.partial(second_kernel, c), out_shape=plane, in_s...]
    ppermute x4, waiting for transfers between devices: 0.98 us -> 2.04 us  [sum_over(): other = lax.ppermute(value, axis, pairs)]
    ppermute x4, starting transfers between devices: 9.27 us -> 8.4 us  [sum_over(): other = lax.ppermute(value, axis, pairs)]
    ppermute x8, starting transfers between devices: 15.7 us -> 15 us  [swap(): lax.ppermute(value, axis, some)]
    pallas_call x1, Pallas kernels: 2.17 us -> 1.63 us  [per_device(): pl.pallas_call(own_kernel, out_shape=[shaped(planes, own_tiles, rows, LAN...]
  transfers between devices with their start and end apart: 12 -> 12, of which waited for: 3 -> 5; matrix products, arithmetic and copies ran while one was open for 0% -> 0% of each run, Pallas kernels for 17% -> 13%
where the time goes in v10:
time: 50.1 us; the launch traced here: 49.7 us
  starting transfers between devices  23.4 us (47%)
  Pallas kernels  22.6 us (45%)
  waiting for transfers between devices  2.9 us (6%)
  between operations  0.75 us (1%)
    ppermute x8, starting transfers between devices, swap(): lax.ppermute(value, axis, some)  15 us
    pallas_call x1, Pallas kernels, per_device(): pl.pallas_call(first_kernel, out_shape=[plane] * 4 + [field] * 5 + [shape...  11.5 us
    ppermute x4, starting transfers between devices, sum_over(): other = lax.ppermute(value, axis, pairs)  8.4 us
    pallas_call x3, Pallas kernels, per_device(): pl.pallas_call(functools.partial(second_kernel, c), out_shape=plane, in_s...  4.36 us
    pallas_call x1, Pallas kernels, per_device(): pl.pallas_call(third_kernel, out_shape=[shaped(chans, rows, cols)] * 3, i...  2.96 us
    ppermute x4, waiting for transfers between devices, sum_over(): other = lax.ppermute(value, axis, pairs)  2.04 us
    pallas_call x1, Pallas kernels, per_device(): pl.pallas_call(own_kernel, out_shape=[shaped(planes, own_tiles, rows, LAN...  1.63 us
    pallas_call x1, Pallas kernels, per_device(): pl.pallas_call(inner_dealt_kernel, out_shape=shaped(planes, tiles - ways,...  1.25 us
  transfers between devices with their start and end apart: 12, of which 5 were waited for; matrix products, arithmetic and copies ran while one was open for 0% of the time, Pallas kernels for 13%

profile of v10, /device:TPU:0, one launch (start us, length us, event | category | flops | bytes accessed | tf_op | source)
XLA Modules:
  0.0 49.7 jit_solution(6278391597803061370)
XLA Ops:
  0.6 1.6 %shard_map.76 = (f32[6,8,64,128]{3,2,1,0:T(8,128)S(1)}, f32[6,8,16,128]{3,2,1,0:T(8,128)S(1)}, f32[6,8,16,128]{3,2,1,0:T(8,128)S(1)}, f32[2,64,128]{2,1,0:T(8,128)S(1)}, f32[2,64,128]{2,1,0:T(8,128)S(1)}) custom-call(s32[3,1,16]{2,1,0:T(1,128)} %bitcast.1, f32[3,64,1024]{2,1,0:T(8,128)} %src_hbm.1, f32[64,1024]{1,0:T(8,128)} %weight_hbm.1, ...), custom_call_target="tpu_custom_call" | custom-call | tf_op jit(solution)/shard_map/pallas_call | solution.py:603
  2.3 3.1 %collective-permute-start.2 = (f32[6,8,16,128]{3,2,1,0:T(8,128)S(1)}, f32[6,8,16,128]{3,2,1,0:T(8,128)S(1)}, u32[]{:S(2)}, u32[]{:S(2)}) collective-permute-start(f32[6,8,16,128]{3,2,1,0:T(8,128)S(1)} %get-tuple-element.37), channel_id=1, source_target_pairs={{0,4},{8,12},{4,0},{12,8},{1,5},{9,13},{5,1},{13,9},{2,6},{10,14},... | collective-permute-start | bytes 1179656 | tf_op jit(solution)/shard_map/ppermute | solution.py:630
  5.4 0.7 %collective-permute-start.3 = (f32[6,8,16,128]{3,2,1,0:T(8,128)S(1)}, f32[6,8,16,128]{3,2,1,0:T(8,128)S(1)}, u32[]{:S(2)}, u32[]{:S(2)}) collective-permute-start(f32[6,8,16,128]{3,2,1,0:T(8,128)S(1)} %get-tuple-element.38), channel_id=1, source_target_pairs={{4,8},{8,4},{5,9},{9,5},{6,10},{10,6},{7,11},{11,7},{20,24},{24,20... | collective-permute-start | bytes 1179656 | tf_op jit(solution)/shard_map/ppermute | solution.py:630
  6.0 0.1 collective-permute-start
  6.1 0.7 %collective-permute-start.1 = (f32[2,64,128]{2,1,0:T(8,128)S(1)}, f32[2,64,128]{2,1,0:T(8,128)S(1)}, u32[]{:S(2)}, u32[]{:S(2)}) collective-permute-start(f32[2,64,128]{2,1,0:T(8,128)S(1)} %get-tuple-element.32), channel_id=1, source_target_pairs={{1,2},{2,1},{5,6},{6,5},{9,10},{10,9},{13,14},{14,13},{17,18},{18,... | collective-permute-start | bytes 196616 | tf_op jit(solution)/shard_map/ppermute | solution.py:630
  6.8 1.2 %shard_map.77.inner_ref = f32[6,6,64,128]{3,2,1,0:T(8,128)S(1)} custom-call(f32[6,8,64,128]{3,2,1,0:T(8,128)S(1)} %get-tuple-element.33.own_ref), custom_call_target="tpu_custom_call" | custom-call | flops 100000000 | bytes 4000000 | tf_op jit(solution)/shard_map/pallas_call | solution.py:633
  8.1 0.0 collective-permute-done.first_ref
  8.1 0.0 collective-permute-done.1.second_ref
  8.1 0.1 shard_map.79
  8.2 4.4 %collective-permute-start.4 = (f32[2,2,16,128]{3,2,1,0:T(8,128)S(1)}, f32[2,2,16,128]{3,2,1,0:T(8,128)S(1)}, u32[]{:S(2)}, u32[]{:S(2)}) collective-permute-start(f32[2,2,16,128]{3,2,1,0:T(8,128)S(1)} %get-tuple-element.39), channel_id=1, source_target_pairs={{0,4},{8,12},{4,0},{12,8},{1,5},{9,13},{5,1},{13,9},{2,6},{10,14},... | collective-permute-start | bytes 98312 | tf_op jit(solution)/shard_map/ppermute | solution.py:630
  12.6 0.7 %collective-permute-start.5 = (f32[2,2,16,128]{3,2,1,0:T(8,128)S(1)}, f32[2,2,16,128]{3,2,1,0:T(8,128)S(1)}, u32[]{:S(2)}, u32[]{:S(2)}) collective-permute-start(f32[2,2,16,128]{3,2,1,0:T(8,128)S(1)} %get-tuple-element.40), channel_id=1, source_target_pairs={{4,8},{8,4},{5,9},{9,5},{6,10},{10,6},{7,11},{11,7},{20,24},{24,20... | collective-permute-start | bytes 98312 | tf_op jit(solution)/shard_map/ppermute | solution.py:630
  13.2 0.8 %shard_map.78.outer_ref = f32[6,3,64,128]{3,2,1,0:T(8,128)S(1)} custom-call(f32[6,8,64,128]{3,2,1,0:T(8,128)S(1)} %get-tuple-element.33.own_ref, f32[2,64,128]{2,1,0:T(8,128)S(1)} %collective-permute-done.first_ref, f32[2,64,128]{2,1,0:T(8,128)S(1)} %collective-permute-done.1.second_ref), custom_call_target="tpu_custom_call" | custom-call | flops 100000000 | bytes 2000000 | tf_op jit(solution)/shard_map/pallas_call | solution.py:652
  14.0 0.8 %collective-permute-done.4.first_corners_ref = f32[2,2,16,128]{3,2,1,0:T(8,128)S(1)} collective-permute-done((f32[2,2,16,128]{3,2,1,0:T(8,128)S(1)}, f32[2,2,16,128]{3,2,1,0:T(8,128)S(1)}, u32[]{:S(2)}, u32[]{:S(2)}) %collective-permute-start.4) | collective-permute-done | bytes 32800 | tf_op jit(solution)/shard_map/ppermute | solution.py:630
  14.8 0.0 collective-permute-done.5.second_corners_ref
  14.8 0.0 collective-permute-done.3.second_rows_ref
  14.8 11.5 %shard_map.80 = (f32[9,96,128]{2,1,0:T(8,128)S(1)}, f32[9,96,128]{2,1,0:T(8,128)S(1)}, f32[9,96,128]{2,1,0:T(8,128)S(1)}, f32[9,96,128]{2,1,0:T(8,128)S(1)}, f32...) custom-call(f32[6,6,64,128]{3,2,1,0:T(8,128)S(1)} %shard_map.77.inne, ...), custom_call_target="tpu_custom_call" | custom-call | tf_op jit(solution)/shard_map/pallas_call | solution.py:665
  26.4 4.8 %collective-permute-start.7 = (f32[3,9,8,128]{3,2,1,0:T(8,128)S(1)}, f32[3,9,8,128]{3,2,1,0:T(8,128)S(1)}, u32[]{:S(2)}, u32[]{:S(2)}) collective-permute-start(f32[3,9,8,128]{3,2,1,0:T(8,128)S(1)} %get-tuple-element.42), channel_id=1, source_target_pairs={{0,4},{8,12},{4,0},{12,8},{1,5},{9,13},{5,1},{13,9},{2,6},{10,14},... | collective-permute-start | bytes 331784 | tf_op jit(solution)/shard_map/ppermute | solution.py:630
  31.2 0.7 %collective-permute-start.8 = (f32[3,9,8,128]{3,2,1,0:T(8,128)S(1)}, f32[3,9,8,128]{3,2,1,0:T(8,128)S(1)}, u32[]{:S(2)}, u32[]{:S(2)}) collective-permute-start(f32[3,9,8,128]{3,2,1,0:T(8,128)S(1)} %get-tuple-element.43), channel_id=1, source_target_pairs={{4,8},{8,4},{5,9},{9,5},{6,10},{10,6},{7,11},{11,7},{20,24},{24,20... | collective-permute-start | bytes 331784 | tf_op jit(solution)/shard_map/ppermute | solution.py:630
  31.9 1.8 %collective-permute-start.6 = (f32[8,128]{1,0:T(8,128)S(1)}, f32[8,128]{1,0:T(8,128)S(1)}, u32[]{:S(2)}, u32[]{:S(2)}) collective-permute-start(f32[8,128]{1,0:T(8,128)S(1)} %get-tuple-element.41), channel_id=1, source_target_pairs={{0,1},{1,0},{2,3},{3,2},{4,5},{5,4},{6,7},{7,6},{8,9},{9,8},{10,11... | collective-permute-start | bytes 12296 | tf_op jit(solution)/shard_map/ppermute | solution.py:579
  33.7 0.8 %collective-permute-done.6 = f32[8,128]{1,0:T(8,128)S(1)} collective-permute-done((f32[8,128]{1,0:T(8,128)S(1)}, f32[8,128]{1,0:T(8,128)S(1)}, u32[]{:S(2)}, u32[]{:S(2)}) %collective-permute-start.6) | collective-permute-done | bytes 4128 | tf_op jit(solution)/shard_map/ppermute | solution.py:579
  34.5 2.5 %collective-permute-start.9 = (f32[8,128]{1,0:T(8,128)S(1)}, f32[8,128]{1,0:T(8,128)S(1)}, u32[]{:S(2)}, u32[]{:S(2)}) collective-permute-start(f32[8,128]{1,0:T(8,128)S(1)} %add.12), channel_id=1, source_target_pairs={{0,2},{1,3},{2,0},{3,1},{4,6},{5,7},{6,4},{7,5},{8,10},{9,11},{10,... | collective-permute-start | bytes 12296 | tf_op jit(solution)/shard_map/ppermute | solution.py:579
  37.0 0.0 collective-permute-done.7.first_late_ref
  37.0 0.0 collective-permute-done.8.second_late_ref
  37.0 1.5 %shard_map.81.refs_0_ = f32[9,96,128]{2,1,0:T(8,128)S(1)} custom-call(f32[3,9,8,128]{3,2,1,0:T(8,128)S(1)} %collective-permute-done.7.first_late_ref, f32[3,9,8,128]{3,2,1,0:T(8,128)S(1)} %collective-permute-done.8.second_late_ref, f32[9,96,128]{2,1,0:T(8,128)S(1)} %get-tuple-element.44.b_right_ref, f32[9,96,128]{2,1,0:T(8,128)S(1)} %get-tuple-element.45.b_down_ref, ...), custom_call_target="tpu_custom_call" | custom-call | flops 100000000 | bytes 10000000 | tf_op jit(solution)/shard_map/pallas_call | solution.py:678
  38.5 0.1 collective-permute-done.9
  38.6 1.3 %collective-permute-start.10 = (f32[8,128]{1,0:T(8,128)S(1)}, f32[8,128]{1,0:T(8,128)S(1)}, u32[]{:S(2)}, u32[]{:S(2)}) collective-permute-start(f32[8,128]{1,0:T(8,128)S(1)} %add.13), channel_id=1, source_target_pairs={{0,4},{4,0},{8,12},{12,8},{1,5},{5,1},{9,13},{13,9},{2,6},{6,2},{1... | collective-permute-start | bytes 12296 | tf_op jit(solution)/shard_map/ppermute | solution.py:579
  39.9 1.4 %shard_map.82.refs_1_ = f32[9,96,128]{2,1,0:T(8,128)S(1)} custom-call(f32[3,9,8,128]{3,2,1,0:T(8,128)S(1)} %collective-permute-done.7.first_late_ref, f32[3,9,8,128]{3,2,1,0:T(8,128)S(1)} %collective-permute-done.8.second_late_ref, f32[9,96,128]{2,1,0:T(8,128)S(1)} %get-tuple-element.44.b_right_ref, f32[9,96,128]{2,1,0:T(8,128)S(1)} %get-tuple-element.45.b_down_ref, ...), custom_call_target="tpu_custom_call" | custom-call | flops 100000000 | bytes 10000000 | tf_op jit(solution)/shard_map/pallas_call | solution.py:678
  41.3 0.9 %collective-permute-done.10 = f32[8,128]{1,0:T(8,128)S(1)} collective-permute-done((f32[8,128]{1,0:T(8,128)S(1)}, f32[8,128]{1,0:T(8,128)S(1)}, u32[]{:S(2)}, u32[]{:S(2)}) %collective-permute-start.10) | collective-permute-done | bytes 4128 | tf_op jit(solution)/shard_map/ppermute | solution.py:579
  42.2 2.8 %collective-permute-start.11 = (f32[8,128]{1,0:T(8,128)S(1)}, f32[8,128]{1,0:T(8,128)S(1)}, u32[]{:S(2)}, u32[]{:S(2)}) collective-permute-start(f32[8,128]{1,0:T(8,128)S(1)} %add.14), channel_id=1, source_target_pairs={{0,8},{4,12},{8,0},{12,4},{1,9},{5,13},{9,1},{13,5},{2,10},{6,14},... | collective-permute-start | bytes 12296 | tf_op jit(solution)/shard_map/ppermute | solution.py:579
  45.0 1.4 %shard_map.83.refs_2_ = f32[9,96,128]{2,1,0:T(8,128)S(1)} custom-call(f32[3,9,8,128]{3,2,1,0:T(8,128)S(1)} %collective-permute-done.7.first_late_ref, f32[3,9,8,128]{3,2,1,0:T(8,128)S(1)} %collective-permute-done.8.second_late_ref, f32[9,96,128]{2,1,0:T(8,128)S(1)} %get-tuple-element.44.b_right_ref, f32[9,96,128]{2,1,0:T(8,128)S(1)} %get-tuple-element.45.b_down_ref, ...), custom_call_target="tpu_custom_call" | custom-call | flops 100000000 | bytes 10000000 | tf_op jit(solution)/shard_map/pallas_call | solution.py:678
  46.5 0.2 collective-permute-done.11
  46.7 3.0 %shard_map.84 = (f32[3,64,1024]{2,1,0:T(8,128)}, f32[3,64,1024]{2,1,0:T(8,128)}, f32[3,64,1024]{2,1,0:T(8,128)}) custom-call(f32[8,128]{1,0:T(8,128)S(1)} %add.15.sums_ref, f32[9,96,128]{2,1,0:T(8,128)S(1)} %get-tuple-element.50.scale_ref, f32[9,96,128]{2,1,0:T(8,128)S(1)} %get-tuple-element.51.root_ref, f32[3,9,96,128]{3,2,1,0:T(8,128)S(1)} %get-tuple-element.52.g0_ref, ...), custom_call_target="tpu_custom_call" | custom-call | tf_op jit(solution)/shard_map/pallas_call | solution.py:690
  (5 shorter events, 0.0 us)
Async XLA Ops:
  2.3 12.6 %collective-permute-start.2 = (f32[6,8,16,128]{3,2,1,0:T(8,128)S(1)}, f32[6,8,16,128]{3,2,1,0:T(8,128)S(1)}, u32[]{:S(2)}, u32[]{:S(2)}) collective-permute-start(f32[6,8,16,128]{3,2,1,0:T(8,128)S(1)} %get-tuple-element.37), channel_id=1, source_target_pairs={{0,4},{8,12},{4,0},{12,8},{1,5},{9,13},{5,1},{13,9},{2,6},{10,14},... | collective-permute-start | bytes 1179656 | tf_op jit(solution)/shard_map/ppermute | solution.py:630
  5.4 9.5 %collective-permute-start.3 = (f32[6,8,16,128]{3,2,1,0:T(8,128)S(1)}, f32[6,8,16,128]{3,2,1,0:T(8,128)S(1)}, u32[]{:S(2)}, u32[]{:S(2)}) collective-permute-start(f32[6,8,16,128]{3,2,1,0:T(8,128)S(1)} %get-tuple-element.38), channel_id=1, source_target_pairs={{4,8},{8,4},{5,9},{9,5},{6,10},{10,6},{7,11},{11,7},{20,24},{24,20... | collective-permute-start | bytes 1179656 | tf_op jit(solution)/shard_map/ppermute | solution.py:630
  6.0 2.0 %collective-permute-start = (f32[2,64,128]{2,1,0:T(8,128)S(1)}, f32[2,64,128]{2,1,0:T(8,128)S(1)}, u32[]{:S(2)}, u32[]{:S(2)}) collective-permute-start(f32[2,64,128]{2,1,0:T(8,128)S(1)} %get-tuple-element.31), channel_id=1, source_target_pairs={{0,1},{2,3},{1,0},{3,2},{4,5},{6,7},{5,4},{7,6},{8,9},{10,11},{9,8... | collective-permute-start | bytes 196616 | tf_op jit(solution)/shard_map/ppermute | solution.py:630
  6.1 1.9 %collective-permute-start.1 = (f32[2,64,128]{2,1,0:T(8,128)S(1)}, f32[2,64,128]{2,1,0:T(8,128)S(1)}, u32[]{:S(2)}, u32[]{:S(2)}) collective-permute-start(f32[2,64,128]{2,1,0:T(8,128)S(1)} %get-tuple-element.32), channel_id=1, source_target_pairs={{1,2},{2,1},{5,6},{6,5},{9,10},{10,9},{13,14},{14,13},{17,18},{18,... | collective-permute-start | bytes 196616 | tf_op jit(solution)/shard_map/ppermute | solution.py:630
  8.2 6.7 %collective-permute-start.4 = (f32[2,2,16,128]{3,2,1,0:T(8,128)S(1)}, f32[2,2,16,128]{3,2,1,0:T(8,128)S(1)}, u32[]{:S(2)}, u32[]{:S(2)}) collective-permute-start(f32[2,2,16,128]{3,2,1,0:T(8,128)S(1)} %get-tuple-element.39), channel_id=1, source_target_pairs={{0,4},{8,12},{4,0},{12,8},{1,5},{9,13},{5,1},{13,9},{2,6},{10,14},... | collective-permute-start | bytes 98312 | tf_op jit(solution)/shard_map/ppermute | solution.py:630
  12.6 2.3 %collective-permute-start.5 = (f32[2,2,16,128]{3,2,1,0:T(8,128)S(1)}, f32[2,2,16,128]{3,2,1,0:T(8,128)S(1)}, u32[]{:S(2)}, u32[]{:S(2)}) collective-permute-start(f32[2,2,16,128]{3,2,1,0:T(8,128)S(1)} %get-tuple-element.40), channel_id=1, source_target_pairs={{4,8},{8,4},{5,9},{9,5},{6,10},{10,6},{7,11},{11,7},{20,24},{24,20... | collective-permute-start | bytes 98312 | tf_op jit(solution)/shard_map/ppermute | solution.py:630
  26.4 10.6 %collective-permute-start.7 = (f32[3,9,8,128]{3,2,1,0:T(8,128)S(1)}, f32[3,9,8,128]{3,2,1,0:T(8,128)S(1)}, u32[]{:S(2)}, u32[]{:S(2)}) collective-permute-start(f32[3,9,8,128]{3,2,1,0:T(8,128)S(1)} %get-tuple-element.42), channel_id=1, source_target_pairs={{0,4},{8,12},{4,0},{12,8},{1,5},{9,13},{5,1},{13,9},{2,6},{10,14},... | collective-permute-start | bytes 331784 | tf_op jit(solution)/shard_map/ppermute | solution.py:630
  31.2 5.8 %collective-permute-start.8 = (f32[3,9,8,128]{3,2,1,0:T(8,128)S(1)}, f32[3,9,8,128]{3,2,1,0:T(8,128)S(1)}, u32[]{:S(2)}, u32[]{:S(2)}) collective-permute-start(f32[3,9,8,128]{3,2,1,0:T(8,128)S(1)} %get-tuple-element.43), channel_id=1, source_target_pairs={{4,8},{8,4},{5,9},{9,5},{6,10},{10,6},{7,11},{11,7},{20,24},{24,20... | collective-permute-start | bytes 331784 | tf_op jit(solution)/shard_map/ppermute | solution.py:630
  31.9 2.6 %collective-permute-start.6 = (f32[8,128]{1,0:T(8,128)S(1)}, f32[8,128]{1,0:T(8,128)S(1)}, u32[]{:S(2)}, u32[]{:S(2)}) collective-permute-start(f32[8,128]{1,0:T(8,128)S(1)} %get-tuple-element.41), channel_id=1, source_target_pairs={{0,1},{1,0},{2,3},{3,2},{4,5},{5,4},{6,7},{7,6},{8,9},{9,8},{10,11... | collective-permute-start | bytes 12296 | tf_op jit(solution)/shard_map/ppermute | solution.py:579
  34.5 4.1 %collective-permute-start.9 = (f32[8,128]{1,0:T(8,128)S(1)}, f32[8,128]{1,0:T(8,128)S(1)}, u32[]{:S(2)}, u32[]{:S(2)}) collective-permute-start(f32[8,128]{1,0:T(8,128)S(1)} %add.12), channel_id=1, source_target_pairs={{0,2},{1,3},{2,0},{3,1},{4,6},{5,7},{6,4},{7,5},{8,10},{9,11},{10,... | collective-permute-start | bytes 12296 | tf_op jit(solution)/shard_map/ppermute | solution.py:579
  38.6 3.6 %collective-permute-start.10 = (f32[8,128]{1,0:T(8,128)S(1)}, f32[8,128]{1,0:T(8,128)S(1)}, u32[]{:S(2)}, u32[]{:S(2)}) collective-permute-start(f32[8,128]{1,0:T(8,128)S(1)} %add.13), channel_id=1, source_target_pairs={{0,4},{4,0},{8,12},{12,8},{1,5},{5,1},{9,13},{13,9},{2,6},{6,2},{1... | collective-permute-start | bytes 12296 | tf_op jit(solution)/shard_map/ppermute | solution.py:579
  42.2 4.5 %collective-permute-start.11 = (f32[8,128]{1,0:T(8,128)S(1)}, f32[8,128]{1,0:T(8,128)S(1)}, u32[]{:S(2)}, u32[]{:S(2)}) collective-permute-start(f32[8,128]{1,0:T(8,128)S(1)} %add.14), channel_id=1, source_target_pairs={{0,8},{4,12},{8,0},{12,4},{1,9},{5,13},{9,1},{13,5},{2,10},{6,14},... | collective-permute-start | bytes 12296 | tf_op jit(solution)/shard_map/ppermute | solution.py:579

commit v11 on v10

--- a/solution.py
+++ b/solution.py
@@ -475,6 +475,7 @@
     for k, part in enumerate(parts):
         sums = jnp.where(sub == k, jnp.sum(part), sums)
     sums_ref[...] = sums
+    first_late_ref[chans * tiles] = sums
 
     def edge(c, j, at):
         s, i = divmod(HALO + at, steps)
@@ -483,8 +484,8 @@
     for c in range(chans):
         for j in range(tiles):
             low, high = edge(c, j, 0), edge(c, j, rows - LATE)
-            first_late_ref[c, j] = jnp.where(odd_row, low, high)
-            second_late_ref[c, j] = jnp.where(odd_row, high, low)
+            first_late_ref[c * tiles + j] = jnp.where(odd_row, low, high)
+            second_late_ref[c * tiles + j] = jnp.where(odd_row, high, low)
 
 
 def second_kernel(
@@ -496,7 +497,7 @@
     odd_row = odd("row")
     for j in range(tiles):
         g_ref[j] = g2_ref[c, j]
-        first, second = first_late_ref[c, j], second_late_ref[c, j]
+        first, second = first_late_ref[c * tiles + j], second_late_ref[c * tiles + j]
         for value, at in ((jnp.where(odd_row, first, second), HALO - LATE), (jnp.where(odd_row, second, first), HALO + rows)):
             done = 0
             while done < LATE:
@@ -566,14 +567,7 @@
         copy.wait()
 
 
-def sum_over(value, axes, beside):
-    steps = []
-    for axis in axes:
-        size = lax.axis_size(axis)
-        if size & (size - 1):
-            value = lax.psum(value, axis)
-            continue
-        steps += [(axis, [(i, i ^ (1 << k)) for i in range(size)]) for k in range(size.bit_length() - 1)]
+def sum_over(value, steps, beside):
     done = []
     for k, (axis, pairs) in enumerate(steps):
         other = lax.ppermute(value, axis, pairs)
@@ -586,6 +580,7 @@
 
 def per_device(source, weight, seam_right, seam_down, offsets):
     chans, rows, cols = source.shape
+    row_axis, col_axis = lax.axis_size("row"), lax.axis_size("col")
     in_vmem = pl.BlockSpec(memory_space=pltpu.VMEM)
     in_hbm = pl.BlockSpec(memory_space=pltpu.HBM)
     params = pltpu.CompilerParams(vmem_limit_bytes=VMEM_LIMIT)
@@ -661,10 +656,10 @@
     height = rows + 2 * HALO
     plane = shaped(tiles, height, LANES)
     field = shaped(chans, tiles, height, LANES)
-    late = shaped(chans, tiles, LATE, LANES)
+    lates = [shaped(chans * tiles + extra, LATE, LANES) for extra in (1, 0)]
     *basis, sums, first_late, second_late = pl.pallas_call(
         first_kernel,
-        out_shape=[plane] * 4 + [field] * 5 + [shaped(SUBS, LANES)] + [late] * 2,
+        out_shape=[plane] * 4 + [field] * 5 + [shaped(SUBS, LANES)] + lates,
         in_specs=[in_vmem] * 6,
         out_specs=[in_vmem] * 12,
         scratch_shapes=[scratch(planes, tiles, height, LANES), scratch(*plane.shape)],
@@ -686,7 +681,17 @@
         )(first_late, second_late, b_right, b_down, g2)
         for c in range(chans)
     ]
-    total, f2 = sum_over(sums, ("col", "row"), f2)
+    if row_axis & (row_axis - 1) or col_axis & (col_axis - 1):
+        total = lax.psum(sums, ("row", "col"))
+    else:
+        steps = [
+            (axis, [(i, i ^ (1 << k)) for i in range(size)])
+            for axis, size, low in (("row", row_axis, 1), ("col", col_axis, 0))
+            for k in range(low, size.bit_length() - 1)
+        ]
+        if row_axis > 1:
+            sums = sums + first_late[chans * tiles]
+        total, f2 = sum_over(sums, steps, f2)
     return pl.pallas_call(
         third_kernel,
         out_shape=[shaped(chans, rows, cols)] * 3,

time: 50.1 us -> 46.9 us (0.936)
  Pallas kernels: 22.6 us -> 20.5 us
  starting transfers between devices: 23.4 us -> 21.9 us
  waiting for transfers between devices: 2.9 us -> 3.52 us
    ppermute x8, waiting for transfers between devices: 0.86 us -> 2.97 us  [swap(): lax.ppermute(value, axis, some)]
    ppermute x4 -> x3, waiting for transfers between devices: 2.04 us -> 0.56 us  [sum_over(): other = lax.ppermute(value, axis, pairs)]
    ppermute x4 -> x3, starting transfers between devices: 8.4 us -> 6.93 us  [sum_over(): other = lax.ppermute(value, axis, pairs)]
    pallas_call x1, Pallas kernels: 11.5 us -> 10.1 us  [per_device(): pl.pallas_call(first_kernel, out_shape=[plane] * 4 + [field] * 5 + [shape...]
  transfers between devices with their start and end apart: 12 -> 11, of which waited for: 5 -> 4; matrix products, arithmetic and copies ran while one was open for 0% -> 0% of each run, Pallas kernels for 13% -> 13%
where the time goes in v11:
time: 46.9 us; the launch traced here: 46.7 us
  starting transfers between devices  21.9 us (47%)
  Pallas kernels  20.5 us (44%)
  waiting for transfers between devices  3.52 us (8%)
  between operations  0.76 us (2%)
    ppermute x8, starting transfers between devices, swap(): lax.ppermute(value, axis, some)  15 us
    pallas_call x1, Pallas kernels, per_device(): pl.pallas_call(first_kernel, out_shape=[plane] * 4 + [field] * 5 + [shape...  10.1 us
    ppermute x3, starting transfers between devices, sum_over(): other = lax.ppermute(value, axis, pairs)  6.93 us
    pallas_call x3, Pallas kernels, per_device(): pl.pallas_call(functools.partial(second_kernel, c), out_shape=plane, in_s...  3.86 us
    ppermute x8, waiting for transfers between devices, swap(): lax.ppermute(value, axis, some)  2.97 us
    pallas_call x1, Pallas kernels, per_device(): pl.pallas_call(third_kernel, out_shape=[shaped(chans, rows, cols)] * 3, i...  2.72 us
    pallas_call x1, Pallas kernels, per_device(): pl.pallas_call(own_kernel, out_shape=[shaped(planes, own_tiles, rows, LAN...  1.63 us
    pallas_call x1, Pallas kernels, per_device(): pl.pallas_call(inner_dealt_kernel, out_shape=shaped(planes, tiles - ways,...  1.25 us
  transfers between devices with their start and end apart: 11, of which 4 were waited for; matrix products, arithmetic and copies ran while one was open for 0% of the time, Pallas kernels for 13%

profile of v11, /device:TPU:0, one launch (start us, length us, event | category | flops | bytes accessed | tf_op | source)
XLA Modules:
  0.0 46.7 jit_solution(16181953798601896999)
XLA Ops:
  0.6 1.6 %shard_map.76 = (f32[6,8,64,128]{3,2,1,0:T(8,128)S(1)}, f32[6,8,16,128]{3,2,1,0:T(8,128)S(1)}, f32[6,8,16,128]{3,2,1,0:T(8,128)S(1)}, f32[2,64,128]{2,1,0:T(8,128)S(1)}, f32[2,64,128]{2,1,0:T(8,128)S(1)}) custom-call(s32[3,1,16]{2,1,0:T(1,128)} %bitcast.5, f32[3,64,1024]{2,1,0:T(8,128)} %src_hbm.1, f32[64,1024]{1,0:T(8,128)} %weight_hbm.1, ...), custom_call_target="tpu_custom_call" | custom-call | tf_op jit(solution)/shard_map/pallas_call | solution.py:598
  2.3 3.1 %collective-permute-start.2 = (f32[6,8,16,128]{3,2,1,0:T(8,128)S(1)}, f32[6,8,16,128]{3,2,1,0:T(8,128)S(1)}, u32[]{:S(2)}, u32[]{:S(2)}) collective-permute-start(f32[6,8,16,128]{3,2,1,0:T(8,128)S(1)} %get-tuple-element.37), channel_id=1, source_target_pairs={{0,4},{8,12},{4,0},{12,8},{1,5},{9,13},{5,1},{13,9},{2,6},{10,14},... | collective-permute-start | bytes 1179656 | tf_op jit(solution)/shard_map/ppermute | solution.py:625
  5.4 0.7 %collective-permute-start.3 = (f32[6,8,16,128]{3,2,1,0:T(8,128)S(1)}, f32[6,8,16,128]{3,2,1,0:T(8,128)S(1)}, u32[]{:S(2)}, u32[]{:S(2)}) collective-permute-start(f32[6,8,16,128]{3,2,1,0:T(8,128)S(1)} %get-tuple-element.38), channel_id=1, source_target_pairs={{4,8},{8,4},{5,9},{9,5},{6,10},{10,6},{7,11},{11,7},{20,24},{24,20... | collective-permute-start | bytes 1179656 | tf_op jit(solution)/shard_map/ppermute | solution.py:625
  6.0 0.1 collective-permute-start
  6.1 0.7 %collective-permute-start.1 = (f32[2,64,128]{2,1,0:T(8,128)S(1)}, f32[2,64,128]{2,1,0:T(8,128)S(1)}, u32[]{:S(2)}, u32[]{:S(2)}) collective-permute-start(f32[2,64,128]{2,1,0:T(8,128)S(1)} %get-tuple-element.32), channel_id=1, source_target_pairs={{1,2},{2,1},{5,6},{6,5},{9,10},{10,9},{13,14},{14,13},{17,18},{18,... | collective-permute-start | bytes 196616 | tf_op jit(solution)/shard_map/ppermute | solution.py:625
  6.8 1.2 %shard_map.77.inner_ref = f32[6,6,64,128]{3,2,1,0:T(8,128)S(1)} custom-call(f32[6,8,64,128]{3,2,1,0:T(8,128)S(1)} %get-tuple-element.33.own_ref), custom_call_target="tpu_custom_call" | custom-call | flops 100000000 | bytes 4000000 | tf_op jit(solution)/shard_map/pallas_call | solution.py:628
  8.1 0.0 collective-permute-done.first_ref
  8.1 0.0 collective-permute-done.1.second_ref
  8.1 0.1 shard_map.79
  8.2 4.4 %collective-permute-start.4 = (f32[2,2,16,128]{3,2,1,0:T(8,128)S(1)}, f32[2,2,16,128]{3,2,1,0:T(8,128)S(1)}, u32[]{:S(2)}, u32[]{:S(2)}) collective-permute-start(f32[2,2,16,128]{3,2,1,0:T(8,128)S(1)} %get-tuple-element.39), channel_id=1, source_target_pairs={{0,4},{8,12},{4,0},{12,8},{1,5},{9,13},{5,1},{13,9},{2,6},{10,14},... | collective-permute-start | bytes 98312 | tf_op jit(solution)/shard_map/ppermute | solution.py:625
  12.6 0.7 %collective-permute-start.5 = (f32[2,2,16,128]{3,2,1,0:T(8,128)S(1)}, f32[2,2,16,128]{3,2,1,0:T(8,128)S(1)}, u32[]{:S(2)}, u32[]{:S(2)}) collective-permute-start(f32[2,2,16,128]{3,2,1,0:T(8,128)S(1)} %get-tuple-element.40), channel_id=1, source_target_pairs={{4,8},{8,4},{5,9},{9,5},{6,10},{10,6},{7,11},{11,7},{20,24},{24,20... | collective-permute-start | bytes 98312 | tf_op jit(solution)/shard_map/ppermute | solution.py:625
  13.2 0.8 %shard_map.78.outer_ref = f32[6,3,64,128]{3,2,1,0:T(8,128)S(1)} custom-call(f32[6,8,64,128]{3,2,1,0:T(8,128)S(1)} %get-tuple-element.33.own_ref, f32[2,64,128]{2,1,0:T(8,128)S(1)} %collective-permute-done.first_ref, f32[2,64,128]{2,1,0:T(8,128)S(1)} %collective-permute-done.1.second_ref), custom_call_target="tpu_custom_call" | custom-call | flops 100000000 | bytes 2000000 | tf_op jit(solution)/shard_map/pallas_call | solution.py:647
  14.0 0.8 %collective-permute-done.4.first_corners_ref = f32[2,2,16,128]{3,2,1,0:T(8,128)S(1)} collective-permute-done((f32[2,2,16,128]{3,2,1,0:T(8,128)S(1)}, f32[2,2,16,128]{3,2,1,0:T(8,128)S(1)}, u32[]{:S(2)}, u32[]{:S(2)}) %collective-permute-start.4) | collective-permute-done | bytes 32800 | tf_op jit(solution)/shard_map/ppermute | solution.py:625
  14.8 0.0 collective-permute-done.5.second_corners_ref
  14.8 0.0 collective-permute-done.2.first_rows_ref
  14.8 0.0 collective-permute-done.3.second_rows_ref
  14.8 10.1 %shard_map.80 = (f32[9,96,128]{2,1,0:T(8,128)S(1)}, f32[9,96,128]{2,1,0:T(8,128)S(1)}, f32[9,96,128]{2,1,0:T(8,128)S(1)}, f32[9,96,128]{2,1,0:T(8,128)S(1)}, f32...) custom-call(f32[6,6,64,128]{3,2,1,0:T(8,128)S(1)} %shard_map.77.inne, ...), custom_call_target="tpu_custom_call" | custom-call | tf_op jit(solution)/shard_map/pallas_call | solution.py:660
  25.0 4.8 %collective-permute-start.6 = (f32[28,8,128]{2,1,0:T(8,128)S(1)}, f32[28,8,128]{2,1,0:T(8,128)S(1)}, u32[]{:S(2)}, u32[]{:S(2)}) collective-permute-start(f32[28,8,128]{2,1,0:T(8,128)S(1)} %get-tuple-element.42), channel_id=1, source_target_pairs={{0,4},{8,12},{4,0},{12,8},{1,5},{9,13},{5,1},{13,9},{2,6},{10,14},... | collective-permute-start | bytes 344072 | tf_op jit(solution)/shard_map/ppermute | solution.py:625
  29.8 0.7 %collective-permute-start.7 = (f32[27,8,128]{2,1,0:T(8,128)S(1)}, f32[27,8,128]{2,1,0:T(8,128)S(1)}, u32[]{:S(2)}, u32[]{:S(2)}) collective-permute-start(f32[27,8,128]{2,1,0:T(8,128)S(1)} %get-tuple-element.43), channel_id=1, source_target_pairs={{4,8},{8,4},{5,9},{9,5},{6,10},{10,6},{7,11},{11,7},{20,24},{24,20... | collective-permute-start | bytes 331784 | tf_op jit(solution)/shard_map/ppermute | solution.py:625
  30.5 2.1 %collective-permute-done.6.first_late_ref = f32[28,8,128]{2,1,0:T(8,128)S(1)} collective-permute-done((f32[28,8,128]{2,1,0:T(8,128)S(1)}, f32[28,8,128]{2,1,0:T(8,128)S(1)}, u32[]{:S(2)}, u32[]{:S(2)}) %collective-permute-start.6) | collective-permute-done | bytes 114720 | tf_op jit(solution)/shard_map/ppermute | solution.py:625
  32.6 4.0 %collective-permute-start.8 = (f32[8,128]{1,0:T(8,128)S(1)}, f32[8,128]{1,0:T(8,128)S(1)}, u32[]{:S(2)}, u32[]{:S(2)}) collective-permute-start(f32[8,128]{1,0:T(8,128)S(1)} %fusion), channel_id=1, source_target_pairs={{0,8},{4,12},{8,0},{12,4},{1,9},{5,13},{9,1},{13,5},{2,10},{6,14},... | collective-permute-start | bytes 12296 | tf_op jit(solution)/shard_map/ppermute | solution.py:573
  36.6 0.0 collective-permute-done.7.second_late_ref
  36.6 1.3 %shard_map.81.refs_0_ = f32[9,96,128]{2,1,0:T(8,128)S(1)} custom-call(f32[28,8,128]{2,1,0:T(8,128)S(1)} %collective-permute-done.6.first_late_ref, f32[27,8,128]{2,1,0:T(8,128)S(1)} %collective-permute-done.7.second_late_ref, f32[9,96,128]{2,1,0:T(8,128)S(1)} %get-tuple-element.44.b_right_ref, f32[9,96,128]{2,1,0:T(8,128)S(1)} %get-tuple-element.45.b_down_ref, ...), custom_call_target="tpu_custom_call" | custom-call | flops 100000000 | bytes 10000000 | tf_op jit(solution)/shard_map/pallas_call | solution.py:673
  38.0 0.2 collective-permute-done.8
  38.2 0.0 collective-permute-start.9
  38.2 1.3 %shard_map.82.refs_1_ = f32[9,96,128]{2,1,0:T(8,128)S(1)} custom-call(f32[28,8,128]{2,1,0:T(8,128)S(1)} %collective-permute-done.6.first_late_ref, f32[27,8,128]{2,1,0:T(8,128)S(1)} %collective-permute-done.7.second_late_ref, f32[9,96,128]{2,1,0:T(8,128)S(1)} %get-tuple-element.44.b_right_ref, f32[9,96,128]{2,1,0:T(8,128)S(1)} %get-tuple-element.45.b_down_ref, ...), custom_call_target="tpu_custom_call" | custom-call | flops 100000000 | bytes 10000000 | tf_op jit(solution)/shard_map/pallas_call | solution.py:673
  39.5 0.0 collective-permute-done.9
  39.5 2.9 %collective-permute-start.10 = (f32[8,128]{1,0:T(8,128)S(1)}, f32[8,128]{1,0:T(8,128)S(1)}, u32[]{:S(2)}, u32[]{:S(2)}) collective-permute-start(f32[8,128]{1,0:T(8,128)S(1)} %add.14), channel_id=1, source_target_pairs={{0,2},{1,3},{2,0},{3,1},{4,6},{5,7},{6,4},{7,5},{8,10},{9,11},{10,... | collective-permute-start | bytes 12296 | tf_op jit(solution)/shard_map/ppermute | solution.py:573
  42.4 1.3 %shard_map.83.refs_2_ = f32[9,96,128]{2,1,0:T(8,128)S(1)} custom-call(f32[28,8,128]{2,1,0:T(8,128)S(1)} %collective-permute-done.6.first_late_ref, f32[27,8,128]{2,1,0:T(8,128)S(1)} %collective-permute-done.7.second_late_ref, f32[9,96,128]{2,1,0:T(8,128)S(1)} %get-tuple-element.44.b_right_ref, f32[9,96,128]{2,1,0:T(8,128)S(1)} %get-tuple-element.45.b_down_ref, ...), custom_call_target="tpu_custom_call" | custom-call | flops 100000000 | bytes 10000000 | tf_op jit(solution)/shard_map/pallas_call | solution.py:673
  43.6 0.3 collective-permute-done.10
  44.0 2.7 %shard_map.84 = (f32[3,64,1024]{2,1,0:T(8,128)}, f32[3,64,1024]{2,1,0:T(8,128)}, f32[3,64,1024]{2,1,0:T(8,128)}) custom-call(f32[8,128]{1,0:T(8,128)S(1)} %add.15.sums_ref, f32[9,96,128]{2,1,0:T(8,128)S(1)} %get-tuple-element.50.scale_ref, f32[9,96,128]{2,1,0:T(8,128)S(1)} %get-tuple-element.51.root_ref, f32[3,9,96,128]{3,2,1,0:T(8,128)S(1)} %get-tuple-element.52.g0_ref, ...), custom_call_target="tpu_custom_call" | custom-call | tf_op jit(solution)/shard_map/pallas_call | solution.py:695
  (4 shorter events, 0.0 us)
Async XLA Ops:
  2.3 12.6 %collective-permute-start.2 = (f32[6,8,16,128]{3,2,1,0:T(8,128)S(1)}, f32[6,8,16,128]{3,2,1,0:T(8,128)S(1)}, u32[]{:S(2)}, u32[]{:S(2)}) collective-permute-start(f32[6,8,16,128]{3,2,1,0:T(8,128)S(1)} %get-tuple-element.37), channel_id=1, source_target_pairs={{0,4},{8,12},{4,0},{12,8},{1,5},{9,13},{5,1},{13,9},{2,6},{10,14},... | collective-permute-start | bytes 1179656 | tf_op jit(solution)/shard_map/ppermute | solution.py:625
  5.4 9.5 %collective-permute-start.3 = (f32[6,8,16,128]{3,2,1,0:T(8,128)S(1)}, f32[6,8,16,128]{3,2,1,0:T(8,128)S(1)}, u32[]{:S(2)}, u32[]{:S(2)}) collective-permute-start(f32[6,8,16,128]{3,2,1,0:T(8,128)S(1)} %get-tuple-element.38), channel_id=1, source_target_pairs={{4,8},{8,4},{5,9},{9,5},{6,10},{10,6},{7,11},{11,7},{20,24},{24,20... | collective-permute-start | bytes 1179656 | tf_op jit(solution)/shard_map/ppermute | solution.py:625
  6.0 2.0 %collective-permute-start = (f32[2,64,128]{2,1,0:T(8,128)S(1)}, f32[2,64,128]{2,1,0:T(8,128)S(1)}, u32[]{:S(2)}, u32[]{:S(2)}) collective-permute-start(f32[2,64,128]{2,1,0:T(8,128)S(1)} %get-tuple-element.31), channel_id=1, source_target_pairs={{0,1},{2,3},{1,0},{3,2},{4,5},{6,7},{5,4},{7,6},{8,9},{10,11},{9,8... | collective-permute-start | bytes 196616 | tf_op jit(solution)/shard_map/ppermute | solution.py:625
  6.1 1.9 %collective-permute-start.1 = (f32[2,64,128]{2,1,0:T(8,128)S(1)}, f32[2,64,128]{2,1,0:T(8,128)S(1)}, u32[]{:S(2)}, u32[]{:S(2)}) collective-permute-start(f32[2,64,128]{2,1,0:T(8,128)S(1)} %get-tuple-element.32), channel_id=1, source_target_pairs={{1,2},{2,1},{5,6},{6,5},{9,10},{10,9},{13,14},{14,13},{17,18},{18,... | collective-permute-start | bytes 196616 | tf_op jit(solution)/shard_map/ppermute | solution.py:625
  8.2 6.7 %collective-permute-start.4 = (f32[2,2,16,128]{3,2,1,0:T(8,128)S(1)}, f32[2,2,16,128]{3,2,1,0:T(8,128)S(1)}, u32[]{:S(2)}, u32[]{:S(2)}) collective-permute-start(f32[2,2,16,128]{3,2,1,0:T(8,128)S(1)} %get-tuple-element.39), channel_id=1, source_target_pairs={{0,4},{8,12},{4,0},{12,8},{1,5},{9,13},{5,1},{13,9},{2,6},{10,14},... | collective-permute-start | bytes 98312 | tf_op jit(solution)/shard_map/ppermute | solution.py:625
  12.6 2.3 %collective-permute-start.5 = (f32[2,2,16,128]{3,2,1,0:T(8,128)S(1)}, f32[2,2,16,128]{3,2,1,0:T(8,128)S(1)}, u32[]{:S(2)}, u32[]{:S(2)}) collective-permute-start(f32[2,2,16,128]{3,2,1,0:T(8,128)S(1)} %get-tuple-element.40), channel_id=1, source_target_pairs={{4,8},{8,4},{5,9},{9,5},{6,10},{10,6},{7,11},{11,7},{20,24},{24,20... | collective-permute-start | bytes 98312 | tf_op jit(solution)/shard_map/ppermute | solution.py:625
  25.0 7.6 %collective-permute-start.6 = (f32[28,8,128]{2,1,0:T(8,128)S(1)}, f32[28,8,128]{2,1,0:T(8,128)S(1)}, u32[]{:S(2)}, u32[]{:S(2)}) collective-permute-start(f32[28,8,128]{2,1,0:T(8,128)S(1)} %get-tuple-element.42), channel_id=1, source_target_pairs={{0,4},{8,12},{4,0},{12,8},{1,5},{9,13},{5,1},{13,9},{2,6},{10,14},... | collective-permute-start | bytes 344072 | tf_op jit(solution)/shard_map/ppermute | solution.py:625
  29.8 6.8 %collective-permute-start.7 = (f32[27,8,128]{2,1,0:T(8,128)S(1)}, f32[27,8,128]{2,1,0:T(8,128)S(1)}, u32[]{:S(2)}, u32[]{:S(2)}) collective-permute-start(f32[27,8,128]{2,1,0:T(8,128)S(1)} %get-tuple-element.43), channel_id=1, source_target_pairs={{4,8},{8,4},{5,9},{9,5},{6,10},{10,6},{7,11},{11,7},{20,24},{24,20... | collective-permute-start | bytes 331784 | tf_op jit(solution)/shard_map/ppermute | solution.py:625
  32.6 5.6 %collective-permute-start.8 = (f32[8,128]{1,0:T(8,128)S(1)}, f32[8,128]{1,0:T(8,128)S(1)}, u32[]{:S(2)}, u32[]{:S(2)}) collective-permute-start(f32[8,128]{1,0:T(8,128)S(1)} %fusion), channel_id=1, source_target_pairs={{0,8},{4,12},{8,0},{12,4},{1,9},{5,13},{9,1},{13,5},{2,10},{6,14},... | collective-permute-start | bytes 12296 | tf_op jit(solution)/shard_map/ppermute | solution.py:573
  38.2 1.3 %collective-permute-start.9 = (f32[8,128]{1,0:T(8,128)S(1)}, f32[8,128]{1,0:T(8,128)S(1)}, u32[]{:S(2)}, u32[]{:S(2)}) collective-permute-start(f32[8,128]{1,0:T(8,128)S(1)} %add.13), channel_id=1, source_target_pairs={{0,1},{1,0},{2,3},{3,2},{4,5},{5,4},{6,7},{7,6},{8,9},{9,8},{10,11... | collective-permute-start | bytes 12296 | tf_op jit(solution)/shard_map/ppermute | solution.py:573
  39.5 4.5 %collective-permute-start.10 = (f32[8,128]{1,0:T(8,128)S(1)}, f32[8,128]{1,0:T(8,128)S(1)}, u32[]{:S(2)}, u32[]{:S(2)}) collective-permute-start(f32[8,128]{1,0:T(8,128)S(1)} %add.14), channel_id=1, source_target_pairs={{0,2},{1,3},{2,0},{3,1},{4,6},{5,7},{6,4},{7,5},{8,10},{9,11},{10,... | collective-permute-start | bytes 12296 | tf_op jit(solution)/shard_map/ppermute | solution.py:573

commit v12 on v11

--- a/solution.py
+++ b/solution.py
@@ -386,7 +386,7 @@
 
 
 def first_kernel(
-    inner_ref, outer_ref, first_rows_ref, second_rows_ref, first_corners_ref, second_corners_ref,
+    inner_ref, outer_ref, second_rows_ref, first_rows_ref, second_corners_ref, first_corners_ref,
     b_right_ref, b_down_ref, scale_ref, root_ref, g0_ref, z0_ref, g1_ref, f1_ref, g2_ref, sums_ref,
     first_late_ref, second_late_ref,
     natural, work_ref,
@@ -475,7 +475,6 @@
     for k, part in enumerate(parts):
         sums = jnp.where(sub == k, jnp.sum(part), sums)
     sums_ref[...] = sums
-    first_late_ref[chans * tiles] = sums
 
     def edge(c, j, at):
         s, i = divmod(HALO + at, steps)
@@ -539,43 +538,49 @@
     matrix = undealing(ways) if ways > 1 else None
     outs = (solution_hbm, residual_hbm, smoothed_hbm)
     copies = []
-    for c, f2_ref in enumerate(f2_refs):
-        for j in range(tiles):
-            for i in range(steps):
-                at = pl.ds(i * SUBS, SUBS)
-                scale = scale_ref[j, at, :]
-                root = root_ref[j, at, :]
-                g0, g1, g2, z0, f1 = [ref[c, j, at, :] for ref in (g0_ref, g1_ref, g2_ref, z0_ref, f1_ref)]
-                f2 = f2_ref[j, at, :]
-                there = pl.ds(i, SUBS, stride=steps)
-                natural[c, 0, j, there, :] = scale * (x0 * z0 + x1 * f1)
-                natural[c, 1, j, there, :] = root * (r0 * g0 + r1 * g1 + r2 * g2)
-                natural[c, 2, j, there, :] = scale * (r0 * z0 + r1 * f1 + r2 * f2)
-        for g in range(0, own_tiles, ways):
-            value = jnp.concatenate(
-                [natural[c, :, g + m, HALO:HALO + rows, :].reshape(3 * rows, LANES) for m in range(ways)], axis=1
-            )
-            width = min(ways, own_tiles - g) * LANES
-            if ways > 1:
-                value = permuted(value, matrix[:, :width], 2)
-            for k in range(len(outs)):
-                done[c, k, :, g * LANES:g * LANES + width] = value[k * rows:(k + 1) * rows]
-        for k, ref in enumerate(outs):
-            copies.append(pltpu.make_async_copy(done.at[c, k], ref.at[c], sems.at[c, k]))
-            copies[-1].start()
+    chans = len(f2_refs)
+    for g in range(0, own_tiles, ways):
+        width = min(ways, own_tiles - g) * LANES
+        for c, f2_ref in enumerate(f2_refs):
+            for j in range(g, g + ways):
+                for i in range(steps):
+                    at = pl.ds(i * SUBS, SUBS)
+                    scale = scale_ref[j, at, :]
+                    root = root_ref[j, at, :]
+                    g0, g1, g2, z0, f1 = [ref[c, j, at, :] for ref in (g0_ref, g1_ref, g2_ref, z0_ref, f1_ref)]
+                    f2 = f2_ref[j, at, :]
+                    there = pl.ds(i, SUBS, stride=steps)
+                    natural[c, 0, j, there, :] = scale * (x0 * z0 + x1 * f1)
+                    natural[c, 1, j, there, :] = root * (r0 * g0 + r1 * g1 + r2 * g2)
+                    natural[c, 2, j, there, :] = scale * (r0 * z0 + r1 * f1 + r2 * f2)
+        value = jnp.concatenate(
+            [natural[:, :, g + m, HALO:HALO + rows, :].reshape(3 * chans * rows, LANES) for m in range(ways)], axis=1
+        )
+        if ways > 1:
+            value = permuted(value, matrix[:, :width], 2)
+        columns = pl.ds(g * LANES, width)
+        for c in range(chans):
+            for k, ref in enumerate(outs):
+                at = (c * 3 + k) * rows
+                done[c, k, :, columns] = value[at:at + rows]
+                copy = pltpu.make_async_copy(
+                    done.at[c, k, :, columns], ref.at[c, :, columns], sems.at[g // ways, c * 3 + k]
+                )
+                copy.start()
+                copies.append(copy)
     for copy in copies:
         copy.wait()
 
 
-def sum_over(value, steps, beside):
+def sum_over(value, steps):
     done = []
-    for k, (axis, pairs) in enumerate(steps):
+    for axis, pairs, beside in steps:
         other = lax.ppermute(value, axis, pairs)
-        if len(steps) - k <= len(beside):
-            value, array = lax.optimization_barrier((value, beside[len(done)]))
-            done.append(array)
+        if beside:
+            value, *arrays = lax.optimization_barrier((value, *beside))
+            done += arrays
         value = value + other
-    return value, done + list(beside[len(done):])
+    return value, done
 
 
 def per_device(source, weight, seam_right, seam_down, offsets):
@@ -618,11 +623,12 @@
         ],
     )
 
-    def swap(first, second, axis):
+    def swap(first, second, axis, order):
         size = lax.axis_size(axis)
         pairs = [[(i, i + 1) for i in range(start, size - 1, 2)] for start in range(2)]
         pairs = [some + [(j, i) for i, j in some] for some in pairs]
-        return [lax.ppermute(value, axis, some) for value, some in zip((first, second), pairs)]
+        received = {k: lax.ppermute((first, second)[k], axis, pairs[k]) for k in order}
+        return received[0], received[1]
 
     ways = ways_of(tiles)
     inner = pl.pallas_call(
@@ -633,8 +639,8 @@
         compiler_params=params,
         cost_estimate=pl.CostEstimate(flops=10**8, bytes_accessed=4 * 10**6, transcendentals=0),
     )(own)
-    first_rows, second_rows = swap(first_rows, second_rows, "row")
-    first_cols, second_cols = swap(first_cols, second_cols, "col")
+    first_rows, second_rows = swap(first_rows, second_rows, "row", (1, 0))
+    first_cols, second_cols = swap(first_cols, second_cols, "col", (0, 1))
     first_cols, second_cols, inner = lax.optimization_barrier((first_cols, second_cols, inner))
     corners = pl.pallas_call(
         functools.partial(corners_kernel, chans),
@@ -643,7 +649,7 @@
         out_specs=[in_vmem] * 2,
         compiler_params=params,
     )(first_cols, second_cols)
-    first_corners, second_corners = swap(*corners, "row")
+    first_corners, second_corners = swap(*corners, "row", (1, 0))
     outer = pl.pallas_call(
         outer_dealt_kernel,
         out_shape=shaped(planes, ways, rows, LANES),
@@ -656,17 +662,17 @@
     height = rows + 2 * HALO
     plane = shaped(tiles, height, LANES)
     field = shaped(chans, tiles, height, LANES)
-    lates = [shaped(chans * tiles + extra, LATE, LANES) for extra in (1, 0)]
+    late = shaped(chans * tiles, LATE, LANES)
     *basis, sums, first_late, second_late = pl.pallas_call(
         first_kernel,
-        out_shape=[plane] * 4 + [field] * 5 + [shaped(SUBS, LANES)] + lates,
+        out_shape=[plane] * 4 + [field] * 5 + [shaped(SUBS, LANES)] + [late] * 2,
         in_specs=[in_vmem] * 6,
         out_specs=[in_vmem] * 12,
         scratch_shapes=[scratch(planes, tiles, height, LANES), scratch(*plane.shape)],
         compiler_params=params,
-    )(inner, outer, first_rows, second_rows, first_corners, second_corners)
-
-    first_late, second_late = swap(first_late, second_late, "row")
+    )(inner, outer, second_rows, first_rows, second_corners, first_corners)
+
+    first_late, second_late = swap(first_late, second_late, "row", (0, 1))
 
     b_right, b_down, scale, root, g0, z0, g1, f1, g2 = basis
     f2 = [
@@ -685,13 +691,15 @@
         total = lax.psum(sums, ("row", "col"))
     else:
         steps = [
-            (axis, [(i, i ^ (1 << k)) for i in range(size)])
-            for axis, size, low in (("row", row_axis, 1), ("col", col_axis, 0))
-            for k in range(low, size.bit_length() - 1)
+            [axis, [(i, i ^ (1 << k)) for i in range(size)], []]
+            for axis, size in (("col", col_axis), ("row", row_axis))
+            for k in range(size.bit_length() - 1)
         ]
-        if row_axis > 1:
-            sums = sums + first_late[chans * tiles]
-        total, f2 = sum_over(sums, steps, f2)
+        if len(steps) > 1:
+            steps[-2][2], steps[-1][2] = f2[:1], f2[1:]
+            total, f2 = sum_over(sums, steps)
+        else:
+            total, _ = sum_over(sums, steps)
     return pl.pallas_call(
         third_kernel,
         out_shape=[shaped(chans, rows, cols)] * 3,
@@ -700,7 +708,7 @@
         scratch_shapes=[
             scratch(chans, 3, tiles, height, LANES),
             scratch(chans, 3, rows, cols),
-            pltpu.SemaphoreType.DMA((chans, 3)),
+            pltpu.SemaphoreType.DMA((-(-own_tiles // ways), chans * 3)),
         ],
         compiler_params=params,
     )(total, scale, root, g0, z0, g1, f1, g2, *f2)

time: 46.9 us -> 50.6 us (1.079)
  waiting for transfers between devices: 3.52 us -> 6.48 us
  Pallas kernels: 20.5 us -> 23 us
  starting transfers between devices: 21.9 us -> 20.1 us
    ppermute x8, starting transfers between devices: 15 us -> 12.2 us  [swap(): lax.ppermute((first, second)[k], axis, pairs[k])]
    ppermute x3 -> x4, waiting for transfers between devices: 0.56 us -> 2.61 us  [sum_over(): other = lax.ppermute(value, axis, pairs)]
    pallas_call x1, Pallas kernels: 10.1 us -> 11.5 us  [per_device(): pl.pallas_call(first_kernel, out_shape=[plane] * 4 + [field] * 5 + [shape...]
    ppermute x3 -> x4, starting transfers between devices: 6.93 us -> 7.91 us  [sum_over(): other = lax.ppermute(value, axis, pairs)]
    ppermute x8, waiting for transfers between devices: 2.97 us -> 3.87 us  [swap(): lax.ppermute((first, second)[k], axis, pairs[k])]
    pallas_call x1, Pallas kernels: 2.72 us -> 3.39 us  [per_device(): pl.pallas_call(third_kernel, out_shape=[shaped(chans, rows, cols)] * 3, i...]
  transfers between devices with their start and end apart: 11 -> 12, of which waited for: 4 -> 4; matrix products, arithmetic and copies ran while one was open for 0% -> 0% of each run, Pallas kernels for 13% -> 13%
where the time goes in v12:
time: 50.6 us; the launch traced here: 50.4 us
  Pallas kernels  23 us (45%)
  starting transfers between devices  20.1 us (40%)
  waiting for transfers between devices  6.48 us (13%)
  between operations  0.76 us (2%)
    ppermute x8, starting transfers between devices, swap(): lax.ppermute((first, second)[k], axis, pairs[k])  12.2 us
    pallas_call x1, Pallas kernels, per_device(): pl.pallas_call(first_kernel, out_shape=[plane] * 4 + [field] * 5 + [shape...  11.5 us
    ppermute x4, starting transfers between devices, sum_over(): other = lax.ppermute(value, axis, pairs)  7.91 us
    pallas_call x3, Pallas kernels, per_device(): pl.pallas_call(functools.partial(second_kernel, c), out_shape=plane, in_s...  4.36 us
    ppermute x8, waiting for transfers between devices, swap(): lax.ppermute((first, second)[k], axis, pairs[k])  3.87 us
    pallas_call x1, Pallas kernels, per_device(): pl.pallas_call(third_kernel, out_shape=[shaped(chans, rows, cols)] * 3, i...  3.39 us
    ppermute x4, waiting for transfers between devices, sum_over(): other = lax.ppermute(value, axis, pairs)  2.61 us
    pallas_call x1, Pallas kernels, per_device(): pl.pallas_call(own_kernel, out_shape=[shaped(planes, own_tiles, rows, LAN...  1.63 us
  transfers between devices with their start and end apart: 12, of which 4 were waited for; matrix products, arithmetic and copies ran while one was open for 0% of the time, Pallas kernels for 13%

profile of v12, /device:TPU:0, one launch (start us, length us, event | category | flops | bytes accessed | tf_op | source)
XLA Modules:
  0.0 50.4 jit_solution(17637052810618068100)
XLA Ops:
  0.6 1.6 %shard_map.76 = (f32[6,8,64,128]{3,2,1,0:T(8,128)S(1)}, f32[6,8,16,128]{3,2,1,0:T(8,128)S(1)}, f32[6,8,16,128]{3,2,1,0:T(8,128)S(1)}, f32[2,64,128]{2,1,0:T(8,128)S(1)}, f32[2,64,128]{2,1,0:T(8,128)S(1)}) custom-call(s32[3,1,16]{2,1,0:T(1,128)} %bitcast.1, f32[3,64,1024]{2,1,0:T(8,128)} %src_hbm.1, f32[64,1024]{1,0:T(8,128)} %weight_hbm.1, ...), custom_call_target="tpu_custom_call" | custom-call | tf_op jit(solution)/shard_map/pallas_call | solution.py:603
  2.3 0.7 %collective-permute-start.2 = (f32[6,8,16,128]{3,2,1,0:T(8,128)S(1)}, f32[6,8,16,128]{3,2,1,0:T(8,128)S(1)}, u32[]{:S(2)}, u32[]{:S(2)}) collective-permute-start(f32[6,8,16,128]{3,2,1,0:T(8,128)S(1)} %get-tuple-element.36), channel_id=1, source_target_pairs={{4,8},{8,4},{5,9},{9,5},{6,10},{10,6},{7,11},{11,7},{20,24},{24,20... | collective-permute-start | bytes 1179656 | tf_op jit(solution)/shard_map/ppermute | solution.py:630
  3.0 5.9 %collective-permute-start.3 = (f32[6,8,16,128]{3,2,1,0:T(8,128)S(1)}, f32[6,8,16,128]{3,2,1,0:T(8,128)S(1)}, u32[]{:S(2)}, u32[]{:S(2)}) collective-permute-start(f32[6,8,16,128]{3,2,1,0:T(8,128)S(1)} %get-tuple-element.37), channel_id=1, source_target_pairs={{0,4},{8,12},{4,0},{12,8},{1,5},{9,13},{5,1},{13,9},{2,6},{10,14},... | collective-permute-start | bytes 1179656 | tf_op jit(solution)/shard_map/ppermute | solution.py:630
  8.9 0.0 collective-permute-start
  8.9 0.7 %collective-permute-start.1 = (f32[2,64,128]{2,1,0:T(8,128)S(1)}, f32[2,64,128]{2,1,0:T(8,128)S(1)}, u32[]{:S(2)}, u32[]{:S(2)}) collective-permute-start(f32[2,64,128]{2,1,0:T(8,128)S(1)} %get-tuple-element.31), channel_id=1, source_target_pairs={{1,2},{2,1},{5,6},{6,5},{9,10},{10,9},{13,14},{14,13},{17,18},{18,... | collective-permute-start | bytes 196616 | tf_op jit(solution)/shard_map/ppermute | solution.py:630
  9.5 1.3 %shard_map.77.inner_ref = f32[6,6,64,128]{3,2,1,0:T(8,128)S(1)} custom-call(f32[6,8,64,128]{3,2,1,0:T(8,128)S(1)} %get-tuple-element.32.own_ref), custom_call_target="tpu_custom_call" | custom-call | flops 100000000 | bytes 4000000 | tf_op jit(solution)/shard_map/pallas_call | solution.py:634
  10.8 0.0 collective-permute-done.first_ref
  10.8 0.0 collective-permute-done.1.second_ref
  10.8 0.1 shard_map.79
  10.9 0.7 %collective-permute-start.4 = (f32[2,2,16,128]{3,2,1,0:T(8,128)S(1)}, f32[2,2,16,128]{3,2,1,0:T(8,128)S(1)}, u32[]{:S(2)}, u32[]{:S(2)}) collective-permute-start(f32[2,2,16,128]{3,2,1,0:T(8,128)S(1)} %get-tuple-element.38), channel_id=1, source_target_pairs={{4,8},{8,4},{5,9},{9,5},{6,10},{10,6},{7,11},{11,7},{20,24},{24,20... | collective-permute-start | bytes 98312 | tf_op jit(solution)/shard_map/ppermute | solution.py:630
  11.5 1.9 %collective-permute-start.5 = (f32[2,2,16,128]{3,2,1,0:T(8,128)S(1)}, f32[2,2,16,128]{3,2,1,0:T(8,128)S(1)}, u32[]{:S(2)}, u32[]{:S(2)}) collective-permute-start(f32[2,2,16,128]{3,2,1,0:T(8,128)S(1)} %get-tuple-element.39), channel_id=1, source_target_pairs={{0,4},{8,12},{4,0},{12,8},{1,5},{9,13},{5,1},{13,9},{2,6},{10,14},... | collective-permute-start | bytes 98312 | tf_op jit(solution)/shard_map/ppermute | solution.py:630
  13.4 0.8 %shard_map.78.outer_ref = f32[6,3,64,128]{3,2,1,0:T(8,128)S(1)} custom-call(f32[6,8,64,128]{3,2,1,0:T(8,128)S(1)} %get-tuple-element.32.own_ref, f32[2,64,128]{2,1,0:T(8,128)S(1)} %collective-permute-done.first_ref, f32[2,64,128]{2,1,0:T(8,128)S(1)} %collective-permute-done.1.second_ref), custom_call_target="tpu_custom_call" | custom-call | flops 100000000 | bytes 2000000 | tf_op jit(solution)/shard_map/pallas_call | solution.py:653
  14.2 0.0 collective-permute-done.4.second_corners_ref
  14.2 3.9 %collective-permute-done.5.first_corners_ref = f32[2,2,16,128]{3,2,1,0:T(8,128)S(1)} collective-permute-done((f32[2,2,16,128]{3,2,1,0:T(8,128)S(1)}, f32[2,2,16,128]{3,2,1,0:T(8,128)S(1)}, u32[]{:S(2)}, u32[]{:S(2)}) %collective-permute-start.5) | collective-permute-done | bytes 32800 | tf_op jit(solution)/shard_map/ppermute | solution.py:630
  18.0 0.0 collective-permute-done.2.second_rows_ref
  18.0 0.0 collective-permute-done.3.first_rows_ref
  18.0 11.5 %shard_map.80 = (f32[9,96,128]{2,1,0:T(8,128)S(1)}, f32[9,96,128]{2,1,0:T(8,128)S(1)}, f32[9,96,128]{2,1,0:T(8,128)S(1)}, f32[9,96,128]{2,1,0:T(8,128)S(1)}, f32...) custom-call(f32[6,6,64,128]{3,2,1,0:T(8,128)S(1)} %shard_map.77.inne, ...), custom_call_target="tpu_custom_call" | custom-call | tf_op jit(solution)/shard_map/pallas_call | solution.py:666
  29.6 1.8 %collective-permute-start.8 = (f32[27,8,128]{2,1,0:T(8,128)S(1)}, f32[27,8,128]{2,1,0:T(8,128)S(1)}, u32[]{:S(2)}, u32[]{:S(2)}) collective-permute-start(f32[27,8,128]{2,1,0:T(8,128)S(1)} %get-tuple-element.41), channel_id=1, source_target_pairs={{0,4},{8,12},{4,0},{12,8},{1,5},{9,13},{5,1},{13,9},{2,6},{10,14},... | collective-permute-start | bytes 331784 | tf_op jit(solution)/shard_map/ppermute | solution.py:630
  31.4 0.7 %collective-permute-start.9 = (f32[27,8,128]{2,1,0:T(8,128)S(1)}, f32[27,8,128]{2,1,0:T(8,128)S(1)}, u32[]{:S(2)}, u32[]{:S(2)}) collective-permute-start(f32[27,8,128]{2,1,0:T(8,128)S(1)} %get-tuple-element.42), channel_id=1, source_target_pairs={{4,8},{8,4},{5,9},{9,5},{6,10},{10,6},{7,11},{11,7},{20,24},{24,20... | collective-permute-start | bytes 331784 | tf_op jit(solution)/shard_map/ppermute | solution.py:630
  32.1 0.3 collective-permute-start.6
  32.4 0.9 %collective-permute-done.6 = f32[8,128]{1,0:T(8,128)S(1)} collective-permute-done((f32[8,128]{1,0:T(8,128)S(1)}, f32[8,128]{1,0:T(8,128)S(1)}, u32[]{:S(2)}, u32[]{:S(2)}) %collective-permute-start.6) | collective-permute-done | bytes 4128 | tf_op jit(solution)/shard_map/ppermute | solution.py:578
  33.3 2.7 %collective-permute-start.7 = (f32[8,128]{1,0:T(8,128)S(1)}, f32[8,128]{1,0:T(8,128)S(1)}, u32[]{:S(2)}, u32[]{:S(2)}) collective-permute-start(f32[8,128]{1,0:T(8,128)S(1)} %add.12), channel_id=1, source_target_pairs={{0,2},{1,3},{2,0},{3,1},{4,6},{5,7},{6,4},{7,5},{8,10},{9,11},{10,... | collective-permute-start | bytes 12296 | tf_op jit(solution)/shard_map/ppermute | solution.py:578
  36.0 1.6 %collective-permute-done.7 = f32[8,128]{1,0:T(8,128)S(1)} collective-permute-done((f32[8,128]{1,0:T(8,128)S(1)}, f32[8,128]{1,0:T(8,128)S(1)}, u32[]{:S(2)}, u32[]{:S(2)}) %collective-permute-start.7) | collective-permute-done | bytes 4128 | tf_op jit(solution)/shard_map/ppermute | solution.py:578
  37.5 2.8 %collective-permute-start.10 = (f32[8,128]{1,0:T(8,128)S(1)}, f32[8,128]{1,0:T(8,128)S(1)}, u32[]{:S(2)}, u32[]{:S(2)}) collective-permute-start(f32[8,128]{1,0:T(8,128)S(1)} %add.13), channel_id=1, source_target_pairs={{0,4},{4,0},{8,12},{12,8},{1,5},{5,1},{9,13},{13,9},{2,6},{6,2},{1... | collective-permute-start | bytes 12296 | tf_op jit(solution)/shard_map/ppermute | solution.py:578
  40.4 0.0 collective-permute-done.9.second_late_ref
  40.4 1.5 %shard_map.81.refs_0_ = f32[9,96,128]{2,1,0:T(8,128)S(1)} custom-call(f32[27,8,128]{2,1,0:T(8,128)S(1)} %collective-permute-done.8.first_late_ref, f32[27,8,128]{2,1,0:T(8,128)S(1)} %collective-permute-done.9.second_late_ref, f32[9,96,128]{2,1,0:T(8,128)S(1)} %get-tuple-element.43.b_right_ref, f32[9,96,128]{2,1,0:T(8,128)S(1)} %get-tuple-element.44.b_down_ref, ...), custom_call_target="tpu_custom_call" | custom-call | flops 100000000 | bytes 10000000 | tf_op jit(solution)/shard_map/pallas_call | solution.py:679
  41.9 0.1 collective-permute-done.10
  42.0 2.1 %collective-permute-start.11 = (f32[8,128]{1,0:T(8,128)S(1)}, f32[8,128]{1,0:T(8,128)S(1)}, u32[]{:S(2)}, u32[]{:S(2)}) collective-permute-start(f32[8,128]{1,0:T(8,128)S(1)} %add.14), channel_id=1, source_target_pairs={{0,8},{4,12},{8,0},{12,4},{1,9},{5,13},{9,1},{13,5},{2,10},{6,14},... | collective-permute-start | bytes 12296 | tf_op jit(solution)/shard_map/ppermute | solution.py:578
  44.1 1.4 %shard_map.83.refs_2_ = f32[9,96,128]{2,1,0:T(8,128)S(1)} custom-call(f32[27,8,128]{2,1,0:T(8,128)S(1)} %collective-permute-done.8.first_late_ref, f32[27,8,128]{2,1,0:T(8,128)S(1)} %collective-permute-done.9.second_late_ref, f32[9,96,128]{2,1,0:T(8,128)S(1)} %get-tuple-element.43.b_right_ref, f32[9,96,128]{2,1,0:T(8,128)S(1)} %get-tuple-element.44.b_down_ref, ...), custom_call_target="tpu_custom_call" | custom-call | flops 100000000 | bytes 10000000 | tf_op jit(solution)/shard_map/pallas_call | solution.py:679
  45.5 1.4 %shard_map.82.refs_1_ = f32[9,96,128]{2,1,0:T(8,128)S(1)} custom-call(f32[27,8,128]{2,1,0:T(8,128)S(1)} %collective-permute-done.8.first_late_ref, f32[27,8,128]{2,1,0:T(8,128)S(1)} %collective-permute-done.9.second_late_ref, f32[9,96,128]{2,1,0:T(8,128)S(1)} %get-tuple-element.43.b_right_ref, f32[9,96,128]{2,1,0:T(8,128)S(1)} %get-tuple-element.44.b_down_ref, ...), custom_call_target="tpu_custom_call" | custom-call | flops 100000000 | bytes 10000000 | tf_op jit(solution)/shard_map/pallas_call | solution.py:679
  47.0 0.0 collective-permute-done.11
  47.0 3.4 %shard_map.84 = (f32[3,64,1024]{2,1,0:T(8,128)}, f32[3,64,1024]{2,1,0:T(8,128)}, f32[3,64,1024]{2,1,0:T(8,128)}) custom-call(f32[8,128]{1,0:T(8,128)S(1)} %add.15.sums_ref, f32[9,96,128]{2,1,0:T(8,128)S(1)} %get-tuple-element.48.scale_ref, f32[9,96,128]{2,1,0:T(8,128)S(1)} %get-tuple-element.49.root_ref, f32[3,9,96,128]{3,2,1,0:T(8,128)S(1)} %get-tuple-element.50.g0_ref, ...), custom_call_target="tpu_custom_call" | custom-call | tf_op jit(solution)/shard_map/pallas_call | solution.py:703
  (5 shorter events, 0.0 us)
Async XLA Ops:
  2.3 15.8 %collective-permute-start.2 = (f32[6,8,16,128]{3,2,1,0:T(8,128)S(1)}, f32[6,8,16,128]{3,2,1,0:T(8,128)S(1)}, u32[]{:S(2)}, u32[]{:S(2)}) collective-permute-start(f32[6,8,16,128]{3,2,1,0:T(8,128)S(1)} %get-tuple-element.36), channel_id=1, source_target_pairs={{4,8},{8,4},{5,9},{9,5},{6,10},{10,6},{7,11},{11,7},{20,24},{24,20... | collective-permute-start | bytes 1179656 | tf_op jit(solution)/shard_map/ppermute | solution.py:630
  3.0 15.1 %collective-permute-start.3 = (f32[6,8,16,128]{3,2,1,0:T(8,128)S(1)}, f32[6,8,16,128]{3,2,1,0:T(8,128)S(1)}, u32[]{:S(2)}, u32[]{:S(2)}) collective-permute-start(f32[6,8,16,128]{3,2,1,0:T(8,128)S(1)} %get-tuple-element.37), channel_id=1, source_target_pairs={{0,4},{8,12},{4,0},{12,8},{1,5},{9,13},{5,1},{13,9},{2,6},{10,14},... | collective-permute-start | bytes 1179656 | tf_op jit(solution)/shard_map/ppermute | solution.py:630
  8.9 1.9 %collective-permute-start = (f32[2,64,128]{2,1,0:T(8,128)S(1)}, f32[2,64,128]{2,1,0:T(8,128)S(1)}, u32[]{:S(2)}, u32[]{:S(2)}) collective-permute-start(f32[2,64,128]{2,1,0:T(8,128)S(1)} %get-tuple-element.30), channel_id=1, source_target_pairs={{0,1},{2,3},{1,0},{3,2},{4,5},{6,7},{5,4},{7,6},{8,9},{10,11},{9,8... | collective-permute-start | bytes 196616 | tf_op jit(solution)/shard_map/ppermute | solution.py:630
  8.9 1.9 %collective-permute-start.1 = (f32[2,64,128]{2,1,0:T(8,128)S(1)}, f32[2,64,128]{2,1,0:T(8,128)S(1)}, u32[]{:S(2)}, u32[]{:S(2)}) collective-permute-start(f32[2,64,128]{2,1,0:T(8,128)S(1)} %get-tuple-element.31), channel_id=1, source_target_pairs={{1,2},{2,1},{5,6},{6,5},{9,10},{10,9},{13,14},{14,13},{17,18},{18,... | collective-permute-start | bytes 196616 | tf_op jit(solution)/shard_map/ppermute | solution.py:630
  10.9 3.3 %collective-permute-start.4 = (f32[2,2,16,128]{3,2,1,0:T(8,128)S(1)}, f32[2,2,16,128]{3,2,1,0:T(8,128)S(1)}, u32[]{:S(2)}, u32[]{:S(2)}) collective-permute-start(f32[2,2,16,128]{3,2,1,0:T(8,128)S(1)} %get-tuple-element.38), channel_id=1, source_target_pairs={{4,8},{8,4},{5,9},{9,5},{6,10},{10,6},{7,11},{11,7},{20,24},{24,20... | collective-permute-start | bytes 98312 | tf_op jit(solution)/shard_map/ppermute | solution.py:630
  11.5 6.5 %collective-permute-start.5 = (f32[2,2,16,128]{3,2,1,0:T(8,128)S(1)}, f32[2,2,16,128]{3,2,1,0:T(8,128)S(1)}, u32[]{:S(2)}, u32[]{:S(2)}) collective-permute-start(f32[2,2,16,128]{3,2,1,0:T(8,128)S(1)} %get-tuple-element.39), channel_id=1, source_target_pairs={{0,4},{8,12},{4,0},{12,8},{1,5},{9,13},{5,1},{13,9},{2,6},{10,14},... | collective-permute-start | bytes 98312 | tf_op jit(solution)/shard_map/ppermute | solution.py:630
  29.6 10.8 %collective-permute-start.8 = (f32[27,8,128]{2,1,0:T(8,128)S(1)}, f32[27,8,128]{2,1,0:T(8,128)S(1)}, u32[]{:S(2)}, u32[]{:S(2)}) collective-permute-start(f32[27,8,128]{2,1,0:T(8,128)S(1)} %get-tuple-element.41), channel_id=1, source_target_pairs={{0,4},{8,12},{4,0},{12,8},{1,5},{9,13},{5,1},{13,9},{2,6},{10,14},... | collective-permute-start | bytes 331784 | tf_op jit(solution)/shard_map/ppermute | solution.py:630
  31.4 9.0 %collective-permute-start.9 = (f32[27,8,128]{2,1,0:T(8,128)S(1)}, f32[27,8,128]{2,1,0:T(8,128)S(1)}, u32[]{:S(2)}, u32[]{:S(2)}) collective-permute-start(f32[27,8,128]{2,1,0:T(8,128)S(1)} %get-tuple-element.42), channel_id=1, source_target_pairs={{4,8},{8,4},{5,9},{9,5},{6,10},{10,6},{7,11},{11,7},{20,24},{24,20... | collective-permute-start | bytes 331784 | tf_op jit(solution)/shard_map/ppermute | solution.py:630
  32.1 1.2 %collective-permute-start.6 = (f32[8,128]{1,0:T(8,128)S(1)}, f32[8,128]{1,0:T(8,128)S(1)}, u32[]{:S(2)}, u32[]{:S(2)}) collective-permute-start(f32[8,128]{1,0:T(8,128)S(1)} %get-tuple-element.40), channel_id=1, source_target_pairs={{0,1},{1,0},{2,3},{3,2},{4,5},{5,4},{6,7},{7,6},{8,9},{9,8},{10,11... | collective-permute-start | bytes 12296 | tf_op jit(solution)/shard_map/ppermute | solution.py:578
  33.3 4.2 %collective-permute-start.7 = (f32[8,128]{1,0:T(8,128)S(1)}, f32[8,128]{1,0:T(8,128)S(1)}, u32[]{:S(2)}, u32[]{:S(2)}) collective-permute-start(f32[8,128]{1,0:T(8,128)S(1)} %add.12), channel_id=1, source_target_pairs={{0,2},{1,3},{2,0},{3,1},{4,6},{5,7},{6,4},{7,5},{8,10},{9,11},{10,... | collective-permute-start | bytes 12296 | tf_op jit(solution)/shard_map/ppermute | solution.py:578
  37.5 4.4 %collective-permute-start.10 = (f32[8,128]{1,0:T(8,128)S(1)}, f32[8,128]{1,0:T(8,128)S(1)}, u32[]{:S(2)}, u32[]{:S(2)}) collective-permute-start(f32[8,128]{1,0:T(8,128)S(1)} %add.13), channel_id=1, source_target_pairs={{0,4},{4,0},{8,12},{12,8},{1,5},{5,1},{9,13},{13,9},{2,6},{6,2},{1... | collective-permute-start | bytes 12296 | tf_op jit(solution)/shard_map/ppermute | solution.py:578
  42.0 5.0 %collective-permute-start.11 = (f32[8,128]{1,0:T(8,128)S(1)}, f32[8,128]{1,0:T(8,128)S(1)}, u32[]{:S(2)}, u32[]{:S(2)}) collective-permute-start(f32[8,128]{1,0:T(8,128)S(1)} %add.14), channel_id=1, source_target_pairs={{0,8},{4,12},{8,0},{12,4},{1,9},{5,13},{9,1},{13,5},{2,10},{6,14},... | collective-permute-start | bytes 12296 | tf_op jit(solution)/shard_map/ppermute | solution.py:578

commit v13 on v11

--- a/solution.py
+++ b/solution.py
@@ -15,6 +15,7 @@
 LATE = 8
 SLOT = 32
 SLOTS = LANES // SLOT
+SPARE = 8
 WAYS = 3
 
 seam_damping = 0.8
@@ -288,7 +289,7 @@
 
 def spread(b_right_ref, b_down_ref, z_ref, emit):
     tiles, height = z_ref.shape[:2]
-    steps = height // SUBS
+    steps = (height - SPARE) // SUBS
     ways = ways_of(tiles)
     lane = lane_index()
     first, last = (lane == 0, lane == LANES - 1)
@@ -362,7 +363,7 @@
 
 def next_residual(b_right_ref, b_down_ref, g_ref, z_ref, next_ref, own_of):
     height = g_ref.shape[1]
-    steps = height // SUBS
+    steps = (height - SPARE) // SUBS
     sums = {}
 
     def emit(i, j, centre, moved):
@@ -386,7 +387,7 @@
 
 
 def first_kernel(
-    inner_ref, outer_ref, first_rows_ref, second_rows_ref, first_corners_ref, second_corners_ref,
+    inner_ref, outer_ref, second_rows_ref, first_rows_ref, second_corners_ref, first_corners_ref,
     b_right_ref, b_down_ref, scale_ref, root_ref, g0_ref, z0_ref, g1_ref, f1_ref, g2_ref, sums_ref,
     first_late_ref, second_late_ref,
     natural, work_ref,
@@ -492,8 +493,8 @@
     c, first_late_ref, second_late_ref, b_right_ref, b_down_ref, g2_ref, f2_ref, g_ref, work_ref
 ):
     tiles, height = b_right_ref.shape[:2]
-    rows = height - 2 * HALO
-    steps = height // SUBS
+    rows = height - SPARE - 2 * HALO
+    steps = (height - SPARE) // SUBS
     odd_row = odd("row")
     for j in range(tiles):
         g_ref[j] = g2_ref[c, j]
@@ -533,7 +534,7 @@
     rows, cols = solution_hbm.shape[1:]
     own_tiles = cols // LANES
     tiles, height = scale_ref.shape[:2]
-    steps = height // SUBS
+    steps = (height - SPARE) // SUBS
     ways = ways_of(tiles)
     x0, x1, r0, r1, r2 = combine(*[jnp.broadcast_to(sums_ref[k:k + 1, :], (SUBS, LANES)) for k in range(4)])
     matrix = undealing(ways) if ways > 1 else None
@@ -618,11 +619,12 @@
         ],
     )
 
-    def swap(first, second, axis):
+    def swap(first, second, axis, order):
         size = lax.axis_size(axis)
         pairs = [[(i, i + 1) for i in range(start, size - 1, 2)] for start in range(2)]
         pairs = [some + [(j, i) for i, j in some] for some in pairs]
-        return [lax.ppermute(value, axis, some) for value, some in zip((first, second), pairs)]
+        received = {k: lax.ppermute((first, second)[k], axis, pairs[k]) for k in order}
+        return received[0], received[1]
 
     ways = ways_of(tiles)
     inner = pl.pallas_call(
@@ -633,8 +635,8 @@
         compiler_params=params,
         cost_estimate=pl.CostEstimate(flops=10**8, bytes_accessed=4 * 10**6, transcendentals=0),
     )(own)
-    first_rows, second_rows = swap(first_rows, second_rows, "row")
-    first_cols, second_cols = swap(first_cols, second_cols, "col")
+    first_rows, second_rows = swap(first_rows, second_rows, "row", (1, 0))
+    first_cols, second_cols = swap(first_cols, second_cols, "col", (0, 1))
     first_cols, second_cols, inner = lax.optimization_barrier((first_cols, second_cols, inner))
     corners = pl.pallas_call(
         functools.partial(corners_kernel, chans),
@@ -643,7 +645,7 @@
         out_specs=[in_vmem] * 2,
         compiler_params=params,
     )(first_cols, second_cols)
-    first_corners, second_corners = swap(*corners, "row")
+    first_corners, second_corners = swap(*corners, "row", (1, 0))
     outer = pl.pallas_call(
         outer_dealt_kernel,
         out_shape=shaped(planes, ways, rows, LANES),
@@ -654,8 +656,8 @@
     )(own, first_cols, second_cols)
 
     height = rows + 2 * HALO
-    plane = shaped(tiles, height, LANES)
-    field = shaped(chans, tiles, height, LANES)
+    plane = shaped(tiles, height + SPARE, LANES)
+    field = shaped(chans, tiles, height + SPARE, LANES)
     lates = [shaped(chans * tiles + extra, LATE, LANES) for extra in (1, 0)]
     *basis, sums, first_late, second_late = pl.pallas_call(
         first_kernel,
@@ -664,9 +666,9 @@
         out_specs=[in_vmem] * 12,
         scratch_shapes=[scratch(planes, tiles, height, LANES), scratch(*plane.shape)],
         compiler_params=params,
-    )(inner, outer, first_rows, second_rows, first_corners, second_corners)
-
-    first_late, second_late = swap(first_late, second_late, "row")
+    )(inner, outer, second_rows, first_rows, second_corners, first_corners)
+
+    first_late, second_late = swap(first_late, second_late, "row", (0, 1))
 
     b_right, b_down, scale, root, g0, z0, g1, f1, g2 = basis
     f2 = [

time: 46.9 us -> 48.1 us (1.026)
  starting transfers between devices: 21.9 us -> 15.1 us
  waiting for transfers between devices: 3.52 us -> 9.91 us
  Pallas kernels: 20.5 us -> 22.2 us
    ppermute x8, waiting for transfers between devices: 2.97 us -> 7.28 us  [swap(): lax.ppermute((first, second)[k], axis, pairs[k])]
    ppermute x3, starting transfers between devices: 6.93 us -> 2.85 us  [sum_over(): other = lax.ppermute(value, axis, pairs)]
    ppermute x8, starting transfers between devices: 15 us -> 12.2 us  [swap(): lax.ppermute((first, second)[k], axis, pairs[k])]
    ppermute x3, waiting for transfers between devices: 0.56 us -> 2.63 us  [sum_over(): other = lax.ppermute(value, axis, pairs)]
    pallas_call x1, Pallas kernels: 10.1 us -> 11.4 us  [per_device(): pl.pallas_call(first_kernel, out_shape=[plane] * 4 + [field] * 5 + [shape...]
where the time goes in v13:
time: 48.1 us; the launch traced here: 47.9 us
  Pallas kernels  22.2 us (46%)
  starting transfers between devices  15.1 us (31%)
  waiting for transfers between devices  9.91 us (21%)
  between operations  0.76 us (2%)
    ppermute x8, starting transfers between devices, swap(): lax.ppermute((first, second)[k], axis, pairs[k])  12.2 us
    pallas_call x1, Pallas kernels, per_device(): pl.pallas_call(first_kernel, out_shape=[plane] * 4 + [field] * 5 + [shape...  11.4 us
    ppermute x8, waiting for transfers between devices, swap(): lax.ppermute((first, second)[k], axis, pairs[k])  7.28 us
    pallas_call x3, Pallas kernels, per_device(): pl.pallas_call(functools.partial(second_kernel, c), out_shape=plane, in_s...  4.05 us
    pallas_call x1, Pallas kernels, per_device(): pl.pallas_call(third_kernel, out_shape=[shaped(chans, rows, cols)] * 3, i...  2.95 us
    ppermute x3, starting transfers between devices, sum_over(): other = lax.ppermute(value, axis, pairs)  2.85 us
    ppermute x3, waiting for transfers between devices, sum_over(): other = lax.ppermute(value, axis, pairs)  2.63 us
    pallas_call x1, Pallas kernels, per_device(): pl.pallas_call(own_kernel, out_shape=[shaped(planes, own_tiles, rows, LAN...  1.63 us
  transfers between devices with their start and end apart: 11, of which 4 were waited for; matrix products, arithmetic and copies ran while one was open for 0% of the time, Pallas kernels for 13%

profile of v13, /device:TPU:0, one launch (start us, length us, event | category | flops | bytes accessed | tf_op | source)
XLA Modules:
  0.0 47.9 jit_solution(2317023134578041508)
XLA Ops:
  0.6 1.6 %shard_map.76 = (f32[6,8,64,128]{3,2,1,0:T(8,128)S(1)}, f32[6,8,16,128]{3,2,1,0:T(8,128)S(1)}, f32[6,8,16,128]{3,2,1,0:T(8,128)S(1)}, f32[2,64,128]{2,1,0:T(8,128)S(1)}, f32[2,64,128]{2,1,0:T(8,128)S(1)}) custom-call(s32[3,1,16]{2,1,0:T(1,128)} %bitcast.5, f32[3,64,1024]{2,1,0:T(8,128)} %src_hbm.1, f32[64,1024]{1,0:T(8,128)} %weight_hbm.1, ...), custom_call_target="tpu_custom_call" | custom-call | tf_op jit(solution)/shard_map/pallas_call | solution.py:599
  2.3 0.7 %collective-permute-start.2 = (f32[6,8,16,128]{3,2,1,0:T(8,128)S(1)}, f32[6,8,16,128]{3,2,1,0:T(8,128)S(1)}, u32[]{:S(2)}, u32[]{:S(2)}) collective-permute-start(f32[6,8,16,128]{3,2,1,0:T(8,128)S(1)} %get-tuple-element.37), channel_id=1, source_target_pairs={{4,8},{8,4},{5,9},{9,5},{6,10},{10,6},{7,11},{11,7},{20,24},{24,20... | collective-permute-start | bytes 1179656 | tf_op jit(solution)/shard_map/ppermute | solution.py:626
  3.0 5.9 %collective-permute-start.3 = (f32[6,8,16,128]{3,2,1,0:T(8,128)S(1)}, f32[6,8,16,128]{3,2,1,0:T(8,128)S(1)}, u32[]{:S(2)}, u32[]{:S(2)}) collective-permute-start(f32[6,8,16,128]{3,2,1,0:T(8,128)S(1)} %get-tuple-element.38), channel_id=1, source_target_pairs={{0,4},{8,12},{4,0},{12,8},{1,5},{9,13},{5,1},{13,9},{2,6},{10,14},... | collective-permute-start | bytes 1179656 | tf_op jit(solution)/shard_map/ppermute | solution.py:626
  8.9 0.0 collective-permute-start
  8.9 0.7 %collective-permute-start.1 = (f32[2,64,128]{2,1,0:T(8,128)S(1)}, f32[2,64,128]{2,1,0:T(8,128)S(1)}, u32[]{:S(2)}, u32[]{:S(2)}) collective-permute-start(f32[2,64,128]{2,1,0:T(8,128)S(1)} %get-tuple-element.32), channel_id=1, source_target_pairs={{1,2},{2,1},{5,6},{6,5},{9,10},{10,9},{13,14},{14,13},{17,18},{18,... | collective-permute-start | bytes 196616 | tf_op jit(solution)/shard_map/ppermute | solution.py:626
  9.5 1.3 %shard_map.77.inner_ref = f32[6,6,64,128]{3,2,1,0:T(8,128)S(1)} custom-call(f32[6,8,64,128]{3,2,1,0:T(8,128)S(1)} %get-tuple-element.33.own_ref), custom_call_target="tpu_custom_call" | custom-call | flops 100000000 | bytes 4000000 | tf_op jit(solution)/shard_map/pallas_call | solution.py:630
  10.8 0.0 collective-permute-done.first_ref
  10.8 0.0 collective-permute-done.1.second_ref
  10.8 0.1 shard_map.79
  10.9 0.7 %collective-permute-start.4 = (f32[2,2,16,128]{3,2,1,0:T(8,128)S(1)}, f32[2,2,16,128]{3,2,1,0:T(8,128)S(1)}, u32[]{:S(2)}, u32[]{:S(2)}) collective-permute-start(f32[2,2,16,128]{3,2,1,0:T(8,128)S(1)} %get-tuple-element.39), channel_id=1, source_target_pairs={{4,8},{8,4},{5,9},{9,5},{6,10},{10,6},{7,11},{11,7},{20,24},{24,20... | collective-permute-start | bytes 98312 | tf_op jit(solution)/shard_map/ppermute | solution.py:626
  11.5 1.9 %collective-permute-start.5 = (f32[2,2,16,128]{3,2,1,0:T(8,128)S(1)}, f32[2,2,16,128]{3,2,1,0:T(8,128)S(1)}, u32[]{:S(2)}, u32[]{:S(2)}) collective-permute-start(f32[2,2,16,128]{3,2,1,0:T(8,128)S(1)} %get-tuple-element.40), channel_id=1, source_target_pairs={{0,4},{8,12},{4,0},{12,8},{1,5},{9,13},{5,1},{13,9},{2,6},{10,14},... | collective-permute-start | bytes 98312 | tf_op jit(solution)/shard_map/ppermute | solution.py:626
  13.4 0.8 %shard_map.78.outer_ref = f32[6,3,64,128]{3,2,1,0:T(8,128)S(1)} custom-call(f32[6,8,64,128]{3,2,1,0:T(8,128)S(1)} %get-tuple-element.33.own_ref, f32[2,64,128]{2,1,0:T(8,128)S(1)} %collective-permute-done.first_ref, f32[2,64,128]{2,1,0:T(8,128)S(1)} %collective-permute-done.1.second_ref), custom_call_target="tpu_custom_call" | custom-call | flops 100000000 | bytes 2000000 | tf_op jit(solution)/shard_map/pallas_call | solution.py:649
  14.2 0.0 collective-permute-done.4.second_corners_ref
  14.2 3.9 %collective-permute-done.5.first_corners_ref = f32[2,2,16,128]{3,2,1,0:T(8,128)S(1)} collective-permute-done((f32[2,2,16,128]{3,2,1,0:T(8,128)S(1)}, f32[2,2,16,128]{3,2,1,0:T(8,128)S(1)}, u32[]{:S(2)}, u32[]{:S(2)}) %collective-permute-start.5) | collective-permute-done | bytes 32800 | tf_op jit(solution)/shard_map/ppermute | solution.py:626
  18.0 0.0 collective-permute-done.2.second_rows_ref
  18.0 0.0 collective-permute-done.3.first_rows_ref
  18.0 11.4 %shard_map.80 = (f32[9,104,128]{2,1,0:T(8,128)S(1)}, f32[9,104,128]{2,1,0:T(8,128)S(1)}, f32[9,104,128]{2,1,0:T(8,128)S(1)}, f32[9,104,128]{2,1,0:T(8,128)S(1)},...) custom-call(f32[6,6,64,128]{3,2,1,0:T(8,128)S(1)} %shard_map.77.inne, ...), custom_call_target="tpu_custom_call" | custom-call | tf_op jit(solution)/shard_map/pallas_call | solution.py:662
  29.5 1.8 %collective-permute-start.6 = (f32[28,8,128]{2,1,0:T(8,128)S(1)}, f32[28,8,128]{2,1,0:T(8,128)S(1)}, u32[]{:S(2)}, u32[]{:S(2)}) collective-permute-start(f32[28,8,128]{2,1,0:T(8,128)S(1)} %get-tuple-element.42), channel_id=1, source_target_pairs={{0,4},{8,12},{4,0},{12,8},{1,5},{9,13},{5,1},{13,9},{2,6},{10,14},... | collective-permute-start | bytes 344072 | tf_op jit(solution)/shard_map/ppermute | solution.py:626
  31.3 0.7 %collective-permute-start.7 = (f32[27,8,128]{2,1,0:T(8,128)S(1)}, f32[27,8,128]{2,1,0:T(8,128)S(1)}, u32[]{:S(2)}, u32[]{:S(2)}) collective-permute-start(f32[27,8,128]{2,1,0:T(8,128)S(1)} %get-tuple-element.43), channel_id=1, source_target_pairs={{4,8},{8,4},{5,9},{9,5},{6,10},{10,6},{7,11},{11,7},{20,24},{24,20... | collective-permute-start | bytes 331784 | tf_op jit(solution)/shard_map/ppermute | solution.py:626
  31.9 3.4 %collective-permute-done.6.first_late_ref = f32[28,8,128]{2,1,0:T(8,128)S(1)} collective-permute-done((f32[28,8,128]{2,1,0:T(8,128)S(1)}, f32[28,8,128]{2,1,0:T(8,128)S(1)}, u32[]{:S(2)}, u32[]{:S(2)}) %collective-permute-start.6) | collective-permute-done | bytes 114720 | tf_op jit(solution)/shard_map/ppermute | solution.py:626
  35.4 1.2 %collective-permute-start.8 = (f32[8,128]{1,0:T(8,128)S(1)}, f32[8,128]{1,0:T(8,128)S(1)}, u32[]{:S(2)}, u32[]{:S(2)}) collective-permute-start(f32[8,128]{1,0:T(8,128)S(1)} %fusion), channel_id=1, source_target_pairs={{0,8},{4,12},{8,0},{12,4},{1,9},{5,13},{9,1},{13,5},{2,10},{6,14},... | collective-permute-start | bytes 12296 | tf_op jit(solution)/shard_map/ppermute | solution.py:574
  36.6 0.0 collective-permute-done.7.second_late_ref
  36.6 1.4 %shard_map.81.refs_0_ = f32[9,104,128]{2,1,0:T(8,128)S(1)} custom-call(f32[28,8,128]{2,1,0:T(8,128)S(1)} %collective-permute-done.6.first_late_ref, f32[27,8,128]{2,1,0:T(8,128)S(1)} %collective-permute-done.7.second_late_ref, f32[9,104,128]{2,1,0:T(8,128)S(1)} %get-tuple-element.44.b_right_ref, f32[9,104,128]{2,1,0:T(8,128)S(1)} %get-tuple-element.45.b_down_ref, ...), custom_call_target="tpu_custom_call" | custom-call | flops 100000000 | bytes 10000000 | tf_op jit(solution)/shard_map/pallas_call | solution.py:675
  37.9 1.9 %collective-permute-done.8 = f32[8,128]{1,0:T(8,128)S(1)} collective-permute-done((f32[8,128]{1,0:T(8,128)S(1)}, f32[8,128]{1,0:T(8,128)S(1)}, u32[]{:S(2)}, u32[]{:S(2)}) %collective-permute-start.8) | collective-permute-done | bytes 4128 | tf_op jit(solution)/shard_map/ppermute | solution.py:574
  39.9 0.0 collective-permute-start.9
  39.9 1.4 %shard_map.82.refs_1_ = f32[9,104,128]{2,1,0:T(8,128)S(1)} custom-call(f32[28,8,128]{2,1,0:T(8,128)S(1)} %collective-permute-done.6.first_late_ref, f32[27,8,128]{2,1,0:T(8,128)S(1)} %collective-permute-done.7.second_late_ref, f32[9,104,128]{2,1,0:T(8,128)S(1)} %get-tuple-element.44.b_right_ref, f32[9,104,128]{2,1,0:T(8,128)S(1)} %get-tuple-element.45.b_down_ref, ...), custom_call_target="tpu_custom_call" | custom-call | flops 100000000 | bytes 10000000 | tf_op jit(solution)/shard_map/pallas_call | solution.py:675
  41.2 0.0 collective-permute-done.9
  41.3 1.6 %collective-permute-start.10 = (f32[8,128]{1,0:T(8,128)S(1)}, f32[8,128]{1,0:T(8,128)S(1)}, u32[]{:S(2)}, u32[]{:S(2)}) collective-permute-start(f32[8,128]{1,0:T(8,128)S(1)} %add.14), channel_id=1, source_target_pairs={{0,2},{1,3},{2,0},{3,1},{4,6},{5,7},{6,4},{7,5},{8,10},{9,11},{10,... | collective-permute-start | bytes 12296 | tf_op jit(solution)/shard_map/ppermute | solution.py:574
  42.9 1.3 %shard_map.83.refs_2_ = f32[9,104,128]{2,1,0:T(8,128)S(1)} custom-call(f32[28,8,128]{2,1,0:T(8,128)S(1)} %collective-permute-done.6.first_late_ref, f32[27,8,128]{2,1,0:T(8,128)S(1)} %collective-permute-done.7.second_late_ref, f32[9,104,128]{2,1,0:T(8,128)S(1)} %get-tuple-element.44.b_right_ref, f32[9,104,128]{2,1,0:T(8,128)S(1)} %get-tuple-element.45.b_down_ref, ...), custom_call_target="tpu_custom_call" | custom-call | flops 100000000 | bytes 10000000 | tf_op jit(solution)/shard_map/pallas_call | solution.py:675
  44.2 0.7 %collective-permute-done.10 = f32[8,128]{1,0:T(8,128)S(1)} collective-permute-done((f32[8,128]{1,0:T(8,128)S(1)}, f32[8,128]{1,0:T(8,128)S(1)}, u32[]{:S(2)}, u32[]{:S(2)}) %collective-permute-start.10) | collective-permute-done | bytes 4128 | tf_op jit(solution)/shard_map/ppermute | solution.py:574
  44.9 3.0 %shard_map.84 = (f32[3,64,1024]{2,1,0:T(8,128)}, f32[3,64,1024]{2,1,0:T(8,128)}, f32[3,64,1024]{2,1,0:T(8,128)}) custom-call(f32[8,128]{1,0:T(8,128)S(1)} %add.15.sums_ref, f32[9,104,128]{2,1,0:T(8,128)S(1)} %get-tuple-element.50.scale_ref, f32[9,104,128]{2,1,0:T(8,128)S(1)} %get-tuple-element.51.root_ref, f32[3,9,104,128]{3,2,1,0:T(8,128)S(1)} %get-tuple-element.52.g0_ref, ...), custom_call_target="tpu_custom_call" | custom-call | tf_op jit(solution)/shard_map/pallas_call | solution.py:697
  (4 shorter events, 0.0 us)
Async XLA Ops:
  2.3 15.8 %collective-permute-start.2 = (f32[6,8,16,128]{3,2,1,0:T(8,128)S(1)}, f32[6,8,16,128]{3,2,1,0:T(8,128)S(1)}, u32[]{:S(2)}, u32[]{:S(2)}) collective-permute-start(f32[6,8,16,128]{3,2,1,0:T(8,128)S(1)} %get-tuple-element.37), channel_id=1, source_target_pairs={{4,8},{8,4},{5,9},{9,5},{6,10},{10,6},{7,11},{11,7},{20,24},{24,20... | collective-permute-start | bytes 1179656 | tf_op jit(solution)/shard_map/ppermute | solution.py:626
  3.0 15.1 %collective-permute-start.3 = (f32[6,8,16,128]{3,2,1,0:T(8,128)S(1)}, f32[6,8,16,128]{3,2,1,0:T(8,128)S(1)}, u32[]{:S(2)}, u32[]{:S(2)}) collective-permute-start(f32[6,8,16,128]{3,2,1,0:T(8,128)S(1)} %get-tuple-element.38), channel_id=1, source_target_pairs={{0,4},{8,12},{4,0},{12,8},{1,5},{9,13},{5,1},{13,9},{2,6},{10,14},... | collective-permute-start | bytes 1179656 | tf_op jit(solution)/shard_map/ppermute | solution.py:626
  8.9 1.9 %collective-permute-start = (f32[2,64,128]{2,1,0:T(8,128)S(1)}, f32[2,64,128]{2,1,0:T(8,128)S(1)}, u32[]{:S(2)}, u32[]{:S(2)}) collective-permute-start(f32[2,64,128]{2,1,0:T(8,128)S(1)} %get-tuple-element.31), channel_id=1, source_target_pairs={{0,1},{2,3},{1,0},{3,2},{4,5},{6,7},{5,4},{7,6},{8,9},{10,11},{9,8... | collective-permute-start | bytes 196616 | tf_op jit(solution)/shard_map/ppermute | solution.py:626
  8.9 1.9 %collective-permute-start.1 = (f32[2,64,128]{2,1,0:T(8,128)S(1)}, f32[2,64,128]{2,1,0:T(8,128)S(1)}, u32[]{:S(2)}, u32[]{:S(2)}) collective-permute-start(f32[2,64,128]{2,1,0:T(8,128)S(1)} %get-tuple-element.32), channel_id=1, source_target_pairs={{1,2},{2,1},{5,6},{6,5},{9,10},{10,9},{13,14},{14,13},{17,18},{18,... | collective-permute-start | bytes 196616 | tf_op jit(solution)/shard_map/ppermute | solution.py:626
  10.9 3.3 %collective-permute-start.4 = (f32[2,2,16,128]{3,2,1,0:T(8,128)S(1)}, f32[2,2,16,128]{3,2,1,0:T(8,128)S(1)}, u32[]{:S(2)}, u32[]{:S(2)}) collective-permute-start(f32[2,2,16,128]{3,2,1,0:T(8,128)S(1)} %get-tuple-element.39), channel_id=1, source_target_pairs={{4,8},{8,4},{5,9},{9,5},{6,10},{10,6},{7,11},{11,7},{20,24},{24,20... | collective-permute-start | bytes 98312 | tf_op jit(solution)/shard_map/ppermute | solution.py:626
  11.5 6.5 %collective-permute-start.5 = (f32[2,2,16,128]{3,2,1,0:T(8,128)S(1)}, f32[2,2,16,128]{3,2,1,0:T(8,128)S(1)}, u32[]{:S(2)}, u32[]{:S(2)}) collective-permute-start(f32[2,2,16,128]{3,2,1,0:T(8,128)S(1)} %get-tuple-element.40), channel_id=1, source_target_pairs={{0,4},{8,12},{4,0},{12,8},{1,5},{9,13},{5,1},{13,9},{2,6},{10,14},... | collective-permute-start | bytes 98312 | tf_op jit(solution)/shard_map/ppermute | solution.py:626
  29.5 5.9 %collective-permute-start.6 = (f32[28,8,128]{2,1,0:T(8,128)S(1)}, f32[28,8,128]{2,1,0:T(8,128)S(1)}, u32[]{:S(2)}, u32[]{:S(2)}) collective-permute-start(f32[28,8,128]{2,1,0:T(8,128)S(1)} %get-tuple-element.42), channel_id=1, source_target_pairs={{0,4},{8,12},{4,0},{12,8},{1,5},{9,13},{5,1},{13,9},{2,6},{10,14},... | collective-permute-start | bytes 344072 | tf_op jit(solution)/shard_map/ppermute | solution.py:626
  31.3 5.3 %collective-permute-start.7 = (f32[27,8,128]{2,1,0:T(8,128)S(1)}, f32[27,8,128]{2,1,0:T(8,128)S(1)}, u32[]{:S(2)}, u32[]{:S(2)}) collective-permute-start(f32[27,8,128]{2,1,0:T(8,128)S(1)} %get-tuple-element.43), channel_id=1, source_target_pairs={{4,8},{8,4},{5,9},{9,5},{6,10},{10,6},{7,11},{11,7},{20,24},{24,20... | collective-permute-start | bytes 331784 | tf_op jit(solution)/shard_map/ppermute | solution.py:626
  35.4 4.5 %collective-permute-start.8 = (f32[8,128]{1,0:T(8,128)S(1)}, f32[8,128]{1,0:T(8,128)S(1)}, u32[]{:S(2)}, u32[]{:S(2)}) collective-permute-start(f32[8,128]{1,0:T(8,128)S(1)} %fusion), channel_id=1, source_target_pairs={{0,8},{4,12},{8,0},{12,4},{1,9},{5,13},{9,1},{13,5},{2,10},{6,14},... | collective-permute-start | bytes 12296 | tf_op jit(solution)/shard_map/ppermute | solution.py:574
  39.9 1.4 %collective-permute-start.9 = (f32[8,128]{1,0:T(8,128)S(1)}, f32[8,128]{1,0:T(8,128)S(1)}, u32[]{:S(2)}, u32[]{:S(2)}) collective-permute-start(f32[8,128]{1,0:T(8,128)S(1)} %add.13), channel_id=1, source_target_pairs={{0,1},{1,0},{2,3},{3,2},{4,5},{5,4},{6,7},{7,6},{8,9},{9,8},{10,11... | collective-permute-start | bytes 12296 | tf_op jit(solution)/shard_map/ppermute | solution.py:574
  41.3 3.7 %collective-permute-start.10 = (f32[8,128]{1,0:T(8,128)S(1)}, f32[8,128]{1,0:T(8,128)S(1)}, u32[]{:S(2)}, u32[]{:S(2)}) collective-permute-start(f32[8,128]{1,0:T(8,128)S(1)} %add.14), channel_id=1, source_target_pairs={{0,2},{1,3},{2,0},{3,1},{4,6},{5,7},{6,4},{7,5},{8,10},{9,11},{10,... | collective-permute-start | bytes 12296 | tf_op jit(solution)/shard_map/ppermute | solution.py:574

commit v14 on v13

--- a/solution.py
+++ b/solution.py
@@ -15,7 +15,6 @@
 LATE = 8
 SLOT = 32
 SLOTS = LANES // SLOT
-SPARE = 8
 WAYS = 3
 
 seam_damping = 0.8
@@ -287,58 +286,71 @@
     return out
 
 
-def spread(b_right_ref, b_down_ref, z_ref, emit):
-    tiles, height = z_ref.shape[:2]
-    steps = (height - SPARE) // SUBS
+SLOTTED = 8
+
+
+class Vectors:
+    def __init__(self, ref, slot=None):
+        self.ref, self.slots, self.slot = ref, 1 if slot is None else SLOTTED, slot or 0
+        self.tiles, self.steps = ref.shape[0], ref.shape[1] // (SUBS * self.slots)
+
+    def row(self, i):
+        return (i * self.slots + self.slot) * SUBS
+
+    def get(self, i, j):
+        return self.ref[j, self.row(i):self.row(i) + SUBS, :]
+
+    def put(self, i, j, value):
+        self.ref[j, self.row(i):self.row(i) + SUBS, :] = value
+
+
+def shared(ref):
+    return [Vectors(ref, slot) for slot in (0, 1, 2, 3, 7)]
+
+
+def spread(b_right, b_down, z, emit):
+    tiles, steps = z.tiles, z.steps
     ways = ways_of(tiles)
     lane = lane_index()
     first, last = (lane == 0, lane == LANES - 1)
-
-    def at(i):
-        return pl.ds(i * SUBS, SUBS)
-
-    from_above = [pltpu.roll(b_down_ref[j, at(steps - 1), :] * z_ref[j, at(steps - 1), :], 1, 0) for j in range(tiles)]
-    centre = [z_ref[j, at(0), :] for j in range(tiles)]
+    from_above = [pltpu.roll(b_down.get(steps - 1, j) * z.get(steps - 1, j), 1, 0) for j in range(tiles)]
+    centre = [z.get(0, j) for j in range(tiles)]
     wrapped = [pltpu.roll(v, SUBS - 1, 0) for v in centre]
     for i in range(steps):
         pushed_out = {
-            g: pltpu.roll(b_right_ref[g + ways - 1, at(i), :] * centre[g + ways - 1], 1, 1)
-            for g in range(0, tiles, ways)
+            g: pltpu.roll(b_right.get(i, g + ways - 1) * centre[g + ways - 1], 1, 1) for g in range(0, tiles, ways)
         }
         ahead = {g: pltpu.roll(centre[g], LANES - 1, 1) for g in range(0, tiles, ways)}
         pushed = None
         below = []
         for j in range(tiles):
             g = j // ways * ways
-            b_right = b_right_ref[j, at(i), :]
-            b_down = b_down_ref[j, at(i), :]
-            below.append(z_ref[j, at(i + 1), :] if i + 1 < steps else wrapped[j])
+            right = b_right.get(i, j)
+            down = b_down.get(i, j)
+            below.append(z.get(i + 1, j) if i + 1 < steps else wrapped[j])
             if j == g:
                 from_left = jnp.where(first, pushed_out[(g - ways) % tiles], pushed_out[g])
             else:
                 from_left = pushed
             if j + 1 < g + ways:
                 to_right = centre[j + 1]
-                pushed = b_right * centre[j]
+                pushed = right * centre[j]
             else:
                 to_right = jnp.where(last, ahead[(g + ways) % tiles], ahead[g])
-            moved = (b_right * to_right + from_left) + (b_down * below[j] + from_above[j])
-            from_above[j] = b_down * centre[j]
+            moved = (right * to_right + from_left) + (down * below[j] + from_above[j])
+            from_above[j] = down * centre[j]
             emit(i, j, centre[j], moved)
         centre = below
 
 
-def precondition(b_right_ref, b_down_ref, g_ref, z_ref, work_ref):
+def precondition(b_right, b_down, g, z, work, out):
     poly = chebyshev_polynomial()
     degree = SWEEPS - 1
 
-    def at(i):
-        return pl.ds(i * SUBS, SUBS)
-
     def first(i, j, centre, moved):
-        z_ref[j, at(i), :] = poly[degree] * moved + poly[degree - 1] * centre
-
-    spread(b_right_ref, b_down_ref, g_ref, first)
+        z.put(i, j, poly[degree] * moved + poly[degree - 1] * centre)
+
+    spread(b_right, b_down, g, first)
 
     def pair(k, carry):
         adds = []
@@ -348,35 +360,35 @@
                 value = jnp.where(k == (degree - 1) // 2 - 1 - later, jnp.float32(poly[2 * later + half]), value)
             adds.append(value)
 
-        def one(target, add):
-            def emit(i, j, centre, moved):
-                target[j, at(i), :] = moved + add * g_ref[j, at(i), :]
-
-            return emit
-
-        spread(b_right_ref, b_down_ref, z_ref, one(work_ref, adds[1]))
-        spread(b_right_ref, b_down_ref, work_ref, one(z_ref, adds[0]))
+        def to_work(i, j, centre, moved):
+            work.put(i, j, moved + adds[1] * g.get(i, j))
+
+        def to_z(i, j, centre, moved):
+            value = moved + adds[0] * g.get(i, j)
+            z.put(i, j, value)
+            out.put(i, j, value)
+
+        spread(b_right, b_down, z, to_work)
+        spread(b_right, b_down, work, to_z)
         return carry
 
     lax.fori_loop(0, (degree - 1) // 2, pair, 0)
 
 
-def next_residual(b_right_ref, b_down_ref, g_ref, z_ref, next_ref, own_of):
-    height = g_ref.shape[1]
-    steps = (height - SPARE) // SUBS
+def next_residual(b_right, b_down, g, z, out, own_of):
     sums = {}
 
     def emit(i, j, centre, moved):
-        at = pl.ds(i * SUBS, SUBS)
-        g = g_ref[j, at, :]
-        following = g - MIX * (centre - moved)
-        next_ref[j, at, :] = following
+        old = g.get(i, j)
+        following = old - MIX * (centre - moved)
+        g.put(i, j, following)
+        out.put(i, j, following)
         key = own_of(i, j)
-        now = (g * centre, following * centre)
+        now = (old * centre, following * centre)
         before = sums.get(key)
         sums[key] = now if before is None else (before[0] + now[0], before[1] + now[1])
 
-    spread(b_right_ref, b_down_ref, z_ref, emit)
+    spread(b_right, b_down, z, emit)
     sub = lax.broadcasted_iota(jnp.int32, (SUBS, LANES), 0)
     lane = lane_index()
     total = [jnp.zeros((SUBS, LANES), jnp.float32)] * 2
@@ -390,7 +402,7 @@
     inner_ref, outer_ref, second_rows_ref, first_rows_ref, second_corners_ref, first_corners_ref,
     b_right_ref, b_down_ref, scale_ref, root_ref, g0_ref, z0_ref, g1_ref, f1_ref, g2_ref, sums_ref,
     first_late_ref, second_late_ref,
-    natural, work_ref,
+    natural, hot_ref,
 ):
     planes, inner, rows = inner_ref.shape[:3]
     tiles = inner + outer_ref.shape[1]
@@ -444,14 +456,19 @@
             scale_ref[j, at(i), :] = jnp.where(inside, scale, 0.0)
             root_ref[j, at(i), :] = safe * scale
             to_up[j] = to_down
+    b_right, b_down, g, z, work = shared(hot_ref)
     wrapped = [pltpu.roll(scale_ref[j, at(0), :], SUBS - 1, 0) for j in range(tiles)]
     for i in range(steps):
         scale = [scale_ref[j, at(i), :] for j in range(tiles)]
         right_scale = rightward(scale)
         for j in range(tiles):
-            b_right_ref[j, at(i), :] = interleaved(chans + 1, i, j) * scale[j] * right_scale[j]
+            value = interleaved(chans + 1, i, j) * scale[j] * right_scale[j]
+            b_right_ref[j, at(i), :] = value
+            b_right.put(i, j, value)
             down_scale = scale_ref[j, at(i + 1), :] if i + 1 < steps else wrapped[j]
-            b_down_ref[j, at(i), :] = interleaved(chans + 2, i, j) * scale[j] * down_scale
+            value = interleaved(chans + 2, i, j) * scale[j] * down_scale
+            b_down_ref[j, at(i), :] = value
+            b_down.put(i, j, value)
             for c in range(chans):
                 g0_ref[c, j, at(i), :] = interleaved(c, i, j) * scale[j]
 
@@ -463,11 +480,14 @@
         return low, high, min(LANES, max(0, -(-left // ways)))
 
     def channel(c, carry):
-        g0, z0, g1, f1, g2 = [ref.at[c] for ref in (g0_ref, z0_ref, g1_ref, f1_ref, g2_ref)]
-        precondition(b_right_ref, b_down_ref, g0, z0, work_ref)
-        sum0, sum1 = next_residual(b_right_ref, b_down_ref, g0, z0, g1, own_of)
-        precondition(b_right_ref, b_down_ref, g1, f1, work_ref)
-        sum2, sum3 = next_residual(b_right_ref, b_down_ref, g1, f1, g2, own_of)
+        g0, z0, g1, f1, g2 = [Vectors(ref.at[c]) for ref in (g0_ref, z0_ref, g1_ref, f1_ref, g2_ref)]
+        for j in range(tiles):
+            for i in range(steps):
+                g.put(i, j, g0.get(i, j))
+        precondition(b_right, b_down, g, z, work, z0)
+        sum0, sum1 = next_residual(b_right, b_down, g, z, g1, own_of)
+        precondition(b_right, b_down, g, z, work, f1)
+        sum2, sum3 = next_residual(b_right, b_down, g, z, g2, own_of)
         return tuple(a + b for a, b in zip(carry, (sum0, sum1, sum2, sum3)))
 
     zero = jnp.zeros((SUBS, LANES), jnp.float32)
@@ -490,23 +510,26 @@
 
 
 def second_kernel(
-    c, first_late_ref, second_late_ref, b_right_ref, b_down_ref, g2_ref, f2_ref, g_ref, work_ref
+    c, first_late_ref, second_late_ref, b_right_ref, b_down_ref, g2_ref, f2_ref, hot_ref
 ):
     tiles, height = b_right_ref.shape[:2]
-    rows = height - SPARE - 2 * HALO
-    steps = (height - SPARE) // SUBS
+    rows = height - 2 * HALO
+    steps = height // SUBS
     odd_row = odd("row")
+    b_right, b_down, g, z, work = shared(hot_ref)
     for j in range(tiles):
-        g_ref[j] = g2_ref[c, j]
+        for target, source in ((b_right, b_right_ref), (b_down, b_down_ref), (g, g2_ref.at[c])):
+            for i in range(steps):
+                target.put(i, j, source[j, i * SUBS:(i + 1) * SUBS, :])
         first, second = first_late_ref[c * tiles + j], second_late_ref[c * tiles + j]
         for value, at in ((jnp.where(odd_row, first, second), HALO - LATE), (jnp.where(odd_row, second, first), HALO + rows)):
             done = 0
             while done < LATE:
                 s, i = divmod(at + done, steps)
                 count = min(LATE - done, steps - i)
-                g_ref[j, pl.ds(i * SUBS + s, count, stride=SUBS), :] = value[done:done + count]
+                hot_ref[j, pl.ds(g.row(i) + s, count, stride=SLOTTED * SUBS), :] = value[done:done + count]
                 done += count
-    precondition(b_right_ref, b_down_ref, g_ref, f2_ref, work_ref)
+    precondition(b_right, b_down, g, z, work, Vectors(f2_ref))
 
 
 def combine(n0, n1, n2, n3):
@@ -534,7 +557,7 @@
     rows, cols = solution_hbm.shape[1:]
     own_tiles = cols // LANES
     tiles, height = scale_ref.shape[:2]
-    steps = (height - SPARE) // SUBS
+    steps = height // SUBS
     ways = ways_of(tiles)
     x0, x1, r0, r1, r2 = combine(*[jnp.broadcast_to(sums_ref[k:k + 1, :], (SUBS, LANES)) for k in range(4)])
     matrix = undealing(ways) if ways > 1 else None
@@ -656,15 +679,16 @@
     )(own, first_cols, second_cols)
 
     height = rows + 2 * HALO
-    plane = shaped(tiles, height + SPARE, LANES)
-    field = shaped(chans, tiles, height + SPARE, LANES)
+    plane = shaped(tiles, height, LANES)
+    field = shaped(chans, tiles, height, LANES)
+    hot = scratch(tiles, height * SLOTTED, LANES)
     lates = [shaped(chans * tiles + extra, LATE, LANES) for extra in (1, 0)]
     *basis, sums, first_late, second_late = pl.pallas_call(
         first_kernel,
         out_shape=[plane] * 4 + [field] * 5 + [shaped(SUBS, LANES)] + lates,
         in_specs=[in_vmem] * 6,
         out_specs=[in_vmem] * 12,
-        scratch_shapes=[scratch(planes, tiles, height, LANES), scratch(*plane.shape)],
+        scratch_shapes=[scratch(planes, tiles, height, LANES), hot],
         compiler_params=params,
     )(inner, outer, second_rows, first_rows, second_corners, first_corners)
 
@@ -677,7 +701,7 @@
             out_shape=plane,
             in_specs=[in_vmem] * 5,
             out_specs=in_vmem,
-            scratch_shapes=[scratch(*plane.shape)] * 2,
+            scratch_shapes=[hot],
             compiler_params=params,
             cost_estimate=pl.CostEstimate(flops=10**8, bytes_accessed=10**7, transcendentals=0),
         )(first_late, second_late, b_right, b_down, g2)

time: 48.1 us -> 46.9 us (0.975)
  Pallas kernels: 22.2 us -> 20.9 us
    pallas_call x1, Pallas kernels: 11.4 us -> 10.4 us  [per_device(): pl.pallas_call(first_kernel, out_shape=[plane] * 4 + [field] * 5 + [shape...]
where the time goes in v14:
time: 46.9 us; the launch traced here: 46.7 us
  Pallas kernels  20.9 us (45%)
  starting transfers between devices  15.1 us (32%)
  waiting for transfers between devices  9.87 us (21%)
  between operations  0.77 us (2%)
    ppermute x8, starting transfers between devices, swap(): lax.ppermute((first, second)[k], axis, pairs[k])  12.2 us
    pallas_call x1, Pallas kernels, per_device(): pl.pallas_call(first_kernel, out_shape=[plane] * 4 + [field] * 5 + [shape...  10.4 us
    ppermute x8, waiting for transfers between devices, swap(): lax.ppermute((first, second)[k], axis, pairs[k])  7.28 us
    pallas_call x3, Pallas kernels, per_device(): pl.pallas_call(functools.partial(second_kernel, c), out_shape=plane, in_s...  4.08 us
    ppermute x3, starting transfers between devices, sum_over(): other = lax.ppermute(value, axis, pairs)  2.85 us
    pallas_call x1, Pallas kernels, per_device(): pl.pallas_call(third_kernel, out_shape=[shaped(chans, rows, cols)] * 3, i...  2.72 us
    ppermute x3, waiting for transfers between devices, sum_over(): other = lax.ppermute(value, axis, pairs)  2.59 us
    pallas_call x1, Pallas kernels, per_device(): pl.pallas_call(own_kernel, out_shape=[shaped(planes, own_tiles, rows, LAN...  1.63 us
  transfers between devices with their start and end apart: 11, of which 4 were waited for; matrix products, arithmetic and copies ran while one was open for 0% of the time, Pallas kernels for 13%

profile of v14, /device:TPU:0, one launch (start us, length us, event | category | flops | bytes accessed | tf_op | source)
XLA Modules:
  0.0 46.7 jit_solution(18314545230991187127)
XLA Ops:
  0.6 1.6 %shard_map.76 = (f32[6,8,64,128]{3,2,1,0:T(8,128)S(1)}, f32[6,8,16,128]{3,2,1,0:T(8,128)S(1)}, f32[6,8,16,128]{3,2,1,0:T(8,128)S(1)}, f32[2,64,128]{2,1,0:T(8,128)S(1)}, f32[2,64,128]{2,1,0:T(8,128)S(1)}) custom-call(s32[3,1,16]{2,1,0:T(1,128)} %bitcast.5, f32[3,64,1024]{2,1,0:T(8,128)} %src_hbm.1, f32[64,1024]{1,0:T(8,128)} %weight_hbm.1, ...), custom_call_target="tpu_custom_call" | custom-call | tf_op jit(solution)/shard_map/pallas_call | solution.py:622
  2.3 0.7 %collective-permute-start.2 = (f32[6,8,16,128]{3,2,1,0:T(8,128)S(1)}, f32[6,8,16,128]{3,2,1,0:T(8,128)S(1)}, u32[]{:S(2)}, u32[]{:S(2)}) collective-permute-start(f32[6,8,16,128]{3,2,1,0:T(8,128)S(1)} %get-tuple-element.37), channel_id=1, source_target_pairs={{4,8},{8,4},{5,9},{9,5},{6,10},{10,6},{7,11},{11,7},{20,24},{24,20... | collective-permute-start | bytes 1179656 | tf_op jit(solution)/shard_map/ppermute | solution.py:649
  3.0 5.9 %collective-permute-start.3 = (f32[6,8,16,128]{3,2,1,0:T(8,128)S(1)}, f32[6,8,16,128]{3,2,1,0:T(8,128)S(1)}, u32[]{:S(2)}, u32[]{:S(2)}) collective-permute-start(f32[6,8,16,128]{3,2,1,0:T(8,128)S(1)} %get-tuple-element.38), channel_id=1, source_target_pairs={{0,4},{8,12},{4,0},{12,8},{1,5},{9,13},{5,1},{13,9},{2,6},{10,14},... | collective-permute-start | bytes 1179656 | tf_op jit(solution)/shard_map/ppermute | solution.py:649
  8.9 0.0 collective-permute-start
  8.9 0.7 %collective-permute-start.1 = (f32[2,64,128]{2,1,0:T(8,128)S(1)}, f32[2,64,128]{2,1,0:T(8,128)S(1)}, u32[]{:S(2)}, u32[]{:S(2)}) collective-permute-start(f32[2,64,128]{2,1,0:T(8,128)S(1)} %get-tuple-element.32), channel_id=1, source_target_pairs={{1,2},{2,1},{5,6},{6,5},{9,10},{10,9},{13,14},{14,13},{17,18},{18,... | collective-permute-start | bytes 196616 | tf_op jit(solution)/shard_map/ppermute | solution.py:649
  9.5 1.3 %shard_map.77.inner_ref = f32[6,6,64,128]{3,2,1,0:T(8,128)S(1)} custom-call(f32[6,8,64,128]{3,2,1,0:T(8,128)S(1)} %get-tuple-element.33.own_ref), custom_call_target="tpu_custom_call" | custom-call | flops 100000000 | bytes 4000000 | tf_op jit(solution)/shard_map/pallas_call | solution.py:653
  10.8 0.0 collective-permute-done.first_ref
  10.8 0.0 collective-permute-done.1.second_ref
  10.8 0.1 shard_map.79
  10.9 0.7 %collective-permute-start.4 = (f32[2,2,16,128]{3,2,1,0:T(8,128)S(1)}, f32[2,2,16,128]{3,2,1,0:T(8,128)S(1)}, u32[]{:S(2)}, u32[]{:S(2)}) collective-permute-start(f32[2,2,16,128]{3,2,1,0:T(8,128)S(1)} %get-tuple-element.39), channel_id=1, source_target_pairs={{4,8},{8,4},{5,9},{9,5},{6,10},{10,6},{7,11},{11,7},{20,24},{24,20... | collective-permute-start | bytes 98312 | tf_op jit(solution)/shard_map/ppermute | solution.py:649
  11.5 1.9 %collective-permute-start.5 = (f32[2,2,16,128]{3,2,1,0:T(8,128)S(1)}, f32[2,2,16,128]{3,2,1,0:T(8,128)S(1)}, u32[]{:S(2)}, u32[]{:S(2)}) collective-permute-start(f32[2,2,16,128]{3,2,1,0:T(8,128)S(1)} %get-tuple-element.40), channel_id=1, source_target_pairs={{0,4},{8,12},{4,0},{12,8},{1,5},{9,13},{5,1},{13,9},{2,6},{10,14},... | collective-permute-start | bytes 98312 | tf_op jit(solution)/shard_map/ppermute | solution.py:649
  13.4 0.8 %shard_map.78.outer_ref = f32[6,3,64,128]{3,2,1,0:T(8,128)S(1)} custom-call(f32[6,8,64,128]{3,2,1,0:T(8,128)S(1)} %get-tuple-element.33.own_ref, f32[2,64,128]{2,1,0:T(8,128)S(1)} %collective-permute-done.first_ref, f32[2,64,128]{2,1,0:T(8,128)S(1)} %collective-permute-done.1.second_ref), custom_call_target="tpu_custom_call" | custom-call | flops 100000000 | bytes 2000000 | tf_op jit(solution)/shard_map/pallas_call | solution.py:672
  14.2 0.0 collective-permute-done.4.second_corners_ref
  14.2 3.9 %collective-permute-done.5.first_corners_ref = f32[2,2,16,128]{3,2,1,0:T(8,128)S(1)} collective-permute-done((f32[2,2,16,128]{3,2,1,0:T(8,128)S(1)}, f32[2,2,16,128]{3,2,1,0:T(8,128)S(1)}, u32[]{:S(2)}, u32[]{:S(2)}) %collective-permute-start.5) | collective-permute-done | bytes 32800 | tf_op jit(solution)/shard_map/ppermute | solution.py:649
  18.0 0.0 collective-permute-done.2.second_rows_ref
  18.0 0.0 collective-permute-done.3.first_rows_ref
  18.0 10.4 %shard_map.80 = (f32[9,96,128]{2,1,0:T(8,128)S(1)}, f32[9,96,128]{2,1,0:T(8,128)S(1)}, f32[9,96,128]{2,1,0:T(8,128)S(1)}, f32[9,96,128]{2,1,0:T(8,128)S(1)}, f32...) custom-call(f32[6,6,64,128]{3,2,1,0:T(8,128)S(1)} %shard_map.77.inne, ...), custom_call_target="tpu_custom_call" | custom-call | tf_op jit(solution)/shard_map/pallas_call | solution.py:686
  28.5 1.8 %collective-permute-start.6 = (f32[28,8,128]{2,1,0:T(8,128)S(1)}, f32[28,8,128]{2,1,0:T(8,128)S(1)}, u32[]{:S(2)}, u32[]{:S(2)}) collective-permute-start(f32[28,8,128]{2,1,0:T(8,128)S(1)} %get-tuple-element.42), channel_id=1, source_target_pairs={{0,4},{8,12},{4,0},{12,8},{1,5},{9,13},{5,1},{13,9},{2,6},{10,14},... | collective-permute-start | bytes 344072 | tf_op jit(solution)/shard_map/ppermute | solution.py:649
  30.3 0.7 %collective-permute-start.7 = (f32[27,8,128]{2,1,0:T(8,128)S(1)}, f32[27,8,128]{2,1,0:T(8,128)S(1)}, u32[]{:S(2)}, u32[]{:S(2)}) collective-permute-start(f32[27,8,128]{2,1,0:T(8,128)S(1)} %get-tuple-element.43), channel_id=1, source_target_pairs={{4,8},{8,4},{5,9},{9,5},{6,10},{10,6},{7,11},{11,7},{20,24},{24,20... | collective-permute-start | bytes 331784 | tf_op jit(solution)/shard_map/ppermute | solution.py:649
  30.9 3.4 %collective-permute-done.6.first_late_ref = f32[28,8,128]{2,1,0:T(8,128)S(1)} collective-permute-done((f32[28,8,128]{2,1,0:T(8,128)S(1)}, f32[28,8,128]{2,1,0:T(8,128)S(1)}, u32[]{:S(2)}, u32[]{:S(2)}) %collective-permute-start.6) | collective-permute-done | bytes 114720 | tf_op jit(solution)/shard_map/ppermute | solution.py:649
  34.3 1.2 %collective-permute-start.8 = (f32[8,128]{1,0:T(8,128)S(1)}, f32[8,128]{1,0:T(8,128)S(1)}, u32[]{:S(2)}, u32[]{:S(2)}) collective-permute-start(f32[8,128]{1,0:T(8,128)S(1)} %fusion), channel_id=1, source_target_pairs={{0,8},{4,12},{8,0},{12,4},{1,9},{5,13},{9,1},{13,5},{2,10},{6,14},... | collective-permute-start | bytes 12296 | tf_op jit(solution)/shard_map/ppermute | solution.py:597
  35.6 0.0 collective-permute-done.7.second_late_ref
  35.6 1.4 %shard_map.81.refs_0_ = f32[9,96,128]{2,1,0:T(8,128)S(1)} custom-call(f32[28,8,128]{2,1,0:T(8,128)S(1)} %collective-permute-done.6.first_late_ref, f32[27,8,128]{2,1,0:T(8,128)S(1)} %collective-permute-done.7.second_late_ref, f32[9,96,128]{2,1,0:T(8,128)S(1)} %get-tuple-element.44.b_right_ref, f32[9,96,128]{2,1,0:T(8,128)S(1)} %get-tuple-element.45.b_down_ref, ...), custom_call_target="tpu_custom_call" | custom-call | flops 100000000 | bytes 10000000 | tf_op jit(solution)/shard_map/pallas_call | solution.py:699
  36.9 1.9 %collective-permute-done.8 = f32[8,128]{1,0:T(8,128)S(1)} collective-permute-done((f32[8,128]{1,0:T(8,128)S(1)}, f32[8,128]{1,0:T(8,128)S(1)}, u32[]{:S(2)}, u32[]{:S(2)}) %collective-permute-start.8) | collective-permute-done | bytes 4128 | tf_op jit(solution)/shard_map/ppermute | solution.py:597
  38.9 0.0 collective-permute-start.9
  38.9 1.4 %shard_map.82.refs_1_ = f32[9,96,128]{2,1,0:T(8,128)S(1)} custom-call(f32[28,8,128]{2,1,0:T(8,128)S(1)} %collective-permute-done.6.first_late_ref, f32[27,8,128]{2,1,0:T(8,128)S(1)} %collective-permute-done.7.second_late_ref, f32[9,96,128]{2,1,0:T(8,128)S(1)} %get-tuple-element.44.b_right_ref, f32[9,96,128]{2,1,0:T(8,128)S(1)} %get-tuple-element.45.b_down_ref, ...), custom_call_target="tpu_custom_call" | custom-call | flops 100000000 | bytes 10000000 | tf_op jit(solution)/shard_map/pallas_call | solution.py:699
  40.2 0.0 collective-permute-done.9
  40.3 1.6 %collective-permute-start.10 = (f32[8,128]{1,0:T(8,128)S(1)}, f32[8,128]{1,0:T(8,128)S(1)}, u32[]{:S(2)}, u32[]{:S(2)}) collective-permute-start(f32[8,128]{1,0:T(8,128)S(1)} %add.14), channel_id=1, source_target_pairs={{0,2},{1,3},{2,0},{3,1},{4,6},{5,7},{6,4},{7,5},{8,10},{9,11},{10,... | collective-permute-start | bytes 12296 | tf_op jit(solution)/shard_map/ppermute | solution.py:597
  41.9 1.4 %shard_map.83.refs_2_ = f32[9,96,128]{2,1,0:T(8,128)S(1)} custom-call(f32[28,8,128]{2,1,0:T(8,128)S(1)} %collective-permute-done.6.first_late_ref, f32[27,8,128]{2,1,0:T(8,128)S(1)} %collective-permute-done.7.second_late_ref, f32[9,96,128]{2,1,0:T(8,128)S(1)} %get-tuple-element.44.b_right_ref, f32[9,96,128]{2,1,0:T(8,128)S(1)} %get-tuple-element.45.b_down_ref, ...), custom_call_target="tpu_custom_call" | custom-call | flops 100000000 | bytes 10000000 | tf_op jit(solution)/shard_map/pallas_call | solution.py:699
  43.3 0.7 %collective-permute-done.10 = f32[8,128]{1,0:T(8,128)S(1)} collective-permute-done((f32[8,128]{1,0:T(8,128)S(1)}, f32[8,128]{1,0:T(8,128)S(1)}, u32[]{:S(2)}, u32[]{:S(2)}) %collective-permute-start.10) | collective-permute-done | bytes 4128 | tf_op jit(solution)/shard_map/ppermute | solution.py:597
  43.9 2.7 %shard_map.84 = (f32[3,64,1024]{2,1,0:T(8,128)}, f32[3,64,1024]{2,1,0:T(8,128)}, f32[3,64,1024]{2,1,0:T(8,128)}) custom-call(f32[8,128]{1,0:T(8,128)S(1)} %add.15.sums_ref, f32[9,96,128]{2,1,0:T(8,128)S(1)} %get-tuple-element.50.scale_ref, f32[9,96,128]{2,1,0:T(8,128)S(1)} %get-tuple-element.51.root_ref, f32[3,9,96,128]{3,2,1,0:T(8,128)S(1)} %get-tuple-element.52.g0_ref, ...), custom_call_target="tpu_custom_call" | custom-call | tf_op jit(solution)/shard_map/pallas_call | solution.py:721
  (4 shorter events, 0.0 us)
Async XLA Ops:
  2.3 15.8 %collective-permute-start.2 = (f32[6,8,16,128]{3,2,1,0:T(8,128)S(1)}, f32[6,8,16,128]{3,2,1,0:T(8,128)S(1)}, u32[]{:S(2)}, u32[]{:S(2)}) collective-permute-start(f32[6,8,16,128]{3,2,1,0:T(8,128)S(1)} %get-tuple-element.37), channel_id=1, source_target_pairs={{4,8},{8,4},{5,9},{9,5},{6,10},{10,6},{7,11},{11,7},{20,24},{24,20... | collective-permute-start | bytes 1179656 | tf_op jit(solution)/shard_map/ppermute | solution.py:649
  3.0 15.1 %collective-permute-start.3 = (f32[6,8,16,128]{3,2,1,0:T(8,128)S(1)}, f32[6,8,16,128]{3,2,1,0:T(8,128)S(1)}, u32[]{:S(2)}, u32[]{:S(2)}) collective-permute-start(f32[6,8,16,128]{3,2,1,0:T(8,128)S(1)} %get-tuple-element.38), channel_id=1, source_target_pairs={{0,4},{8,12},{4,0},{12,8},{1,5},{9,13},{5,1},{13,9},{2,6},{10,14},... | collective-permute-start | bytes 1179656 | tf_op jit(solution)/shard_map/ppermute | solution.py:649
  8.9 1.9 %collective-permute-start = (f32[2,64,128]{2,1,0:T(8,128)S(1)}, f32[2,64,128]{2,1,0:T(8,128)S(1)}, u32[]{:S(2)}, u32[]{:S(2)}) collective-permute-start(f32[2,64,128]{2,1,0:T(8,128)S(1)} %get-tuple-element.31), channel_id=1, source_target_pairs={{0,1},{2,3},{1,0},{3,2},{4,5},{6,7},{5,4},{7,6},{8,9},{10,11},{9,8... | collective-permute-start | bytes 196616 | tf_op jit(solution)/shard_map/ppermute | solution.py:649
  8.9 1.9 %collective-permute-start.1 = (f32[2,64,128]{2,1,0:T(8,128)S(1)}, f32[2,64,128]{2,1,0:T(8,128)S(1)}, u32[]{:S(2)}, u32[]{:S(2)}) collective-permute-start(f32[2,64,128]{2,1,0:T(8,128)S(1)} %get-tuple-element.32), channel_id=1, source_target_pairs={{1,2},{2,1},{5,6},{6,5},{9,10},{10,9},{13,14},{14,13},{17,18},{18,... | collective-permute-start | bytes 196616 | tf_op jit(solution)/shard_map/ppermute | solution.py:649
  10.9 3.3 %collective-permute-start.4 = (f32[2,2,16,128]{3,2,1,0:T(8,128)S(1)}, f32[2,2,16,128]{3,2,1,0:T(8,128)S(1)}, u32[]{:S(2)}, u32[]{:S(2)}) collective-permute-start(f32[2,2,16,128]{3,2,1,0:T(8,128)S(1)} %get-tuple-element.39), channel_id=1, source_target_pairs={{4,8},{8,4},{5,9},{9,5},{6,10},{10,6},{7,11},{11,7},{20,24},{24,20... | collective-permute-start | bytes 98312 | tf_op jit(solution)/shard_map/ppermute | solution.py:649
  11.5 6.5 %collective-permute-start.5 = (f32[2,2,16,128]{3,2,1,0:T(8,128)S(1)}, f32[2,2,16,128]{3,2,1,0:T(8,128)S(1)}, u32[]{:S(2)}, u32[]{:S(2)}) collective-permute-start(f32[2,2,16,128]{3,2,1,0:T(8,128)S(1)} %get-tuple-element.40), channel_id=1, source_target_pairs={{0,4},{8,12},{4,0},{12,8},{1,5},{9,13},{5,1},{13,9},{2,6},{10,14},... | collective-permute-start | bytes 98312 | tf_op jit(solution)/shard_map/ppermute | solution.py:649
  28.5 5.9 %collective-permute-start.6 = (f32[28,8,128]{2,1,0:T(8,128)S(1)}, f32[28,8,128]{2,1,0:T(8,128)S(1)}, u32[]{:S(2)}, u32[]{:S(2)}) collective-permute-start(f32[28,8,128]{2,1,0:T(8,128)S(1)} %get-tuple-element.42), channel_id=1, source_target_pairs={{0,4},{8,12},{4,0},{12,8},{1,5},{9,13},{5,1},{13,9},{2,6},{10,14},... | collective-permute-start | bytes 344072 | tf_op jit(solution)/shard_map/ppermute | solution.py:649
  30.3 5.3 %collective-permute-start.7 = (f32[27,8,128]{2,1,0:T(8,128)S(1)}, f32[27,8,128]{2,1,0:T(8,128)S(1)}, u32[]{:S(2)}, u32[]{:S(2)}) collective-permute-start(f32[27,8,128]{2,1,0:T(8,128)S(1)} %get-tuple-element.43), channel_id=1, source_target_pairs={{4,8},{8,4},{5,9},{9,5},{6,10},{10,6},{7,11},{11,7},{20,24},{24,20... | collective-permute-start | bytes 331784 | tf_op jit(solution)/shard_map/ppermute | solution.py:649
  34.3 4.5 %collective-permute-start.8 = (f32[8,128]{1,0:T(8,128)S(1)}, f32[8,128]{1,0:T(8,128)S(1)}, u32[]{:S(2)}, u32[]{:S(2)}) collective-permute-start(f32[8,128]{1,0:T(8,128)S(1)} %fusion), channel_id=1, source_target_pairs={{0,8},{4,12},{8,0},{12,4},{1,9},{5,13},{9,1},{13,5},{2,10},{6,14},... | collective-permute-start | bytes 12296 | tf_op jit(solution)/shard_map/ppermute | solution.py:597
  38.9 1.4 %collective-permute-start.9 = (f32[8,128]{1,0:T(8,128)S(1)}, f32[8,128]{1,0:T(8,128)S(1)}, u32[]{:S(2)}, u32[]{:S(2)}) collective-permute-start(f32[8,128]{1,0:T(8,128)S(1)} %add.13), channel_id=1, source_target_pairs={{0,1},{1,0},{2,3},{3,2},{4,5},{5,4},{6,7},{7,6},{8,9},{9,8},{10,11... | collective-permute-start | bytes 12296 | tf_op jit(solution)/shard_map/ppermute | solution.py:597
  40.3 3.7 %collective-permute-start.10 = (f32[8,128]{1,0:T(8,128)S(1)}, f32[8,128]{1,0:T(8,128)S(1)}, u32[]{:S(2)}, u32[]{:S(2)}) collective-permute-start(f32[8,128]{1,0:T(8,128)S(1)} %add.14), channel_id=1, source_target_pairs={{0,2},{1,3},{2,0},{3,1},{4,6},{5,7},{6,4},{7,5},{8,10},{9,11},{10,... | collective-permute-start | bytes 12296 | tf_op jit(solution)/shard_map/ppermute | solution.py:597

commit v15 on v13

--- a/solution.py
+++ b/solution.py
@@ -15,7 +15,6 @@
 LATE = 8
 SLOT = 32
 SLOTS = LANES // SLOT
-SPARE = 8
 WAYS = 3
 
 seam_damping = 0.8
@@ -289,7 +288,7 @@
 
 def spread(b_right_ref, b_down_ref, z_ref, emit):
     tiles, height = z_ref.shape[:2]
-    steps = (height - SPARE) // SUBS
+    steps = height // SUBS
     ways = ways_of(tiles)
     lane = lane_index()
     first, last = (lane == 0, lane == LANES - 1)
@@ -363,7 +362,7 @@
 
 def next_residual(b_right_ref, b_down_ref, g_ref, z_ref, next_ref, own_of):
     height = g_ref.shape[1]
-    steps = (height - SPARE) // SUBS
+    steps = height // SUBS
     sums = {}
 
     def emit(i, j, centre, moved):
@@ -493,8 +492,8 @@
     c, first_late_ref, second_late_ref, b_right_ref, b_down_ref, g2_ref, f2_ref, g_ref, work_ref
 ):
     tiles, height = b_right_ref.shape[:2]
-    rows = height - SPARE - 2 * HALO
-    steps = (height - SPARE) // SUBS
+    rows = height - 2 * HALO
+    steps = height // SUBS
     odd_row = odd("row")
     for j in range(tiles):
         g_ref[j] = g2_ref[c, j]
@@ -534,7 +533,7 @@
     rows, cols = solution_hbm.shape[1:]
     own_tiles = cols // LANES
     tiles, height = scale_ref.shape[:2]
-    steps = (height - SPARE) // SUBS
+    steps = height // SUBS
     ways = ways_of(tiles)
     x0, x1, r0, r1, r2 = combine(*[jnp.broadcast_to(sums_ref[k:k + 1, :], (SUBS, LANES)) for k in range(4)])
     matrix = undealing(ways) if ways > 1 else None
@@ -656,8 +655,8 @@
     )(own, first_cols, second_cols)
 
     height = rows + 2 * HALO
-    plane = shaped(tiles, height + SPARE, LANES)
-    field = shaped(chans, tiles, height + SPARE, LANES)
+    plane = shaped(tiles, height, LANES)
+    field = shaped(chans, tiles, height, LANES)
     lates = [shaped(chans * tiles + extra, LATE, LANES) for extra in (1, 0)]
     *basis, sums, first_late, second_late = pl.pallas_call(
         first_kernel,

time: 48.1 us -> 46.5 us (0.967)
  Pallas kernels: 22.2 us -> 20.5 us
    pallas_call x1, Pallas kernels: 11.4 us -> 10.1 us  [per_device(): pl.pallas_call(first_kernel, out_shape=[plane] * 4 + [field] * 5 + [shape...]
where the time goes in v15:
time: 46.5 us; the launch traced here: 46.3 us
  Pallas kernels  20.5 us (44%)
  starting transfers between devices  15.1 us (32%)
  waiting for transfers between devices  9.99 us (21%)
  between operations  0.76 us (2%)
    ppermute x8, starting transfers between devices, swap(): lax.ppermute((first, second)[k], axis, pairs[k])  12.2 us
    pallas_call x1, Pallas kernels, per_device(): pl.pallas_call(first_kernel, out_shape=[plane] * 4 + [field] * 5 + [shape...  10.1 us
    ppermute x8, waiting for transfers between devices, swap(): lax.ppermute((first, second)[k], axis, pairs[k])  7.28 us
    pallas_call x3, Pallas kernels, per_device(): pl.pallas_call(functools.partial(second_kernel, c), out_shape=plane, in_s...  3.86 us
    ppermute x3, starting transfers between devices, sum_over(): other = lax.ppermute(value, axis, pairs)  2.85 us
    pallas_call x1, Pallas kernels, per_device(): pl.pallas_call(third_kernel, out_shape=[shaped(chans, rows, cols)] * 3, i...  2.72 us
    ppermute x3, waiting for transfers between devices, sum_over(): other = lax.ppermute(value, axis, pairs)  2.71 us
    pallas_call x1, Pallas kernels, per_device(): pl.pallas_call(own_kernel, out_shape=[shaped(planes, own_tiles, rows, LAN...  1.63 us
  transfers between devices with their start and end apart: 11, of which 4 were waited for; matrix products, arithmetic and copies ran while one was open for 0% of the time, Pallas kernels for 13%

profile of v15, /device:TPU:0, one launch (start us, length us, event | category | flops | bytes accessed | tf_op | source)
XLA Modules:
  0.0 46.3 jit_solution(8921114412271825831)
XLA Ops:
  0.6 1.6 %shard_map.76 = (f32[6,8,64,128]{3,2,1,0:T(8,128)S(1)}, f32[6,8,16,128]{3,2,1,0:T(8,128)S(1)}, f32[6,8,16,128]{3,2,1,0:T(8,128)S(1)}, f32[2,64,128]{2,1,0:T(8,128)S(1)}, f32[2,64,128]{2,1,0:T(8,128)S(1)}) custom-call(s32[3,1,16]{2,1,0:T(1,128)} %bitcast.5, f32[3,64,1024]{2,1,0:T(8,128)} %src_hbm.1, f32[64,1024]{1,0:T(8,128)} %weight_hbm.1, ...), custom_call_target="tpu_custom_call" | custom-call | tf_op jit(solution)/shard_map/pallas_call | solution.py:598
  2.3 0.7 %collective-permute-start.2 = (f32[6,8,16,128]{3,2,1,0:T(8,128)S(1)}, f32[6,8,16,128]{3,2,1,0:T(8,128)S(1)}, u32[]{:S(2)}, u32[]{:S(2)}) collective-permute-start(f32[6,8,16,128]{3,2,1,0:T(8,128)S(1)} %get-tuple-element.37), channel_id=1, source_target_pairs={{4,8},{8,4},{5,9},{9,5},{6,10},{10,6},{7,11},{11,7},{20,24},{24,20... | collective-permute-start | bytes 1179656 | tf_op jit(solution)/shard_map/ppermute | solution.py:625
  3.0 5.9 %collective-permute-start.3 = (f32[6,8,16,128]{3,2,1,0:T(8,128)S(1)}, f32[6,8,16,128]{3,2,1,0:T(8,128)S(1)}, u32[]{:S(2)}, u32[]{:S(2)}) collective-permute-start(f32[6,8,16,128]{3,2,1,0:T(8,128)S(1)} %get-tuple-element.38), channel_id=1, source_target_pairs={{0,4},{8,12},{4,0},{12,8},{1,5},{9,13},{5,1},{13,9},{2,6},{10,14},... | collective-permute-start | bytes 1179656 | tf_op jit(solution)/shard_map/ppermute | solution.py:625
  8.9 0.0 collective-permute-start
  8.9 0.7 %collective-permute-start.1 = (f32[2,64,128]{2,1,0:T(8,128)S(1)}, f32[2,64,128]{2,1,0:T(8,128)S(1)}, u32[]{:S(2)}, u32[]{:S(2)}) collective-permute-start(f32[2,64,128]{2,1,0:T(8,128)S(1)} %get-tuple-element.32), channel_id=1, source_target_pairs={{1,2},{2,1},{5,6},{6,5},{9,10},{10,9},{13,14},{14,13},{17,18},{18,... | collective-permute-start | bytes 196616 | tf_op jit(solution)/shard_map/ppermute | solution.py:625
  9.5 1.3 %shard_map.77.inner_ref = f32[6,6,64,128]{3,2,1,0:T(8,128)S(1)} custom-call(f32[6,8,64,128]{3,2,1,0:T(8,128)S(1)} %get-tuple-element.33.own_ref), custom_call_target="tpu_custom_call" | custom-call | flops 100000000 | bytes 4000000 | tf_op jit(solution)/shard_map/pallas_call | solution.py:629
  10.8 0.0 collective-permute-done.first_ref
  10.8 0.0 collective-permute-done.1.second_ref
  10.8 0.1 shard_map.79
  10.9 0.7 %collective-permute-start.4 = (f32[2,2,16,128]{3,2,1,0:T(8,128)S(1)}, f32[2,2,16,128]{3,2,1,0:T(8,128)S(1)}, u32[]{:S(2)}, u32[]{:S(2)}) collective-permute-start(f32[2,2,16,128]{3,2,1,0:T(8,128)S(1)} %get-tuple-element.39), channel_id=1, source_target_pairs={{4,8},{8,4},{5,9},{9,5},{6,10},{10,6},{7,11},{11,7},{20,24},{24,20... | collective-permute-start | bytes 98312 | tf_op jit(solution)/shard_map/ppermute | solution.py:625
  11.5 1.9 %collective-permute-start.5 = (f32[2,2,16,128]{3,2,1,0:T(8,128)S(1)}, f32[2,2,16,128]{3,2,1,0:T(8,128)S(1)}, u32[]{:S(2)}, u32[]{:S(2)}) collective-permute-start(f32[2,2,16,128]{3,2,1,0:T(8,128)S(1)} %get-tuple-element.40), channel_id=1, source_target_pairs={{0,4},{8,12},{4,0},{12,8},{1,5},{9,13},{5,1},{13,9},{2,6},{10,14},... | collective-permute-start | bytes 98312 | tf_op jit(solution)/shard_map/ppermute | solution.py:625
  13.4 0.8 %shard_map.78.outer_ref = f32[6,3,64,128]{3,2,1,0:T(8,128)S(1)} custom-call(f32[6,8,64,128]{3,2,1,0:T(8,128)S(1)} %get-tuple-element.33.own_ref, f32[2,64,128]{2,1,0:T(8,128)S(1)} %collective-permute-done.first_ref, f32[2,64,128]{2,1,0:T(8,128)S(1)} %collective-permute-done.1.second_ref), custom_call_target="tpu_custom_call" | custom-call | flops 100000000 | bytes 2000000 | tf_op jit(solution)/shard_map/pallas_call | solution.py:648
  14.2 0.0 collective-permute-done.4.second_corners_ref
  14.2 3.9 %collective-permute-done.5.first_corners_ref = f32[2,2,16,128]{3,2,1,0:T(8,128)S(1)} collective-permute-done((f32[2,2,16,128]{3,2,1,0:T(8,128)S(1)}, f32[2,2,16,128]{3,2,1,0:T(8,128)S(1)}, u32[]{:S(2)}, u32[]{:S(2)}) %collective-permute-start.5) | collective-permute-done | bytes 32800 | tf_op jit(solution)/shard_map/ppermute | solution.py:625
  18.0 0.0 collective-permute-done.2.second_rows_ref
  18.0 0.0 collective-permute-done.3.first_rows_ref
  18.0 10.1 %shard_map.80 = (f32[9,96,128]{2,1,0:T(8,128)S(1)}, f32[9,96,128]{2,1,0:T(8,128)S(1)}, f32[9,96,128]{2,1,0:T(8,128)S(1)}, f32[9,96,128]{2,1,0:T(8,128)S(1)}, f32...) custom-call(f32[6,6,64,128]{3,2,1,0:T(8,128)S(1)} %shard_map.77.inne, ...), custom_call_target="tpu_custom_call" | custom-call | tf_op jit(solution)/shard_map/pallas_call | solution.py:661
  28.2 1.8 %collective-permute-start.6 = (f32[28,8,128]{2,1,0:T(8,128)S(1)}, f32[28,8,128]{2,1,0:T(8,128)S(1)}, u32[]{:S(2)}, u32[]{:S(2)}) collective-permute-start(f32[28,8,128]{2,1,0:T(8,128)S(1)} %get-tuple-element.42), channel_id=1, source_target_pairs={{0,4},{8,12},{4,0},{12,8},{1,5},{9,13},{5,1},{13,9},{2,6},{10,14},... | collective-permute-start | bytes 344072 | tf_op jit(solution)/shard_map/ppermute | solution.py:625
  30.0 0.7 %collective-permute-start.7 = (f32[27,8,128]{2,1,0:T(8,128)S(1)}, f32[27,8,128]{2,1,0:T(8,128)S(1)}, u32[]{:S(2)}, u32[]{:S(2)}) collective-permute-start(f32[27,8,128]{2,1,0:T(8,128)S(1)} %get-tuple-element.43), channel_id=1, source_target_pairs={{4,8},{8,4},{5,9},{9,5},{6,10},{10,6},{7,11},{11,7},{20,24},{24,20... | collective-permute-start | bytes 331784 | tf_op jit(solution)/shard_map/ppermute | solution.py:625
  30.7 3.4 %collective-permute-done.6.first_late_ref = f32[28,8,128]{2,1,0:T(8,128)S(1)} collective-permute-done((f32[28,8,128]{2,1,0:T(8,128)S(1)}, f32[28,8,128]{2,1,0:T(8,128)S(1)}, u32[]{:S(2)}, u32[]{:S(2)}) %collective-permute-start.6) | collective-permute-done | bytes 114720 | tf_op jit(solution)/shard_map/ppermute | solution.py:625
  34.1 1.2 %collective-permute-start.8 = (f32[8,128]{1,0:T(8,128)S(1)}, f32[8,128]{1,0:T(8,128)S(1)}, u32[]{:S(2)}, u32[]{:S(2)}) collective-permute-start(f32[8,128]{1,0:T(8,128)S(1)} %fusion), channel_id=1, source_target_pairs={{0,8},{4,12},{8,0},{12,4},{1,9},{5,13},{9,1},{13,5},{2,10},{6,14},... | collective-permute-start | bytes 12296 | tf_op jit(solution)/shard_map/ppermute | solution.py:573
  35.3 0.0 collective-permute-done.7.second_late_ref
  35.3 1.3 %shard_map.81.refs_0_ = f32[9,96,128]{2,1,0:T(8,128)S(1)} custom-call(f32[28,8,128]{2,1,0:T(8,128)S(1)} %collective-permute-done.6.first_late_ref, f32[27,8,128]{2,1,0:T(8,128)S(1)} %collective-permute-done.7.second_late_ref, f32[9,96,128]{2,1,0:T(8,128)S(1)} %get-tuple-element.44.b_right_ref, f32[9,96,128]{2,1,0:T(8,128)S(1)} %get-tuple-element.45.b_down_ref, ...), custom_call_target="tpu_custom_call" | custom-call | flops 100000000 | bytes 10000000 | tf_op jit(solution)/shard_map/pallas_call | solution.py:674
  36.6 1.9 %collective-permute-done.8 = f32[8,128]{1,0:T(8,128)S(1)} collective-permute-done((f32[8,128]{1,0:T(8,128)S(1)}, f32[8,128]{1,0:T(8,128)S(1)}, u32[]{:S(2)}, u32[]{:S(2)}) %collective-permute-start.8) | collective-permute-done | bytes 4128 | tf_op jit(solution)/shard_map/ppermute | solution.py:573
  38.6 0.0 collective-permute-start.9
  38.6 1.3 %shard_map.82.refs_1_ = f32[9,96,128]{2,1,0:T(8,128)S(1)} custom-call(f32[28,8,128]{2,1,0:T(8,128)S(1)} %collective-permute-done.6.first_late_ref, f32[27,8,128]{2,1,0:T(8,128)S(1)} %collective-permute-done.7.second_late_ref, f32[9,96,128]{2,1,0:T(8,128)S(1)} %get-tuple-element.44.b_right_ref, f32[9,96,128]{2,1,0:T(8,128)S(1)} %get-tuple-element.45.b_down_ref, ...), custom_call_target="tpu_custom_call" | custom-call | flops 100000000 | bytes 10000000 | tf_op jit(solution)/shard_map/pallas_call | solution.py:674
  39.9 0.0 collective-permute-done.9
  39.9 1.6 %collective-permute-start.10 = (f32[8,128]{1,0:T(8,128)S(1)}, f32[8,128]{1,0:T(8,128)S(1)}, u32[]{:S(2)}, u32[]{:S(2)}) collective-permute-start(f32[8,128]{1,0:T(8,128)S(1)} %add.14), channel_id=1, source_target_pairs={{0,2},{1,3},{2,0},{3,1},{4,6},{5,7},{6,4},{7,5},{8,10},{9,11},{10,... | collective-permute-start | bytes 12296 | tf_op jit(solution)/shard_map/ppermute | solution.py:573
  41.5 1.3 %shard_map.83.refs_2_ = f32[9,96,128]{2,1,0:T(8,128)S(1)} custom-call(f32[28,8,128]{2,1,0:T(8,128)S(1)} %collective-permute-done.6.first_late_ref, f32[27,8,128]{2,1,0:T(8,128)S(1)} %collective-permute-done.7.second_late_ref, f32[9,96,128]{2,1,0:T(8,128)S(1)} %get-tuple-element.44.b_right_ref, f32[9,96,128]{2,1,0:T(8,128)S(1)} %get-tuple-element.45.b_down_ref, ...), custom_call_target="tpu_custom_call" | custom-call | flops 100000000 | bytes 10000000 | tf_op jit(solution)/shard_map/pallas_call | solution.py:674
  42.8 0.8 %collective-permute-done.10 = f32[8,128]{1,0:T(8,128)S(1)} collective-permute-done((f32[8,128]{1,0:T(8,128)S(1)}, f32[8,128]{1,0:T(8,128)S(1)}, u32[]{:S(2)}, u32[]{:S(2)}) %collective-permute-start.10) | collective-permute-done | bytes 4128 | tf_op jit(solution)/shard_map/ppermute | solution.py:573
  43.6 2.7 %shard_map.84 = (f32[3,64,1024]{2,1,0:T(8,128)}, f32[3,64,1024]{2,1,0:T(8,128)}, f32[3,64,1024]{2,1,0:T(8,128)}) custom-call(f32[8,128]{1,0:T(8,128)S(1)} %add.15.sums_ref, f32[9,96,128]{2,1,0:T(8,128)S(1)} %get-tuple-element.50.scale_ref, f32[9,96,128]{2,1,0:T(8,128)S(1)} %get-tuple-element.51.root_ref, f32[3,9,96,128]{3,2,1,0:T(8,128)S(1)} %get-tuple-element.52.g0_ref, ...), custom_call_target="tpu_custom_call" | custom-call | tf_op jit(solution)/shard_map/pallas_call | solution.py:696
  (4 shorter events, 0.0 us)
Async XLA Ops:
  2.3 15.8 %collective-permute-start.2 = (f32[6,8,16,128]{3,2,1,0:T(8,128)S(1)}, f32[6,8,16,128]{3,2,1,0:T(8,128)S(1)}, u32[]{:S(2)}, u32[]{:S(2)}) collective-permute-start(f32[6,8,16,128]{3,2,1,0:T(8,128)S(1)} %get-tuple-element.37), channel_id=1, source_target_pairs={{4,8},{8,4},{5,9},{9,5},{6,10},{10,6},{7,11},{11,7},{20,24},{24,20... | collective-permute-start | bytes 1179656 | tf_op jit(solution)/shard_map/ppermute | solution.py:625
  3.0 15.1 %collective-permute-start.3 = (f32[6,8,16,128]{3,2,1,0:T(8,128)S(1)}, f32[6,8,16,128]{3,2,1,0:T(8,128)S(1)}, u32[]{:S(2)}, u32[]{:S(2)}) collective-permute-start(f32[6,8,16,128]{3,2,1,0:T(8,128)S(1)} %get-tuple-element.38), channel_id=1, source_target_pairs={{0,4},{8,12},{4,0},{12,8},{1,5},{9,13},{5,1},{13,9},{2,6},{10,14},... | collective-permute-start | bytes 1179656 | tf_op jit(solution)/shard_map/ppermute | solution.py:625
  8.9 1.9 %collective-permute-start = (f32[2,64,128]{2,1,0:T(8,128)S(1)}, f32[2,64,128]{2,1,0:T(8,128)S(1)}, u32[]{:S(2)}, u32[]{:S(2)}) collective-permute-start(f32[2,64,128]{2,1,0:T(8,128)S(1)} %get-tuple-element.31), channel_id=1, source_target_pairs={{0,1},{2,3},{1,0},{3,2},{4,5},{6,7},{5,4},{7,6},{8,9},{10,11},{9,8... | collective-permute-start | bytes 196616 | tf_op jit(solution)/shard_map/ppermute | solution.py:625
  8.9 1.9 %collective-permute-start.1 = (f32[2,64,128]{2,1,0:T(8,128)S(1)}, f32[2,64,128]{2,1,0:T(8,128)S(1)}, u32[]{:S(2)}, u32[]{:S(2)}) collective-permute-start(f32[2,64,128]{2,1,0:T(8,128)S(1)} %get-tuple-element.32), channel_id=1, source_target_pairs={{1,2},{2,1},{5,6},{6,5},{9,10},{10,9},{13,14},{14,13},{17,18},{18,... | collective-permute-start | bytes 196616 | tf_op jit(solution)/shard_map/ppermute | solution.py:625
  10.9 3.3 %collective-permute-start.4 = (f32[2,2,16,128]{3,2,1,0:T(8,128)S(1)}, f32[2,2,16,128]{3,2,1,0:T(8,128)S(1)}, u32[]{:S(2)}, u32[]{:S(2)}) collective-permute-start(f32[2,2,16,128]{3,2,1,0:T(8,128)S(1)} %get-tuple-element.39), channel_id=1, source_target_pairs={{4,8},{8,4},{5,9},{9,5},{6,10},{10,6},{7,11},{11,7},{20,24},{24,20... | collective-permute-start | bytes 98312 | tf_op jit(solution)/shard_map/ppermute | solution.py:625
  11.5 6.5 %collective-permute-start.5 = (f32[2,2,16,128]{3,2,1,0:T(8,128)S(1)}, f32[2,2,16,128]{3,2,1,0:T(8,128)S(1)}, u32[]{:S(2)}, u32[]{:S(2)}) collective-permute-start(f32[2,2,16,128]{3,2,1,0:T(8,128)S(1)} %get-tuple-element.40), channel_id=1, source_target_pairs={{0,4},{8,12},{4,0},{12,8},{1,5},{9,13},{5,1},{13,9},{2,6},{10,14},... | collective-permute-start | bytes 98312 | tf_op jit(solution)/shard_map/ppermute | solution.py:625
  28.2 5.9 %collective-permute-start.6 = (f32[28,8,128]{2,1,0:T(8,128)S(1)}, f32[28,8,128]{2,1,0:T(8,128)S(1)}, u32[]{:S(2)}, u32[]{:S(2)}) collective-permute-start(f32[28,8,128]{2,1,0:T(8,128)S(1)} %get-tuple-element.42), channel_id=1, source_target_pairs={{0,4},{8,12},{4,0},{12,8},{1,5},{9,13},{5,1},{13,9},{2,6},{10,14},... | collective-permute-start | bytes 344072 | tf_op jit(solution)/shard_map/ppermute | solution.py:625
  30.0 5.3 %collective-permute-start.7 = (f32[27,8,128]{2,1,0:T(8,128)S(1)}, f32[27,8,128]{2,1,0:T(8,128)S(1)}, u32[]{:S(2)}, u32[]{:S(2)}) collective-permute-start(f32[27,8,128]{2,1,0:T(8,128)S(1)} %get-tuple-element.43), channel_id=1, source_target_pairs={{4,8},{8,4},{5,9},{9,5},{6,10},{10,6},{7,11},{11,7},{20,24},{24,20... | collective-permute-start | bytes 331784 | tf_op jit(solution)/shard_map/ppermute | solution.py:625
  34.1 4.5 %collective-permute-start.8 = (f32[8,128]{1,0:T(8,128)S(1)}, f32[8,128]{1,0:T(8,128)S(1)}, u32[]{:S(2)}, u32[]{:S(2)}) collective-permute-start(f32[8,128]{1,0:T(8,128)S(1)} %fusion), channel_id=1, source_target_pairs={{0,8},{4,12},{8,0},{12,4},{1,9},{5,13},{9,1},{13,5},{2,10},{6,14},... | collective-permute-start | bytes 12296 | tf_op jit(solution)/shard_map/ppermute | solution.py:573
  38.6 1.3 %collective-permute-start.9 = (f32[8,128]{1,0:T(8,128)S(1)}, f32[8,128]{1,0:T(8,128)S(1)}, u32[]{:S(2)}, u32[]{:S(2)}) collective-permute-start(f32[8,128]{1,0:T(8,128)S(1)} %add.13), channel_id=1, source_target_pairs={{0,1},{1,0},{2,3},{3,2},{4,5},{5,4},{6,7},{7,6},{8,9},{9,8},{10,11... | collective-permute-start | bytes 12296 | tf_op jit(solution)/shard_map/ppermute | solution.py:573
  39.9 3.7 %collective-permute-start.10 = (f32[8,128]{1,0:T(8,128)S(1)}, f32[8,128]{1,0:T(8,128)S(1)}, u32[]{:S(2)}, u32[]{:S(2)}) collective-permute-start(f32[8,128]{1,0:T(8,128)S(1)} %add.14), channel_id=1, source_target_pairs={{0,2},{1,3},{2,0},{3,1},{4,6},{5,7},{6,4},{7,5},{8,10},{9,11},{10,... | collective-permute-start | bytes 12296 | tf_op jit(solution)/shard_map/ppermute | solution.py:573

commit v16 on v15

--- a/solution.py
+++ b/solution.py
@@ -567,14 +567,22 @@
         copy.wait()
 
 
-def sum_over(value, steps, beside):
+def sum_over(value, rounds, beside):
     done = []
-    for k, (axis, pairs) in enumerate(steps):
-        other = lax.ppermute(value, axis, pairs)
-        if len(steps) - k <= len(beside):
-            value, array = lax.optimization_barrier((value, beside[len(done)]))
-            done.append(array)
-        value = value + other
+    for k, (axis, bits) in enumerate(rounds):
+        size = lax.axis_size(axis)
+        others = [
+            lax.ppermute(value, axis, [(i, i ^ mask) for i in range(size)])
+            for mask in ((bits[0],) if len(bits) == 1 else (bits[0], bits[1], bits[0] | bits[1]))
+        ]
+        left = len(rounds) - k
+        if left <= len(beside):
+            now = beside[len(done):] if left == 1 else beside[len(done):len(done) + 1]
+            value, *arrays = lax.optimization_barrier((value, *now))
+            done += arrays
+        value = value + others[0]
+        if len(others) > 1:
+            value = value + (others[1] + others[2])
     return value, done + list(beside[len(done):])
 
 
@@ -685,14 +693,13 @@
     if row_axis & (row_axis - 1) or col_axis & (col_axis - 1):
         total = lax.psum(sums, ("row", "col"))
     else:
-        steps = [
-            (axis, [(i, i ^ (1 << k)) for i in range(size)])
-            for axis, size, low in (("row", row_axis, 1), ("col", col_axis, 0))
-            for k in range(low, size.bit_length() - 1)
-        ]
+        rounds = []
+        for axis, size, low in (("row", row_axis, 1), ("col", col_axis, 0)):
+            bits = [1 << k for k in range(low, size.bit_length() - 1)]
+            rounds += [(axis, bits[k:k + 2]) for k in range(0, len(bits), 2)]
         if row_axis > 1:
             sums = sums + first_late[chans * tiles]
-        total, f2 = sum_over(sums, steps, f2)
+        total, f2 = sum_over(sums, rounds, f2)
     return pl.pallas_call(
         third_kernel,
         out_shape=[shaped(chans, rows, cols)] * 3,

time: 46.5 us -> 46.3 us (level)
  waiting for transfers between devices: 9.99 us -> 8.24 us
  starting transfers between devices: 15.1 us -> 16.2 us
    ppermute x3 -> x4, waiting for transfers between devices: 2.71 us -> 0.96 us  [sum_over(): lax.ppermute(value, axis, [(i, i ^ mask) for i in range(size)])]
    ppermute x3 -> x4, starting transfers between devices: 2.85 us -> 3.95 us  [sum_over(): lax.ppermute(value, axis, [(i, i ^ mask) for i in range(size)])]
  transfers between devices with their start and end apart: 11 -> 12, of which waited for: 4 -> 4; matrix products, arithmetic and copies ran while one was open for 0% -> 0% of each run, Pallas kernels for 13% -> 13%
where the time goes in v16:
time: 46.3 us; the launch traced here: 45.6 us
  Pallas kernels  20.5 us (44%)
  starting transfers between devices  16.2 us (35%)
  waiting for transfers between devices  8.24 us (18%)
  between operations  0.75 us (2%)
    ppermute x8, starting transfers between devices, swap(): lax.ppermute((first, second)[k], axis, pairs[k])  12.2 us
    pallas_call x1, Pallas kernels, per_device(): pl.pallas_call(first_kernel, out_shape=[plane] * 4 + [field] * 5 + [shape...  10.1 us
    ppermute x8, waiting for transfers between devices, swap(): lax.ppermute((first, second)[k], axis, pairs[k])  7.28 us
    ppermute x4, starting transfers between devices, sum_over(): lax.ppermute(value, axis, [(i, i ^ mask) for i in range(size)])  3.95 us
    pallas_call x3, Pallas kernels, per_device(): pl.pallas_call(functools.partial(second_kernel, c), out_shape=plane, in_s...  3.86 us
    pallas_call x1, Pallas kernels, per_device(): pl.pallas_call(third_kernel, out_shape=[shaped(chans, rows, cols)] * 3, i...  2.72 us
    pallas_call x1, Pallas kernels, per_device(): pl.pallas_call(own_kernel, out_shape=[shaped(planes, own_tiles, rows, LAN...  1.63 us
    pallas_call x1, Pallas kernels, per_device(): pl.pallas_call(inner_dealt_kernel, out_shape=shaped(planes, tiles - ways,...  1.25 us
  transfers between devices with their start and end apart: 12, of which 4 were waited for; matrix products, arithmetic and copies ran while one was open for 0% of the time, Pallas kernels for 13%

profile of v16, /device:TPU:0, one launch (start us, length us, event | category | flops | bytes accessed | tf_op | source)
XLA Modules:
  0.0 45.6 jit_solution(1241170743578260542)
XLA Ops:
  0.6 1.6 %shard_map.76 = (f32[6,8,64,128]{3,2,1,0:T(8,128)S(1)}, f32[6,8,16,128]{3,2,1,0:T(8,128)S(1)}, f32[6,8,16,128]{3,2,1,0:T(8,128)S(1)}, f32[2,64,128]{2,1,0:T(8,128)S(1)}, f32[2,64,128]{2,1,0:T(8,128)S(1)}) custom-call(s32[3,1,16]{2,1,0:T(1,128)} %bitcast.5, f32[3,64,1024]{2,1,0:T(8,128)} %src_hbm.1, f32[64,1024]{1,0:T(8,128)} %weight_hbm.1, ...), custom_call_target="tpu_custom_call" | custom-call | tf_op jit(solution)/shard_map/pallas_call | solution.py:606
  2.3 0.7 %collective-permute-start.2 = (f32[6,8,16,128]{3,2,1,0:T(8,128)S(1)}, f32[6,8,16,128]{3,2,1,0:T(8,128)S(1)}, u32[]{:S(2)}, u32[]{:S(2)}) collective-permute-start(f32[6,8,16,128]{3,2,1,0:T(8,128)S(1)} %get-tuple-element.36), channel_id=1, source_target_pairs={{4,8},{8,4},{5,9},{9,5},{6,10},{10,6},{7,11},{11,7},{20,24},{24,20... | collective-permute-start | bytes 1179656 | tf_op jit(solution)/shard_map/ppermute | solution.py:633
  3.0 5.9 %collective-permute-start.3 = (f32[6,8,16,128]{3,2,1,0:T(8,128)S(1)}, f32[6,8,16,128]{3,2,1,0:T(8,128)S(1)}, u32[]{:S(2)}, u32[]{:S(2)}) collective-permute-start(f32[6,8,16,128]{3,2,1,0:T(8,128)S(1)} %get-tuple-element.37), channel_id=1, source_target_pairs={{0,4},{8,12},{4,0},{12,8},{1,5},{9,13},{5,1},{13,9},{2,6},{10,14},... | collective-permute-start | bytes 1179656 | tf_op jit(solution)/shard_map/ppermute | solution.py:633
  8.9 0.0 collective-permute-start
  8.9 0.7 %collective-permute-start.1 = (f32[2,64,128]{2,1,0:T(8,128)S(1)}, f32[2,64,128]{2,1,0:T(8,128)S(1)}, u32[]{:S(2)}, u32[]{:S(2)}) collective-permute-start(f32[2,64,128]{2,1,0:T(8,128)S(1)} %get-tuple-element.31), channel_id=1, source_target_pairs={{1,2},{2,1},{5,6},{6,5},{9,10},{10,9},{13,14},{14,13},{17,18},{18,... | collective-permute-start | bytes 196616 | tf_op jit(solution)/shard_map/ppermute | solution.py:633
  9.5 1.3 %shard_map.77.inner_ref = f32[6,6,64,128]{3,2,1,0:T(8,128)S(1)} custom-call(f32[6,8,64,128]{3,2,1,0:T(8,128)S(1)} %get-tuple-element.32.own_ref), custom_call_target="tpu_custom_call" | custom-call | flops 100000000 | bytes 4000000 | tf_op jit(solution)/shard_map/pallas_call | solution.py:637
  10.8 0.0 collective-permute-done.first_ref
  10.8 0.0 collective-permute-done.1.second_ref
  10.8 0.1 shard_map.79
  10.9 0.7 %collective-permute-start.4 = (f32[2,2,16,128]{3,2,1,0:T(8,128)S(1)}, f32[2,2,16,128]{3,2,1,0:T(8,128)S(1)}, u32[]{:S(2)}, u32[]{:S(2)}) collective-permute-start(f32[2,2,16,128]{3,2,1,0:T(8,128)S(1)} %get-tuple-element.38), channel_id=1, source_target_pairs={{4,8},{8,4},{5,9},{9,5},{6,10},{10,6},{7,11},{11,7},{20,24},{24,20... | collective-permute-start | bytes 98312 | tf_op jit(solution)/shard_map/ppermute | solution.py:633
  11.5 1.9 %collective-permute-start.5 = (f32[2,2,16,128]{3,2,1,0:T(8,128)S(1)}, f32[2,2,16,128]{3,2,1,0:T(8,128)S(1)}, u32[]{:S(2)}, u32[]{:S(2)}) collective-permute-start(f32[2,2,16,128]{3,2,1,0:T(8,128)S(1)} %get-tuple-element.39), channel_id=1, source_target_pairs={{0,4},{8,12},{4,0},{12,8},{1,5},{9,13},{5,1},{13,9},{2,6},{10,14},... | collective-permute-start | bytes 98312 | tf_op jit(solution)/shard_map/ppermute | solution.py:633
  13.4 0.8 %shard_map.78.outer_ref = f32[6,3,64,128]{3,2,1,0:T(8,128)S(1)} custom-call(f32[6,8,64,128]{3,2,1,0:T(8,128)S(1)} %get-tuple-element.32.own_ref, f32[2,64,128]{2,1,0:T(8,128)S(1)} %collective-permute-done.first_ref, f32[2,64,128]{2,1,0:T(8,128)S(1)} %collective-permute-done.1.second_ref), custom_call_target="tpu_custom_call" | custom-call | flops 100000000 | bytes 2000000 | tf_op jit(solution)/shard_map/pallas_call | solution.py:656
  14.2 0.0 collective-permute-done.4.second_corners_ref
  14.2 3.9 %collective-permute-done.5.first_corners_ref = f32[2,2,16,128]{3,2,1,0:T(8,128)S(1)} collective-permute-done((f32[2,2,16,128]{3,2,1,0:T(8,128)S(1)}, f32[2,2,16,128]{3,2,1,0:T(8,128)S(1)}, u32[]{:S(2)}, u32[]{:S(2)}) %collective-permute-start.5) | collective-permute-done | bytes 32800 | tf_op jit(solution)/shard_map/ppermute | solution.py:633
  18.0 0.0 collective-permute-done.2.second_rows_ref
  18.0 0.0 collective-permute-done.3.first_rows_ref
  18.0 10.1 %shard_map.80 = (f32[9,96,128]{2,1,0:T(8,128)S(1)}, f32[9,96,128]{2,1,0:T(8,128)S(1)}, f32[9,96,128]{2,1,0:T(8,128)S(1)}, f32[9,96,128]{2,1,0:T(8,128)S(1)}, f32...) custom-call(f32[6,6,64,128]{3,2,1,0:T(8,128)S(1)} %shard_map.77.inne, ...), custom_call_target="tpu_custom_call" | custom-call | tf_op jit(solution)/shard_map/pallas_call | solution.py:669
  28.2 1.8 %collective-permute-start.6 = (f32[28,8,128]{2,1,0:T(8,128)S(1)}, f32[28,8,128]{2,1,0:T(8,128)S(1)}, u32[]{:S(2)}, u32[]{:S(2)}) collective-permute-start(f32[28,8,128]{2,1,0:T(8,128)S(1)} %get-tuple-element.41), channel_id=1, source_target_pairs={{0,4},{8,12},{4,0},{12,8},{1,5},{9,13},{5,1},{13,9},{2,6},{10,14},... | collective-permute-start | bytes 344072 | tf_op jit(solution)/shard_map/ppermute | solution.py:633
  30.0 0.7 %collective-permute-start.7 = (f32[27,8,128]{2,1,0:T(8,128)S(1)}, f32[27,8,128]{2,1,0:T(8,128)S(1)}, u32[]{:S(2)}, u32[]{:S(2)}) collective-permute-start(f32[27,8,128]{2,1,0:T(8,128)S(1)} %get-tuple-element.42), channel_id=1, source_target_pairs={{4,8},{8,4},{5,9},{9,5},{6,10},{10,6},{7,11},{11,7},{20,24},{24,20... | collective-permute-start | bytes 331784 | tf_op jit(solution)/shard_map/ppermute | solution.py:633
  30.7 3.4 %collective-permute-done.6.first_late_ref = f32[28,8,128]{2,1,0:T(8,128)S(1)} collective-permute-done((f32[28,8,128]{2,1,0:T(8,128)S(1)}, f32[28,8,128]{2,1,0:T(8,128)S(1)}, u32[]{:S(2)}, u32[]{:S(2)}) %collective-permute-start.6) | collective-permute-done | bytes 114720 | tf_op jit(solution)/shard_map/ppermute | solution.py:633
  34.1 1.2 %collective-permute-start.8 = (f32[8,128]{1,0:T(8,128)S(1)}, f32[8,128]{1,0:T(8,128)S(1)}, u32[]{:S(2)}, u32[]{:S(2)}) collective-permute-start(f32[8,128]{1,0:T(8,128)S(1)} %fusion), channel_id=1, source_target_pairs={{0,8},{4,12},{8,0},{12,4},{1,9},{5,13},{9,1},{13,5},{2,10},{6,14},... | collective-permute-start | bytes 12296 | tf_op jit(solution)/shard_map/ppermute | solution.py:575
  35.3 0.0 collective-permute-done.7.second_late_ref
  35.3 1.3 %shard_map.83.refs_2_ = f32[9,96,128]{2,1,0:T(8,128)S(1)} custom-call(f32[28,8,128]{2,1,0:T(8,128)S(1)} %collective-permute-done.6.first_late_ref, f32[27,8,128]{2,1,0:T(8,128)S(1)} %collective-permute-done.7.second_late_ref, f32[9,96,128]{2,1,0:T(8,128)S(1)} %get-tuple-element.43.b_right_ref, f32[9,96,128]{2,1,0:T(8,128)S(1)} %get-tuple-element.44.b_down_ref, ...), custom_call_target="tpu_custom_call" | custom-call | flops 100000000 | bytes 10000000 | tf_op jit(solution)/shard_map/pallas_call | solution.py:682
  36.6 1.3 %shard_map.81.refs_0_ = f32[9,96,128]{2,1,0:T(8,128)S(1)} custom-call(f32[28,8,128]{2,1,0:T(8,128)S(1)} %collective-permute-done.6.first_late_ref, f32[27,8,128]{2,1,0:T(8,128)S(1)} %collective-permute-done.7.second_late_ref, f32[9,96,128]{2,1,0:T(8,128)S(1)} %get-tuple-element.43.b_right_ref, f32[9,96,128]{2,1,0:T(8,128)S(1)} %get-tuple-element.44.b_down_ref, ...), custom_call_target="tpu_custom_call" | custom-call | flops 100000000 | bytes 10000000 | tf_op jit(solution)/shard_map/pallas_call | solution.py:682
  37.9 0.7 %collective-permute-done.8 = f32[8,128]{1,0:T(8,128)S(1)} collective-permute-done((f32[8,128]{1,0:T(8,128)S(1)}, f32[8,128]{1,0:T(8,128)S(1)}, u32[]{:S(2)}, u32[]{:S(2)}) %collective-permute-start.8) | collective-permute-done | bytes 4128 | tf_op jit(solution)/shard_map/ppermute | solution.py:575
  38.6 0.0 collective-permute-start.11
  38.6 2.7 %collective-permute-start.10 = (f32[8,128]{1,0:T(8,128)S(1)}, f32[8,128]{1,0:T(8,128)S(1)}, u32[]{:S(2)}, u32[]{:S(2)}) collective-permute-start(f32[8,128]{1,0:T(8,128)S(1)} %add.16), channel_id=1, source_target_pairs={{0,2},{1,3},{2,0},{3,1},{4,6},{5,7},{6,4},{7,5},{8,10},{9,11},{10,... | collective-permute-start | bytes 12296 | tf_op jit(solution)/shard_map/ppermute | solution.py:575
  41.3 0.0 collective-permute-start.9
  41.3 1.3 %shard_map.82.refs_1_ = f32[9,96,128]{2,1,0:T(8,128)S(1)} custom-call(f32[28,8,128]{2,1,0:T(8,128)S(1)} %collective-permute-done.6.first_late_ref, f32[27,8,128]{2,1,0:T(8,128)S(1)} %collective-permute-done.7.second_late_ref, f32[9,96,128]{2,1,0:T(8,128)S(1)} %get-tuple-element.43.b_right_ref, f32[9,96,128]{2,1,0:T(8,128)S(1)} %get-tuple-element.44.b_down_ref, ...), custom_call_target="tpu_custom_call" | custom-call | flops 100000000 | bytes 10000000 | tf_op jit(solution)/shard_map/pallas_call | solution.py:682
  42.6 0.0 collective-permute-done.11
  42.6 0.3 collective-permute-done.10
  42.9 2.7 %shard_map.84 = (f32[3,64,1024]{2,1,0:T(8,128)}, f32[3,64,1024]{2,1,0:T(8,128)}, f32[3,64,1024]{2,1,0:T(8,128)}) custom-call(f32[8,128]{1,0:T(8,128)S(1)} %add_add_fusion.sums_ref, f32[9,96,128]{2,1,0:T(8,128)S(1)} %get-tuple-element.48.scale_ref, f32[9,96,128]{2,1,0:T(8,128)S(1)} %get-tuple-element.49.root_ref, ...), custom_call_target="tpu_custom_call" | custom-call | tf_op jit(solution)/shard_map/pallas_call | solution.py:703
  (4 shorter events, 0.0 us)
Async XLA Ops:
  2.3 15.8 %collective-permute-start.2 = (f32[6,8,16,128]{3,2,1,0:T(8,128)S(1)}, f32[6,8,16,128]{3,2,1,0:T(8,128)S(1)}, u32[]{:S(2)}, u32[]{:S(2)}) collective-permute-start(f32[6,8,16,128]{3,2,1,0:T(8,128)S(1)} %get-tuple-element.36), channel_id=1, source_target_pairs={{4,8},{8,4},{5,9},{9,5},{6,10},{10,6},{7,11},{11,7},{20,24},{24,20... | collective-permute-start | bytes 1179656 | tf_op jit(solution)/shard_map/ppermute | solution.py:633
  3.0 15.1 %collective-permute-start.3 = (f32[6,8,16,128]{3,2,1,0:T(8,128)S(1)}, f32[6,8,16,128]{3,2,1,0:T(8,128)S(1)}, u32[]{:S(2)}, u32[]{:S(2)}) collective-permute-start(f32[6,8,16,128]{3,2,1,0:T(8,128)S(1)} %get-tuple-element.37), channel_id=1, source_target_pairs={{0,4},{8,12},{4,0},{12,8},{1,5},{9,13},{5,1},{13,9},{2,6},{10,14},... | collective-permute-start | bytes 1179656 | tf_op jit(solution)/shard_map/ppermute | solution.py:633
  8.9 1.9 %collective-permute-start = (f32[2,64,128]{2,1,0:T(8,128)S(1)}, f32[2,64,128]{2,1,0:T(8,128)S(1)}, u32[]{:S(2)}, u32[]{:S(2)}) collective-permute-start(f32[2,64,128]{2,1,0:T(8,128)S(1)} %get-tuple-element.30), channel_id=1, source_target_pairs={{0,1},{2,3},{1,0},{3,2},{4,5},{6,7},{5,4},{7,6},{8,9},{10,11},{9,8... | collective-permute-start | bytes 196616 | tf_op jit(solution)/shard_map/ppermute | solution.py:633
  8.9 1.9 %collective-permute-start.1 = (f32[2,64,128]{2,1,0:T(8,128)S(1)}, f32[2,64,128]{2,1,0:T(8,128)S(1)}, u32[]{:S(2)}, u32[]{:S(2)}) collective-permute-start(f32[2,64,128]{2,1,0:T(8,128)S(1)} %get-tuple-element.31), channel_id=1, source_target_pairs={{1,2},{2,1},{5,6},{6,5},{9,10},{10,9},{13,14},{14,13},{17,18},{18,... | collective-permute-start | bytes 196616 | tf_op jit(solution)/shard_map/ppermute | solution.py:633
  10.9 3.3 %collective-permute-start.4 = (f32[2,2,16,128]{3,2,1,0:T(8,128)S(1)}, f32[2,2,16,128]{3,2,1,0:T(8,128)S(1)}, u32[]{:S(2)}, u32[]{:S(2)}) collective-permute-start(f32[2,2,16,128]{3,2,1,0:T(8,128)S(1)} %get-tuple-element.38), channel_id=1, source_target_pairs={{4,8},{8,4},{5,9},{9,5},{6,10},{10,6},{7,11},{11,7},{20,24},{24,20... | collective-permute-start | bytes 98312 | tf_op jit(solution)/shard_map/ppermute | solution.py:633
  11.5 6.5 %collective-permute-start.5 = (f32[2,2,16,128]{3,2,1,0:T(8,128)S(1)}, f32[2,2,16,128]{3,2,1,0:T(8,128)S(1)}, u32[]{:S(2)}, u32[]{:S(2)}) collective-permute-start(f32[2,2,16,128]{3,2,1,0:T(8,128)S(1)} %get-tuple-element.39), channel_id=1, source_target_pairs={{0,4},{8,12},{4,0},{12,8},{1,5},{9,13},{5,1},{13,9},{2,6},{10,14},... | collective-permute-start | bytes 98312 | tf_op jit(solution)/shard_map/ppermute | solution.py:633
  28.2 5.9 %collective-permute-start.6 = (f32[28,8,128]{2,1,0:T(8,128)S(1)}, f32[28,8,128]{2,1,0:T(8,128)S(1)}, u32[]{:S(2)}, u32[]{:S(2)}) collective-permute-start(f32[28,8,128]{2,1,0:T(8,128)S(1)} %get-tuple-element.41), channel_id=1, source_target_pairs={{0,4},{8,12},{4,0},{12,8},{1,5},{9,13},{5,1},{13,9},{2,6},{10,14},... | collective-permute-start | bytes 344072 | tf_op jit(solution)/shard_map/ppermute | solution.py:633
  30.0 5.3 %collective-permute-start.7 = (f32[27,8,128]{2,1,0:T(8,128)S(1)}, f32[27,8,128]{2,1,0:T(8,128)S(1)}, u32[]{:S(2)}, u32[]{:S(2)}) collective-permute-start(f32[27,8,128]{2,1,0:T(8,128)S(1)} %get-tuple-element.42), channel_id=1, source_target_pairs={{4,8},{8,4},{5,9},{9,5},{6,10},{10,6},{7,11},{11,7},{20,24},{24,20... | collective-permute-start | bytes 331784 | tf_op jit(solution)/shard_map/ppermute | solution.py:633
  34.1 4.5 %collective-permute-start.8 = (f32[8,128]{1,0:T(8,128)S(1)}, f32[8,128]{1,0:T(8,128)S(1)}, u32[]{:S(2)}, u32[]{:S(2)}) collective-permute-start(f32[8,128]{1,0:T(8,128)S(1)} %fusion), channel_id=1, source_target_pairs={{0,8},{4,12},{8,0},{12,4},{1,9},{5,13},{9,1},{13,5},{2,10},{6,14},... | collective-permute-start | bytes 12296 | tf_op jit(solution)/shard_map/ppermute | solution.py:575
  38.6 4.0 %collective-permute-start.11 = (f32[8,128]{1,0:T(8,128)S(1)}, f32[8,128]{1,0:T(8,128)S(1)}, u32[]{:S(2)}, u32[]{:S(2)}) collective-permute-start(f32[8,128]{1,0:T(8,128)S(1)} %add.16), channel_id=1, source_target_pairs={{0,3},{1,2},{2,1},{3,0},{4,7},{5,6},{6,5},{7,4},{8,11},{9,10},{10,... | collective-permute-start | bytes 12296 | tf_op jit(solution)/shard_map/ppermute | solution.py:575
  38.6 4.3 %collective-permute-start.10 = (f32[8,128]{1,0:T(8,128)S(1)}, f32[8,128]{1,0:T(8,128)S(1)}, u32[]{:S(2)}, u32[]{:S(2)}) collective-permute-start(f32[8,128]{1,0:T(8,128)S(1)} %add.16), channel_id=1, source_target_pairs={{0,2},{1,3},{2,0},{3,1},{4,6},{5,7},{6,4},{7,5},{8,10},{9,11},{10,... | collective-permute-start | bytes 12296 | tf_op jit(solution)/shard_map/ppermute | solution.py:575
  41.3 1.6 %collective-permute-start.9 = (f32[8,128]{1,0:T(8,128)S(1)}, f32[8,128]{1,0:T(8,128)S(1)}, u32[]{:S(2)}, u32[]{:S(2)}) collective-permute-start(f32[8,128]{1,0:T(8,128)S(1)} %add.16), channel_id=1, source_target_pairs={{0,1},{1,0},{2,3},{3,2},{4,5},{5,4},{6,7},{7,6},{8,9},{9,8},{10,11... | collective-permute-start | bytes 12296 | tf_op jit(solution)/shard_map/ppermute | solution.py:575

commit v17 on v16

--- a/solution.py
+++ b/solution.py
@@ -559,10 +559,11 @@
             if ways > 1:
                 value = permuted(value, matrix[:, :width], 2)
             for k in range(len(outs)):
-                done[c, k, :, g * LANES:g * LANES + width] = value[k * rows:(k + 1) * rows]
-        for k, ref in enumerate(outs):
-            copies.append(pltpu.make_async_copy(done.at[c, k], ref.at[c], sems.at[c, k]))
-            copies[-1].start()
+                columns = pl.ds(g * LANES, width)
+                done[c, k, :, columns] = value[k * rows:(k + 1) * rows]
+                there = outs[k].at[c, :, columns]
+                copies.append(pltpu.make_async_copy(done.at[c, k, :, columns], there, sems.at[c, k, g // ways]))
+                copies[-1].start()
     for copy in copies:
         copy.wait()
 
@@ -708,7 +709,7 @@
         scratch_shapes=[
             scratch(chans, 3, tiles, height, LANES),
             scratch(chans, 3, rows, cols),
-            pltpu.SemaphoreType.DMA((chans, 3)),
+            pltpu.SemaphoreType.DMA((chans, 3, -(-own_tiles // ways_of(tiles)))),
         ],
         compiler_params=params,
     )(total, scale, root, g0, z0, g1, f1, g2, *f2)

time: 46.3 us -> 46.4 us (level)
  no operation moved by 1% of the time
where the time goes in v17:
time: 46.4 us; the launch traced here: 45.7 us
  Pallas kernels  20.6 us (44%)
  starting transfers between devices  16.2 us (35%)
  waiting for transfers between devices  8.24 us (18%)
  between operations  0.75 us (2%)
    ppermute x8, starting transfers between devices, swap(): lax.ppermute((first, second)[k], axis, pairs[k])  12.2 us
    pallas_call x1, Pallas kernels, per_device(): pl.pallas_call(first_kernel, out_shape=[plane] * 4 + [field] * 5 + [shape...  10.1 us
    ppermute x8, waiting for transfers between devices, swap(): lax.ppermute((first, second)[k], axis, pairs[k])  7.28 us
    ppermute x4, starting transfers between devices, sum_over(): lax.ppermute(value, axis, [(i, i ^ mask) for i in range(size)])  3.95 us
    pallas_call x3, Pallas kernels, per_device(): pl.pallas_call(functools.partial(second_kernel, c), out_shape=plane, in_s...  3.86 us
    pallas_call x1, Pallas kernels, per_device(): pl.pallas_call(third_kernel, out_shape=[shaped(chans, rows, cols)] * 3, i...  2.83 us
    pallas_call x1, Pallas kernels, per_device(): pl.pallas_call(own_kernel, out_shape=[shaped(planes, own_tiles, rows, LAN...  1.63 us
    pallas_call x1, Pallas kernels, per_device(): pl.pallas_call(inner_dealt_kernel, out_shape=shaped(planes, tiles - ways,...  1.25 us
  transfers between devices with their start and end apart: 12, of which 4 were waited for; matrix products, arithmetic and copies ran while one was open for 0% of the time, Pallas kernels for 13%

profile of v17, /device:TPU:0, one launch (start us, length us, event | category | flops | bytes accessed | tf_op | source)
XLA Modules:
  0.0 45.7 jit_solution(6098570447973442388)
XLA Ops:
  0.6 1.6 %shard_map.76 = (f32[6,8,64,128]{3,2,1,0:T(8,128)S(1)}, f32[6,8,16,128]{3,2,1,0:T(8,128)S(1)}, f32[6,8,16,128]{3,2,1,0:T(8,128)S(1)}, f32[2,64,128]{2,1,0:T(8,128)S(1)}, f32[2,64,128]{2,1,0:T(8,128)S(1)}) custom-call(s32[3,1,16]{2,1,0:T(1,128)} %bitcast.5, f32[3,64,1024]{2,1,0:T(8,128)} %src_hbm.1, f32[64,1024]{1,0:T(8,128)} %weight_hbm.1, ...), custom_call_target="tpu_custom_call" | custom-call | tf_op jit(solution)/shard_map/pallas_call | solution.py:607
  2.3 0.7 %collective-permute-start.2 = (f32[6,8,16,128]{3,2,1,0:T(8,128)S(1)}, f32[6,8,16,128]{3,2,1,0:T(8,128)S(1)}, u32[]{:S(2)}, u32[]{:S(2)}) collective-permute-start(f32[6,8,16,128]{3,2,1,0:T(8,128)S(1)} %get-tuple-element.36), channel_id=1, source_target_pairs={{4,8},{8,4},{5,9},{9,5},{6,10},{10,6},{7,11},{11,7},{20,24},{24,20... | collective-permute-start | bytes 1179656 | tf_op jit(solution)/shard_map/ppermute | solution.py:634
  3.0 5.9 %collective-permute-start.3 = (f32[6,8,16,128]{3,2,1,0:T(8,128)S(1)}, f32[6,8,16,128]{3,2,1,0:T(8,128)S(1)}, u32[]{:S(2)}, u32[]{:S(2)}) collective-permute-start(f32[6,8,16,128]{3,2,1,0:T(8,128)S(1)} %get-tuple-element.37), channel_id=1, source_target_pairs={{0,4},{8,12},{4,0},{12,8},{1,5},{9,13},{5,1},{13,9},{2,6},{10,14},... | collective-permute-start | bytes 1179656 | tf_op jit(solution)/shard_map/ppermute | solution.py:634
  8.9 0.0 collective-permute-start
  8.9 0.7 %collective-permute-start.1 = (f32[2,64,128]{2,1,0:T(8,128)S(1)}, f32[2,64,128]{2,1,0:T(8,128)S(1)}, u32[]{:S(2)}, u32[]{:S(2)}) collective-permute-start(f32[2,64,128]{2,1,0:T(8,128)S(1)} %get-tuple-element.31), channel_id=1, source_target_pairs={{1,2},{2,1},{5,6},{6,5},{9,10},{10,9},{13,14},{14,13},{17,18},{18,... | collective-permute-start | bytes 196616 | tf_op jit(solution)/shard_map/ppermute | solution.py:634
  9.5 1.3 %shard_map.77.inner_ref = f32[6,6,64,128]{3,2,1,0:T(8,128)S(1)} custom-call(f32[6,8,64,128]{3,2,1,0:T(8,128)S(1)} %get-tuple-element.32.own_ref), custom_call_target="tpu_custom_call" | custom-call | flops 100000000 | bytes 4000000 | tf_op jit(solution)/shard_map/pallas_call | solution.py:638
  10.8 0.0 collective-permute-done.first_ref
  10.8 0.0 collective-permute-done.1.second_ref
  10.8 0.1 shard_map.79
  10.9 0.7 %collective-permute-start.4 = (f32[2,2,16,128]{3,2,1,0:T(8,128)S(1)}, f32[2,2,16,128]{3,2,1,0:T(8,128)S(1)}, u32[]{:S(2)}, u32[]{:S(2)}) collective-permute-start(f32[2,2,16,128]{3,2,1,0:T(8,128)S(1)} %get-tuple-element.38), channel_id=1, source_target_pairs={{4,8},{8,4},{5,9},{9,5},{6,10},{10,6},{7,11},{11,7},{20,24},{24,20... | collective-permute-start | bytes 98312 | tf_op jit(solution)/shard_map/ppermute | solution.py:634
  11.5 1.9 %collective-permute-start.5 = (f32[2,2,16,128]{3,2,1,0:T(8,128)S(1)}, f32[2,2,16,128]{3,2,1,0:T(8,128)S(1)}, u32[]{:S(2)}, u32[]{:S(2)}) collective-permute-start(f32[2,2,16,128]{3,2,1,0:T(8,128)S(1)} %get-tuple-element.39), channel_id=1, source_target_pairs={{0,4},{8,12},{4,0},{12,8},{1,5},{9,13},{5,1},{13,9},{2,6},{10,14},... | collective-permute-start | bytes 98312 | tf_op jit(solution)/shard_map/ppermute | solution.py:634
  13.4 0.8 %shard_map.78.outer_ref = f32[6,3,64,128]{3,2,1,0:T(8,128)S(1)} custom-call(f32[6,8,64,128]{3,2,1,0:T(8,128)S(1)} %get-tuple-element.32.own_ref, f32[2,64,128]{2,1,0:T(8,128)S(1)} %collective-permute-done.first_ref, f32[2,64,128]{2,1,0:T(8,128)S(1)} %collective-permute-done.1.second_ref), custom_call_target="tpu_custom_call" | custom-call | flops 100000000 | bytes 2000000 | tf_op jit(solution)/shard_map/pallas_call | solution.py:657
  14.2 0.0 collective-permute-done.4.second_corners_ref
  14.2 3.9 %collective-permute-done.5.first_corners_ref = f32[2,2,16,128]{3,2,1,0:T(8,128)S(1)} collective-permute-done((f32[2,2,16,128]{3,2,1,0:T(8,128)S(1)}, f32[2,2,16,128]{3,2,1,0:T(8,128)S(1)}, u32[]{:S(2)}, u32[]{:S(2)}) %collective-permute-start.5) | collective-permute-done | bytes 32800 | tf_op jit(solution)/shard_map/ppermute | solution.py:634
  18.0 0.0 collective-permute-done.2.second_rows_ref
  18.0 0.0 collective-permute-done.3.first_rows_ref
  18.0 10.1 %shard_map.80 = (f32[9,96,128]{2,1,0:T(8,128)S(1)}, f32[9,96,128]{2,1,0:T(8,128)S(1)}, f32[9,96,128]{2,1,0:T(8,128)S(1)}, f32[9,96,128]{2,1,0:T(8,128)S(1)}, f32...) custom-call(f32[6,6,64,128]{3,2,1,0:T(8,128)S(1)} %shard_map.77.inne, ...), custom_call_target="tpu_custom_call" | custom-call | tf_op jit(solution)/shard_map/pallas_call | solution.py:670
  28.2 1.8 %collective-permute-start.6 = (f32[28,8,128]{2,1,0:T(8,128)S(1)}, f32[28,8,128]{2,1,0:T(8,128)S(1)}, u32[]{:S(2)}, u32[]{:S(2)}) collective-permute-start(f32[28,8,128]{2,1,0:T(8,128)S(1)} %get-tuple-element.41), channel_id=1, source_target_pairs={{0,4},{8,12},{4,0},{12,8},{1,5},{9,13},{5,1},{13,9},{2,6},{10,14},... | collective-permute-start | bytes 344072 | tf_op jit(solution)/shard_map/ppermute | solution.py:634
  30.0 0.7 %collective-permute-start.7 = (f32[27,8,128]{2,1,0:T(8,128)S(1)}, f32[27,8,128]{2,1,0:T(8,128)S(1)}, u32[]{:S(2)}, u32[]{:S(2)}) collective-permute-start(f32[27,8,128]{2,1,0:T(8,128)S(1)} %get-tuple-element.42), channel_id=1, source_target_pairs={{4,8},{8,4},{5,9},{9,5},{6,10},{10,6},{7,11},{11,7},{20,24},{24,20... | collective-permute-start | bytes 331784 | tf_op jit(solution)/shard_map/ppermute | solution.py:634
  30.7 3.4 %collective-permute-done.6.first_late_ref = f32[28,8,128]{2,1,0:T(8,128)S(1)} collective-permute-done((f32[28,8,128]{2,1,0:T(8,128)S(1)}, f32[28,8,128]{2,1,0:T(8,128)S(1)}, u32[]{:S(2)}, u32[]{:S(2)}) %collective-permute-start.6) | collective-permute-done | bytes 114720 | tf_op jit(solution)/shard_map/ppermute | solution.py:634
  34.1 1.2 %collective-permute-start.8 = (f32[8,128]{1,0:T(8,128)S(1)}, f32[8,128]{1,0:T(8,128)S(1)}, u32[]{:S(2)}, u32[]{:S(2)}) collective-permute-start(f32[8,128]{1,0:T(8,128)S(1)} %fusion), channel_id=1, source_target_pairs={{0,8},{4,12},{8,0},{12,4},{1,9},{5,13},{9,1},{13,5},{2,10},{6,14},... | collective-permute-start | bytes 12296 | tf_op jit(solution)/shard_map/ppermute | solution.py:576
  35.3 1.3 %shard_map.83.refs_2_ = f32[9,96,128]{2,1,0:T(8,128)S(1)} custom-call(f32[28,8,128]{2,1,0:T(8,128)S(1)} %collective-permute-done.6.first_late_ref, f32[27,8,128]{2,1,0:T(8,128)S(1)} %collective-permute-done.7.second_late_ref, f32[9,96,128]{2,1,0:T(8,128)S(1)} %get-tuple-element.43.b_right_ref, f32[9,96,128]{2,1,0:T(8,128)S(1)} %get-tuple-element.44.b_down_ref, ...), custom_call_target="tpu_custom_call" | custom-call | flops 100000000 | bytes 10000000 | tf_op jit(solution)/shard_map/pallas_call | solution.py:683
  36.6 1.3 %shard_map.81.refs_0_ = f32[9,96,128]{2,1,0:T(8,128)S(1)} custom-call(f32[28,8,128]{2,1,0:T(8,128)S(1)} %collective-permute-done.6.first_late_ref, f32[27,8,128]{2,1,0:T(8,128)S(1)} %collective-permute-done.7.second_late_ref, f32[9,96,128]{2,1,0:T(8,128)S(1)} %get-tuple-element.43.b_right_ref, f32[9,96,128]{2,1,0:T(8,128)S(1)} %get-tuple-element.44.b_down_ref, ...), custom_call_target="tpu_custom_call" | custom-call | flops 100000000 | bytes 10000000 | tf_op jit(solution)/shard_map/pallas_call | solution.py:683
  37.9 0.7 %collective-permute-done.8 = f32[8,128]{1,0:T(8,128)S(1)} collective-permute-done((f32[8,128]{1,0:T(8,128)S(1)}, f32[8,128]{1,0:T(8,128)S(1)}, u32[]{:S(2)}, u32[]{:S(2)}) %collective-permute-start.8) | collective-permute-done | bytes 4128 | tf_op jit(solution)/shard_map/ppermute | solution.py:576
  38.6 0.0 collective-permute-start.11
  38.6 2.7 %collective-permute-start.10 = (f32[8,128]{1,0:T(8,128)S(1)}, f32[8,128]{1,0:T(8,128)S(1)}, u32[]{:S(2)}, u32[]{:S(2)}) collective-permute-start(f32[8,128]{1,0:T(8,128)S(1)} %add.16), channel_id=1, source_target_pairs={{0,2},{1,3},{2,0},{3,1},{4,6},{5,7},{6,4},{7,5},{8,10},{9,11},{10,... | collective-permute-start | bytes 12296 | tf_op jit(solution)/shard_map/ppermute | solution.py:576
  41.3 0.0 collective-permute-start.9
  41.3 1.3 %shard_map.82.refs_1_ = f32[9,96,128]{2,1,0:T(8,128)S(1)} custom-call(f32[28,8,128]{2,1,0:T(8,128)S(1)} %collective-permute-done.6.first_late_ref, f32[27,8,128]{2,1,0:T(8,128)S(1)} %collective-permute-done.7.second_late_ref, f32[9,96,128]{2,1,0:T(8,128)S(1)} %get-tuple-element.43.b_right_ref, f32[9,96,128]{2,1,0:T(8,128)S(1)} %get-tuple-element.44.b_down_ref, ...), custom_call_target="tpu_custom_call" | custom-call | flops 100000000 | bytes 10000000 | tf_op jit(solution)/shard_map/pallas_call | solution.py:683
  42.6 0.0 collective-permute-done.11
  42.6 0.3 collective-permute-done.10
  42.9 0.0 collective-permute-done.9
  42.9 2.8 %shard_map.84 = (f32[3,64,1024]{2,1,0:T(8,128)}, f32[3,64,1024]{2,1,0:T(8,128)}, f32[3,64,1024]{2,1,0:T(8,128)}) custom-call(f32[8,128]{1,0:T(8,128)S(1)} %add_add_fusion.sums_ref, f32[9,96,128]{2,1,0:T(8,128)S(1)} %get-tuple-element.48.scale_ref, f32[9,96,128]{2,1,0:T(8,128)S(1)} %get-tuple-element.49.root_ref, ...), custom_call_target="tpu_custom_call" | custom-call | tf_op jit(solution)/shard_map/pallas_call | solution.py:704
  (4 shorter events, 0.0 us)
Async XLA Ops:
  2.3 15.8 %collective-permute-start.2 = (f32[6,8,16,128]{3,2,1,0:T(8,128)S(1)}, f32[6,8,16,128]{3,2,1,0:T(8,128)S(1)}, u32[]{:S(2)}, u32[]{:S(2)}) collective-permute-start(f32[6,8,16,128]{3,2,1,0:T(8,128)S(1)} %get-tuple-element.36), channel_id=1, source_target_pairs={{4,8},{8,4},{5,9},{9,5},{6,10},{10,6},{7,11},{11,7},{20,24},{24,20... | collective-permute-start | bytes 1179656 | tf_op jit(solution)/shard_map/ppermute | solution.py:634
  3.0 15.1 %collective-permute-start.3 = (f32[6,8,16,128]{3,2,1,0:T(8,128)S(1)}, f32[6,8,16,128]{3,2,1,0:T(8,128)S(1)}, u32[]{:S(2)}, u32[]{:S(2)}) collective-permute-start(f32[6,8,16,128]{3,2,1,0:T(8,128)S(1)} %get-tuple-element.37), channel_id=1, source_target_pairs={{0,4},{8,12},{4,0},{12,8},{1,5},{9,13},{5,1},{13,9},{2,6},{10,14},... | collective-permute-start | bytes 1179656 | tf_op jit(solution)/shard_map/ppermute | solution.py:634
  8.9 1.9 %collective-permute-start = (f32[2,64,128]{2,1,0:T(8,128)S(1)}, f32[2,64,128]{2,1,0:T(8,128)S(1)}, u32[]{:S(2)}, u32[]{:S(2)}) collective-permute-start(f32[2,64,128]{2,1,0:T(8,128)S(1)} %get-tuple-element.30), channel_id=1, source_target_pairs={{0,1},{2,3},{1,0},{3,2},{4,5},{6,7},{5,4},{7,6},{8,9},{10,11},{9,8... | collective-permute-start | bytes 196616 | tf_op jit(solution)/shard_map/ppermute | solution.py:634
  8.9 1.9 %collective-permute-start.1 = (f32[2,64,128]{2,1,0:T(8,128)S(1)}, f32[2,64,128]{2,1,0:T(8,128)S(1)}, u32[]{:S(2)}, u32[]{:S(2)}) collective-permute-start(f32[2,64,128]{2,1,0:T(8,128)S(1)} %get-tuple-element.31), channel_id=1, source_target_pairs={{1,2},{2,1},{5,6},{6,5},{9,10},{10,9},{13,14},{14,13},{17,18},{18,... | collective-permute-start | bytes 196616 | tf_op jit(solution)/shard_map/ppermute | solution.py:634
  10.9 3.3 %collective-permute-start.4 = (f32[2,2,16,128]{3,2,1,0:T(8,128)S(1)}, f32[2,2,16,128]{3,2,1,0:T(8,128)S(1)}, u32[]{:S(2)}, u32[]{:S(2)}) collective-permute-start(f32[2,2,16,128]{3,2,1,0:T(8,128)S(1)} %get-tuple-element.38), channel_id=1, source_target_pairs={{4,8},{8,4},{5,9},{9,5},{6,10},{10,6},{7,11},{11,7},{20,24},{24,20... | collective-permute-start | bytes 98312 | tf_op jit(solution)/shard_map/ppermute | solution.py:634
  11.5 6.5 %collective-permute-start.5 = (f32[2,2,16,128]{3,2,1,0:T(8,128)S(1)}, f32[2,2,16,128]{3,2,1,0:T(8,128)S(1)}, u32[]{:S(2)}, u32[]{:S(2)}) collective-permute-start(f32[2,2,16,128]{3,2,1,0:T(8,128)S(1)} %get-tuple-element.39), channel_id=1, source_target_pairs={{0,4},{8,12},{4,0},{12,8},{1,5},{9,13},{5,1},{13,9},{2,6},{10,14},... | collective-permute-start | bytes 98312 | tf_op jit(solution)/shard_map/ppermute | solution.py:634
  28.2 5.9 %collective-permute-start.6 = (f32[28,8,128]{2,1,0:T(8,128)S(1)}, f32[28,8,128]{2,1,0:T(8,128)S(1)}, u32[]{:S(2)}, u32[]{:S(2)}) collective-permute-start(f32[28,8,128]{2,1,0:T(8,128)S(1)} %get-tuple-element.41), channel_id=1, source_target_pairs={{0,4},{8,12},{4,0},{12,8},{1,5},{9,13},{5,1},{13,9},{2,6},{10,14},... | collective-permute-start | bytes 344072 | tf_op jit(solution)/shard_map/ppermute | solution.py:634
  30.0 5.3 %collective-permute-start.7 = (f32[27,8,128]{2,1,0:T(8,128)S(1)}, f32[27,8,128]{2,1,0:T(8,128)S(1)}, u32[]{:S(2)}, u32[]{:S(2)}) collective-permute-start(f32[27,8,128]{2,1,0:T(8,128)S(1)} %get-tuple-element.42), channel_id=1, source_target_pairs={{4,8},{8,4},{5,9},{9,5},{6,10},{10,6},{7,11},{11,7},{20,24},{24,20... | collective-permute-start | bytes 331784 | tf_op jit(solution)/shard_map/ppermute | solution.py:634
  34.1 4.5 %collective-permute-start.8 = (f32[8,128]{1,0:T(8,128)S(1)}, f32[8,128]{1,0:T(8,128)S(1)}, u32[]{:S(2)}, u32[]{:S(2)}) collective-permute-start(f32[8,128]{1,0:T(8,128)S(1)} %fusion), channel_id=1, source_target_pairs={{0,8},{4,12},{8,0},{12,4},{1,9},{5,13},{9,1},{13,5},{2,10},{6,14},... | collective-permute-start | bytes 12296 | tf_op jit(solution)/shard_map/ppermute | solution.py:576
  38.6 4.0 %collective-permute-start.11 = (f32[8,128]{1,0:T(8,128)S(1)}, f32[8,128]{1,0:T(8,128)S(1)}, u32[]{:S(2)}, u32[]{:S(2)}) collective-permute-start(f32[8,128]{1,0:T(8,128)S(1)} %add.16), channel_id=1, source_target_pairs={{0,3},{1,2},{2,1},{3,0},{4,7},{5,6},{6,5},{7,4},{8,11},{9,10},{10,... | collective-permute-start | bytes 12296 | tf_op jit(solution)/shard_map/ppermute | solution.py:576
  38.6 4.3 %collective-permute-start.10 = (f32[8,128]{1,0:T(8,128)S(1)}, f32[8,128]{1,0:T(8,128)S(1)}, u32[]{:S(2)}, u32[]{:S(2)}) collective-permute-start(f32[8,128]{1,0:T(8,128)S(1)} %add.16), channel_id=1, source_target_pairs={{0,2},{1,3},{2,0},{3,1},{4,6},{5,7},{6,4},{7,5},{8,10},{9,11},{10,... | collective-permute-start | bytes 12296 | tf_op jit(solution)/shard_map/ppermute | solution.py:576
  41.3 1.6 %collective-permute-start.9 = (f32[8,128]{1,0:T(8,128)S(1)}, f32[8,128]{1,0:T(8,128)S(1)}, u32[]{:S(2)}, u32[]{:S(2)}) collective-permute-start(f32[8,128]{1,0:T(8,128)S(1)} %add.16), channel_id=1, source_target_pairs={{0,1},{1,0},{2,3},{3,2},{4,5},{5,4},{6,7},{7,6},{8,9},{9,8},{10,11... | collective-permute-start | bytes 12296 | tf_op jit(solution)/shard_map/ppermute | solution.py:576
